TPU v7x, 32 devices: a whole 2x2x4 slice. The times are simulated.
32 devices in a mesh: dp: 4 (over x, core), ep: 2 (over y), tp: 4 (over z).
Axes of the slice: x: 2, y: 2, z: 4, core: 2. Of those that a mesh axis runs over, the one named last changes fastest.
Arguments:
- tokens: bfloat16 [4096, 2048], P(('dp', 'ep'), 'tp'), may hold values from -6 to 6
- norm_attn: bfloat16 [2048], P('tp'), may hold values from 0.5 to 1.5
- w_query: bfloat16 [2048, 2048], P(None, 'tp'), may hold values from -0.125 to 0.125
- w_key: bfloat16 [2048, 2048], P(None, 'tp'), may hold values from -0.125 to 0.125
- w_value: bfloat16 [2048, 2048], P(None, 'tp'), may hold values from -0.125 to 0.125
- w_output: bfloat16 [2048, 2048], P('tp'), may hold values from -2 to 2
- norm_ffn: bfloat16 [2048], P('tp'), may hold values from 0.5 to 1.5
- w_router: bfloat16 [2048, 8], replicated, may hold values from -0.0625 to 0.0625
- shared_switch: bfloat16 [2048], replicated, may hold values from -0.125 to 0.125
- shared_gate: bfloat16 [2048, 5632], P(None, 'tp'), may hold values from -0.125 to 0.125
- shared_up: bfloat16 [2048, 5632], P(None, 'tp'), may hold values from -0.125 to 0.125
- shared_down: bfloat16 [5632, 2048], P('tp'), may hold values from -0.15625 to 0.15625
- expert_gate: bfloat16 [8, 2048, 1408], P('ep', None, 'tp'), may hold values from -0.125 to 0.125
- expert_up: bfloat16 [8, 2048, 1408], P('ep', None, 'tp'), may hold values from -0.125 to 0.125
- expert_down: bfloat16 [8, 1408, 2048], P('ep', 'tp'), may hold values from -0.625 to 0.625
- routes: int32 [4096, 4], P(('dp', 'ep')), may hold values from 0 to 7, all different within a row; in each aligned block of 512 rows (0 to 511, 512 to 1023, ...) at most 320 rows name the same one
- segments: int32 [4096], P('dp'), may hold values from 0 to 4, as said below
- output_gradient: bfloat16 [4096, 2048], P(('dp', 'ep'), 'tp'), may hold values from -6 to 6
Outputs:
- layer_out: bfloat16 [4096, 2048], P(('dp', 'ep'), 'tp')
- tokens_grad: float32 [4096, 2048], P(('dp', 'ep'), 'tp')
- norm_attn_grad: float32 [2048], P('tp')
- w_query_grad: float32 [2048, 2048], P(None, 'tp')
- w_key_grad: float32 [2048, 2048], P(None, 'tp')
- w_value_grad: float32 [2048, 2048], P(None, 'tp')
- w_output_grad: float32 [2048, 2048], P('tp')
- norm_ffn_grad: float32 [2048], P('tp')
- w_router_grad: float32 [2048, 8], replicated
- shared_switch_grad: float32 [2048], replicated
- shared_gate_grad: float32 [2048, 5632], P(None, 'tp')
- shared_up_grad: float32 [2048, 5632], P(None, 'tp')
- shared_down_grad: float32 [5632, 2048], P('tp')
- expert_gate_grad: float32 [8, 2048, 1408], P('ep', None, 'tp')
- expert_up_grad: float32 [8, 2048, 1408], P('ep', None, 'tp')
- expert_down_grad: float32 [8, 1408, 2048], P('ep', 'tp')
Inputs may be any that keep to these rules, and one draw needn't show every extreme that they name: `routes`: in the rows of one device no expert is named by more than 320 rows. `segments`: within each sequence of 1024 tokens the ids never fall and start at 0; each sequence holds five documents.
All inputs are finite; a program needn't handle non-finite values.
Results may differ from a plain program's by a relative error of at most 0.02.
Values may be sent and summed in bfloat16 or wider, within the bound.
A program may use at most 448 MiB of HBM per device.

v0:
```python
import math

import jax
import jax.numpy as jnp
from jax import lax
from jax.sharding import PartitionSpec as P

HD = 128


EPS = 1e-06
ROPE_BASE = 1000000.0
NEG = -1e30


def from_behind(shard, axis, by):
    count = lax.axis_size(axis)
    pairs = [(i, i + by) for i in range(count) if 0 <= i + by < count]
    return lax.ppermute(shard, axis, pairs)


def rope_tables(positions, feat_width):
    half_width = feat_width // 2
    inv_freq = ROPE_BASE ** (-(jnp.arange(half_width, dtype=jnp.float32) * 2.0) / feat_width)
    angles = positions.astype(jnp.float32)[:, None] * inv_freq[None, :]
    return (jnp.cos(angles), jnp.sin(angles))


def rotate(tensor, cos_table, sin_table):
    half_width = tensor.shape[-1] // 2
    first_half = tensor[..., :half_width]
    second_half = tensor[..., half_width:]
    cos_b = cos_table[:, None, :]
    sin_b = sin_table[:, None, :]
    return jnp.concatenate(
        [first_half * cos_b - second_half * sin_b, second_half * cos_b + first_half * sin_b],
        axis=-1,
    )


def silu_parts(pre_act):
    sigmoid_val = jax.nn.sigmoid(pre_act)
    return (pre_act * sigmoid_val, sigmoid_val * (1.0 + pre_act * (1.0 - sigmoid_val)))


def expert_forward(inputs, gate_w, up_w, down_w):
    gate_pre = jnp.einsum("send,edf->senf", inputs, gate_w, preferred_element_type=jnp.float32)
    up_pre = jnp.einsum("send,edf->senf", inputs, up_w, preferred_element_type=jnp.float32)
    hidden = (silu_parts(gate_pre)[0] * up_pre).astype(jnp.bfloat16)
    return jnp.einsum("senf,efd->send", hidden, down_w, preferred_element_type=jnp.float32)


def routed_expert_pullback(inputs, grad_out, gate_w, up_w, down_w):
    gate_pre = jnp.einsum("send,edf->senf", inputs, gate_w, preferred_element_type=jnp.float32)
    up_pre = jnp.einsum("send,edf->senf", inputs, up_w, preferred_element_type=jnp.float32)
    activ, slope = silu_parts(gate_pre)
    hidden = (activ * up_pre).astype(jnp.bfloat16)
    grad_hidden = jnp.einsum("send,efd->senf", grad_out, down_w, preferred_element_type=jnp.float32)
    grad_gate = (grad_hidden * up_pre * slope).astype(jnp.bfloat16)
    grad_upper = (grad_hidden * activ).astype(jnp.bfloat16)
    grad_down_w = jnp.einsum("senf,send->efd", hidden, grad_out, preferred_element_type=jnp.float32)
    grad_gate_w = jnp.einsum(
        "send,senf->edf", inputs, grad_gate, preferred_element_type=jnp.float32
    )
    grad_up_w = jnp.einsum("send,senf->edf", inputs, grad_upper, preferred_element_type=jnp.float32)
    input_gradient_rows = jnp.einsum(
        "senf,edf->send", grad_gate, gate_w, preferred_element_type=jnp.float32
    ) + jnp.einsum("senf,edf->send", grad_upper, up_w, preferred_element_type=jnp.float32)
    return (input_gradient_rows, grad_gate_w, grad_up_w, grad_down_w)


def body(
    tokens,
    norm_attn,
    w_query,
    w_key,
    w_value,
    w_output,
    norm_ffn,
    w_router,
    shared_switch,
    shared_gate,
    shared_up,
    shared_down,
    expert_gate,
    expert_up,
    expert_down,
    routes,
    segments,
    output_gradient,
):
    tp_count = lax.axis_size("tp")
    ep_count = lax.axis_size("ep")
    tp_rank = lax.axis_index("tp")
    ep_rank = lax.axis_index("ep")
    tok_rows = tokens.shape[0]
    width_own = tokens.shape[1]
    width_all = width_own * tp_count
    heads_own = w_query.shape[1] // HD
    top_count = routes.shape[1]
    experts_own = expert_gate.shape[0]
    experts_all = experts_own * ep_count
    capacity = tok_rows * top_count * 5 // (4 * experts_all)
    q_block = min(512, tok_rows)
    block_count = tok_rows // q_block
    score_scale = 1.0 / math.sqrt(HD)

    def to_owner(payload):
        return lax.all_to_all(payload, "ep", split_axis=0, concat_axis=1, tiled=True)

    def to_source(payload):
        return lax.all_to_all(payload, "ep", split_axis=1, concat_axis=0, tiled=True)

    gathered = (
        lax.all_gather(tokens, "tp", axis=1, tiled=True),
        lax.all_gather(norm_attn.reshape(1, width_own), "tp", axis=1, tiled=True),
        lax.all_gather(norm_ffn.reshape(1, width_own), "tp", axis=1, tiled=True),
        lax.all_gather(output_gradient, "tp", axis=1, tiled=True),
    )
    x_full = gathered[0].astype(jnp.float32)
    gain_one = gathered[1][0].astype(jnp.float32)
    gain_two = gathered[2][0].astype(jnp.float32)
    grad_full = gathered[3].astype(jnp.float32)
    inv_one = lax.rsqrt(jnp.mean(x_full * x_full, axis=1, keepdims=True) + EPS)
    normed = (x_full * inv_one * gain_one).astype(jnp.bfloat16)
    q_pre = jnp.dot(normed, w_query, preferred_element_type=jnp.float32)
    k_pre = jnp.dot(normed, w_key, preferred_element_type=jnp.float32)
    v_pre = jnp.dot(normed, w_value, preferred_element_type=jnp.float32)
    positions = ep_rank * tok_rows + jnp.arange(tok_rows, dtype=jnp.int32)
    cos_table, sin_table = rope_tables(positions, HD)
    query = rotate(q_pre.reshape(tok_rows, heads_own, HD), cos_table, sin_table).astype(
        jnp.bfloat16
    )
    key_own = rotate(k_pre.reshape(tok_rows, heads_own, HD), cos_table, sin_table).astype(
        jnp.bfloat16
    )
    value_own = v_pre.astype(jnp.bfloat16).reshape(tok_rows, heads_own, HD)
    earlier = from_behind(jnp.stack([key_own, value_own]), "ep", 1)
    key_rows = jnp.concatenate([earlier[0], key_own], axis=0)
    value_rows = jnp.concatenate([earlier[1], value_own], axis=0)
    key_pos = (ep_rank - 1) * tok_rows + jnp.arange(2 * tok_rows, dtype=jnp.int32)
    key_seg = jnp.where(key_pos >= 0, jnp.take(segments, jnp.maximum(key_pos, 0)), -1)
    query_seg = lax.dynamic_slice_in_dim(segments, ep_rank * tok_rows, tok_rows, 0)

    def block_scores(blk_start):
        piece_pos = ep_rank * tok_rows + blk_start + jnp.arange(q_block, dtype=jnp.int32)
        allowed = (query_seg[:, None] == key_seg[None, :]) & (
            key_pos[None, :] <= piece_pos[:, None]
        )
        scores = (
            jnp.einsum("qhd,khd->hqk", query, key_rows, preferred_element_type=jnp.float32)
            * score_scale
        )
        return (query, jnp.where(allowed[None], scores, NEG))

    def block_forward(blk_start):
        q_piece, scores = block_scores(blk_start)
        row_top = jnp.max(scores, axis=2, keepdims=True)
        shifted_exp = jnp.exp(scores - row_top)
        row_total = jnp.sum(shifted_exp, axis=2, keepdims=True)
        weights = (shifted_exp / row_total).astype(jnp.bfloat16)
        result_rows = jnp.einsum(
            "hqk,khd->qhd", weights, value_rows, preferred_element_type=jnp.float32
        )
        return (result_rows.astype(jnp.bfloat16), row_top[:, :, 0] + jnp.log(row_total[:, :, 0]))

    starts = jnp.arange(block_count, dtype=jnp.int32) * q_block
    attended, log_norm = lax.map(block_forward, starts)
    attn_rows = attended.reshape(tok_rows, heads_own * HD)
    attn_total = lax.psum(jnp.dot(attn_rows, w_output, preferred_element_type=jnp.float32), "tp")
    resid = x_full + attn_total
    inv_two = lax.rsqrt(jnp.mean(resid * resid, axis=1, keepdims=True) + EPS)
    mixed = (resid * inv_two * gain_two).astype(jnp.bfloat16)
    router_prob = jax.nn.softmax(
        jnp.dot(mixed, w_router, preferred_element_type=jnp.float32), axis=1
    )
    route_hot = (
        routes[:, :, None] == jnp.arange(experts_all, dtype=jnp.int32)[None, None, :]
    ).astype(jnp.float32)
    gates = jnp.sum(route_hot * router_prob[:, None, :], axis=2)
    switch = jax.nn.sigmoid(jnp.dot(mixed, shared_switch, preferred_element_type=jnp.float32))
    gate_shared = jnp.dot(mixed, shared_gate, preferred_element_type=jnp.float32)
    up_shared = jnp.dot(mixed, shared_up, preferred_element_type=jnp.float32)
    act_shared, slope_shared = silu_parts(gate_shared)
    hidden_shared = (act_shared * up_shared).astype(jnp.bfloat16)
    partial_shared = jnp.dot(hidden_shared, shared_down, preferred_element_type=jnp.float32)
    flat_routes = routes.reshape(tok_rows * top_count)
    flat_hot = (flat_routes[:, None] == jnp.arange(experts_all, dtype=jnp.int32)[None, :]).astype(
        jnp.int32
    )
    slot_index = jnp.sum((jnp.cumsum(flat_hot, axis=0) - flat_hot) * flat_hot, axis=1)
    slot_place = flat_routes * capacity + slot_index
    owner_rows = (
        jnp.full((experts_all * capacity,), tok_rows * top_count, jnp.int32)
        .at[slot_place]
        .set(jnp.arange(tok_rows * top_count, dtype=jnp.int32))
    )
    mixed_pad = jnp.concatenate([mixed, jnp.zeros((1, width_all), jnp.bfloat16)], axis=0)
    send_rows = jnp.take(mixed_pad, owner_rows // top_count, axis=0)
    expert_in = to_owner(send_rows.reshape(ep_count, 1, experts_own, capacity, width_all)).reshape(
        ep_count, experts_own, capacity, width_all
    )
    owner_out = expert_forward(expert_in, expert_gate, expert_up, expert_down)
    returned = to_source(owner_out.reshape(1, ep_count, experts_own, capacity, width_all))
    picked = jnp.take(returned.reshape(experts_all * capacity, -1), slot_place, axis=0).reshape(
        tok_rows, top_count, -1
    )
    expert_mix = jnp.sum(gates[:, :, None] * picked, axis=1)
    resid_own = lax.dynamic_slice_in_dim(resid, tp_rank * width_own, width_own, 1)
    shared_term = switch[:, None] * partial_shared
    gate_dots = jnp.sum(picked * grad_full[:, None, :], axis=2)
    ffn_term = expert_mix + shared_term
    ffn_share = lax.psum_scatter(
        ffn_term.astype(jnp.bfloat16), "tp", scatter_dimension=1, tiled=True
    ).astype(jnp.float32)
    layer_out = (resid_own + ffn_share).astype(jnp.bfloat16)
    grad_shared = (switch[:, None] * grad_full).astype(jnp.bfloat16)
    switch_dots = jnp.sum(grad_full * partial_shared, axis=1)
    grad_sdown = jnp.einsum(
        "tf,td->fd", hidden_shared, grad_shared, preferred_element_type=jnp.float32
    )
    grad_hshared = jnp.einsum(
        "td,fd->tf", grad_shared, shared_down, preferred_element_type=jnp.float32
    )
    grad_gshared = (grad_hshared * up_shared * slope_shared).astype(jnp.bfloat16)
    grad_ushared = (grad_hshared * act_shared).astype(jnp.bfloat16)
    grad_sgate = jnp.einsum("td,tf->df", mixed, grad_gshared, preferred_element_type=jnp.float32)
    grad_sup = jnp.einsum("td,tf->df", mixed, grad_ushared, preferred_element_type=jnp.float32)
    grad_mixed = jnp.einsum(
        "tf,df->td", grad_gshared, shared_gate, preferred_element_type=jnp.float32
    ) + jnp.einsum("tf,df->td", grad_ushared, shared_up, preferred_element_type=jnp.float32)
    grad_routed = (
        (gates[:, :, None] * grad_full[:, None, :])
        .astype(jnp.bfloat16)
        .reshape(tok_rows * top_count, width_all)
    )
    grad_pad = jnp.concatenate([grad_routed, jnp.zeros((1, width_all), jnp.bfloat16)], axis=0)
    grad_send = jnp.take(grad_pad, owner_rows, axis=0)
    grad_recv = to_owner(grad_send.reshape(ep_count, 1, experts_own, capacity, width_all)).reshape(
        ep_count, experts_own, capacity, width_all
    )
    (
        input_gradient_rows,
        expert_gate_weight_gradient,
        expert_up_weight_gradient,
        expert_down_weight_gradient,
    ) = routed_expert_pullback(expert_in, grad_recv, expert_gate, expert_up, expert_down)
    grad_back = to_source(
        input_gradient_rows.reshape(1, ep_count, experts_own, capacity, width_all)
    )
    grad_picked = jnp.take(
        grad_back.reshape(experts_all * capacity, -1), slot_place, axis=0
    ).reshape(tok_rows, top_count, -1)
    picked_total = jnp.sum(grad_picked, axis=1)
    grad_mixed = grad_mixed + picked_total
    dot_cols = jnp.concatenate([gate_dots, switch_dots[:, None]], axis=1)
    grad_mixed, dot_cols = lax.psum((grad_mixed, dot_cols), "tp")
    grad_gates = dot_cols[:, :top_count]
    grad_switch = dot_cols[:, top_count]
    grad_prob = jnp.sum(route_hot * grad_gates[:, :, None], axis=1)
    grad_logits = (
        router_prob * (grad_prob - jnp.sum(router_prob * grad_prob, axis=1, keepdims=True))
    ).astype(jnp.bfloat16)
    grad_router = jnp.einsum("td,te->de", mixed, grad_logits, preferred_element_type=jnp.float32)
    grad_slogit = (grad_switch * switch * (1.0 - switch)).astype(jnp.bfloat16)
    grad_switch_w = jnp.einsum("td,t->d", mixed, grad_slogit, preferred_element_type=jnp.float32)
    grad_mixed = (
        grad_mixed
        + jnp.einsum("te,de->td", grad_logits, w_router, preferred_element_type=jnp.float32)
        + grad_slogit.astype(jnp.float32)[:, None] * shared_switch.astype(jnp.float32)[None, :]
    )
    row_dot = jnp.mean(grad_mixed * gain_two * resid, axis=1, keepdims=True)
    grad_resid = (
        grad_full
        + inv_two * gain_two * grad_mixed
        - resid * (inv_two * inv_two * inv_two) * row_dot
    )
    grad_gain_two = lax.dynamic_slice_in_dim(
        jnp.sum(grad_mixed * resid * inv_two, axis=0), tp_rank * width_own, width_own, 0
    )
    resid_low = grad_resid.astype(jnp.bfloat16)
    grad_wout = jnp.einsum("tc,td->cd", attn_rows, resid_low, preferred_element_type=jnp.float32)
    grad_attn = (
        jnp.einsum("td,cd->tc", resid_low, w_output, preferred_element_type=jnp.float32)
        .astype(jnp.bfloat16)
        .reshape(tok_rows, heads_own, HD)
    )

    def block_backward(carry, inputs):
        blk_start, log_piece = inputs
        q_piece, scores = block_scores(blk_start)
        probs = jnp.exp(scores - log_piece[:, :, None])
        grad_probs = jnp.einsum(
            "qhd,khd->hqk", grad_attn, value_rows, preferred_element_type=jnp.float32
        )
        grad_scores = (
            probs * (grad_probs - jnp.sum(probs * grad_probs, axis=2, keepdims=True))
        ).astype(jnp.bfloat16)
        grad_query = (
            jnp.einsum("hqk,khd->qhd", grad_scores, key_rows, preferred_element_type=jnp.float32)
            * score_scale
        )
        grad_keys = (
            carry[0]
            + jnp.einsum("hqk,qhd->khd", grad_scores, q_piece, preferred_element_type=jnp.float32)
            * score_scale
        )
        grad_values = carry[1] + jnp.einsum(
            "hqk,qhd->khd",
            probs.astype(jnp.bfloat16),
            grad_attn,
            preferred_element_type=jnp.float32,
        )
        return ((grad_keys, grad_values), grad_query)

    zero_keys = jnp.zeros((2 * tok_rows, heads_own, HD), jnp.float32)
    carried, grad_query = lax.scan(block_backward, (zero_keys, zero_keys), (starts, log_norm))
    later = from_behind(
        jnp.stack([carried[0][:tok_rows], carried[1][:tok_rows]]).astype(jnp.bfloat16), "ep", -1
    ).astype(jnp.float32)
    grad_key = carried[0][tok_rows:] + later[0]
    grad_value = carried[1][tok_rows:] + later[1]
    grad_qpre = (
        rotate(grad_query.reshape(tok_rows, heads_own, HD), cos_table, -sin_table)
        .astype(jnp.bfloat16)
        .reshape(tok_rows, heads_own * HD)
    )
    grad_kpre = (
        rotate(grad_key, cos_table, -sin_table)
        .astype(jnp.bfloat16)
        .reshape(tok_rows, heads_own * HD)
    )
    grad_vpre = grad_value.astype(jnp.bfloat16).reshape(tok_rows, heads_own * HD)
    grad_wq = jnp.einsum("td,tc->dc", normed, grad_qpre, preferred_element_type=jnp.float32)
    grad_wk = jnp.einsum("td,tc->dc", normed, grad_kpre, preferred_element_type=jnp.float32)
    grad_wv = jnp.einsum("td,tc->dc", normed, grad_vpre, preferred_element_type=jnp.float32)
    grad_normed = (
        jnp.einsum("tc,dc->td", grad_qpre, w_query, preferred_element_type=jnp.float32)
        + jnp.einsum("tc,dc->td", grad_kpre, w_key, preferred_element_type=jnp.float32)
        + jnp.einsum("tc,dc->td", grad_vpre, w_value, preferred_element_type=jnp.float32)
    )
    row_part = jnp.sum(grad_normed * gain_one * x_full, axis=1, keepdims=True)
    normed_own, row_total = (
        lax.psum_scatter(
            grad_normed.astype(jnp.bfloat16), "tp", scatter_dimension=1, tiled=True
        ).astype(jnp.float32),
        lax.psum_scatter(
            jnp.tile(row_part, (1, tp_count)).astype(jnp.bfloat16),
            "tp",
            scatter_dimension=1,
            tiled=True,
        ).astype(jnp.float32),
    )
    x_own = tokens.astype(jnp.float32)
    gain_own = norm_attn.astype(jnp.float32)
    grad_tokens = (
        lax.dynamic_slice_in_dim(grad_resid, tp_rank * width_own, width_own, 1)
        + inv_one * gain_own * normed_own
        - x_own * (inv_one * inv_one * inv_one) * row_total / width_all
    )
    grad_gain_one = jnp.sum(normed_own * x_own * inv_one, axis=0)
    dense = (
        lax.psum(grad_gain_one.astype(jnp.bfloat16), ("dp", "ep")).astype(jnp.float32),
        lax.psum(grad_wq.astype(jnp.bfloat16), ("dp", "ep")).astype(jnp.float32),
        lax.psum(grad_wk.astype(jnp.bfloat16), ("dp", "ep")).astype(jnp.float32),
        lax.psum(grad_wv.astype(jnp.bfloat16), ("dp", "ep")).astype(jnp.float32),
        lax.psum(grad_wout.astype(jnp.bfloat16), ("dp", "ep")).astype(jnp.float32),
        lax.psum(grad_gain_two.astype(jnp.bfloat16), ("dp", "ep")).astype(jnp.float32),
        lax.psum(grad_router.astype(jnp.bfloat16), ("dp", "ep")).astype(jnp.float32),
        lax.psum(grad_switch_w.astype(jnp.bfloat16), ("dp", "ep")).astype(jnp.float32),
        lax.psum(grad_sgate.astype(jnp.bfloat16), ("dp", "ep")).astype(jnp.float32),
        lax.psum(grad_sup.astype(jnp.bfloat16), ("dp", "ep")).astype(jnp.float32),
        lax.psum(grad_sdown.astype(jnp.bfloat16), ("dp", "ep")).astype(jnp.float32),
    )
    routed_experts_total = (
        lax.psum(expert_gate_weight_gradient.astype(jnp.bfloat16), "dp").astype(jnp.float32),
        lax.psum(expert_up_weight_gradient.astype(jnp.bfloat16), "dp").astype(jnp.float32),
        lax.psum(expert_down_weight_gradient.astype(jnp.bfloat16), "dp").astype(jnp.float32),
    )
    return (
        layer_out,
        grad_tokens,
        dense[0],
        dense[1],
        dense[2],
        dense[3],
        dense[4],
        dense[5],
        dense[6],
        dense[7],
        dense[8],
        dense[9],
        dense[10],
        routed_experts_total[0],
        routed_experts_total[1],
        routed_experts_total[2],
    )


def solution(mesh):
    placed = (
        P(("dp", "ep"), "tp"),
        P("tp"),
        P(None, "tp"),
        P(None, "tp"),
        P(None, "tp"),
        P("tp", None),
        P("tp"),
        P(),
        P(),
        P(None, "tp"),
        P(None, "tp"),
        P("tp", None),
        P("ep", None, "tp"),
        P("ep", None, "tp"),
        P("ep", "tp", None),
        P(("dp", "ep"), None),
        P("dp"),
        P(("dp", "ep"), "tp"),
    )
    return jax.shard_map(
        body,
        mesh=mesh,
        in_specs=placed,
        out_specs=(
            P(("dp", "ep"), "tp"),
            P(("dp", "ep"), "tp"),
            P("tp"),
            P(None, "tp"),
            P(None, "tp"),
            P(None, "tp"),
            P("tp", None),
            P("tp"),
            P(),
            P(),
            P(None, "tp"),
            P(None, "tp"),
            P("tp", None),
            P("ep", None, "tp"),
            P("ep", None, "tp"),
            P("ep", "tp", None),
        ),
        check_vma=False,
    )
```

profile of v0, /device:TPU:0, one launch (start us, length us, event | category | flops | bytes accessed | tf_op | source)
XLA Modules:
  0.0 2216.7 jit_solution(14538106271740412682)
XLA Ops:
  8.7 13.5 all-gather.2
  24.1 34.2 %all-gather.7.cloned.1.call-done = bf16[512,2048]{1,0:T(8,128)(2,1)} async-done(((bf16[512,512]{1,0:T(8,128)(2,1)}), bf16[512,2048]{1,0:T(8,128)(2,1)}) %all-gather.7.cloned.1.call-update) | async-done | bytes 2097168 | tf_op jit(solution)/shard_map/all_gather | solution.py:115
  102.2 13.5 collective-permute-done
  131.6 12.0 all-gather.3
  146.9 8.5 scatter_custom_fusion
  155.5 130.7 %all-reduce.11.cloned.1.call-done = f32[512,2048]{1,0:T(8,128)} async-done(((f32[512,2048]{1,0:T(8,128)}), f32[512,2048]{1,0:T(8,128)}) %all-reduce.11.cloned.1.call-update) | async-done | bytes 4194320 | tf_op jit(solution)/shard_map/psum | solution.py:170
  295.1 22.0 gather_fusion.1
  317.1 5.8 select_bitcast_fusion.1
  322.9 118.3 %all_to_all.16 = bf16[2,1,4,320,2048]{4,3,2,1,0:T(8,128)(2,1)S(1)} all-to-all(bf16[2,1,4,320,2048]{4,3,2,1,0:T(8,128)(2,1)S(1)} %select_bitcast_fusion.1), channel_id=1, replica_groups=mesh['dp'=4,'ep'=2,'tp'=4] {'ep'}, dimensions={0} | all-to-all | bytes 20971520 | tf_op jit(solution)/shard_map/all_to_all | solution.py:109
  441.2 11.0 fusion.10
  452.1 10.7 fusion.44
  462.8 7.9 convolution_bitcast_fusion
  470.7 7.4 copy.119
  478.1 11.2 all-to-all-start.1
  490.2 47.2 %all-gather.9.cloned.1.call-done = bf16[512,2048]{1,0:T(8,128)(2,1)} async-done(((bf16[512,512]{1,0:T(8,128)(2,1)}), bf16[512,2048]{1,0:T(8,128)(2,1)}) %all-gather.9.cloned.1.call-update) | async-done | bytes 2097168 | tf_op jit(solution)/shard_map/all_gather | solution.py:118
  537.4 9.7 mul.576
  547.2 19.4 mul.577
  569.4 7.1 fusion.103
  576.6 8.7 multiply_convert_fusion.6
  586.5 5.0 multiply_reduce_fusion.5
  591.6 124.3 %all-to-all-done.1 = f32[1,2,4,320,2048]{4,3,2,0,1:T(8,128)} async-done(((f32[1,2,4,320,2048]{4,3,2,0,1:T(8,128)}), f32[1,2,4,320,2048]{4,3,2,0,1:T(8,128)}, u32[]{:S(2)}, u32[]{:S(2)}) %all-to-all-start.1) | async-done | bytes 20971552 | tf_op jit(solution)/shard_map/all_to_all | solution.py:112
  715.9 23.5 %gather_fusion.3 = f32[2048,2048]{1,0:T(8,128)} fusion(f32[2560,2048]{1,0:T(8,128)} %bitcast.29, s32[2048]{0:T(1024)S(1)} %broadcast_clamp_fusion), kind=kCustom, calls=%fused_computation.clone | custom fusion | bytes 33562624 | tf_op jit(solution)/shard_map/jit(_take)/gather | solution.py:205
  739.4 17.9 multiply_reduce_fusion
  757.8 17.0 psum.121
  775.7 9.3 multiply_convert_fusion
  784.9 8.5 concatenate.53
  793.4 24.6 %gather_fusion.2 = bf16[2560,2048]{1,0:T(8,128)(2,1)} fusion(bf16[2049,2048]{1,0:T(8,128)(2,1)} %concatenate.53, s32[3072]{0:T(1024)S(1)} %pad_clamp_fusion), kind=kCustom, calls=%fused_computation.4 | custom fusion | bytes 20981760 | tf_op jit(solution)/shard_map/jit(_take)/gather | solution.py:238
  818.0 5.8 select_bitcast_fusion
  823.8 115.0 %all_to_all.17 = bf16[2,1,4,320,2048]{4,3,2,1,0:T(8,128)(2,1)} all-to-all(bf16[2,1,4,320,2048]{4,3,2,1,0:T(8,128)(2,1)S(1)} %select_bitcast_fusion), channel_id=1, replica_groups=mesh['dp'=4,'ep'=2,'tp'=4] {'ep'}, dimensions={0} | all-to-all | bytes 20971520 | tf_op jit(solution)/shard_map/all_to_all | solution.py:109
  938.8 12.6 fusion.43
  951.4 12.2 fusion.22
  963.6 15.7 add_bitcast_fusion
  979.4 16.1 copy.123
  995.5 11.3 all-to-all-start.3
  1010.2 10.2 multiply_convert_fusion.4
  1021.5 7.6 fusion.104
  1029.1 198.9 %all-to-all-done.3 = f32[1,2,4,320,2048]{4,3,2,0,1:T(8,128)} async-done(((f32[1,2,4,320,2048]{4,3,2,0,1:T(8,128)}), f32[1,2,4,320,2048]{4,3,2,0,1:T(8,128)}, u32[]{:S(2)}, u32[]{:S(2)}) %all-to-all-start.3) | async-done | bytes 20971552 | tf_op jit(solution)/shard_map/all_to_all | solution.py:112
  1228.1 23.5 %gather_fusion.4 = f32[2048,2048]{1,0:T(8,128)} fusion(f32[2560,2048]{1,0:T(8,128)} %bitcast.40, s32[2048]{0:T(1024)S(1)} %broadcast_clamp_fusion), kind=kCustom, calls=%fused_computation.1.clone | custom fusion | bytes 33562624 | tf_op jit(solution)/shard_map/jit(_take)/gather | solution.py:251
  1251.6 11.8 broadcast_select_fusion
  1263.4 19.0 reshape.474
  1282.4 15.1 reduce_sum.167
  1297.5 11.0 add_add_fusion.1
  1309.2 18.9 reshape.470
  1328.1 14.6 multiply_reduce_fusion.1
  1344.7 9.8 bitcast_convert_fusion.2
  1354.5 9.2 bitcast_convert_fusion.1
  1363.7 11.2 bitcast_convert_fusion
  1375.3 86.4 %all-reduce.13.cloned.1.call-done = f32[512,2048]{1,0:T(8,128)} async-done(((f32[512,2048]{1,0:T(8,128)}), f32[512,2048]{1,0:T(8,128)}) %all-reduce.13.cloned.1.call-update) | async-done | bytes 4194320 | tf_op jit(solution)/shard_map/psum | solution.py:257
  1468.1 4.8 convolution_convert_fusion.8
  1485.9 23.0 %collective-permute-done.1 = bf16[2,512,4,128]{3,1,2,0:T(8,128)(2,1)S(1)} collective-permute-done((bf16[2,512,4,128]{3,1,2,0:T(8,128)(2,1)S(1)}, bf16[2,512,4,128]{3,1,2,0:T(8,128)(2,1)S(1)}, u32[]{:S(2)}, u32[]{:S(2)}) %collective-permute-start.1) | collective-permute-done | bytes 1048608 | tf_op jit(solution)/shard_map/ppermute | solution.py:19
  1528.2 8.1 convolution_convert_fusion.2
  1536.4 5.3 convolution_convert_fusion.1
  1541.7 5.3 convolution_convert_fusion
  1566.0 241.7 %all-reduce.17.cloned.1.call-done = (bf16[4,2048,352]{1,2,0:T(8,128)(2,1)}, bf16[4,2048,352]{1,2,0:T(8,128)(2,1)}, bf16[4,352,2048]{2,1,0:T(8,128)(2,1)}) async-done(((bf16[4,2048,352]{1,2,0:T(8,128)(2,1)}, bf16[4,2048,352]{1,2,0:T(8,128)(2,1)}, bf16[4,352,2048]{2,1,0:T(8,128)(2,1)}), (bf16[4,2048,352]{1,2,0:T(8,128)(2,1)}, bf16[4,2048,352]{1,2,0:T(8,128)(2,1)}, ...) | async-done | bytes 17301520 | tf_op jit(solution)/shard_map/psum | solution.py:376
  1807.7 8.8 convert_element_type.295
  1816.5 6.0 convert_element_type.297
  1822.5 6.0 convert_element_type.299
  1828.6 12.4 all-reduce.2
  1841.6 13.2 reduce-scatter.5.cloned.1.call-done
  1857.7 26.2 %all-reduce.3 = (bf16[512]{0:T(512)(128)(2,1)S(1)}, bf16[512]{0:T(512)(128)(2,1)S(1)}, bf16[2048,8]{0,1:T(8,128)(2,1)S(1)}, bf16[2048]{0:T(1024)(128)(2,1)S(1)}) all-reduce(bf16[512]{0:T(512)(128)(2,1)S(1)} %get-tuple-element.129, bf16[512]{0:T(512)(128)(2,1)S(1)} %dynamic_slice.27, ...), channel_id=1, replica_groups=mesh['dp'=4,'ep'=2,'tp'=4] {'dp','ep'}, use_global_device_ids=true, to_apply=%region_27.29 | all-reduce | flops 19456 | bytes 77824 | tf_op jit(solution)/shard_map/psum | solution.py:363
  1886.4 292.9 %all-reduce.15.cloned.1.call-done = (bf16[2048,512]{1,0:T(8,128)(2,1)}, bf16[2048,512]{1,0:T(8,128)(2,1)}, bf16[2048,512]{1,0:T(8,128)(2,1)}, bf16[512,2048]{1,0...) async-done(((bf16[2048,512]{1,0:T(8,128)(2,1)}, bf16[2048,512]{1,0:T(8,128)(2,1)}, bf16[2048,512]{1,0:T(8,128)(2,1)}, ...) | async-done | bytes 25690128 | tf_op jit(solution)/shard_map/psum | solution.py:364
  2192.7 5.7 convert_element_type.289
  2198.4 5.2 convert_element_type.291
  2203.6 6.0 convert_element_type.293
  (352 shorter events, 165.4 us)
Async XLA Ops:
  7.2 71.6 %copy-start = (bf16[2048,512]{1,0:T(8,128)(2,1)S(1)}, bf16[2048,512]{1,0:T(8,128)(2,1)}, u32[]{:S(2)}) copy-start(bf16[2048,512]{1,0:T(8,128)(2,1)} %param.24) | copy-start | bytes 6291460
  7.2 51.1 %all-gather.7.cloned.1.call-start = ((), (), s32[]{:S(2)}) async-start(), calls=%async_computation.6 | async-start | bytes 2621440 | tf_op jit(solution)/shard_map/all_gather | solution.py:115
  7.9 278.3 %all-reduce.11.cloned.1.call-start = ((), (), s32[]{:S(2)}) async-start(), calls=%async_computation.7 | async-start | bytes 8388608 | tf_op jit(solution)/shard_map/psum | solution.py:170
  22.2 56.6 %copy-start.61 = (f32[4,1,512]{2,1,0:T(1,128)}, f32[4,1,512]{2,1,0:T(1,128)S(1)}, u32[]{:S(2)}) copy-start(f32[4,1,512]{2,1,0:T(1,128)S(1)} %mul.642) | copy-start | bytes 24580
  24.1 60.5 %copy-start.18 = (f32[512,64]{1,0:T(8,128)}, f32[512,64]{1,0:T(8,128)S(1)}, u32[]{:S(2)}) copy-start(f32[512,64]{1,0:T(8,128)S(1)} %get-tuple-element.144) | copy-start | bytes 393220
  60.9 17.8 copy-start.75
  84.6 9.6 copy-start.1
  89.4 27.5 %copy-start.25 = (bf16[512,4,64]{2,0,1:T(8,128)(2,1)S(1)}, bf16[512,4,64]{2,0,1:T(8,128)(2,1)}, u32[]{:S(2)}) copy-start(bf16[512,4,64]{2,0,1:T(8,128)(2,1)} %get-tuple-element.119) | copy-start | bytes 786436
  89.4 27.5 %copy-start.27 = (bf16[512,4,64]{2,0,1:T(8,128)(2,1)S(1)}, bf16[512,4,64]{2,0,1:T(8,128)(2,1)}, u32[]{:S(2)}) copy-start(bf16[512,4,64]{2,0,1:T(8,128)(2,1)} %get-tuple-element.120) | copy-start | bytes 786436
  89.4 26.2 %collective-permute-start = (bf16[2,512,4,128]{3,1,2,0:T(8,128)(2,1)}, bf16[2,512,4,128]{3,1,2,0:T(8,128)(2,1)}, u32[]{:S(2)}, u32[]{:S(2)}) collective-permute-start(bf16[2,512,4,128]{3,1,2,0:T(8,128)(2,1)} %pad_maximum_fusion), channel_id=1, source_target_pairs={{0,4},{1,5},{2,6},{3,7},{8,12},{9,13},{10,14},{11,15},{16,20},{17,... | collective-permute-start | bytes 3145736 | tf_op jit(solution)/shard_map/ppermute | solution.py:19
  116.9 6.0 copy-start.41
  143.6 146.8 %copy-start.55 = (f32[4,1,512]{2,1,0:T(1,128)}, f32[4,1,512]{2,1,0:T(1,128)S(1)}, u32[]{:S(2)}) copy-start(f32[4,1,512]{2,1,0:T(1,128)S(1)} %mul.643) | copy-start | bytes 24580
  441.2 11.0 copy-start.10
  478.1 237.8 %all-to-all-start.1 = ((f32[1,2,4,320,2048]{4,3,2,0,1:T(8,128)}), f32[1,2,4,320,2048]{4,3,2,0,1:T(8,128)}, u32[]{:S(2)}, u32[]{:S(2)}) async-start(f32[1,2,4,320,2048]{4,3,2,0,1:T(8,128)} %copy.119), calls=%async_computation.1 | async-start | bytes 41943040 | tf_op jit(solution)/shard_map/all_to_all | solution.py:112
  489.3 48.1 %all-gather.9.cloned.1.call-start = ((), (), s32[]{:S(2)}) async-start(), calls=%async_computation.9 | async-start | bytes 2621440 | tf_op jit(solution)/shard_map/all_gather | solution.py:118
  490.2 249.2 %copy-start.71 = (pred[2048]{0:T(1024)(128)(4,1)}, pred[2048]{0:T(1024)(128)(4,1)S(1)}, u32[]{:S(2)}) copy-start(pred[2048]{0:T(1024)(128)(4,1)S(1)} %compare_and_fusion.3) | copy-start | bytes 6148
  547.2 19.4 copy-start.53
  568.8 7.8 copy-start.59
  569.4 7.2 copy-start.63
  569.4 7.2 copy-start.6
  569.4 17.1 slice-start.12
  576.6 8.8 copy-start.86
  576.6 9.9 copy-start.11
  576.6 9.9 slice-start.13
  739.4 35.3 %copy-start.58 = (s32[512,4]{0,1:T(4,128)S(1)}, s32[512,4]{0,1:T(4,128)}, u32[]{:S(2)}) copy-start(s32[512,4]{0,1:T(4,128)} %param.35) | copy-start | bytes 24580
  775.5 9.4 copy-start.20
  823.8 127.6 %slice-start.2 = ((s8[5767168]{0:T(1024)(128)(4,1)}), s8[4194304]{0:T(1024)(128)(4,1)S(1)}, s32[]{:S(2)}) async-start(s8[5767168]{0:T(1024)(128)(4,1)} %bitcast.235), calls=%async_computation.16 | async-start | bytes 8388608
  938.8 12.6 slice-start.3
  951.4 12.2 copy-start.44
  995.5 11.8 copy-start.73
  995.5 232.5 %all-to-all-start.3 = ((f32[1,2,4,320,2048]{4,3,2,0,1:T(8,128)}), f32[1,2,4,320,2048]{4,3,2,0,1:T(8,128)}, u32[]{:S(2)}, u32[]{:S(2)}) async-start(f32[1,2,4,320,2048]{4,3,2,0,1:T(8,128)} %copy.123), calls=%async_computation.4 | async-start | bytes 41943040 | tf_op jit(solution)/shard_map/all_to_all | solution.py:112
  1006.9 454.8 %all-reduce.13.cloned.1.call-start = ((), (), s32[]{:S(2)}) async-start(), calls=%async_computation.10 | async-start | bytes 8388608 | tf_op jit(solution)/shard_map/psum | solution.py:257
  1228.1 23.5 %copy-start.72 = (pred[2048]{0:T(1024)(128)(4,1)S(1)}, pred[2048]{0:T(1024)(128)(4,1)}, u32[]{:S(2)}) copy-start(pred[2048]{0:T(1024)(128)(4,1)} %copy-done.71) | copy-start | bytes 6148
  1308.5 255.2 %reduce-scatter.3.cloned.1.call-start = ((), (), s32[]{:S(2)}) async-start(), calls=%async_computation.8 | async-start | bytes 2621440 | tf_op jit(solution)/shard_map/reduce_scatter | solution.py:213
  1309.2 18.9 copy-start.21
  1328.1 14.7 copy-start.17
  1344.6 463.1 %all-reduce.17.cloned.1.call-start = ((), (), s32[]{:S(2)}) async-start(), calls=%async_computation.13 | async-start | bytes 34603008 | tf_op jit(solution)/shard_map/psum | solution.py:376
  1344.7 9.8 copy-start.45
  1354.5 9.2 copy-start.43
  1375.0 86.7 %copy-start.54 = (bf16[2048,8]{0,1:T(8,128)(2,1)S(1)}, bf16[2048,8]{0,1:T(8,128)(2,1)}, u32[]{:S(2)}) copy-start(bf16[2048,8]{0,1:T(8,128)(2,1)} %param.27) | copy-start | bytes 98308
  1375.0 86.7 %copy-start.56 = (f32[4,1,512]{2,1,0:T(1,128)S(1)}, f32[4,1,512]{2,1,0:T(1,128)}, u32[]{:S(2)}) copy-start(f32[4,1,512]{2,1,0:T(1,128)} %copy-done.55) | copy-start | bytes 24580
  1375.0 86.7 %copy-start.70 = (f32[512]{0:T(512)S(1)}, f32[512]{0:T(512)}, u32[]{:S(2)}) copy-start(f32[512]{0:T(512)} %copy-done.69) | copy-start | bytes 6148
  1375.0 479.9 %reduce-scatter.5.cloned.1.call-start = ((), (), s32[]{:S(2)}) async-start(), calls=%async_computation.11 | async-start | bytes 2621440 | tf_op jit(solution)/shard_map/reduce_scatter | solution.py:344
  1461.7 5.3 copy-start.12
  1461.7 5.3 copy-start.77
  1461.7 11.1 slice-start
  1467.0 5.8 slice-start.1
  1468.1 7.2 copy-start.14
  1482.0 26.8 %collective-permute-start.1 = (bf16[2,512,4,128]{3,1,2,0:T(8,128)(2,1)S(1)}, bf16[2,512,4,128]{3,1,2,0:T(8,128)(2,1)S(1)}, u32[]{:S(2)}, u32[]{:S(2)}) collective-permute-start(bf16[2,512,4,128]{3,1,2,0:T(8,128)(2,1)S(1)} %pad_maximum_fusion.2), channel_id=1, source_target_pairs={{4,0},{5,1},{6,2},{7,3},{12,8},{13,9},{14,10},{15,11},{20,16},{21,... | collective-permute-start | bytes 3145736 | tf_op jit(solution)/shard_map/ppermute | solution.py:19
  1527.7 651.6 %all-reduce.15.cloned.1.call-start = ((), (), s32[]{:S(2)}) async-start(), calls=%async_computation.12 | async-start | bytes 51380224 | tf_op jit(solution)/shard_map/psum | solution.py:364
  1528.2 8.2 copy-start.7
  1528.2 8.2 copy-start.82
  1541.7 5.3 copy-start.15
  1541.7 5.3 copy-start.49
  1807.7 8.8 copy-start.16
  1807.7 14.8 slice-start.4
  1816.5 6.0 slice-start.5
  1822.5 32.3 %copy-start.29 = (bf16[512,512]{1,0:T(8,128)(2,1)S(1)}, bf16[512,512]{1,0:T(8,128)(2,1)}, u32[]{:S(2)}) copy-start(bf16[512,512]{1,0:T(8,128)(2,1)} %param.20) | copy-start | bytes 1572868
  1822.5 32.3 %copy-start.74 = (f32[512]{0:T(512)S(1)}, f32[512]{0:T(512)}, u32[]{:S(2)}) copy-start(f32[512]{0:T(512)} %get-tuple-element.145) | copy-start | bytes 6148
  2183.6 9.1 slice-start.10
  2186.3 6.4 slice-start.11
  2190.0 8.4 slice-start.8
  2192.7 5.7 slice-start.9
  2192.7 10.9 slice-start.6
  (49 other events, 125.0 us)
Sparse Core Ops, SparseCore 0:
  9.6 48.6 all-gather.6
  131.0 155.0 all-reduce.10
  491.8 45.5 all-gather.8
  1308.6 153.0 all-reduce.12
  1464.4 42.8 reduce-scatter.2
  1510.8 296.7 all-reduce.16
  1810.5 44.2 reduce-scatter.4
  1861.4 317.8 all-reduce.14
where the time goes:
time: 2230 us; the launch traced here: 2220 us
  waiting for transfers between devices  1210 us (54%)
  blocking collectives  314 us (14%)
  local copies, waits for them, and re-layouts  242 us (11%)
  matrix products  235 us (11%)
  other arithmetic  172 us (8%)
  starting transfers between devices  30.6 us (1%)
    all_to_all x2, waiting for transfers between devices, to_source(): lax.all_to_all(payload, 'ep', split_axis=1, concat_axis=0, tiled=True)  323 us
    psum x1, waiting for transfers between devices, body(): lax.psum(grad_wq.astype(jnp.bfloat16), ('dp', 'ep')).astype(jnp.float32)  293 us
    psum x1, waiting for transfers between devices, body(): lax.psum(expert_gate_weight_gradient.astype(jnp.bfloat16), 'dp')  242 us
    all_to_all x2, blocking collectives, to_owner(): lax.all_to_all(payload, 'ep', split_axis=0, concat_axis=1, tiled=True)  233 us
    psum x1, waiting for transfers between devices, body(): lax.psum(jnp.dot(attn_rows, w_output, preferred_element_type=jnp.float32)...  131 us
    psum x1, waiting for transfers between devices, body(): grad_mixed, dot_cols = lax.psum((grad_mixed, dot_cols), 'tp')  86.4 us
    all_gather x1, waiting for transfers between devices, body(): lax.all_gather(output_gradient, 'tp', axis=1, tiled=True)  47.2 us
  transfers between devices with their start and end apart: 12, of which 11 were waited for; matrix products, arithmetic and copies ran while one was open for 12% of the time, Pallas kernels for 0%

commit v1 on v0

v1 whole, which is shorter than its diff:
```python
import math

import jax
import jax.numpy as jnp
from jax import lax
from jax.sharding import PartitionSpec as P

HD = 128
EPS = 1e-06
ROPE_BASE = 1000000.0
NEG = -1e30
F32 = jnp.float32
BF16 = jnp.bfloat16


def mm(left, right):
    return lax.dot_general(left, right, (((1,), (0,)), ((), ())), preferred_element_type=F32)


def mm_nt(left, right):
    return lax.dot_general(left, right, (((1,), (1,)), ((), ())), preferred_element_type=F32)


def mm_tn(left, right):
    return lax.dot_general(left, right, (((0,), (0,)), ((), ())), preferred_element_type=F32)


def swap(value, axis, bit):
    count = lax.axis_size(axis)
    return lax.ppermute(value, axis, [(i, i ^ bit) for i in range(count)])


def bit_of(axis, bit):
    return (lax.axis_index(axis) // bit) % 2


def half(value, which, dim):
    size = value.shape[dim] // 2
    return lax.dynamic_slice_in_dim(value, which * size, size, dim)


def halve(value, axis, bit, dim):
    mine = bit_of(axis, bit)
    got = swap(half(value, 1 - mine, dim), axis, bit)
    return (half(value, mine, dim).astype(F32) + got.astype(F32)).astype(BF16)


def double(value, axis, bit, dim):
    got = swap(value, axis, bit)
    mine = bit_of(axis, bit) == 0
    return jnp.concatenate([jnp.where(mine, value, got), jnp.where(mine, got, value)], axis=dim)


def rope_tables(positions, feat_width):
    half_width = feat_width // 2
    inv_freq = ROPE_BASE ** (-(jnp.arange(half_width, dtype=F32) * 2.0) / feat_width)
    angles = positions.astype(F32)[:, None] * inv_freq[None, :]
    return (jnp.cos(angles), jnp.sin(angles))


def rotate(tensor, cos_table, sin_table):
    half_width = tensor.shape[-1] // 2
    first_half = tensor[..., :half_width]
    second_half = tensor[..., half_width:]
    cos_b = cos_table[:, None, :]
    sin_b = sin_table[:, None, :]
    return jnp.concatenate(
        [first_half * cos_b - second_half * sin_b, second_half * cos_b + first_half * sin_b],
        axis=-1,
    )


def ffn_pieces(rows, grads, scale, gate_w, up_w, down_w, groups):
    count = rows.shape[0]
    hidden_width = gate_w.shape[1]
    gate_pre = mm(rows, gate_w)
    up_pre = mm(rows, up_w)
    grad_hidden = mm_nt(grads, down_w)
    sig = jax.nn.sigmoid(gate_pre)
    act = gate_pre * sig
    slope = sig * (1.0 + gate_pre * (1.0 - sig))
    hidden = (act * up_pre).astype(BF16).astype(F32)
    wide = jnp.repeat(scale, hidden_width // groups, axis=1, total_repeat_length=hidden_width)
    scaled_hidden = (hidden * wide).astype(BF16)
    dots = jnp.sum((hidden * grad_hidden).reshape(count, groups, -1), axis=2)
    grad_scaled = grad_hidden * wide
    grad_gate = (grad_scaled * up_pre * slope).astype(BF16)
    grad_up = (grad_scaled * act).astype(BF16)
    along = jnp.sum(grad_gate.astype(F32) * gate_pre + grad_up.astype(F32) * up_pre, axis=1)
    return scaled_hidden, grad_gate, grad_up, dots, along


def body(
    tokens,
    norm_attn,
    w_query,
    w_key,
    w_value,
    w_output,
    norm_ffn,
    w_router,
    shared_switch,
    shared_gate,
    shared_up,
    shared_down,
    expert_gate,
    expert_up,
    expert_down,
    routes,
    segments,
    output_gradient,
):
    tp_count = lax.axis_size("tp")
    ep_count = lax.axis_size("ep")
    dp_count = lax.axis_size("dp")
    tp_rank = lax.axis_index("tp")
    ep_rank = lax.axis_index("ep")
    rows = tokens.shape[0]
    width_own = tokens.shape[1]
    width = width_own * tp_count
    heads = w_query.shape[1] // HD
    experts_own = expert_gate.shape[0]
    experts = experts_own * ep_count
    expert_width = expert_gate.shape[2]
    score_scale = 1.0 / math.sqrt(HD)
    far_bits = [1 << b for b in range(1, dp_count.bit_length() - 1)]

    def own_columns(value):
        return lax.dynamic_slice_in_dim(value, tp_rank * width_own, width_own, value.ndim - 1)

    def total_dense(value, dims):
        stages = [("ep", 1)] + [("dp", b) for b in far_bits]
        for axis, bit in stages:
            value = halve(value, axis, bit, dims)
        for axis, bit in reversed(stages):
            value = double(value, axis, bit, dims)
        return value

    def total_expert(value, dims):
        stages = [("dp", b) for b in far_bits]
        for axis, bit in stages:
            value = halve(value, axis, bit, dims)
        for axis, bit in reversed(stages):
            value = double(value, axis, bit, dims)
        return value

    near = bit_of("dp", 1)

    def pair_rows(left, right):
        send = mm_tn(half(left, 1 - near, 1), right).astype(BF16)
        got = swap(send, "dp", 1)
        return (mm_tn(half(left, near, 1), right) + got.astype(F32)).astype(BF16)

    def pair_columns(left, right):
        send = mm_tn(left, half(right, 1 - near, 1)).astype(BF16)
        got = swap(send, "dp", 1)
        return (mm_tn(left, half(right, near, 1)) + got.astype(F32)).astype(BF16)

    def spread(value, dim):
        got = swap(value, "dp", 1)
        first = near == 0
        return (
            jnp.concatenate([jnp.where(first, value, got), jnp.where(first, got, value)], axis=dim)
        ).astype(F32)

    packed = jnp.concatenate(
        [tokens, norm_attn[None, :], norm_ffn[None, :], jnp.zeros((14, width_own), BF16)], axis=0
    )
    packed = lax.all_gather(packed, "tp", axis=1, tiled=True)
    x_full = packed[:rows].astype(F32)
    gain_one = packed[rows].astype(F32)
    gain_two = packed[rows + 1].astype(F32)
    grad_rows = lax.all_gather(output_gradient, "tp", axis=1, tiled=True)
    grad_peer = swap(grad_rows, "ep", 1)
    route_hot = jnp.sum(
        (routes[:, :, None] == jnp.arange(experts, dtype=jnp.int32)[None, None, :]).astype(F32),
        axis=1,
    )
    route_hot_peer = swap(route_hot, "ep", 1)

    inv_one = lax.rsqrt(jnp.mean(x_full * x_full, axis=1, keepdims=True) + EPS)
    normed = (x_full * inv_one * gain_one).astype(BF16)
    q_pre = mm(normed, w_query)
    k_pre = mm(normed, w_key)
    v_pre = mm(normed, w_value)
    positions = ep_rank * rows + jnp.arange(rows, dtype=jnp.int32)
    cos_table, sin_table = rope_tables(positions, HD)
    query = rotate(q_pre.reshape(rows, heads, HD), cos_table, sin_table).astype(BF16)
    key_own = rotate(k_pre.reshape(rows, heads, HD), cos_table, sin_table).astype(BF16)
    value_own = v_pre.astype(BF16).reshape(rows, heads, HD)
    forth = [(i, i + 1) for i in range(ep_count - 1)]
    back = [(i + 1, i) for i in range(ep_count - 1)]
    earlier = lax.ppermute(jnp.stack([key_own, value_own]), "ep", forth)
    key_rows = jnp.concatenate([earlier[0], key_own], axis=0)
    value_rows = jnp.concatenate([earlier[1], value_own], axis=0)
    key_pos = (ep_rank - 1) * rows + jnp.arange(2 * rows, dtype=jnp.int32)
    seg_rows = segments.reshape(ep_count, rows)
    query_seg = lax.dynamic_index_in_dim(seg_rows, ep_rank, 0, keepdims=False)
    before_seg = lax.dynamic_index_in_dim(
        seg_rows, jnp.maximum(ep_rank - 1, 0), 0, keepdims=False
    )
    key_seg = jnp.concatenate([jnp.where(ep_rank > 0, before_seg, -1), query_seg])
    allowed = (query_seg[:, None] == key_seg[None, :]) & (key_pos[None, :] <= positions[:, None])

    def masked_scores():
        scores = (
            jnp.einsum("qhd,khd->hqk", query, key_rows, preferred_element_type=F32) * score_scale
        )
        return jnp.where(allowed[None], scores, NEG)

    scores = masked_scores()
    row_top = jnp.max(scores, axis=2, keepdims=True)
    shifted = jnp.exp(scores - row_top)
    row_total = jnp.sum(shifted, axis=2, keepdims=True)
    weights = (shifted / row_total).astype(BF16)
    attended = jnp.einsum("hqk,khd->qhd", weights, value_rows, preferred_element_type=F32)
    attn_rows = attended.astype(BF16).reshape(rows, heads * HD)
    log_norm = row_top + jnp.log(row_total)

    attn_part = mm(attn_rows, w_output).astype(BF16)
    attn_own = lax.psum_scatter(attn_part, "tp", scatter_dimension=1, tiled=True)
    attn_total = lax.all_gather(attn_own, "tp", axis=1, tiled=True)
    resid = x_full + attn_total.astype(F32)
    inv_two = lax.rsqrt(jnp.mean(resid * resid, axis=1, keepdims=True) + EPS)
    mixed = (resid * inv_two * gain_two).astype(BF16)
    mixed_peer = swap(mixed, "ep", 1)
    resid_own = own_columns(resid)

    def router(values):
        logits = mm(values, w_router)
        return logits, jax.nn.softmax(logits, axis=1)

    logits, router_prob = router(mixed)
    combine = router_prob * route_hot
    combine_peer = router(mixed_peer)[1] * route_hot_peer
    switch_logit = mm(mixed, shared_switch[:, None])
    switch = jax.nn.sigmoid(switch_logit)

    def own_experts(value):
        return lax.dynamic_slice_in_dim(value, ep_rank * experts_own, experts_own, 1)

    hidden_s, gate_s, up_s, dots_s, along_s = ffn_pieces(
        mixed, grad_rows, switch, shared_gate, shared_up, shared_down, 1
    )
    gate_up_s = jnp.concatenate([gate_s, up_s], axis=1)
    total_s = pair_rows(mixed, gate_up_s)
    total_sd = pair_columns(hidden_s, grad_rows)
    grad_s = mm_nt(gate_s, shared_gate) + mm_nt(up_s, shared_up)
    out_s = mm(hidden_s, shared_down)

    hidden_width = experts_own * expert_width
    gate_w = jnp.transpose(expert_gate, (1, 0, 2)).reshape(width, hidden_width)
    up_w = jnp.transpose(expert_up, (1, 0, 2)).reshape(width, hidden_width)
    down_w = expert_down.reshape(hidden_width, width)
    both = jnp.concatenate([mixed, mixed_peer], axis=0)
    both_grad = jnp.concatenate([grad_rows, grad_peer], axis=0)
    scale_e = jnp.concatenate([own_experts(combine), own_experts(combine_peer)], axis=0)
    hidden_e, gate_e, up_e, dots_e, along_e = ffn_pieces(
        both, both_grad, scale_e, gate_w, up_w, down_w, experts_own
    )
    grad_e = mm_nt(gate_e, gate_w) + mm_nt(up_e, up_w)
    grad_e_back = swap(grad_e[rows:].astype(BF16), "ep", 1)
    small_e = jnp.concatenate([dots_e, along_e[:, None]], axis=1)
    small_back = swap(small_e[rows:], "ep", 1)
    grad_part = (grad_s + grad_e[:rows] + grad_back_f32(grad_e_back)).astype(BF16)
    grad_own = lax.psum_scatter(grad_part, "tp", scatter_dimension=1, tiled=True).astype(F32)

    gate_up_e = jnp.concatenate([gate_e, up_e], axis=1)
    total_e = pair_rows(both, gate_up_e)
    total_ed = pair_columns(hidden_e, both_grad)
    out_e = mm(hidden_e, down_w)
    out_e_back = swap(out_e[rows:].astype(BF16), "ep", 1)

    first = ep_rank == 0
    dots_here, dots_there = dots_e[:rows], small_back[:, :experts_own]
    dots_all = jnp.concatenate(
        [jnp.where(first, dots_here, dots_there), jnp.where(first, dots_there, dots_here)], axis=1
    )
    along = along_s + along_e[:rows] + small_back[:, experts_own]
    small = lax.psum(jnp.concatenate([dots_all, dots_s, along[:, None]], axis=1), "tp")
    grad_prob = small[:, :experts] * route_hot
    grad_switch = small[:, experts : experts + 1]
    along = small[:, experts + 1 : experts + 2]
    grad_logits = (
        router_prob * (grad_prob - jnp.sum(router_prob * grad_prob, axis=1, keepdims=True))
    ).astype(BF16)
    grad_slogit = (grad_switch * switch * (1.0 - switch)).astype(BF16)
    grad_router = mm_tn(mixed, grad_logits)
    grad_switch_w = mm_tn(mixed, grad_slogit)
    tp_rows = lax.dynamic_slice_in_dim(w_router, tp_rank * width_own, width_own, 0)
    grad_own = (
        grad_own
        + mm_nt(grad_logits, tp_rows)
        + grad_slogit.astype(F32) * own_columns(shared_switch).astype(F32)[None, :]
    )
    along = (
        along
        + jnp.sum(grad_logits.astype(F32) * logits, axis=1, keepdims=True)
        + grad_slogit.astype(F32) * switch_logit
    )
    gain_two_own = norm_ffn.astype(F32)
    grad_resid = (
        output_gradient.astype(F32)
        + inv_two * gain_two_own * grad_own
        - resid_own * (inv_two * inv_two) * (along / width)
    )
    grad_gain_two = jnp.sum(grad_own * resid_own * inv_two, axis=0)
    resid_low = lax.all_gather(grad_resid.astype(BF16), "tp", axis=1, tiled=True)

    ffn_part = (out_s + out_e[:rows] + out_e_back.astype(F32)).astype(BF16)
    ffn_own = lax.psum_scatter(ffn_part, "tp", scatter_dimension=1, tiled=True)
    layer_out = (resid_own + ffn_own.astype(F32)).astype(BF16)

    total_wo = pair_columns(attn_rows, resid_low)
    grad_attn = mm_nt(resid_low, w_output).astype(BF16).reshape(rows, heads, HD)
    probs = jnp.exp(masked_scores() - log_norm)
    grad_probs = jnp.einsum("qhd,khd->hqk", grad_attn, value_rows, preferred_element_type=F32)
    grad_scores = (
        probs * (grad_probs - jnp.sum(probs * grad_probs, axis=2, keepdims=True))
    ).astype(BF16)
    grad_query = (
        jnp.einsum("hqk,khd->qhd", grad_scores, key_rows, preferred_element_type=F32) * score_scale
    )
    grad_keys = (
        jnp.einsum("hqk,qhd->khd", grad_scores, query, preferred_element_type=F32) * score_scale
    )
    grad_values = jnp.einsum(
        "hqk,qhd->khd", probs.astype(BF16), grad_attn, preferred_element_type=F32
    )
    later = lax.ppermute(
        jnp.stack([grad_keys[:rows], grad_values[:rows]]).astype(BF16), "ep", back
    ).astype(F32)
    grad_key = grad_keys[rows:] + later[0]
    grad_value = grad_values[rows:] + later[1]
    shape = (rows, heads * HD)
    grad_qpre = rotate(grad_query, cos_table, -sin_table).astype(BF16).reshape(shape)
    grad_kpre = rotate(grad_key, cos_table, -sin_table).astype(BF16).reshape(shape)
    grad_vpre = grad_value.astype(BF16).reshape(shape)
    grad_normed = (
        mm_nt(grad_qpre, w_query) + mm_nt(grad_kpre, w_key) + mm_nt(grad_vpre, w_value)
    ).astype(BF16)
    normed_own = lax.psum_scatter(grad_normed, "tp", scatter_dimension=1, tiled=True).astype(F32)
    row_part = jnp.sum(
        grad_qpre.astype(F32) * q_pre
        + grad_kpre.astype(F32) * k_pre
        + grad_vpre.astype(F32) * v_pre,
        axis=1,
        keepdims=True,
    )
    row_total = lax.psum(row_part, "tp")
    total_qkv = pair_rows(normed, jnp.concatenate([grad_qpre, grad_kpre, grad_vpre], axis=1))
    x_own = tokens.astype(F32)
    grad_tokens = (
        grad_resid
        + inv_one * norm_attn.astype(F32) * normed_own
        - x_own * (inv_one * inv_one) * (row_total / width)
    )
    grad_gain_one = jnp.sum(normed_own * x_own * inv_one, axis=0)

    flat = jnp.concatenate(
        [grad_gain_two, grad_router.reshape(-1), grad_switch_w.reshape(-1), grad_gain_one]
    )
    flat = lax.psum(flat, ("dp", "ep"))
    grad_gain_two = flat[:width_own]
    grad_router = flat[width_own : width_own + width * experts].reshape(width, experts)
    grad_switch_w = flat[width_own + width * experts : width_own + width * (experts + 1)]
    grad_gain_one = flat[width_own + width * (experts + 1) :]

    shared_gu = spread(total_dense(total_s, 0), 0)
    shared_d = spread(total_dense(total_sd, 0), 1)
    expert_gu = spread(total_expert(total_e, 0), 0)
    expert_d = spread(total_expert(total_ed, 0), 1)
    wo_grad = spread(total_dense(total_wo, 0), 1)
    qkv_grad = spread(total_dense(total_qkv, 0), 0)
    qkv = heads * HD

    def per_expert(value):
        return jnp.transpose(value.reshape(width, experts_own, expert_width), (1, 0, 2))

    return (
        layer_out,
        grad_tokens,
        grad_gain_one,
        qkv_grad[:, :qkv],
        qkv_grad[:, qkv : 2 * qkv],
        qkv_grad[:, 2 * qkv :],
        wo_grad,
        grad_gain_two,
        grad_router,
        grad_switch_w,
        shared_gu[:, : shared_gate.shape[1]],
        shared_gu[:, shared_gate.shape[1] :],
        shared_d,
        per_expert(expert_gu[:, :hidden_width]),
        per_expert(expert_gu[:, hidden_width:]),
        expert_d.reshape(experts_own, expert_width, width),
    )


def grad_back_f32(value):
    return value.astype(F32)


def solution(mesh):
    placed = (
        P(("dp", "ep"), "tp"),
        P("tp"),
        P(None, "tp"),
        P(None, "tp"),
        P(None, "tp"),
        P("tp", None),
        P("tp"),
        P(),
        P(),
        P(None, "tp"),
        P(None, "tp"),
        P("tp", None),
        P("ep", None, "tp"),
        P("ep", None, "tp"),
        P("ep", "tp", None),
        P(("dp", "ep"), None),
        P("dp"),
        P(("dp", "ep"), "tp"),
    )
    return jax.shard_map(
        body,
        mesh=mesh,
        in_specs=placed,
        out_specs=(
            P(("dp", "ep"), "tp"),
            P(("dp", "ep"), "tp"),
            P("tp"),
            P(None, "tp"),
            P(None, "tp"),
            P(None, "tp"),
            P("tp", None),
            P("tp"),
            P(),
            P(),
            P(None, "tp"),
            P(None, "tp"),
            P("tp", None),
            P("ep", None, "tp"),
            P("ep", None, "tp"),
            P("ep", "tp", None),
        ),
        check_vma=False,
    )
```

time: 2230 us -> 1150 us (0.52)
  waiting for transfers between devices: 1210 us -> 530 us
  blocking collectives: 314 us -> 27.9 us
  local copies, waits for them, and re-layouts: 242 us -> 133 us
    psum x4 -> x1, waiting for transfers between devices: 752 us -> 44.1 us  [body(): flat = lax.psum(flat, ('dp', 'ep'))]
    ppermute x2 -> x40, waiting for transfers between devices: 36.5 us -> 365 us  [the longest x38 334 us: swap(): return lax.ppermute(value, axis, [(i, i ^ bit) for i in range(count)])]
    all_to_all x2 -> x0, waiting for transfers between devices: 323 us -> none  [to_source(): lax.all_to_all(payload, 'ep', split_axis=1, concat_axis=0, tiled=True)]
    all_to_all x2 -> x0, blocking collectives: 233 us -> none  [to_owner(): lax.all_to_all(payload, 'ep', split_axis=0, concat_axis=1, tiled=True)]
    gather x5 -> x2, local copies, waits for them, and re-layouts: 98.2 us -> 11.6 us  [ffn_pieces(): jnp.repeat(scale, hidden_width // groups, axis=1, total_repeat_length=hid...]
    reshape x5 -> x3, local copies, waits for them, and re-layouts: 63.5 us -> 3.13 us  [the longest x1 2.04 us: body(): value_own = v_pre.astype(BF16).reshape(rows, heads, HD)]
    slice x3 -> x12, local copies, waits for them, and re-layouts: 0.3 us -> 57.8 us  [the longest x2 20.3 us: body(): expert_gu[:, hidden_width:]]
    reduce_sum x8 -> x7, other arithmetic: 53.7 us -> 5.65 us  [the longest x1 3.01 us: ffn_pieces(): dots = jnp.sum((hidden * grad_hidden).reshape(count, groups, -1), axis=2)]
  transfers between devices with their start and end apart: 12 -> 49, of which waited for: 11 -> 20; matrix products, arithmetic and copies ran while one was open for 12% -> 40% of each run, Pallas kernels for 0% -> 0%
where the time goes in v1:
time: 1150 us
  waiting for transfers between devices  530 us (46%)
  matrix products  222 us (19%)
  other arithmetic  177 us (15%)
  local copies, waits for them, and re-layouts  133 us (12%)
  starting transfers between devices  38.6 us (3%)
  blocking collectives  27.9 us (2%)
  between operations  16.3 us (1%)
    ppermute x38, waiting for transfers between devices, swap(): return lax.ppermute(value, axis, [(i, i ^ bit) for i in range(count)])  334 us
    dot_general x14, matrix products, mm_tn(): lax.dot_general(left, right, (((0,), (0,)), ((), ())), preferred_element_...  70.6 us
    dot_general x11, matrix products, mm_nt(): lax.dot_general(left, right, (((1,), (1,)), ((), ())), preferred_element_...  67.5 us
    dot_general x13, matrix products, mm(): lax.dot_general(left, right, (((1,), (0,)), ((), ())), preferred_element_...  66.6 us
    all_gather x1, waiting for transfers between devices, body(): packed = lax.all_gather(packed, 'tp', axis=1, tiled=True)  48.2 us
    psum x1, waiting for transfers between devices, body(): flat = lax.psum(flat, ('dp', 'ep'))  44.1 us
    reduce_scatter x1, waiting for transfers between devices, body(): lax.psum_scatter(attn_part, 'tp', scatter_dimension=1, tiled=True)  41.5 us
    convert_element_type x6, other arithmetic, spread(): return jnp.concatenate([jnp.where(first, value, got), jnp.where(first, go...  37.2 us
  transfers between devices with their start and end apart: 49, of which 20 were waited for; matrix products, arithmetic and copies ran while one was open for 40% of the time, Pallas kernels for 0%

profile of v1, /device:TPU:0, one launch (start us, length us, event | category | flops | bytes accessed | tf_op | source)
XLA Modules:
  0.0 1145.0 jit_solution(16398593393237618623)
XLA Ops:
  12.8 48.2 %all-gather.5.cloned.1.call-done = bf16[528,2048]{1,0:T(8,128)(2,1)} async-done(((bf16[528,512]{1,0:T(8,128)(2,1)}), bf16[528,2048]{1,0:T(8,128)(2,1)}) %all-gather.5.cloned.1.call-update) | async-done | bytes 2162704 | tf_op jit(solution)/shard_map/all_gather | solution.py:169
  84.2 4.0 fusion.111
  95.1 4.4 collective-permute-start
  103.2 18.0 %collective-permute-done = bf16[2,512,4,128]{3,1,2,0:T(8,128)(2,1)} collective-permute-done((bf16[2,512,4,128]{3,1,2,0:T(8,128)(2,1)}, bf16[2,512,4,128]{3,1,2,0:T(8,128)(2,1)}, u32[]{:S(2)}, u32[]{:S(2)}) %collective-permute-start) | collective-permute-done | bytes 1048608 | tf_op jit(solution)/shard_map/ppermute | solution.py:193
  122.5 4.0 fusion.112
  135.1 8.4 all-gather.9.cloned.1.call-done
  147.4 41.5 %reduce-scatter.5.cloned.1.call-done = bf16[512,512]{1,0:T(8,128)(2,1)} async-done(((bf16[512,2048]{1,0:T(8,128)(2,1)}), bf16[512,512]{1,0:T(8,128)(2,1)}) %reduce-scatter.5.cloned.1.call-update) | async-done | bytes 524304 | tf_op jit(solution)/shard_map/reduce_scatter | solution.py:221
  189.0 8.4 fusion.120
  202.0 10.8 fusion.122
  212.8 22.9 %all-gather.7.cloned.1.call-done = bf16[512,2048]{1,0:T(8,128)(2,1)} async-done(((bf16[512,512]{1,0:T(8,128)(2,1)}), bf16[512,2048]{1,0:T(8,128)(2,1)}) %all-gather.7.cloned.1.call-update) | async-done | bytes 2097168 | tf_op jit(solution)/shard_map/all_gather | solution.py:222
  235.7 5.2 convert_add_fusion
  248.9 5.5 add_reduce_fusion.1
  254.4 5.2 convolution_convert_fusion
  264.4 5.0 fusion.121
  269.4 20.5 %collective-permute-done.1 = bf16[512,2048]{1,0:T(8,128)(2,1)S(1)} collective-permute-done((bf16[512,2048]{1,0:T(8,128)(2,1)S(1)}, bf16[512,2048]{1,0:T(8,128)(2,1)S(1)}, u32[]{:S(2)}, u32[]{:S(2)}) %collective-permute-start.1) | collective-permute-done | bytes 2097184 | tf_op jit(solution)/shard_map/ppermute | solution.py:30
  291.3 5.4 gather_fusion
  296.7 6.2 copy.84
  302.9 11.6 %fusion.19 = f32[1024,1408]{1,0:T(8,128)} fusion(bf16[2048,1408]{0,1:T(8,128)(2,1)} %bitcast.194, bf16[512,2048]{1,0:T(8,128)(2,1)} %copy-done.62, bf16[512,2048]{1,0:T(8,128)(2,1)} %copy-done.2), kind=kOutput, calls=%fused_computation.100 | convolution fusion | flops 5913968640 | bytes 15728640 | tf_op jit(solution)/shard_map/dot_general | solution.py:17
  314.5 18.1 %add_reduce_fusion = (f32[1024]{0:T(1024)S(1)}, bf16[1024,1408]{1,0:T(8,128)(2,1)}, bf16[1024,1408]{1,0:T(8,128)(2,1)}, f32[1024,1408]{1,0:T(8,128)}, bf16[1024,1408]{1,0:T(8,128)(2,1)}) fusion(f32[1024,1408]{1,0:T(8,128)} %fusion.19, f32[1024,1408]{1,0:T(8,128)} %fusion.122, f32[1408,1024]{0,1:T(8,128)} %copy.84, bf16[2048,1408]{0,1:T(8,128)(2,1)} %bitcast.196, ...), kind=kOutput, calls=%fused_computation.31 | convolution fusion | flops 5948570624 | bytes 41684992 | tf_op jit(solution)/shard_map/dot_general | solution.py:17
  332.6 6.4 copy.85
  343.6 11.7 %fusion.123 = f32[1024,2048]{1,0:T(8,128)} fusion(bf16[1024,1408]{1,0:T(8,128)(2,1)} %get-tuple-element.100, bf16[2048,1408]{0,1:T(8,128)(2,1)} %bitcast.195), kind=kOutput, calls=%fused_computation.310 | convolution fusion | flops 5905580032 | bytes 17039360 | tf_op jit(solution)/shard_map/dot_general | solution.py:21
  358.7 11.8 %convolution_add_fusion = f32[1024,2048]{1,0:T(8,128)S(1)} fusion(f32[1024,2048]{1,0:T(8,128)} %fusion.123, bf16[1024,1408]{1,0:T(8,128)(2,1)} %get-tuple-element.101, bf16[2048,1408]{0,1:T(8,128)(2,1)} %bitcast.197), kind=kOutput, calls=%fused_computation.65 | convolution fusion | flops 5907677184 | bytes 25427968 | tf_op jit(solution)/shard_map/dot_general | solution.py:21
  370.6 14.2 %convolution_convert_fusion.1 = bf16[1024,2816]{1,0:T(8,128)(2,1)} fusion(bf16[1024,1408]{1,0:T(8,128)(2,1)} %get-tuple-element.101, bf16[1024,1408]{1,0:T(8,128)(2,1)} %get-tuple-element.100, s32[]{:T(128)S(6)} %select_n.416, bf16[512,2048]{1,0:T(8,128)(2,1)S(1)} %copy-done.3, bf16[512,2048]{1,0:T(8,128)(2,1)S(1)} %copy-done.63), kind=kOutput, calls=%fused_computation.42 | convolution fusion | flops 5924192256 | bytes 15728644 | tf_op jit(solution)/shard_map/dot_general | solution.py:25
  384.8 6.7 fusion.119
  391.5 4.6 convolution_convert_fusion.4
  408.5 17.1 %psum.21 = f32[512,10]{0,1:T(8,128)S(1)} all-reduce(f32[512,10]{0,1:T(8,128)S(1)} %pad_maximum_fusion.35), channel_id=1, replica_groups=mesh['dp'=4,'ep'=2,'tp'=4] {'tp'}, use_global_device_ids=true, to_apply=%region_16.17 | all-reduce | flops 5120 | bytes 40960 | tf_op jit(solution)/shard_map/psum | solution.py:280
  432.3 87.8 %collective-permute-done.27 = bf16[704,1024]{1,0:T(8,128)(2,1)} collective-permute-done((bf16[704,1024]{1,0:T(8,128)(2,1)}, bf16[704,1024]{1,0:T(8,128)(2,1)}, u32[]{:S(2)}, u32[]{:S(2)}) %collective-permute-start.27) | collective-permute-done | bytes 1441824 | tf_op jit(solution)/shard_map/ppermute | solution.py:30
  524.9 8.6 fusion.10
  535.9 6.4 collective-permute-done.28
  545.2 5.7 add_convert_fusion.3
  552.8 10.0 collective-permute-done.29
  565.5 6.2 add_convert_fusion.1
  576.1 8.0 fusion.12
  584.3 8.1 collective-permute-done.37
  595.9 3.9 collective-permute-done.30
  605.6 10.8 add_convert_fusion
  616.4 41.8 %collective-permute-done.21 = bf16[512,2816]{1,0:T(8,128)(2,1)} collective-permute-done((bf16[512,2816]{1,0:T(8,128)(2,1)}, bf16[512,2816]{1,0:T(8,128)(2,1)}, u32[]{:S(2)}, u32[]{:S(2)}) %collective-permute-start.21) | collective-permute-done | bytes 2883616 | tf_op jit(solution)/shard_map/ppermute | solution.py:30
  670.1 4.0 fusion.101
  674.5 22.5 %collective-permute-done.22 = bf16[256,2816]{1,0:T(8,128)(2,1)} collective-permute-done((bf16[256,2816]{1,0:T(8,128)(2,1)}, bf16[256,2816]{1,0:T(8,128)(2,1)}, u32[]{:S(2)}, u32[]{:S(2)}) %collective-permute-start.22) | collective-permute-done | bytes 1441824 | tf_op jit(solution)/shard_map/ppermute | solution.py:30
  704.8 5.9 maximum_convert_fusion.3
  710.7 48.1 %collective-permute-done.33 = bf16[512,2816]{1,0:T(8,128)(2,1)} collective-permute-done((bf16[512,2816]{1,0:T(8,128)(2,1)}, bf16[512,2816]{1,0:T(8,128)(2,1)}, u32[]{:S(2)}, u32[]{:S(2)}) %collective-permute-start.33) | collective-permute-done | bytes 2883616 | tf_op jit(solution)/shard_map/ppermute | solution.py:30
  758.8 4.2 add_convert_fusion.4
  767.3 5.9 maximum_convert_fusion.4
  773.2 3.7 convolution_convert_fusion.7
  776.9 4.8 fusion.27
  800.2 12.4 %collective-permute-done.7 = bf16[2,512,4,128]{3,1,2,0:T(8,128)(2,1)S(1)} collective-permute-done((bf16[2,512,4,128]{3,1,2,0:T(8,128)(2,1)S(1)}, bf16[2,512,4,128]{3,1,2,0:T(8,128)(2,1)S(1)}, u32[]{:S(2)}, u32[]{:S(2)}) %collective-permute-start.7) | collective-permute-done | bytes 1048608 | tf_op jit(solution)/shard_map/ppermute | solution.py:330
  834.6 45.7 %collective-permute-done.15 = bf16[256,1024]{1,0:T(8,128)(2,1)S(1)} collective-permute-done((bf16[256,1024]{1,0:T(8,128)(2,1)S(1)}, bf16[256,1024]{1,0:T(8,128)(2,1)S(1)}, u32[]{:S(2)}, u32[]{:S(2)}) %collective-permute-start.15) | collective-permute-done | bytes 524320 | tf_op jit(solution)/shard_map/ppermute | solution.py:30
  885.5 5.7 collective-permute-done.16
  901.4 4.1 add_convert_fusion.2
  909.8 10.9 psum.22
  926.0 23.7 %collective-permute-done.9 = bf16[512,1536]{1,0:T(8,128)(2,1)} collective-permute-done((bf16[512,1536]{1,0:T(8,128)(2,1)}, bf16[512,1536]{1,0:T(8,128)(2,1)}, u32[]{:S(2)}, u32[]{:S(2)}) %collective-permute-start.9) | collective-permute-done | bytes 1572896 | tf_op jit(solution)/shard_map/ppermute | solution.py:30
  962.7 10.3 collective-permute-done.10
  977.3 4.1 maximum_convert_fusion.5
  981.4 44.1 %all-reduce.2.cloned.1.call-done = f32[19456]{0:T(1024)} async-done(((f32[19456]{0:T(1024)}), f32[19456]{0:T(1024)}) %all-reduce.2.cloned.1.call-update) | async-done | bytes 77840 | tf_op jit(solution)/shard_map/psum | solution.py:363
  1036.6 11.0 broadcast_select_fusion.1
  1047.6 6.9 maximum_convert_fusion.1
  1054.4 8.4 fusion.105
  1062.9 11.9 %copy.96 = f32[2048,1408]{0,1:T(8,128)} copy(f32[2048,1408]{1,0:T(8,128)} %get-tuple-element.105) | data formatting | bytes 23068672 | tf_op jit(solution)/shard_map/slice | solution.py:394
  1074.8 11.9 %copy.97 = f32[2048,1408]{0,1:T(8,128)} copy(f32[2048,1408]{1,0:T(8,128)} %get-tuple-element.104) | data formatting | bytes 23068672 | tf_op jit(solution)/shard_map/slice | solution.py:395
  1086.7 10.6 broadcast_select_fusion.3
  1102.0 8.1 maximum_convert_fusion
  1110.1 8.4 fusion.106
  1121.9 6.3 maximum_convert_fusion.2
  1128.3 9.8 fusion.107
  (516 shorter events, 252.6 us)
Async XLA Ops:
  7.2 77.0 %copy-start = (bf16[2048,512]{1,0:T(8,128)(2,1)S(1)}, bf16[2048,512]{1,0:T(8,128)(2,1)}, u32[]{:S(2)}) copy-start(bf16[2048,512]{1,0:T(8,128)(2,1)} %param.28) | copy-start | bytes 6291460
  7.2 53.8 %all-gather.5.cloned.1.call-start = ((), (), s32[]{:S(2)}) async-start(), calls=%async_computation.4 | async-start | bytes 2703360 | tf_op jit(solution)/shard_map/all_gather | solution.py:169
  10.9 132.6 %all-gather.9.cloned.1.call-start = ((), (), s32[]{:S(2)}) async-start(), calls=%async_computation.8 | async-start | bytes 2621440 | tf_op jit(solution)/shard_map/all_gather | solution.py:173
  12.8 77.5 %copy-start.55 = (f32[512,64]{1,0:T(8,128)}, f32[512,64]{1,0:T(8,128)S(1)}, u32[]{:S(2)}) copy-start(f32[512,64]{1,0:T(8,128)S(1)} %get-tuple-element.183) | copy-start | bytes 393220
  95.1 26.0 %collective-permute-start = (bf16[2,512,4,128]{3,1,2,0:T(8,128)(2,1)}, bf16[2,512,4,128]{3,1,2,0:T(8,128)(2,1)}, u32[]{:S(2)}, u32[]{:S(2)}) collective-permute-start(bf16[2,512,4,128]{3,1,2,0:T(8,128)(2,1)} %pad_maximum_fusion.20), channel_id=1, source_target_pairs={{0,4},{1,5},{2,6},{3,7},{8,12},{9,13},{10,14},{11,15},{16,20},{17,... | collective-permute-start | bytes 3145736 | tf_op jit(solution)/shard_map/ppermute | solution.py:193
  99.5 89.4 %reduce-scatter.5.cloned.1.call-start = ((), (), s32[]{:S(2)}) async-start(), calls=%async_computation.5 | async-start | bytes 2621440 | tf_op jit(solution)/shard_map/reduce_scatter | solution.py:221
  135.0 100.7 %all-gather.7.cloned.1.call-start = ((), (), s32[]{:S(2)}) async-start(), calls=%async_computation.6 | async-start | bytes 2621440 | tf_op jit(solution)/shard_map/all_gather | solution.py:222
  143.5 54.8 %collective-permute-start.4 = (bf16[512,2048]{1,0:T(8,128)(2,1)}, bf16[512,2048]{1,0:T(8,128)(2,1)}, u32[]{:S(2)}, u32[]{:S(2)}) collective-permute-start(bf16[512,2048]{1,0:T(8,128)(2,1)} %all-gather.9.cloned.1.call-done), channel_id=1, source_target_pairs={{0,4},{4,0},{1,5},{5,1},{2,6},{6,2},{3,7},{7,3},{8,12},{12,8},{9,1... | collective-permute-start | bytes 6291464 | tf_op jit(solution)/shard_map/ppermute | solution.py:30
  144.9 145.7 %collective-permute-start.2 = (f32[512,8]{0,1:T(8,128)S(1)}, f32[512,8]{0,1:T(8,128)S(1)}, u32[]{:S(2)}, u32[]{:S(2)}) collective-permute-start(f32[512,8]{0,1:T(8,128)S(1)} %convert_reduce_fusion), channel_id=1, source_target_pairs={{0,4},{4,0},{1,5},{5,1},{2,6},{6,2},{3,7},{7,3},{8,12},{12,8},{9,1... | collective-permute-start | bytes 49160 | tf_op jit(solution)/shard_map/ppermute | solution.py:30
  189.0 481.1 %reduce-scatter.9.cloned.1.call-start = ((), (), s32[]{:S(2)}) async-start(), calls=%async_computation.9 | async-start | bytes 2621440 | tf_op jit(solution)/shard_map/reduce_scatter | solution.py:266
  242.6 47.4 %collective-permute-start.1 = (bf16[512,2048]{1,0:T(8,128)(2,1)S(1)}, bf16[512,2048]{1,0:T(8,128)(2,1)S(1)}, u32[]{:S(2)}, u32[]{:S(2)}) collective-permute-start(bf16[512,2048]{1,0:T(8,128)(2,1)S(1)} %multiply_convert_fusion.4), channel_id=1, source_target_pairs={{0,4},{4,0},{1,5},{5,1},{2,6},{6,2},{3,7},{7,3},{8,12},{12,8},{9,1... | collective-permute-start | bytes 6291464 | tf_op jit(solution)/shard_map/ppermute | solution.py:30
  259.7 305.8 %collective-permute-start.20 = (bf16[1024,2816]{1,0:T(8,128)(2,1)}, bf16[1024,2816]{1,0:T(8,128)(2,1)}, u32[]{:S(2)}, u32[]{:S(2)}) collective-permute-start(bf16[1024,2816]{1,0:T(8,128)(2,1)} %convolution_convert_fusion), channel_id=1, source_target_pairs={{0,8},{8,0},{16,24},{24,16},{1,9},{9,1},{17,25},{25,17},{2,10},{10... | collective-permute-start | bytes 17301512 | tf_op jit(solution)/shard_map/ppermute | solution.py:30
  263.2 138.2 %collective-permute-start.26 = (bf16[1408,1024]{1,0:T(8,128)(2,1)}, bf16[1408,1024]{1,0:T(8,128)(2,1)}, u32[]{:S(2)}, u32[]{:S(2)}) collective-permute-start(bf16[1408,1024]{1,0:T(8,128)(2,1)} %convolution_convert_fusion.2), channel_id=1, source_target_pairs={{0,8},{8,0},{16,24},{24,16},{1,9},{9,1},{17,25},{25,17},{2,10},{10... | collective-permute-start | bytes 8650760 | tf_op jit(solution)/shard_map/ppermute | solution.py:30
  342.1 59.3 %collective-permute-start.6 = (f32[512,5]{0,1:T(8,128)S(1)}, f32[512,5]{0,1:T(8,128)S(1)}, u32[]{:S(2)}, u32[]{:S(2)}) collective-permute-start(f32[512,5]{0,1:T(8,128)S(1)} %pad_maximum_fusion.36), channel_id=1, source_target_pairs={{0,4},{4,0},{1,5},{5,1},{2,6},{6,2},{3,7},{7,3},{8,12},{12,8},{9,1... | collective-permute-start | bytes 30728 | tf_op jit(solution)/shard_map/ppermute | solution.py:30
  355.3 29.4 %slice-start.10 = ((s8[5767168]{0:T(1024)(128)(4,1)}), s8[4194304]{0:T(1024)(128)(4,1)S(1)}, s32[]{:S(2)}) async-start(s8[5767168]{0:T(1024)(128)(4,1)} %bitcast.199), calls=%async_computation.23 | async-start | bytes 8388608
  358.7 32.8 %copy-start.50 = (bf16[1024,1408]{1,0:T(8,128)(2,1)}, bf16[1024,1408]{1,0:T(8,128)(2,1)S(1)}, u32[]{:S(2)}) copy-start(bf16[1024,1408]{1,0:T(8,128)(2,1)S(1)} %fusion.2) | copy-start | bytes 8650756
  397.7 125.7 %collective-permute-start.5 = (bf16[512,2048]{1,0:T(8,128)(2,1)}, bf16[512,2048]{1,0:T(8,128)(2,1)}, u32[]{:S(2)}, u32[]{:S(2)}) collective-permute-start(bf16[512,2048]{1,0:T(8,128)(2,1)} %slice.327), channel_id=1, source_target_pairs={{0,4},{4,0},{1,5},{5,1},{2,6},{6,2},{3,7},{7,3},{8,12},{12,8},{9,1... | collective-permute-start | bytes 6291464 | tf_op jit(solution)/shard_map/ppermute | solution.py:30
  399.9 176.1 %collective-permute-start.3 = (bf16[512,2048]{1,0:T(8,128)(2,1)}, bf16[512,2048]{1,0:T(8,128)(2,1)}, u32[]{:S(2)}, u32[]{:S(2)}) collective-permute-start(bf16[512,2048]{1,0:T(8,128)(2,1)} %slice.328), channel_id=1, source_target_pairs={{0,4},{4,0},{1,5},{5,1},{2,6},{6,2},{3,7},{7,3},{8,12},{12,8},{9,1... | collective-permute-start | bytes 6291464 | tf_op jit(solution)/shard_map/ppermute | solution.py:30
  401.4 143.8 %collective-permute-start.36 = (bf16[1408,1024]{1,0:T(8,128)(2,1)}, bf16[1408,1024]{1,0:T(8,128)(2,1)}, u32[]{:S(2)}, u32[]{:S(2)}) collective-permute-start(bf16[1408,1024]{1,0:T(8,128)(2,1)} %convolution_convert_fusion.4), channel_id=1, source_target_pairs={{0,8},{8,0},{16,24},{24,16},{1,9},{9,1},{17,25},{25,17},{2,10},{10... | collective-permute-start | bytes 8650760 | tf_op jit(solution)/shard_map/ppermute | solution.py:30
  408.0 112.1 %collective-permute-start.27 = (bf16[704,1024]{1,0:T(8,128)(2,1)}, bf16[704,1024]{1,0:T(8,128)(2,1)}, u32[]{:S(2)}, u32[]{:S(2)}) collective-permute-start(bf16[704,1024]{1,0:T(8,128)(2,1)} %constant_dynamic-slice_fusion.4), channel_id=1, source_target_pairs={{0,4},{4,0},{1,5},{5,1},{2,6},{6,2},{3,7},{7,3},{8,12},{12,8},{9,1... | collective-permute-start | bytes 4325384 | tf_op jit(solution)/shard_map/ppermute | solution.py:30
  432.3 92.6 %copy-start.117 = (f32[512,2048]{1,0:T(8,128)S(1)}, f32[512,2048]{1,0:T(8,128)}, u32[]{:S(2)}) copy-start(f32[512,2048]{1,0:T(8,128)} %fusion.121) | copy-start | bytes 12582916
  432.3 92.6 %copy-start.121 = (bf16[512,1408]{1,0:T(8,128)(2,1)S(1)}, bf16[512,1408]{1,0:T(8,128)(2,1)}, u32[]{:S(2)}) copy-start(bf16[512,1408]{1,0:T(8,128)(2,1)} %copy-done.120) | copy-start | bytes 4325380
  520.1 84.6 %collective-permute-start.32 = (bf16[1024,2816]{1,0:T(8,128)(2,1)}, bf16[1024,2816]{1,0:T(8,128)(2,1)}, u32[]{:S(2)}, u32[]{:S(2)}) collective-permute-start(bf16[1024,2816]{1,0:T(8,128)(2,1)} %convolution_convert_fusion.1), channel_id=1, source_target_pairs={{0,8},{8,0},{16,24},{24,16},{1,9},{9,1},{17,25},{25,17},{2,10},{10... | collective-permute-start | bytes 17301512 | tf_op jit(solution)/shard_map/ppermute | solution.py:30
  523.5 18.9 %collective-permute-start.28 = (bf16[352,1024]{1,0:T(8,128)(2,1)}, bf16[352,1024]{1,0:T(8,128)(2,1)}, u32[]{:S(2)}, u32[]{:S(2)}) collective-permute-start(bf16[352,1024]{1,0:T(8,128)(2,1)} %constant_dynamic-slice_fusion.3), channel_id=1, source_target_pairs={{0,16},{8,24},{16,0},{24,8},{1,17},{9,25},{17,1},{25,9},{2,18},{10... | collective-permute-start | bytes 2162696 | tf_op jit(solution)/shard_map/ppermute | solution.py:30
  533.5 136.6 %reduce-scatter.7.cloned.1.call-start = ((), (), s32[]{:S(2)}) async-start(), calls=%async_computation.7 | async-start | bytes 2621440 | tf_op jit(solution)/shard_map/reduce_scatter | solution.py:311
  543.7 19.1 %collective-permute-start.29 = (bf16[352,1024]{1,0:T(8,128)(2,1)S(1)}, bf16[352,1024]{1,0:T(8,128)(2,1)S(1)}, u32[]{:S(2)}, u32[]{:S(2)}) collective-permute-start(bf16[352,1024]{1,0:T(8,128)(2,1)S(1)} %add_convert_fusion.14), channel_id=1, source_target_pairs={{0,16},{8,24},{16,0},{24,8},{1,17},{9,25},{17,1},{25,9},{2,18},{10... | collective-permute-start | bytes 2162696 | tf_op jit(solution)/shard_map/ppermute | solution.py:30
  552.3 40.1 %collective-permute-start.37 = (bf16[704,1024]{1,0:T(8,128)(2,1)}, bf16[704,1024]{1,0:T(8,128)(2,1)S(1)}, u32[]{:S(2)}, u32[]{:S(2)}) collective-permute-start(bf16[704,1024]{1,0:T(8,128)(2,1)} %constant_dynamic-slice_fusion.14), channel_id=1, source_target_pairs={{0,16},{8,24},{16,0},{24,8},{1,17},{9,25},{17,1},{25,9},{2,18},{10... | collective-permute-start | bytes 4325384 | tf_op jit(solution)/shard_map/ppermute | solution.py:30
  565.0 34.8 %collective-permute-start.30 = (bf16[704,1024]{1,0:T(8,128)(2,1)}, bf16[704,1024]{1,0:T(8,128)(2,1)}, u32[]{:S(2)}, u32[]{:S(2)}) collective-permute-start(bf16[704,1024]{1,0:T(8,128)(2,1)} %pad_maximum_fusion.19), channel_id=1, source_target_pairs={{0,4},{4,0},{1,5},{5,1},{2,6},{6,2},{3,7},{7,3},{8,12},{12,8},{9,1... | collective-permute-start | bytes 4325384 | tf_op jit(solution)/shard_map/ppermute | solution.py:30
  575.1 83.2 %collective-permute-start.21 = (bf16[512,2816]{1,0:T(8,128)(2,1)}, bf16[512,2816]{1,0:T(8,128)(2,1)}, u32[]{:S(2)}, u32[]{:S(2)}) collective-permute-start(bf16[512,2816]{1,0:T(8,128)(2,1)} %constant_dynamic-slice_fusion.6), channel_id=1, source_target_pairs={{0,4},{4,0},{1,5},{5,1},{2,6},{6,2},{3,7},{7,3},{8,12},{12,8},{9,1... | collective-permute-start | bytes 8650760 | tf_op jit(solution)/shard_map/ppermute | solution.py:30
  584.1 189.2 %all-gather.11.cloned.1.call-start = ((), (), s32[]{:S(2)}) async-start(), calls=%async_computation.10 | async-start | bytes 2621440 | tf_op jit(solution)/shard_map/all_gather | solution.py:308
  594.4 71.6 %collective-permute-start.38 = (bf16[704,1024]{1,0:T(8,128)(2,1)S(1)}, bf16[704,1024]{1,0:T(8,128)(2,1)}, u32[]{:S(2)}, u32[]{:S(2)}) collective-permute-start(bf16[704,1024]{1,0:T(8,128)(2,1)S(1)} %add_convert_fusion.9), channel_id=1, source_target_pairs={{0,16},{8,24},{16,0},{24,8},{1,17},{9,25},{17,1},{25,9},{2,18},{10... | collective-permute-start | bytes 4325384 | tf_op jit(solution)/shard_map/ppermute | solution.py:30
  602.5 55.8 %slice-start.4 = ((s8[5767168]{0:T(1024)(128)(4,1)}), s8[4194304]{0:T(1024)(128)(4,1)S(1)}, s32[]{:S(2)}) async-start(s8[5767168]{0:T(1024)(128)(4,1)} %bitcast.159), calls=%async_computation.17 | async-start | bytes 8388608
  604.7 53.6 %slice-start.5 = ((s8[5767168]{0:T(1024)(128)(4,1)}), s8[1572864]{0:T(1024)(128)(4,1)S(1)}, s32[]{:S(2)}) async-start(s8[5767168]{0:T(1024)(128)(4,1)} %bitcast.159), calls=%async_computation.18 | async-start | bytes 3145728
  604.7 97.1 %collective-permute-start.31 = (bf16[1408,1024]{1,0:T(8,128)(2,1)}, bf16[1408,1024]{1,0:T(8,128)(2,1)}, u32[]{:S(2)}, u32[]{:S(2)}) collective-permute-start(bf16[1408,1024]{1,0:T(8,128)(2,1)} %pad_maximum_fusion.9), channel_id=1, source_target_pairs={{0,8},{8,0},{16,24},{24,16},{1,9},{9,1},{17,25},{25,17},{2,10},{10... | collective-permute-start | bytes 8650760 | tf_op jit(solution)/shard_map/ppermute | solution.py:30
  616.4 47.2 %copy-start.37 = (bf16[1024,2816]{1,0:T(8,128)(2,1)}, bf16[1024,2816]{1,0:T(8,128)(2,1)S(1)}, u32[]{:S(2)}) copy-start(bf16[1024,2816]{1,0:T(8,128)(2,1)S(1)} %add_convert_fusion) | copy-start | bytes 17301508
  662.2 34.8 %collective-permute-start.22 = (bf16[256,2816]{1,0:T(8,128)(2,1)}, bf16[256,2816]{1,0:T(8,128)(2,1)}, u32[]{:S(2)}, u32[]{:S(2)}) collective-permute-start(bf16[256,2816]{1,0:T(8,128)(2,1)} %constant_dynamic-slice_fusion.5), channel_id=1, source_target_pairs={{0,16},{8,24},{16,0},{24,8},{1,17},{9,25},{17,1},{25,9},{2,18},{10... | collective-permute-start | bytes 4325384 | tf_op jit(solution)/shard_map/ppermute | solution.py:30
  665.4 93.4 %collective-permute-start.33 = (bf16[512,2816]{1,0:T(8,128)(2,1)}, bf16[512,2816]{1,0:T(8,128)(2,1)}, u32[]{:S(2)}, u32[]{:S(2)}) collective-permute-start(bf16[512,2816]{1,0:T(8,128)(2,1)} %constant_dynamic-slice_fusion.2), channel_id=1, source_target_pairs={{0,16},{8,24},{16,0},{24,8},{1,17},{9,25},{17,1},{25,9},{2,18},{10... | collective-permute-start | bytes 8650760 | tf_op jit(solution)/shard_map/ppermute | solution.py:30
  670.1 94.4 %collective-permute-start.39 = (bf16[1408,1024]{1,0:T(8,128)(2,1)}, bf16[1408,1024]{1,0:T(8,128)(2,1)}, u32[]{:S(2)}, u32[]{:S(2)}) collective-permute-start(bf16[1408,1024]{1,0:T(8,128)(2,1)} %pad_maximum_fusion.10), channel_id=1, source_target_pairs={{0,8},{8,0},{16,24},{24,16},{1,9},{9,1},{17,25},{25,17},{2,10},{10... | collective-permute-start | bytes 8650760 | tf_op jit(solution)/shard_map/ppermute | solution.py:30
  674.1 285.8 %reduce-scatter.11.cloned.1.call-start = ((), (), s32[]{:S(2)}) async-start(), calls=%async_computation.11 | async-start | bytes 2621440 | tf_op jit(solution)/shard_map/reduce_scatter | solution.py:342
  700.3 93.2 %collective-permute-start.23 = (bf16[256,2816]{1,0:T(8,128)(2,1)}, bf16[256,2816]{1,0:T(8,128)(2,1)}, u32[]{:S(2)}, u32[]{:S(2)}) collective-permute-start(bf16[256,2816]{1,0:T(8,128)(2,1)} %add_convert_fusion.11), channel_id=1, source_target_pairs={{0,16},{8,24},{16,0},{24,8},{1,17},{9,25},{17,1},{25,9},{2,18},{10... | collective-permute-start | bytes 4325384 | tf_op jit(solution)/shard_map/ppermute | solution.py:30
  701.7 57.1 %slice-start.2 = ((s8[5767168]{0:T(1024)(128)(4,1)}), s8[4194304]{0:T(1024)(128)(4,1)S(1)}, s32[]{:S(2)}) async-start(s8[5767168]{0:T(1024)(128)(4,1)} %bitcast.157), calls=%async_computation.15 | async-start | bytes 8388608
  704.8 54.1 %slice-start.3 = ((s8[5767168]{0:T(1024)(128)(4,1)}), s8[1572864]{0:T(1024)(128)(4,1)S(1)}, s32[]{:S(2)}) async-start(s8[5767168]{0:T(1024)(128)(4,1)} %bitcast.157), calls=%async_computation.16 | async-start | bytes 3145728
  710.7 53.8 %copy-start.20 = (bf16[704,1024]{1,0:T(8,128)(2,1)S(1)}, bf16[704,1024]{1,0:T(8,128)(2,1)}, u32[]{:S(2)}) copy-start(bf16[704,1024]{1,0:T(8,128)(2,1)} %copy-done.19) | copy-start | bytes 4325380
  710.7 53.8 %copy-start.22 = (bf16[704,1024]{1,0:T(8,128)(2,1)S(1)}, bf16[704,1024]{1,0:T(8,128)(2,1)}, u32[]{:S(2)}) copy-start(bf16[704,1024]{1,0:T(8,128)(2,1)} %copy-done.21) | copy-start | bytes 4325380
  763.0 130.0 %collective-permute-start.34 = (bf16[512,2816]{1,0:T(8,128)(2,1)}, bf16[512,2816]{1,0:T(8,128)(2,1)}, u32[]{:S(2)}, u32[]{:S(2)}) collective-permute-start(bf16[512,2816]{1,0:T(8,128)(2,1)} %add_convert_fusion.4), channel_id=1, source_target_pairs={{0,16},{8,24},{16,0},{24,8},{1,17},{9,25},{17,1},{25,9},{2,18},{10... | collective-permute-start | bytes 8650760 | tf_op jit(solution)/shard_map/ppermute | solution.py:30
  788.7 23.8 %collective-permute-start.7 = (bf16[2,512,4,128]{3,1,2,0:T(8,128)(2,1)S(1)}, bf16[2,512,4,128]{3,1,2,0:T(8,128)(2,1)S(1)}, u32[]{:S(2)}, u32[]{:S(2)}) collective-permute-start(bf16[2,512,4,128]{3,1,2,0:T(8,128)(2,1)S(1)} %pad_maximum_fusion.22), channel_id=1, source_target_pairs={{4,0},{5,1},{6,2},{7,3},{12,8},{13,9},{14,10},{15,11},{20,16},{21,... | collective-permute-start | bytes 3145736 | tf_op jit(solution)/shard_map/ppermute | solution.py:330
  792.2 32.9 %collective-permute-start.14 = (bf16[512,1024]{1,0:T(8,128)(2,1)}, bf16[512,1024]{1,0:T(8,128)(2,1)}, u32[]{:S(2)}, u32[]{:S(2)}) collective-permute-start(bf16[512,1024]{1,0:T(8,128)(2,1)} %convolution_convert_fusion.6), channel_id=1, source_target_pairs={{0,8},{8,0},{16,24},{24,16},{1,9},{9,1},{17,25},{25,17},{2,10},{10... | collective-permute-start | bytes 3145736 | tf_op jit(solution)/shard_map/ppermute | solution.py:30
  797.5 125.8 %collective-permute-start.24 = (bf16[512,2816]{1,0:T(8,128)(2,1)}, bf16[512,2816]{1,0:T(8,128)(2,1)}, u32[]{:S(2)}, u32[]{:S(2)}) collective-permute-start(bf16[512,2816]{1,0:T(8,128)(2,1)} %pad_maximum_fusion.8), channel_id=1, source_target_pairs={{0,4},{4,0},{1,5},{5,1},{2,6},{6,2},{3,7},{7,3},{8,12},{12,8},{9,1... | collective-permute-start | bytes 8650760 | tf_op jit(solution)/shard_map/ppermute | solution.py:30
  827.7 52.5 %collective-permute-start.15 = (bf16[256,1024]{1,0:T(8,128)(2,1)S(1)}, bf16[256,1024]{1,0:T(8,128)(2,1)S(1)}, u32[]{:S(2)}, u32[]{:S(2)}) collective-permute-start(bf16[256,1024]{1,0:T(8,128)(2,1)S(1)} %constant_dynamic-slice_fusion.8), channel_id=1, source_target_pairs={{0,4},{4,0},{1,5},{5,1},{2,6},{6,2},{3,7},{7,3},{8,12},{12,8},{9,1... | collective-permute-start | bytes 1572872 | tf_op jit(solution)/shard_map/ppermute | solution.py:30
  833.3 68.0 %collective-permute-start.8 = (bf16[1024,1536]{1,0:T(8,128)(2,1)}, bf16[1024,1536]{1,0:T(8,128)(2,1)}, u32[]{:S(2)}, u32[]{:S(2)}) collective-permute-start(bf16[1024,1536]{1,0:T(8,128)(2,1)} %convolution_convert_fusion.3), channel_id=1, source_target_pairs={{0,8},{8,0},{16,24},{24,16},{1,9},{9,1},{17,25},{25,17},{2,10},{10... | collective-permute-start | bytes 9437192 | tf_op jit(solution)/shard_map/ppermute | solution.py:30
  882.0 9.2 collective-permute-start.16
  885.3 140.3 %all-reduce.2.cloned.1.call-start = ((), (), s32[]{:S(2)}) async-start(), calls=%async_computation.12 | async-start | bytes 155648 | tf_op jit(solution)/shard_map/psum | solution.py:363
  892.3 8.0 collective-permute-start.17
  900.3 136.2 %collective-permute-start.35 = (bf16[1024,2816]{1,0:T(8,128)(2,1)}, bf16[1024,2816]{1,0:T(8,128)(2,1)}, u32[]{:S(2)}, u32[]{:S(2)}) collective-permute-start(bf16[1024,2816]{1,0:T(8,128)(2,1)} %pad_maximum_fusion.2), channel_id=1, source_target_pairs={{0,8},{8,0},{16,24},{24,16},{1,9},{9,1},{17,25},{25,17},{2,10},{10... | collective-permute-start | bytes 17301512 | tf_op jit(solution)/shard_map/ppermute | solution.py:30
  901.3 19.4 %collective-permute-start.18 = (bf16[256,1024]{1,0:T(8,128)(2,1)}, bf16[256,1024]{1,0:T(8,128)(2,1)}, u32[]{:S(2)}, u32[]{:S(2)}) collective-permute-start(bf16[256,1024]{1,0:T(8,128)(2,1)} %pad_maximum_fusion.31), channel_id=1, source_target_pairs={{0,4},{4,0},{1,5},{5,1},{2,6},{6,2},{3,7},{7,3},{8,12},{12,8},{9,1... | collective-permute-start | bytes 1572872 | tf_op jit(solution)/shard_map/ppermute | solution.py:30
  906.8 42.8 %collective-permute-start.9 = (bf16[512,1536]{1,0:T(8,128)(2,1)}, bf16[512,1536]{1,0:T(8,128)(2,1)}, u32[]{:S(2)}, u32[]{:S(2)}) collective-permute-start(bf16[512,1536]{1,0:T(8,128)(2,1)} %constant_dynamic-slice_fusion.10), channel_id=1, source_target_pairs={{0,4},{4,0},{1,5},{5,1},{2,6},{6,2},{3,7},{7,3},{8,12},{12,8},{9,1... | collective-permute-start | bytes 4718600 | tf_op jit(solution)/shard_map/ppermute | solution.py:30
  923.3 34.7 %collective-permute-start.19 = (bf16[512,1024]{1,0:T(8,128)(2,1)}, bf16[512,1024]{1,0:T(8,128)(2,1)S(1)}, u32[]{:S(2)}, u32[]{:S(2)}) collective-permute-start(bf16[512,1024]{1,0:T(8,128)(2,1)} %pad_maximum_fusion.23), channel_id=1, source_target_pairs={{0,8},{8,0},{16,24},{24,16},{1,9},{9,1},{17,25},{25,17},{2,10},{10... | collective-permute-start | bytes 3145736 | tf_op jit(solution)/shard_map/ppermute | solution.py:30
  926.0 29.0 %copy-start.11 = (bf16[512,2816]{1,0:T(8,128)(2,1)}, bf16[512,2816]{1,0:T(8,128)(2,1)S(1)}, u32[]{:S(2)}) copy-start(bf16[512,2816]{1,0:T(8,128)(2,1)S(1)} %get-tuple-element.128) | copy-start | bytes 8650756
  926.0 29.0 %copy-start.12 = (bf16[512,2816]{1,0:T(8,128)(2,1)}, bf16[512,2816]{1,0:T(8,128)(2,1)S(1)}, u32[]{:S(2)}) copy-start(bf16[512,2816]{1,0:T(8,128)(2,1)S(1)} %get-tuple-element.129) | copy-start | bytes 8650756
  953.6 19.5 %collective-permute-start.10 = (bf16[256,1536]{1,0:T(8,128)(2,1)}, bf16[256,1536]{1,0:T(8,128)(2,1)}, u32[]{:S(2)}, u32[]{:S(2)}) collective-permute-start(bf16[256,1536]{1,0:T(8,128)(2,1)} %constant_dynamic-slice_fusion.9), channel_id=1, source_target_pairs={{0,16},{8,24},{16,0},{24,8},{1,17},{9,25},{17,1},{25,9},{2,18},{10... | collective-permute-start | bytes 2359304 | tf_op jit(solution)/shard_map/ppermute | solution.py:30
  957.9 128.8 %collective-permute-start.25 = (bf16[1024,2816]{1,0:T(8,128)(2,1)}, bf16[1024,2816]{1,0:T(8,128)(2,1)}, u32[]{:S(2)}, u32[]{:S(2)}) collective-permute-start(bf16[1024,2816]{1,0:T(8,128)(2,1)} %pad_maximum_fusion), channel_id=1, source_target_pairs={{0,8},{8,0},{16,24},{24,16},{1,9},{9,1},{17,25},{25,17},{2,10},{10... | collective-permute-start | bytes 17301512 | tf_op jit(solution)/shard_map/ppermute | solution.py:30
  975.2 55.3 %collective-permute-start.11 = (bf16[256,1536]{1,0:T(8,128)(2,1)}, bf16[256,1536]{1,0:T(8,128)(2,1)}, u32[]{:S(2)}, u32[]{:S(2)}) collective-permute-start(bf16[256,1536]{1,0:T(8,128)(2,1)} %add_convert_fusion.13), channel_id=1, source_target_pairs={{0,16},{8,24},{16,0},{24,8},{1,17},{9,25},{17,1},{25,9},{2,18},{10... | collective-permute-start | bytes 2359304 | tf_op jit(solution)/shard_map/ppermute | solution.py:30
  1034.3 63.0 %collective-permute-start.12 = (bf16[512,1536]{1,0:T(8,128)(2,1)}, bf16[512,1536]{1,0:T(8,128)(2,1)}, u32[]{:S(2)}, u32[]{:S(2)}) collective-permute-start(bf16[512,1536]{1,0:T(8,128)(2,1)} %pad_maximum_fusion.18), channel_id=1, source_target_pairs={{0,4},{4,0},{1,5},{5,1},{2,6},{6,2},{3,7},{7,3},{8,12},{12,8},{9,1... | collective-permute-start | bytes 4718600 | tf_op jit(solution)/shard_map/ppermute | solution.py:30
  1102.0 16.6 %collective-permute-start.13 = (bf16[1024,1536]{1,0:T(8,128)(2,1)}, bf16[1024,1536]{1,0:T(8,128)(2,1)}, u32[]{:S(2)}, u32[]{:S(2)}) collective-permute-start(bf16[1024,1536]{1,0:T(8,128)(2,1)} %pad_maximum_fusion.6), channel_id=1, source_target_pairs={{0,8},{8,0},{16,24},{24,16},{1,9},{9,1},{17,25},{25,17},{2,10},{10... | collective-permute-start | bytes 9437192 | tf_op jit(solution)/shard_map/ppermute | solution.py:30
  (123 other events, 807.0 us)
Sparse Core Ops, SparseCore 0:
  11.0 49.9 all-gather.4
  99.7 43.7 all-gather.8
  146.3 42.5 reduce-scatter.4
  190.5 45.2 all-gather.6
  533.6 41.3 reduce-scatter.8
  584.2 42.7 reduce-scatter.6
  674.2 44.4 all-gather.10
  885.4 42.4 reduce-scatter.10
  977.5 48.0 all-reduce.1

commit v2 on v1

v2 whole, which is shorter than its diff:
```python
import functools
import math

import jax
import jax.numpy as jnp
from jax import lax
from jax.experimental import pallas as pl
from jax.experimental.pallas import tpu as pltpu
from jax.sharding import PartitionSpec as P

HD = 128
EPS = 1e-06
ROPE_BASE = 1000000.0
NEG = -1e30
F32 = jnp.float32
BF16 = jnp.bfloat16


def mm(left, right):
    return lax.dot_general(left, right, (((1,), (0,)), ((), ())), preferred_element_type=F32)


def mm_nt(left, right):
    return lax.dot_general(left, right, (((1,), (1,)), ((), ())), preferred_element_type=F32)


def mm_tn(left, right):
    return lax.dot_general(left, right, (((0,), (0,)), ((), ())), preferred_element_type=F32)


def swap(value, axis, bit):
    count = lax.axis_size(axis)
    return lax.ppermute(value, axis, [(i, i ^ bit) for i in range(count)])


def bit_of(axis, bit):
    return (lax.axis_index(axis) // bit) % 2


def half(value, which, dim):
    size = value.shape[dim] // 2
    return lax.dynamic_slice_in_dim(value, which * size, size, dim)


def halve(value, axis, bit, dim):
    mine = bit_of(axis, bit)
    got = swap(half(value, 1 - mine, dim), axis, bit)
    return (half(value, mine, dim).astype(F32) + got.astype(F32)).astype(BF16)


def after(value, *others):
    return lax.optimization_barrier((value, *others))[0]


def reduce_send(value, axis, bit):
    return swap(half(value, 1 - bit_of(axis, bit), 0), axis, bit)


def reduce_add(value, got, axis, bit):
    return (half(value, bit_of(axis, bit), 0).astype(F32) + got.astype(F32)).astype(BF16)


def gather_pieces(pieces, axis, bit):
    return pieces + [(mask | {(axis, bit)}, swap(rows, axis, bit)) for mask, rows in pieces]


def assemble_kernel(count, widths, row_of, column_of, *refs):
    inputs, outputs = refs[:count], refs[count:]
    for p in range(count):

        @pl.when(pl.program_id(0) == p)
        def _(p=p):
            start = 0
            for out, width in zip(outputs, widths):
                out[...] = inputs[p][:, start : start + width].astype(F32)
                start += width


def assemble(pieces, stages, column_stage, widths):
    count = len(pieces)
    rows, columns = pieces[0][1].shape
    row_of, column_of = [], []
    for mask, _ in pieces:
        place = jnp.int32(0)
        for stage in stages:
            bit = bit_of(*stage)
            place = place * 2 + (1 - bit if stage in mask else bit)
        row_of.append(place)
        bit = bit_of(*column_stage) if column_stage else jnp.int32(0)
        column_of.append(1 - bit if column_stage in mask else bit)
    row_of, column_of = jnp.stack(row_of), jnp.stack(column_of)
    parts = 1
    while rows // parts * columns > (1 << 18) and rows % (32 * parts) == 0:
        parts *= 2
    step = rows // parts

    def source(p):
        def at(i, s, row_of, column_of):
            return (jnp.where(i < p, 0, jnp.where(i == p, s, parts - 1)), 0)

        return pl.BlockSpec((step, columns), at)

    total_rows = rows << len(stages)
    if column_stage:
        specs = [pl.BlockSpec((step, columns), lambda i, s, r, c: (r[i] * parts + s, c[i]))]
        shapes = [jax.ShapeDtypeStruct((total_rows, 2 * columns), F32)]
    else:
        specs = [
            pl.BlockSpec((step, width), lambda i, s, r, c: (r[i] * parts + s, 0))
            for width in widths
        ]
        shapes = [jax.ShapeDtypeStruct((total_rows, width), F32) for width in widths]
    moved = count * rows * columns
    return pl.pallas_call(
        functools.partial(assemble_kernel, count, widths),
        grid_spec=pltpu.PrefetchScalarGridSpec(
            num_scalar_prefetch=2,
            grid=(count, parts),
            in_specs=[source(p) for p in range(count)],
            out_specs=specs,
        ),
        out_shape=shapes,
        compiler_params=pltpu.CompilerParams(vmem_limit_bytes=32 << 20),
        cost_estimate=pl.CostEstimate(flops=moved, bytes_accessed=6 * moved, transcendentals=0),
    )(row_of, column_of, *[rows for _, rows in pieces])


def rope_tables(positions, feat_width):
    half_width = feat_width // 2
    inv_freq = ROPE_BASE ** (-(jnp.arange(half_width, dtype=F32) * 2.0) / feat_width)
    angles = positions.astype(F32)[:, None] * inv_freq[None, :]
    return (jnp.cos(angles), jnp.sin(angles))


def rotate(tensor, cos_table, sin_table):
    half_width = tensor.shape[-1] // 2
    first_half = tensor[..., :half_width]
    second_half = tensor[..., half_width:]
    cos_b = cos_table[:, None, :]
    sin_b = sin_table[:, None, :]
    return jnp.concatenate(
        [first_half * cos_b - second_half * sin_b, second_half * cos_b + first_half * sin_b],
        axis=-1,
    )


def ffn_kernel(groups, with_base, flipped, *refs):
    rows, grads, scale, gate_w, up_w, down_w = refs[:6]
    refs = refs[6:]
    if with_base:
        base_out, base_dx = refs[:2]
        refs = refs[2:]
    hid_ref, dgate_ref, dup_ref, out_ref, dx_ref, small_ref = refs
    width = down_w.shape[0]
    into, back = (mm_nt, mm) if flipped else (mm, mm_nt)
    gate_pre = into(rows[...], gate_w[...])
    up_pre = into(rows[...], up_w[...])
    grad_hidden = mm_nt(grads[...], down_w[...])
    sig = 1.0 / (1.0 + jnp.exp(-gate_pre))
    act = gate_pre * sig
    slope = sig + act * (1.0 - sig)
    hidden = (act * up_pre).astype(BF16).astype(F32)
    each = width // groups
    column = lax.broadcasted_iota(jnp.int32, (1, width), 1)
    wide = scale[:, 0:1]
    for e in range(1, groups):
        wide = jnp.where(column >= e * each, scale[:, e:e+1], wide)
    prod = hidden * grad_hidden
    for e in range(groups):
        part = prod if groups == 1 else jnp.where((column >= e*each) & (column < (e+1)*each), prod, 0.0)
        small_ref[:, e:e+1] = jnp.sum(part, axis=1, keepdims=True)
    hid = (hidden * wide).astype(BF16)
    hid_ref[...] = hid
    scaled = grad_hidden * wide
    dgate = (scaled * up_pre * slope).astype(BF16)
    dup = (scaled * act).astype(BF16)
    dgate_ref[...] = dgate
    dup_ref[...] = dup
    small_ref[:, groups:groups+1] = jnp.sum(dgate.astype(F32)*gate_pre + dup.astype(F32)*up_pre, axis=1, keepdims=True)
    out = mm(hid, down_w[...])
    dx = back(dgate, gate_w[...]) + back(dup, up_w[...])
    if with_base:
        out = out + base_out[...].astype(F32)
        dx = dx + base_dx[...].astype(F32)
    out_ref[...] = out.astype(BF16)
    dx_ref[...] = dx.astype(BF16)

def ffn(rows, grads, scale, gate_w, up_w, down_w, base=(), flipped=False, block=256):
    count, width = rows.shape
    hidden = down_w.shape[0]
    groups = scale.shape[1]
    block = min(block, count)
    def by_row(n): return pl.BlockSpec((block, n), lambda i: (i, 0))
    def held(a): return pl.BlockSpec(a.shape, lambda i: (0, 0), pipeline_mode=pl.Buffered(1))
    return pl.pallas_call(
        functools.partial(ffn_kernel, groups, bool(base), flipped),
        grid=(count // block,),
        in_specs=[by_row(width), by_row(width), by_row(groups), held(gate_w), held(up_w), held(down_w)] + [by_row(width)] * len(base),
        out_specs=[by_row(hidden)] * 3 + [by_row(width)] * 2 + [by_row(groups + 1)],
        out_shape=[jax.ShapeDtypeStruct((count, hidden), BF16)] * 3 + [jax.ShapeDtypeStruct((count, width), BF16)] * 2 + [jax.ShapeDtypeStruct((count, groups + 1), F32)],
        compiler_params=pltpu.CompilerParams(vmem_limit_bytes=62 << 20),
        cost_estimate=pl.CostEstimate(flops=12*count*width*hidden, bytes_accessed=6*width*hidden + 12*count*width, transcendentals=count*hidden),
    )(rows, grads, scale, gate_w, up_w, down_w, *base)


def line_sum(rows, width_own, depth, prepare, settle, gathered, part, came, came_two, spread, sems):
    n = lax.axis_size("tp")
    me = lax.axis_index("tp")
    chunks, _, step, _ = part.shape
    sum_send, sum_recv, two_recv, out_send, out_recv = sems

    def send(source, target, send_sem, recv_sem, to):
        return pltpu.make_async_remote_copy(
            src_ref=source, dst_ref=target, send_sem=send_sem, recv_sem=recv_sem,
            device_id={"tp": to}, device_id_type=pl.DeviceIdType.MESH,
        )

    def sum_copy(c, s, to_right, two):
        target = came_two.at[c] if two else came.at[c, s]
        sem = two_recv.at[c] if two else sum_recv.at[c, s]
        return send(part.at[c, s], target, sum_send.at[c, s], sem, me + 1 if to_right else me - 1)

    def out_copy(c, s, to_right):
        return send(
            spread.at[c, s], spread.at[c, s], out_send.at[c, s, 1 if to_right else 0],
            out_recv.at[c, s], me + 1 if to_right else me - 1,
        )

    def within(c):
        return (c >= 0) & (c < chunks)

    def pass_sums(t):
        @pl.when(within(t))
        def _():
            prepare(t)

        for s in range(n):
            c = t - me * depth

            @pl.when((me < s) & within(c))
            def _(s=s, c=c):
                @pl.when(me > 0)
                def _():
                    sum_copy(c, s, True, False).wait_recv()
                    part[c, s] = (part[c, s].astype(F32) + came[c, s].astype(F32)).astype(BF16)

                sum_copy(c, s, True, False).start()

        for s in range(n):
            c = t - (n - 1 - me) * depth

            @pl.when((me > s) & within(c))
            def _(s=s, c=c):
                @pl.when(me < n - 1)
                def _():
                    sum_copy(c, s, False, False).wait_recv()
                    part[c, s] = (part[c, s].astype(F32) + came[c, s].astype(F32)).astype(BF16)

                @pl.when(me - 1 == s)
                def _():
                    sum_copy(c, s, False, True).start()

                @pl.when(me - 1 > s)
                def _():
                    sum_copy(c, s, False, False).start()

    def pass_own(t):
        c = t - (n - 1) * depth
        for s in range(n):

            @pl.when((me == s) & within(c))
            def _(s=s):
                if s > 0:
                    sum_copy(c, s, True, False).wait_recv()
                if s < n - 1:
                    sum_copy(c, s, False, True).wait_recv()
                total = part[c, s].astype(F32)
                if s > 0:
                    total = total + came[c, s].astype(F32)
                if s < n - 1:
                    total = total + came_two[c].astype(F32)
                spread[c, s] = settle(c, total)
                if s > 0:
                    out_copy(c, s, False).start()
                if s < n - 1:
                    out_copy(c, s, True).start()

    def pass_out(t):
        for s in range(n):
            right = t - (n - 1 + me - s) * depth
            left = t - (n - 1 + s - me) * depth

            @pl.when((me > s) & within(right))
            def _(s=s, c=right):
                out_copy(c, s, True).wait_recv()

                @pl.when(me < n - 1)
                def _():
                    out_copy(c, s, True).start()

            @pl.when((me < s) & within(left))
            def _(s=s, c=left):
                out_copy(c, s, False).wait_recv()

                @pl.when(me > 0)
                def _():
                    out_copy(c, s, False).start()

        last = t - 2 * (n - 1) * depth

        @pl.when(within(last))
        def _():
            gathered(last)

    def turn(t, carry):
        pass_sums(t)
        pass_own(t)
        pass_out(t)
        return carry

    lax.fori_loop(0, chunks + 2 * (n - 1) * depth, turn, 0)

    def drain(c, carry):
        for s in range(n):

            @pl.when(me != s)
            def _(s=s):
                sum_copy(c, s, True, False).wait_send()

            @pl.when((me < n - 1) & (s <= me))
            def _(s=s):
                out_copy(c, s, True).wait_send()

            @pl.when((me > 0) & (s >= me))
            def _(s=s):
                out_copy(c, s, False).wait_send()

        return carry

    lax.fori_loop(0, chunks, drain, 0)


def line_scratch(rows, width_own):
    n = lax.axis_size("tp")
    chunks = max(1, min(16, 128 // n))
    step = rows // chunks
    slots = pltpu.VMEM((chunks, n, step, width_own), BF16)
    dma = pltpu.SemaphoreType.DMA
    return chunks, step, [
        slots, slots, pltpu.VMEM((chunks, step, width_own), BF16), slots,
        dma((chunks, n)), dma((chunks, n)), dma((chunks,)), dma((chunks, n, 2)), dma((chunks, n)),
    ]


def greet(peers):
    n = lax.axis_size("tp")
    me = lax.axis_index("tp")
    barrier = pltpu.get_barrier_semaphore()

    def signal(where):
        pl.semaphore_signal(barrier, inc=1, device_id=where, device_id_type=pl.DeviceIdType.MESH)

    @pl.when(me > 0)
    def _():
        signal({"tp": me - 1})

    @pl.when(me < n - 1)
    def _():
        signal({"tp": me + 1})

    for where in peers:
        signal(where)

    beside = jnp.where(me > 0, 1, 0) + jnp.where(me < n - 1, 1, 0)
    pl.semaphore_wait(barrier, beside + len(peers))


def attend_out_kernel(
    chunks, step, depth, eps, attn, w_out, x, gain,
    mixed, mixed_peer, resid_own, inv_out,
    part, came, came_two, spread, s0, s1, s2, s3, s4, y_send, y_recv,
):
    n = lax.axis_size("tp")
    me = lax.axis_index("tp")
    own = part.shape[3]
    rows = attn.shape[0]
    other = {"ep": 1 - lax.axis_index("ep")}
    greet([other])
    block = max(step, min(rows, 128))

    def product(b, carry):
        start = pl.multiple_of(b * block, block)
        value = mm(attn[pl.ds(start, block), :], w_out[...]).astype(BF16)
        for s in range(n):
            for k in range(block // step):
                part[b * (block // step) + k, s] = value[k * step:(k + 1) * step, s * own:(s + 1) * own]
        return carry

    lax.fori_loop(0, rows // block, product, 0)

    def at(c):
        return pl.ds(pl.multiple_of(c * step, step), step)

    def peer_copy(c):
        return pltpu.make_async_remote_copy(
            src_ref=mixed.at[at(c)], dst_ref=mixed_peer.at[at(c)], send_sem=y_send.at[c], recv_sem=y_recv.at[c],
            device_id=other, device_id_type=pl.DeviceIdType.MESH,
        )

    def prepare(c):
        pass

    def settle(c, total):
        return total.astype(BF16)

    def gathered(c):
        resid = []
        square = jnp.zeros((step, 1), F32)
        for s in range(n):
            piece = x[at(c), s * own:(s + 1) * own].astype(F32) + spread[c, s].astype(F32)
            resid.append(piece)
            square = square + jnp.sum(piece * piece, axis=1, keepdims=True)
        inv = lax.rsqrt(square / (n * own) + eps)
        inv_out[at(c), :] = inv
        for s in range(n):
            mixed[at(c), s * own:(s + 1) * own] = (resid[s] * inv * gain[:, s * own:(s + 1) * own]).astype(BF16)

            @pl.when(me == s)
            def _(s=s):
                resid_own[at(c), :] = resid[s]

        peer_copy(c).start()

    line_sum(rows, own, depth, prepare, settle, gathered, part, came, came_two, spread, (s0, s1, s2, s3, s4))

    def last(c, carry):
        peer_copy(c).wait_recv()
        peer_copy(c).wait_send()
        return carry

    lax.fori_loop(0, chunks, last, 0)


def attend_out(attn, w_out, x, gain, width_own, depth=1):
    rows, width = x.shape
    chunks, step, scratch = line_scratch(rows, width_own)
    vmem = pl.BlockSpec(memory_space=pltpu.VMEM)
    dma = pltpu.SemaphoreType.DMA
    return pl.pallas_call(
        functools.partial(attend_out_kernel, chunks, step, depth, EPS),
        out_shape=[
            jax.ShapeDtypeStruct((rows, width), BF16), jax.ShapeDtypeStruct((rows, width), BF16),
            jax.ShapeDtypeStruct((rows, width_own), F32), jax.ShapeDtypeStruct((rows, 1), F32),
        ],
        in_specs=[vmem] * 4,
        out_specs=[vmem] * 4,
        scratch_shapes=scratch + [dma((chunks,)), dma((chunks,))],
        compiler_params=pltpu.CompilerParams(collective_id=1, has_side_effects=True, vmem_limit_bytes=40 << 20),
        cost_estimate=pl.CostEstimate(flops=0, bytes_accessed=0, transcendentals=0),
    )(attn, w_out, x, gain)


def resid_grad_kernel(
    chunks, step, depth, grad, grad_p, out_p, router, along, g_own, resid_own, inv_two, gain,
    low, grad_resid, gain_grad, out_back,
    part, came, came_two, spread, s0, s1, s2, s3, s4, back, y_send, y_recv, o_send, o_recv,
):
    n = lax.axis_size("tp")
    own = part.shape[3]
    rows = grad.shape[0]
    other = {"ep": 1 - lax.axis_index("ep")}

    def at(c):
        return pl.ds(pl.multiple_of(c * step, step), step)

    def peer_copy(c):
        return pltpu.make_async_remote_copy(
            src_ref=grad_p.at[at(c)], dst_ref=back.at[at(c)], send_sem=y_send.at[c], recv_sem=y_recv.at[c],
            device_id=other, device_id_type=pl.DeviceIdType.MESH,
        )

    def out_copy():
        return pltpu.make_async_remote_copy(
            src_ref=out_p, dst_ref=out_back, send_sem=o_send, recv_sem=o_recv,
            device_id=other, device_id_type=pl.DeviceIdType.MESH,
        )

    greet([other])

    def begin(c, carry):
        peer_copy(c).start()
        return carry

    lax.fori_loop(0, chunks, begin, 0)
    out_copy().start()
    gain_grad[...] = jnp.zeros_like(gain_grad)

    def prepare(c):
        peer_copy(c).wait_recv()
        for s in range(n):
            columns = slice(s * own, (s + 1) * own)
            part[c, s] = (grad[at(c), columns].astype(F32) + back[at(c), columns].astype(F32)).astype(BF16)

    def settle(c, total):
        total = total + router[at(c), :]
        inv = inv_two[at(c), :]
        resid = resid_own[at(c), :]
        gain_grad[...] += jnp.sum(total * resid * inv, axis=0, keepdims=True)
        result = g_own[at(c), :].astype(F32) + inv * gain[...] * total - resid * (inv * inv * along[at(c), :] / (n * own))
        grad_resid[at(c), :] = result
        return result.astype(BF16)

    def gathered(c):
        for s in range(n):
            low[at(c), s * own:(s + 1) * own] = spread[c, s]

    line_sum(rows, own, depth, prepare, settle, gathered, part, came, came_two, spread, (s0, s1, s2, s3, s4))

    def last(c, carry):
        peer_copy(c).wait_send()
        return carry

    lax.fori_loop(0, chunks, last, 0)
    out_copy().wait()


def resid_grad(grad, grad_p, out_p, router, along, g_own, resid_own, inv_two, gain, depth=1):
    rows, width = grad.shape
    width_own = g_own.shape[1]
    chunks, step, scratch = line_scratch(rows, width_own)
    vmem = pl.BlockSpec(memory_space=pltpu.VMEM)
    far = pl.BlockSpec(memory_space=pl.ANY)
    dma = pltpu.SemaphoreType.DMA
    return pl.pallas_call(
        functools.partial(resid_grad_kernel, chunks, step, depth),
        out_shape=[
            jax.ShapeDtypeStruct((rows, width), BF16), jax.ShapeDtypeStruct((rows, width_own), F32),
            jax.ShapeDtypeStruct((1, width_own), F32), jax.ShapeDtypeStruct((rows, width), BF16),
        ],
        in_specs=[vmem] + [far] * 2 + [vmem] * 6,
        out_specs=[vmem] * 3 + [far],
        scratch_shapes=scratch + [pltpu.VMEM((rows, width), BF16), dma((chunks,)), dma((chunks,)), dma, dma],
        compiler_params=pltpu.CompilerParams(collective_id=2, has_side_effects=True, vmem_limit_bytes=40 << 20),
        cost_estimate=pl.CostEstimate(flops=0, bytes_accessed=0, transcendentals=0),
    )(grad, grad_p, out_p, router, along, g_own, resid_own, inv_two, gain)


def body(
    tokens,
    norm_attn,
    w_query,
    w_key,
    w_value,
    w_output,
    norm_ffn,
    w_router,
    shared_switch,
    shared_gate,
    shared_up,
    shared_down,
    expert_gate,
    expert_up,
    expert_down,
    routes,
    segments,
    output_gradient,
):
    tp_count = lax.axis_size("tp")
    ep_count = lax.axis_size("ep")
    dp_count = lax.axis_size("dp")
    tp_rank = lax.axis_index("tp")
    ep_rank = lax.axis_index("ep")
    rows = tokens.shape[0]
    width_own = tokens.shape[1]
    width = width_own * tp_count
    heads = w_query.shape[1] // HD
    experts_own = expert_gate.shape[0]
    experts = experts_own * ep_count
    expert_width = expert_gate.shape[2]
    score_scale = 1.0 / math.sqrt(HD)
    far_bits = [1 << b for b in range(1, dp_count.bit_length() - 1)]

    def own_columns(value):
        return lax.dynamic_slice_in_dim(value, tp_rank * width_own, width_own, value.ndim - 1)

    near = bit_of("dp", 1)

    def pair_send(left, right, columns):
        if columns:
            right = half(right, 1 - near, 1)
        else:
            left = half(left, 1 - near, 1)
        return swap(mm_tn(left, right).astype(BF16), "dp", 1)

    def pair_keep(left, right, columns, got):
        if columns:
            right = half(right, near, 1)
        else:
            left = half(left, near, 1)
        return (mm_tn(left, right) + got.astype(F32)).astype(BF16)

    core = ("dp", 1)
    far = [("dp", b) for b in far_bits]
    line = [("ep", 1)]

    def alone(value):
        return [(frozenset(), value)]

    def whole(pieces, stages, columns, widths):
        if columns:
            return assemble(pieces, stages, core, widths)
        return assemble(pieces, [core] + stages, None, widths)

    def over_tp(value):
        bit = 1
        while bit < tp_count:
            value = value + swap(value, "tp", bit)
            bit *= 2
        return value

    def over_rows(value):
        for axis, bit in [core] + far + line:
            value = value + swap(value, axis, bit)
        return value

    packed = jnp.concatenate(
        [tokens, norm_attn[None, :], norm_ffn[None, :], jnp.zeros((14, width_own), BF16)], axis=0
    )
    packed = lax.all_gather(packed, "tp", axis=1, tiled=True)
    x_full = packed[:rows].astype(F32)
    gain_one = packed[rows].astype(F32)
    gain_two = packed[rows + 1].astype(F32)
    grad_rows = lax.all_gather(output_gradient, "tp", axis=1, tiled=True)
    grad_peer = swap(grad_rows, "ep", 1)
    route_hot = jnp.sum(
        (routes[:, :, None] == jnp.arange(experts, dtype=jnp.int32)[None, None, :]).astype(F32),
        axis=1,
    )
    route_hot_peer = swap(route_hot, "ep", 1)

    inv_one = lax.rsqrt(jnp.mean(x_full * x_full, axis=1, keepdims=True) + EPS)
    normed = (x_full * inv_one * gain_one).astype(BF16)
    q_pre = mm(normed, w_query)
    k_pre = mm(normed, w_key)
    v_pre = mm(normed, w_value)
    positions = ep_rank * rows + jnp.arange(rows, dtype=jnp.int32)
    cos_table, sin_table = rope_tables(positions, HD)
    query = rotate(q_pre.reshape(rows, heads, HD), cos_table, sin_table).astype(BF16)
    key_own = rotate(k_pre.reshape(rows, heads, HD), cos_table, sin_table).astype(BF16)
    value_own = v_pre.astype(BF16).reshape(rows, heads, HD)
    forth = [(i, i + 1) for i in range(ep_count - 1)]
    back = [(i + 1, i) for i in range(ep_count - 1)]
    earlier = lax.ppermute(jnp.stack([key_own, value_own]), "ep", forth)
    earlier = after(earlier, grad_rows)
    key_rows = jnp.concatenate([earlier[0], key_own], axis=0)
    value_rows = jnp.concatenate([earlier[1], value_own], axis=0)
    key_pos = (ep_rank - 1) * rows + jnp.arange(2 * rows, dtype=jnp.int32)
    seg_rows = segments.reshape(ep_count, rows)
    query_seg = lax.dynamic_index_in_dim(seg_rows, ep_rank, 0, keepdims=False)
    before_seg = lax.dynamic_index_in_dim(
        seg_rows, jnp.maximum(ep_rank - 1, 0), 0, keepdims=False
    )
    key_seg = jnp.concatenate([jnp.where(ep_rank > 0, before_seg, -1), query_seg])
    allowed = (query_seg[:, None] == key_seg[None, :]) & (key_pos[None, :] <= positions[:, None])

    def masked_scores():
        scores = (
            jnp.einsum("qhd,khd->hqk", query, key_rows, preferred_element_type=F32) * score_scale
        )
        return jnp.where(allowed[None], scores, NEG)

    scores = masked_scores()
    row_top = jnp.max(scores, axis=2, keepdims=True)
    shifted = jnp.exp(scores - row_top)
    row_total = jnp.sum(shifted, axis=2, keepdims=True)
    weights = (shifted / row_total).astype(BF16)
    attended = jnp.einsum("hqk,khd->qhd", weights, value_rows, preferred_element_type=F32)
    attn_rows = attended.astype(BF16).reshape(rows, heads * HD)
    log_norm = row_top + jnp.log(row_total)

    mixed, mixed_peer, resid_own, inv_two = attend_out(
        attn_rows, w_output, after(packed[:rows], grad_peer), gain_two[None, :], width_own
    )

    def router(values):
        logits = mm(values, w_router)
        return logits, jax.nn.softmax(logits, axis=1)

    logits, router_prob = router(mixed)
    combine = router_prob * route_hot
    combine_peer = router(mixed_peer)[1] * route_hot_peer
    switch_logit = mm(mixed, shared_switch[:, None])
    switch = jax.nn.sigmoid(switch_logit)

    def own_experts(value):
        return lax.dynamic_slice_in_dim(value, ep_rank * experts_own, experts_own, 1)

    x_link = far[0]
    y_link = line[0]

    hid_s, gate_s, up_s, out_s, grad_s, small_s = ffn(
        mixed, grad_rows, switch, shared_gate, shared_up, shared_down
    )
    got_sg = pair_send(mixed, gate_s, False)
    got_sd = pair_send(hid_s, after(grad_rows, got_sg), True)
    got_su = pair_send(after(mixed, got_sd), up_s, False)
    sum_sg = pair_keep(mixed, gate_s, False, got_sg)
    got_sg = reduce_send(sum_sg, *x_link)
    sum_sd = pair_keep(hid_s, after(grad_rows, sum_sg), True, got_sd)
    got_sd = reduce_send(sum_sd, *x_link)
    sum_su = pair_keep(after(mixed, sum_sd), up_s, False, got_su)
    got_su = reduce_send(sum_su, *y_link)

    hidden_width = experts_own * expert_width
    gate_w = jnp.transpose(expert_gate, (0, 2, 1)).reshape(hidden_width, width)
    up_w = jnp.transpose(expert_up, (0, 2, 1)).reshape(hidden_width, width)
    down_w = expert_down.reshape(hidden_width, width)
    peer_rows = after(mixed_peer, sum_su)
    hid_p, gate_p, up_p, out_p, grad_p, small_p = ffn(
        peer_rows, grad_peer, own_experts(combine_peer), gate_w, up_w, down_w, (), True
    )
    small_back = swap(small_p.T, "ep", 1)
    sum_sg = reduce_add(sum_sg, after(got_sg, grad_p), *x_link)
    got_sg = reduce_send(sum_sg, *y_link)
    own_rows = after(mixed, sum_sg)
    hid_e, gate_e, up_e, out_e, grad_e, small_e = ffn(
        own_rows, grad_rows, own_experts(combine), gate_w, up_w, down_w, (out_s, grad_s), True
    )

    first = ep_rank == 0
    small_e = small_e.T
    dots_here, dots_there = small_e[:experts_own], small_back[:experts_own]
    small = jnp.concatenate(
        [
            jnp.where(first, dots_here, dots_there),
            jnp.where(first, dots_there, dots_here),
            small_s.T[:1],
            small_s.T[1:] + small_e[experts_own:] + small_back[experts_own:],
        ],
        axis=0,
    )
    small = over_tp(small)

    sum_su = reduce_add(sum_su, after(got_su, grad_e), *y_link)
    got_su = reduce_send(sum_su, *x_link)
    sum_sd = reduce_add(sum_sd, after(got_sd, sum_su), *x_link)
    got_sd = reduce_send(sum_sd, *y_link)

    both = after(jnp.concatenate([mixed, mixed_peer], axis=0), sum_sd)
    both_grad = jnp.concatenate([grad_rows, grad_peer], axis=0)
    gate_b = jnp.concatenate([gate_e, gate_p], axis=0)
    up_b = jnp.concatenate([up_e, up_p], axis=0)
    hid_b = jnp.concatenate([hid_e, hid_p], axis=0)
    got_eg = pair_send(gate_b, both, True)
    got_eu = pair_send(up_b, after(both, got_eg), True)
    got_ed = pair_send(hid_b, after(both_grad, got_eu), True)
    sum_eg = pair_keep(gate_b, both, True, got_eg)
    got_eg = reduce_send(sum_eg, *x_link)
    sum_eu = pair_keep(up_b, after(both, sum_eg), True, got_eu)
    got_eu = reduce_send(sum_eu, *x_link)
    sum_ed = pair_keep(hid_b, after(both_grad, sum_eu), True, got_ed)
    got_ed = reduce_send(sum_ed, *x_link)
    sum_su = reduce_add(sum_su, after(got_su, sum_ed), *x_link)
    piece_su = gather_pieces(alone(sum_su), *x_link)
    sum_sg = reduce_add(sum_sg, after(got_sg, sum_su), *y_link)
    piece_sg = gather_pieces(alone(sum_sg), *x_link)
    sum_sd = reduce_add(sum_sd, after(got_sd, sum_sg), *y_link)
    piece_sd = gather_pieces(alone(sum_sd), *x_link)

    small = small.T
    grad_prob = small[:, :experts] * route_hot
    grad_switch = small[:, experts : experts + 1]
    along = small[:, experts + 1 : experts + 2]
    grad_logits = (
        router_prob * (grad_prob - jnp.sum(router_prob * grad_prob, axis=1, keepdims=True))
    ).astype(BF16)
    grad_slogit = (grad_switch * switch * (1.0 - switch)).astype(BF16)
    tp_rows = lax.dynamic_slice_in_dim(w_router, tp_rank * width_own, width_own, 0)
    router_part = (
        mm_nt(grad_logits, tp_rows)
        + grad_slogit.astype(F32) * own_columns(shared_switch).astype(F32)[None, :]
    )
    grad_router = mm_tn(grad_logits, mixed)
    grad_switch_w = mm_tn(grad_slogit, mixed)
    along = (
        along
        + jnp.sum(grad_logits.astype(F32) * logits, axis=1, keepdims=True)
        + grad_slogit.astype(F32) * switch_logit
    )
    resid_low, grad_resid, grad_gain_two, out_back = resid_grad(
        after(grad_e, sum_sd), grad_p, out_p, router_part, along, output_gradient, resid_own, inv_two, norm_ffn.astype(F32)[None, :]
    )
    flat = jnp.concatenate(
        [grad_gain_two.reshape(-1), grad_router.reshape(-1), grad_switch_w.reshape(-1)]
    ).reshape(-1, 128)
    ffn_part = (out_e.astype(F32) + out_back.astype(F32)).astype(BF16)

    grad_attn = mm_nt(resid_low, w_output).astype(BF16).reshape(rows, heads, HD)
    probs = jnp.exp(masked_scores() - log_norm)
    grad_probs = jnp.einsum("qhd,khd->hqk", grad_attn, value_rows, preferred_element_type=F32)
    grad_scores = (
        probs * (grad_probs - jnp.sum(probs * grad_probs, axis=2, keepdims=True))
    ).astype(BF16)
    grad_query = (
        jnp.einsum("hqk,khd->qhd", grad_scores, key_rows, preferred_element_type=F32) * score_scale
    )
    grad_keys = (
        jnp.einsum("hqk,qhd->khd", grad_scores, query, preferred_element_type=F32) * score_scale
    )
    grad_values = jnp.einsum(
        "hqk,qhd->khd", probs.astype(BF16), grad_attn, preferred_element_type=F32
    )
    later = lax.ppermute(
        jnp.stack([grad_keys[:rows], grad_values[:rows]]).astype(BF16), "ep", back
    )
    ffn_own = lax.psum_scatter(
        after(ffn_part, grad_keys), "tp", scatter_dimension=1, tiled=True
    )
    layer_out = (resid_own + ffn_own.astype(F32)).astype(BF16)
    flat = over_rows(after(flat, grad_keys))
    sum_eg = reduce_add(sum_eg, after(got_eg, grad_keys), *x_link)
    piece_eg = gather_pieces(alone(sum_eg), *x_link)
    sum_eu = reduce_add(sum_eu, after(got_eu, sum_eg), *x_link)
    piece_eu = gather_pieces(alone(sum_eu), *x_link)
    sum_ed = reduce_add(sum_ed, after(got_ed, sum_eu), *x_link)
    piece_ed = gather_pieces(alone(sum_ed), *x_link)
    got_wo = pair_send(after(attn_rows, sum_ed), resid_low, True)
    sum_wo = pair_keep(after(attn_rows, got_wo), resid_low, True, got_wo)
    got_wo = reduce_send(sum_wo, *y_link)
    later = after(later, sum_wo).astype(F32)
    grad_key = grad_keys[rows:] + later[0]
    grad_value = grad_values[rows:] + later[1]
    shape = (rows, heads * HD)
    grad_qpre = rotate(grad_query, cos_table, -sin_table).astype(BF16).reshape(shape)
    grad_kpre = rotate(grad_key, cos_table, -sin_table).astype(BF16).reshape(shape)
    grad_vpre = grad_value.astype(BF16).reshape(shape)
    grad_qkv = jnp.concatenate([grad_qpre, grad_kpre, grad_vpre], axis=1)
    got_qkv = pair_send(normed, grad_qkv, False)
    grad_qkv = after(grad_qkv, got_qkv)
    sum_qkv = pair_keep(normed, grad_qkv, False, got_qkv)
    got_qkv = reduce_send(sum_qkv, *y_link)
    grad_normed = (
        mm_nt(after(grad_qpre, sum_qkv), w_query)
        + mm_nt(grad_kpre, w_key)
        + mm_nt(grad_vpre, w_value)
    ).astype(BF16)
    normed_own = lax.psum_scatter(grad_normed, "tp", scatter_dimension=1, tiled=True).astype(F32)
    row_part = jnp.sum(
        grad_qpre.astype(F32) * q_pre
        + grad_kpre.astype(F32) * k_pre
        + grad_vpre.astype(F32) * v_pre,
        axis=1,
    )
    row_total = over_tp(row_part[None, :]).T

    y_then_x, x_then_y = line + far, far + line
    qkv = heads * HD
    inner = shared_gate.shape[1]

    def later_pieces(pieces, other, stage):
        (mask, rows_), *rest = pieces
        return gather_pieces([(mask, after(rows_, other))] + rest, *stage)

    piece_su = later_pieces(piece_su, grad_normed, y_link)
    piece_sg = later_pieces(piece_sg, piece_su[1][1], y_link)
    piece_sd = later_pieces(piece_sd, piece_sg[1][1], y_link)
    sum_wo = reduce_add(sum_wo, after(got_wo, grad_normed), *y_link)
    got_wo = reduce_send(sum_wo, *x_link)
    sum_qkv = reduce_add(sum_qkv, after(got_qkv, sum_wo), *y_link)
    got_qkv = reduce_send(sum_qkv, *x_link)
    piece_su = later_pieces(piece_su, sum_qkv, core)
    piece_sg = later_pieces(piece_sg, piece_su[3][1], core)
    (su_grad,) = whole(piece_su, y_then_x, False, (inner,))
    piece_sd = later_pieces(piece_sd, piece_sg[3][1], core)
    (sg_grad,) = whole(piece_sg, x_then_y, False, (inner,))
    (sd_grad,) = whole(piece_sd, x_then_y, True, (width // 2,))
    piece_eg = later_pieces(piece_eg, sum_qkv, core)
    (eg_grad,) = whole(piece_eg, far, True, (width // 2,))
    piece_eu = later_pieces(piece_eu, piece_eg[1][1], core)
    (eu_grad,) = whole(piece_eu, far, True, (width // 2,))
    piece_ed = later_pieces(piece_ed, piece_eu[1][1], core)
    (ed_grad,) = whole(piece_ed, far, True, (width // 2,))
    sum_wo = reduce_add(sum_wo, after(got_wo, piece_ed[1][1]), *x_link)
    sum_qkv = reduce_add(sum_qkv, after(got_qkv, sum_wo), *x_link)
    piece_qkv = gather_pieces(alone(sum_qkv), *x_link)
    piece_wo = gather_pieces(alone(sum_wo), *x_link)
    piece_qkv = gather_pieces(piece_qkv, *y_link)
    piece_wo = gather_pieces(piece_wo, *y_link)
    piece_wo = gather_pieces(piece_wo, *core)
    piece_qkv = gather_pieces(piece_qkv, *core)
    (wo_grad,) = whole(piece_wo, y_then_x, True, (width // 2,))
    wq_grad, wk_grad, wv_grad = whole(piece_qkv, y_then_x, False, (qkv,) * 3)

    x_own = tokens.astype(F32)
    grad_tokens = (
        grad_resid
        + inv_one * norm_attn.astype(F32) * normed_own
        - x_own * (inv_one * inv_one) * (row_total / width)
    )
    grad_gain_one = jnp.sum(normed_own * x_own * inv_one, axis=0)

    flat = flat.reshape(-1)
    grad_gain_two = flat[:width_own]
    grad_router = flat[width_own : width_own + width * experts].reshape(experts, width).T
    grad_switch_w = flat[width_own + width * experts :]
    grad_gain_one = over_rows(grad_gain_one.reshape(-1, 128)).reshape(-1)

    def per_expert(value):
        return value.reshape(experts_own, expert_width, width)

    return (
        layer_out,
        grad_tokens,
        grad_gain_one,
        wq_grad,
        wk_grad,
        wv_grad,
        wo_grad,
        grad_gain_two,
        grad_router,
        grad_switch_w,
        sg_grad,
        su_grad,
        sd_grad,
        jnp.transpose(per_expert(eg_grad), (0, 2, 1)),
        jnp.transpose(per_expert(eu_grad), (0, 2, 1)),
        per_expert(ed_grad),
    )


def solution(mesh):
    placed = (
        P(("dp", "ep"), "tp"),
        P("tp"),
        P(None, "tp"),
        P(None, "tp"),
        P(None, "tp"),
        P("tp", None),
        P("tp"),
        P(),
        P(),
        P(None, "tp"),
        P(None, "tp"),
        P("tp", None),
        P("ep", None, "tp"),
        P("ep", None, "tp"),
        P("ep", "tp", None),
        P(("dp", "ep"), None),
        P("dp"),
        P(("dp", "ep"), "tp"),
    )
    return jax.shard_map(
        body,
        mesh=mesh,
        in_specs=placed,
        out_specs=(
            P(("dp", "ep"), "tp"),
            P(("dp", "ep"), "tp"),
            P("tp"),
            P(None, "tp"),
            P(None, "tp"),
            P(None, "tp"),
            P("tp", None),
            P("tp"),
            P(),
            P(),
            P(None, "tp"),
            P(None, "tp"),
            P("tp", None),
            P("ep", None, "tp"),
            P("ep", None, "tp"),
            P("ep", "tp", None),
        ),
        check_vma=False,
    )
```

time: 1150 us -> 1070 us (0.930)
  Pallas kernels: 0 us -> 351 us
  waiting for transfers between devices: 530 us -> 381 us
  matrix products: 222 us -> 100 us
  other arithmetic: 177 us -> 72 us
  local copies, waits for them, and re-layouts: 133 us -> 83.7 us
  blocking collectives: 27.9 us -> 0 us
  starting transfers between devices: 38.6 us -> 55.9 us
    pallas_call x0 -> x13, Pallas kernels: none -> 351 us  [the longest x1 95.8 us: resid_grad(): pl.pallas_call(functools.partial(resid_grad_kernel, chunks, step, depth),...]
    dot_general x11 -> x5, matrix products: 67.5 us -> 7.25 us  [mm_nt(): lax.dot_general(left, right, (((1,), (1,)), ((), ())), preferred_element_...]
    slice x11 -> x3, local copies, waits for them, and re-layouts: 56.5 us -> 2.39 us  [the longest x1 1.78 us: body(): x_full = packed[:rows].astype(F32)]
    dot_general x13 -> x6, matrix products: 66.6 us -> 13.1 us  [mm(): lax.dot_general(left, right, (((1,), (0,)), ((), ())), preferred_element_...]
    select_n x16 -> x0, other arithmetic: 49.9 us -> none  [the longest x6 32.8 us: spread(): jnp.where(first, value, got)]
    psum x1 -> x0, waiting for transfers between devices: 44.1 us -> none  [body(): flat = lax.psum(flat, ('dp', 'ep'))]
    reduce_scatter x3 -> x1, waiting for transfers between devices: 41.5 us -> 0.01 us  [body(): lax.psum_scatter(after(ffn_part, grad_keys), 'tp', scatter_dimension=1, t...]
    ppermute x38 -> x78, waiting for transfers between devices: 334 us -> 293 us  [swap(): return lax.ppermute(value, axis, [(i, i ^ bit) for i in range(count)])]
  transfers between devices with their start and end apart: 49 -> 84, of which waited for: 20 -> 32; matrix products, arithmetic and copies ran while one was open for 40% -> 17% of each run, Pallas kernels for 0% -> 22%
where the time goes in v2:
time: 1070 us; the launch traced here: 1060 us
  waiting for transfers between devices  381 us (36%)
  Pallas kernels  351 us (33%)
  matrix products  100 us (9%)
  local copies, waits for them, and re-layouts  83.7 us (8%)
  other arithmetic  72 us (7%)
  starting transfers between devices  55.9 us (5%)
  between operations  15.7 us (1%)
    ppermute x78, waiting for transfers between devices, swap(): return lax.ppermute(value, axis, [(i, i ^ bit) for i in range(count)])  293 us
    pallas_call x1, Pallas kernels, resid_grad(): pl.pallas_call(functools.partial(resid_grad_kernel, chunks, step, depth),...  95.8 us
    pallas_call x8, Pallas kernels, assemble(): pl.pallas_call(functools.partial(assemble_kernel, count, widths), grid_sp...  90.6 us
    pallas_call x3, Pallas kernels, ffn(): pl.pallas_call(functools.partial(ffn_kernel, groups, bool(base), flipped)...  88 us
    pallas_call x1, Pallas kernels, attend_out(): pl.pallas_call(functools.partial(attend_out_kernel, chunks, step, depth,...  76.3 us
    dot_general x18, matrix products, mm_tn(): lax.dot_general(left, right, (((0,), (0,)), ((), ())), preferred_element_...  64.3 us
    ppermute x78, starting transfers between devices, swap(): return lax.ppermute(value, axis, [(i, i ^ bit) for i in range(count)])  49.5 us
    unnamed x306, local copies, waits for them, and re-layouts  49.2 us
  transfers between devices with their start and end apart: 84, of which 32 were waited for; matrix products, arithmetic and copies ran while one was open for 17% of the time, Pallas kernels for 22%

profile of v2, /device:TPU:0, one launch (start us, length us, event | category | flops | bytes accessed | tf_op | source)
XLA Modules:
  0.0 1059.4 jit_solution(2797268852145357984)
XLA Ops:
  13.4 47.4 %all-gather.3.cloned.1.call-done = bf16[528,2048]{1,0:T(8,128)(2,1)} async-done(((bf16[528,512]{1,0:T(8,128)(2,1)}), bf16[528,2048]{1,0:T(8,128)(2,1)}) %all-gather.3.cloned.1.call-update) | async-done | bytes 2162704 | tf_op jit(solution)/shard_map/all_gather | solution.py:629
  69.8 3.5 fusion.89
  79.1 4.7 fusion.85
  85.8 2.9 subtract_convert_fusion.2
  90.1 4.6 collective-permute-start
  96.0 11.1 %all-gather.5.cloned.1.call-done.refs_1_ = bf16[512,2048]{1,0:T(8,128)(2,1)} async-done(((bf16[512,512]{1,0:T(8,128)(2,1)}), bf16[512,2048]{1,0:T(8,128)(2,1)}) %all-gather.5.cloned.1.call-update) | async-done | bytes 2097168 | tf_op jit(solution)/shard_map/all_gather | solution.py:633
  111.4 6.0 collective-permute-done
  127.9 33.3 %collective-permute-done.1.refs_1_ = bf16[512,2048]{1,0:T(8,128)(2,1)} collective-permute-done((bf16[512,2048]{1,0:T(8,128)(2,1)}, bf16[512,2048]{1,0:T(8,128)(2,1)}, u32[]{:S(2)}, u32[]{:S(2)}) %collective-permute-start.1) | collective-permute-done | bytes 2097184 | tf_op jit(solution)/shard_map/ppermute | solution.py:33
  163.8 76.3 %shard_map.297 = (bf16[512,2048]{1,0:T(8,128)(2,1)S(1)}, bf16[512,2048]{1,0:T(8,128)(2,1)S(1)}, f32[512,512]{1,0:T(8,128)S(1)}, f32[512,1]{1,0:T(8,128)S(1)}) custom-call(bf16[512,512]{1,0:T(8,128)(2,1)S(1)} %copy-done.18, bf16[512,2048]{1,0:T(8,128)(2,1)S(1)} %copy-done.20, bf16[512,2048]{1,0:T(8,128)(2,1)S(1)} %slice.136.x, ...), custom_call_target="tpu_custom_call" | custom-call | tf_op jit(solution)/shard_map/pallas_call | solution.py:449
  243.0 29.1 %shard_map.298 = (bf16[512,1408]{1,0:T(8,128)(2,1)}, bf16[512,1408]{1,0:T(8,128)(2,1)}, bf16[512,1408]{1,0:T(8,128)(2,1)}, bf16[512,2048]{1,0:T(8,128)(2,1)}, bf...) custom-call(bf16[512,2048]{1,0:T(8,128)(2,1)} %copy-done.2, bf16[512,2048]{1,0:T(8,128)(2,1)} %all-gather.5.cloned.1.call-done.refs_1_, ...), custom_call_target="tpu_custom_call" | custom-call | flops 17716740096 | bytes 29884416 | tf_op jit(solution)/shard_map/pallas_call | solution.py:195
  272.2 3.7 convolution_convert_fusion.3
  275.9 5.3 collective-permute-done.2
  282.8 3.3 convolution_convert_fusion.2
  292.0 4.8 convolution_convert_fusion.1
  315.1 3.5 add_convert_fusion.5
  321.1 5.5 add_convert_fusion.4
  326.5 28.7 %shard_map.299 = (bf16[512,1408]{1,0:T(8,128)(2,1)}, bf16[512,1408]{1,0:T(8,128)(2,1)}, bf16[512,1408]{1,0:T(8,128)(2,1)}, bf16[512,2048]{1,0:T(8,128)(2,1)}, bf...) custom-call(bf16[512,2048]{1,0:T(8,128)(2,1)} %copy-done.5, bf16[512,2048]{1,0:T(8,128)(2,1)} %collective-permute-done.1.refs_1_, ...), custom_call_target="tpu_custom_call" | custom-call | flops 17716740096 | bytes 29884416 | tf_op jit(solution)/shard_map/pallas_call | solution.py:195
  355.3 3.4 add_convert_fusion.15
  361.6 30.2 %shard_map.300 = (bf16[512,1408]{1,0:T(8,128)(2,1)}, bf16[512,1408]{1,0:T(8,128)(2,1)}, bf16[512,1408]{1,0:T(8,128)(2,1)}, bf16[512,2048]{1,0:T(8,128)(2,1)}, bf...) custom-call(bf16[512,2048]{1,0:T(8,128)(2,1)} %copy-done.2, bf16[512,2048]{1,0:T(8,128)(2,1)} %all-gather.5.cloned.1.call-done.refs_1_, ...), custom_call_target="tpu_custom_call" | custom-call | flops 17716740096 | bytes 29884416 | tf_op jit(solution)/shard_map/pallas_call | solution.py:195
  396.3 3.1 add_convert_fusion.14
  399.4 3.2 add_convert_fusion.13
  402.6 4.5 convolution_convert_fusion.6
  409.1 3.6 collective-permute-done.12
  412.7 4.9 convolution_convert_fusion.5
  417.8 3.2 constant_dynamic-update-slice_fusion.3
  422.7 3.3 constant_dynamic-update-slice_fusion.2
  429.0 6.2 collective-permute-done.15
  436.0 7.1 collective-permute-done.16
  444.6 11.5 %collective-permute-done.17 = f32[10,512]{0,1:T(8,128)S(1)} collective-permute-done((f32[10,512]{0,1:T(8,128)S(1)}, f32[10,512]{0,1:T(8,128)S(1)}, u32[]{:S(2)}, u32[]{:S(2)}) %collective-permute-start.17) | collective-permute-done | bytes 20512 | tf_op jit(solution)/shard_map/ppermute | solution.py:33
  457.4 4.5 convolution_convert_fusion.4
  466.3 6.6 add_convert_fusion.3
  476.4 5.0 add_convert_fusion.2
  484.8 5.0 add_convert_fusion.1
  495.7 95.8 %shard_map.301 = (bf16[512,2048]{1,0:T(8,128)(2,1)S(1)}, f32[512,512]{1,0:T(8,128)S(1)}, f32[1,512]{1,0:T(1,128)S(1)}, bf16[512,2048]{1,0:T(8,128)(2,1)S(1)}) custom-call(bf16[512,2048]{1,0:T(8,128)(2,1)S(1)} %copy-done.16, bf16[512,2048]{1,0:T(8,128)(2,1)S(1)} %copy-done.15, bf16[512,2048]{1,0:T(8,128)(2,1)} %get-tuple-element.125.out_p, ...), custom_call_target="tpu_custom_call" | custom-call | tf_op jit(solution)/shard_map/pallas_call | solution.py:534
  594.1 5.5 multiply_reduce_fusion
  605.9 3.1 add_convert_fusion.11.refs_0_
  611.5 14.3 %collective-permute-done.19 = bf16[704,1024]{1,0:T(8,128)(2,1)S(1)} collective-permute-done((bf16[704,1024]{1,0:T(8,128)(2,1)}, bf16[704,1024]{1,0:T(8,128)(2,1)S(1)}, u32[]{:S(2)}, u32[]{:S(2)}) %collective-permute-start.19) | collective-permute-done | bytes 1441824 | tf_op jit(solution)/shard_map/ppermute | solution.py:33
  633.2 22.7 %collective-permute-done.18 = bf16[2,512,4,128]{3,1,2,0:T(8,128)(2,1)S(1)} collective-permute-done((bf16[2,512,4,128]{3,1,2,0:T(8,128)(2,1)S(1)}, bf16[2,512,4,128]{3,1,2,0:T(8,128)(2,1)S(1)}, u32[]{:S(2)}, u32[]{:S(2)}) %collective-permute-start.18) | collective-permute-done | bytes 1048608 | tf_op jit(solution)/shard_map/ppermute | solution.py:813
  660.0 3.4 convolution_convert_fusion
  669.2 3.5 add_convert_fusion
  674.3 3.1 add_convert_fusion.7
  684.1 31.1 %collective-permute-done.49 = f32[148,128]{1,0:T(8,128)S(1)} collective-permute-done((f32[148,128]{1,0:T(8,128)S(1)}, f32[148,128]{1,0:T(8,128)S(1)}, u32[]{:S(2)}, u32[]{:S(2)}) %collective-permute-start.49) | collective-permute-done | bytes 75808 | tf_op jit(solution)/shard_map/ppermute | solution.py:33
  717.3 5.7 collective-permute-done.50
  725.1 13.4 %collective-permute-done.52.refs_3_ = bf16[256,1408]{1,0:T(8,128)(2,1)S(1)} collective-permute-done((bf16[256,1408]{1,0:T(8,128)(2,1)}, bf16[256,1408]{1,0:T(8,128)(2,1)S(1)}, u32[]{:S(2)}, u32[]{:S(2)}) %collective-permute-start.52) | collective-permute-done | bytes 720928 | tf_op jit(solution)/shard_map/ppermute | solution.py:33
  738.5 15.4 %collective-permute-done.54.refs_2_ = bf16[256,1408]{1,0:T(8,128)(2,1)S(1)} collective-permute-done((bf16[256,1408]{1,0:T(8,128)(2,1)S(1)}, bf16[256,1408]{1,0:T(8,128)(2,1)S(1)}, u32[]{:S(2)}, u32[]{:S(2)}) %collective-permute-start.54) | collective-permute-done | bytes 720928 | tf_op jit(solution)/shard_map/ppermute | solution.py:33
  755.2 13.1 %collective-permute-done.55.refs_3_ = bf16[256,1408]{1,0:T(8,128)(2,1)S(1)} collective-permute-done((bf16[256,1408]{1,0:T(8,128)(2,1)S(1)}, bf16[256,1408]{1,0:T(8,128)(2,1)S(1)}, u32[]{:S(2)}, u32[]{:S(2)}) %collective-permute-start.55) | collective-permute-done | bytes 720928 | tf_op jit(solution)/shard_map/ppermute | solution.py:33
  773.5 9.7 collective-permute-done.30
  784.5 14.3 %collective-permute-done.66.refs_2_ = bf16[352,1024]{1,0:T(8,128)(2,1)} collective-permute-done((bf16[352,1024]{1,0:T(8,128)(2,1)}, bf16[352,1024]{1,0:T(8,128)(2,1)}, u32[]{:S(2)}, u32[]{:S(2)}) %collective-permute-start.66) | collective-permute-done | bytes 720928 | tf_op jit(solution)/shard_map/ppermute | solution.py:33
  798.8 13.6 %collective-permute-done.67.refs_3_ = bf16[352,1024]{1,0:T(8,128)(2,1)} collective-permute-done((bf16[352,1024]{1,0:T(8,128)(2,1)S(1)}, bf16[352,1024]{1,0:T(8,128)(2,1)}, u32[]{:S(2)}, u32[]{:S(2)}) %collective-permute-start.67) | collective-permute-done | bytes 720928 | tf_op jit(solution)/shard_map/ppermute | solution.py:33
  836.6 14.4 %collective-permute-done.33.refs_1_ = bf16[704,1024]{1,0:T(8,128)(2,1)} collective-permute-done((bf16[704,1024]{1,0:T(8,128)(2,1)S(1)}, bf16[704,1024]{1,0:T(8,128)(2,1)}, u32[]{:S(2)}, u32[]{:S(2)}) %collective-permute-start.33) | collective-permute-done | bytes 1441824 | tf_op jit(solution)/shard_map/ppermute | solution.py:33
  851.0 21.5 %collective-permute-done.32 = bf16[128,1024]{1,0:T(8,128)(2,1)S(1)} collective-permute-done((bf16[128,1024]{1,0:T(8,128)(2,1)S(1)}, bf16[128,1024]{1,0:T(8,128)(2,1)S(1)}, u32[]{:S(2)}, u32[]{:S(2)}) %collective-permute-start.32) | collective-permute-done | bytes 262176 | tf_op jit(solution)/shard_map/ppermute | solution.py:33
  880.5 21.2 %collective-permute-done.41.refs_1_ = bf16[128,1024]{1,0:T(8,128)(2,1)S(1)} collective-permute-done((bf16[128,1024]{1,0:T(8,128)(2,1)S(1)}, bf16[128,1024]{1,0:T(8,128)(2,1)S(1)}, u32[]{:S(2)}, u32[]{:S(2)}) %collective-permute-start.41) | collective-permute-done | bytes 262176 | tf_op jit(solution)/shard_map/ppermute | solution.py:33
  904.4 4.8 collective-permute-done.43.refs_3_
  913.2 3.0 fusion.24
  921.2 10.7 %collective-permute-done.35.refs_2_ = bf16[256,1536]{1,0:T(8,128)(2,1)} collective-permute-done((bf16[256,1536]{1,0:T(8,128)(2,1)}, bf16[256,1536]{1,0:T(8,128)(2,1)}, u32[]{:S(2)}, u32[]{:S(2)}) %collective-permute-start.35) | collective-permute-done | bytes 786464 | tf_op jit(solution)/shard_map/ppermute | solution.py:33
  931.9 15.9 %collective-permute-done.36.refs_3_ = bf16[256,1536]{1,0:T(8,128)(2,1)} collective-permute-done((bf16[256,1536]{1,0:T(8,128)(2,1)}, bf16[256,1536]{1,0:T(8,128)(2,1)}, u32[]{:S(2)}, u32[]{:S(2)}) %collective-permute-start.36) | collective-permute-done | bytes 786464 | tf_op jit(solution)/shard_map/ppermute | solution.py:33
  958.4 8.4 shard_map.304
  966.8 12.6 %shard_map.306 = f32[1408,2048]{1,0:T(8,128)} custom-call(s32[8]{0:T(128)S(1)} %stack.213.row_of, s32[8]{0:T(128)S(1)} %stack.199.column_of, bf16[352,1024]{1,0:T(8,128)(2,1)} %add_convert_fusion.18.refs_0_, bf16[352,1024]{1,0:T(8,128)(2,1)S(1)} %copy-done.28, bf16[352,1024]{1,0:T(8,128)(2,1)} %collective-permute-done.66.refs_2_, ...), custom_call_target="tpu_custom_call" | custom-call | flops 2883584 | bytes 17301504 | tf_op jit(solution)/shard_map/pallas_call | solution.py:114
  979.4 13.0 %shard_map.308 = f32[1408,2048]{1,0:T(8,128)} custom-call(s32[4]{0:T(128)S(1)} %pad_add_fusion.1.row_of, s32[4]{0:T(128)S(1)} %pad_add_fusion.2.column_of, bf16[704,1024]{1,0:T(8,128)(2,1)} %add_convert_fusion.11.refs_0_, bf16[704,1024]{1,0:T(8,128)(2,1)} %collective-permute-done.75.refs_1_, bf16[704,1024]{1,0:T(8,128)(2,1)} %collective-permute-done.76.refs_2_, ...), custom_call_target="tpu_custom_call" | custom-call | flops 2883584 | bytes 17301504 | tf_op jit(solution)/shard_map/pallas_call | solution.py:114
  995.4 12.4 %shard_map.309 = f32[1408,2048]{1,0:T(8,128)} custom-call(s32[4]{0:T(128)S(1)} %pad_add_fusion.1.row_of, s32[4]{0:T(128)S(1)} %pad_add_fusion.2.column_of, bf16[704,1024]{1,0:T(8,128)(2,1)S(1)} %copy-done.8, bf16[704,1024]{1,0:T(8,128)(2,1)} %collective-permute-done.33.refs_1_, bf16[704,1024]{1,0:T(8,128)(2,1)} %collective-permute-done.78.refs_2_, ...), custom_call_target="tpu_custom_call" | custom-call | flops 2883584 | bytes 17301504 | tf_op jit(solution)/shard_map/pallas_call | solution.py:114
  1007.9 5.2 shard_map.303
  1013.1 12.1 %shard_map.305 = f32[2048,1408]{1,0:T(8,128)} custom-call(s32[8]{0:T(128)S(1)} %stack.93.row_of, s32[8]{0:T(128)S(1)} %broadcast_5_column_of.2.column_of, bf16[256,1408]{1,0:T(8,128)(2,1)} %add_convert_fusion.20.refs_0_, bf16[256,1408]{1,0:T(8,128)(2,1)} %collective-permute-done.51.refs_1_, bf16[256,1408]{1,0:T(8,128)(2,1)} %collective-permute-done.60.refs_2_, ...), custom_call_target="tpu_custom_call" | custom-call | flops 2883584 | bytes 17301504 | tf_op jit(solution)/shard_map/pallas_call | solution.py:114
  1025.2 12.4 %shard_map.307 = f32[1408,2048]{1,0:T(8,128)} custom-call(s32[4]{0:T(128)S(1)} %pad_add_fusion.1.row_of, s32[4]{0:T(128)S(1)} %pad_add_fusion.2.column_of, bf16[704,1024]{1,0:T(8,128)(2,1)S(1)} %copy-done.7, bf16[704,1024]{1,0:T(8,128)(2,1)} %collective-permute-done.72.refs_1_, bf16[704,1024]{1,0:T(8,128)(2,1)} %collective-permute-done.73.refs_2_, ...), custom_call_target="tpu_custom_call" | custom-call | flops 2883584 | bytes 17301504 | tf_op jit(solution)/shard_map/pallas_call | solution.py:114
  1038.2 14.4 %shard_map.302 = (f32[2048,512]{1,0:T(8,128)}, f32[2048,512]{1,0:T(8,128)}, f32[2048,512]{1,0:T(8,128)}) custom-call(s32[8]{0:T(128)S(1)} %stack.93.row_of, s32[8]{0:T(128)S(1)} %broadcast_5_column_of.2.column_of, bf16[256,1536]{1,0:T(8,128)(2,1)} %add_convert_fusion.17.refs_0_, bf16[256,1536]{1,0:T(8,128)(2,1)} %collective-permute-done.34.refs_1_, ...), custom_call_target="tpu_custom_call" | custom-call | flops 3145728 | bytes 18874368 | tf_op jit(solution)/shard_map/pallas_call | solution.py:114
  (586 shorter events, 215.0 us)
Async XLA Ops:
  7.2 53.6 %all-gather.3.cloned.1.call-start = ((), (), s32[]{:S(2)}) async-start(), calls=%async_computation.2 | async-start | bytes 2703360 | tf_op jit(solution)/shard_map/all_gather | solution.py:629
  10.7 96.4 %all-gather.5.cloned.1.call-start = ((), (), s32[]{:S(2)}) async-start(), calls=%async_computation.3 | async-start | bytes 2621440 | tf_op jit(solution)/shard_map/all_gather | solution.py:633
  11.5 901.7 %reduce-scatter.5.cloned.1.call-start = ((), (), s32[]{:S(2)}) async-start(), calls=%async_computation.5 | async-start | bytes 2621440 | tf_op jit(solution)/shard_map/reduce_scatter | solution.py:847
  90.1 27.3 %collective-permute-start = (bf16[2,512,4,128]{3,1,2,0:T(8,128)(2,1)}, bf16[2,512,4,128]{3,1,2,0:T(8,128)(2,1)}, u32[]{:S(2)}, u32[]{:S(2)}) collective-permute-start(bf16[2,512,4,128]{3,1,2,0:T(8,128)(2,1)} %pad_maximum_fusion.2), channel_id=1, source_target_pairs={{0,4},{1,5},{2,6},{3,7},{8,12},{9,13},{10,14},{11,15},{16,20},{17,... | collective-permute-start | bytes 3145736 | tf_op jit(solution)/shard_map/ppermute | solution.py:653
  107.1 54.1 %collective-permute-start.1 = (bf16[512,2048]{1,0:T(8,128)(2,1)}, bf16[512,2048]{1,0:T(8,128)(2,1)}, u32[]{:S(2)}, u32[]{:S(2)}) collective-permute-start(bf16[512,2048]{1,0:T(8,128)(2,1)} %all-gather.5.cloned.1.call-done.refs_1_), channel_id=1, source_target_pairs={{0,4},{4,0},{1,5},{5,1},{2,6},{6,2},{3,7},{7,3},{8,12},{12,8},{9,1... | collective-permute-start | bytes 6291464 | tf_op jit(solution)/shard_map/ppermute | solution.py:33
  287.1 16.9 %collective-permute-start.6 = (f32[512,8]{1,0:T(8,128)}, f32[512,8]{1,0:T(8,128)}, u32[]{:S(2)}, u32[]{:S(2)}) collective-permute-start(f32[512,8]{1,0:T(8,128)} %copy.154), channel_id=1, source_target_pairs={{0,4},{4,0},{1,5},{5,1},{2,6},{6,2},{3,7},{7,3},{8,12},{12,8},{9,1... | collective-permute-start | bytes 49160 | tf_op jit(solution)/shard_map/ppermute | solution.py:33
  296.8 24.0 %collective-permute-start.5 = (bf16[1024,1408]{1,0:T(8,128)(2,1)}, bf16[1024,1408]{1,0:T(8,128)(2,1)}, u32[]{:S(2)}, u32[]{:S(2)}) collective-permute-start(bf16[1024,1408]{1,0:T(8,128)(2,1)} %convolution_convert_fusion.1), channel_id=1, source_target_pairs={{0,8},{8,0},{16,24},{24,16},{1,9},{9,1},{17,25},{25,17},{2,10},{10... | collective-permute-start | bytes 8650760 | tf_op jit(solution)/shard_map/ppermute | solution.py:33
  313.7 41.6 %collective-permute-start.3 = (bf16[512,1408]{1,0:T(8,128)(2,1)}, bf16[512,1408]{1,0:T(8,128)(2,1)}, u32[]{:S(2)}, u32[]{:S(2)}) collective-permute-start(bf16[512,1408]{1,0:T(8,128)(2,1)} %constant_dynamic-slice_fusion.13), channel_id=1, source_target_pairs={{0,16},{8,24},{16,0},{24,8},{1,17},{9,25},{17,1},{25,9},{2,18},{10... | collective-permute-start | bytes 4325384 | tf_op jit(solution)/shard_map/ppermute | solution.py:33
  319.9 79.5 %collective-permute-start.7 = (bf16[704,1024]{1,0:T(8,128)(2,1)}, bf16[704,1024]{1,0:T(8,128)(2,1)}, u32[]{:S(2)}, u32[]{:S(2)}) collective-permute-start(bf16[704,1024]{1,0:T(8,128)(2,1)} %constant_dynamic-slice_fusion.12), channel_id=1, source_target_pairs={{0,16},{8,24},{16,0},{24,8},{1,17},{9,25},{17,1},{25,9},{2,18},{10... | collective-permute-start | bytes 4325384 | tf_op jit(solution)/shard_map/ppermute | solution.py:33
  360.0 34.0 %collective-permute-start.8 = (bf16[512,1408]{1,0:T(8,128)(2,1)}, bf16[512,1408]{1,0:T(8,128)(2,1)}, u32[]{:S(2)}, u32[]{:S(2)}) collective-permute-start(bf16[512,1408]{1,0:T(8,128)(2,1)} %constant_dynamic-slice_fusion.11), channel_id=1, source_target_pairs={{0,4},{4,0},{1,5},{5,1},{2,6},{6,2},{3,7},{7,3},{8,12},{12,8},{9,1... | collective-permute-start | bytes 4325384 | tf_op jit(solution)/shard_map/ppermute | solution.py:33
  417.6 39.8 %collective-permute-start.13 = (bf16[1408,1024]{1,0:T(8,128)(2,1)}, bf16[1408,1024]{1,0:T(8,128)(2,1)}, u32[]{:S(2)}, u32[]{:S(2)}) collective-permute-start(bf16[1408,1024]{1,0:T(8,128)(2,1)} %convolution_convert_fusion.5), channel_id=1, source_target_pairs={{0,8},{8,0},{16,24},{24,16},{1,9},{9,1},{17,25},{25,17},{2,10},{10... | collective-permute-start | bytes 8650760 | tf_op jit(solution)/shard_map/ppermute | solution.py:33
  426.0 9.1 collective-permute-start.15
  427.4 63.7 %collective-permute-start.10 = (bf16[256,1408]{1,0:T(8,128)(2,1)}, bf16[256,1408]{1,0:T(8,128)(2,1)}, u32[]{:S(2)}, u32[]{:S(2)}) collective-permute-start(bf16[256,1408]{1,0:T(8,128)(2,1)} %constant_dynamic-slice_fusion.9), channel_id=1, source_target_pairs={{0,4},{4,0},{1,5},{5,1},{2,6},{6,2},{3,7},{7,3},{8,12},{12,8},{9,1... | collective-permute-start | bytes 2162696 | tf_op jit(solution)/shard_map/ppermute | solution.py:33
  443.1 13.0 %collective-permute-start.17 = (f32[10,512]{0,1:T(8,128)S(1)}, f32[10,512]{0,1:T(8,128)S(1)}, u32[]{:S(2)}, u32[]{:S(2)}) collective-permute-start(f32[10,512]{0,1:T(8,128)S(1)} %add.639), channel_id=1, source_target_pairs={{0,2},{1,3},{2,0},{3,1},{4,6},{5,7},{6,4},{7,5},{8,10},{9,11},{10,... | collective-permute-start | bytes 61448 | tf_op jit(solution)/shard_map/ppermute | solution.py:33
  461.9 20.7 %collective-permute-start.14 = (bf16[1408,1024]{1,0:T(8,128)(2,1)}, bf16[1408,1024]{1,0:T(8,128)(2,1)}, u32[]{:S(2)}, u32[]{:S(2)}) collective-permute-start(bf16[1408,1024]{1,0:T(8,128)(2,1)} %convolution_convert_fusion.4), channel_id=1, source_target_pairs={{0,8},{8,0},{16,24},{24,16},{1,9},{9,1},{17,25},{25,17},{2,10},{10... | collective-permute-start | bytes 8650760 | tf_op jit(solution)/shard_map/ppermute | solution.py:33
  464.8 29.8 %collective-permute-start.9 = (bf16[352,1024]{1,0:T(8,128)(2,1)S(1)}, bf16[352,1024]{1,0:T(8,128)(2,1)S(1)}, u32[]{:S(2)}, u32[]{:S(2)}) collective-permute-start(bf16[352,1024]{1,0:T(8,128)(2,1)S(1)} %constant_dynamic-slice_fusion.10), channel_id=1, source_target_pairs={{0,4},{4,0},{1,5},{5,1},{2,6},{6,2},{3,7},{7,3},{8,12},{12,8},{9,1... | collective-permute-start | bytes 2162696 | tf_op jit(solution)/shard_map/ppermute | solution.py:33
  465.4 24.4 %collective-permute-start.11 = (bf16[256,1408]{1,0:T(8,128)(2,1)S(1)}, bf16[256,1408]{1,0:T(8,128)(2,1)S(1)}, u32[]{:S(2)}, u32[]{:S(2)}) collective-permute-start(bf16[256,1408]{1,0:T(8,128)(2,1)S(1)} %constant_dynamic-slice_fusion.8), channel_id=1, source_target_pairs={{0,16},{8,24},{16,0},{24,8},{1,17},{9,25},{17,1},{25,9},{2,18},{10... | collective-permute-start | bytes 2162696 | tf_op jit(solution)/shard_map/ppermute | solution.py:33
  474.2 129.4 %collective-permute-start.21 = (bf16[704,1024]{1,0:T(8,128)(2,1)}, bf16[704,1024]{1,0:T(8,128)(2,1)S(1)}, u32[]{:S(2)}, u32[]{:S(2)}) collective-permute-start(bf16[704,1024]{1,0:T(8,128)(2,1)} %constant_dynamic-slice_fusion.4), channel_id=1, source_target_pairs={{0,16},{8,24},{16,0},{24,8},{1,17},{9,25},{17,1},{25,9},{2,18},{10... | collective-permute-start | bytes 4325384 | tf_op jit(solution)/shard_map/ppermute | solution.py:33
  482.6 122.7 %collective-permute-start.20 = (bf16[704,1024]{1,0:T(8,128)(2,1)}, bf16[704,1024]{1,0:T(8,128)(2,1)}, u32[]{:S(2)}, u32[]{:S(2)}) collective-permute-start(bf16[704,1024]{1,0:T(8,128)(2,1)} %constant_dynamic-slice_fusion.5), channel_id=1, source_target_pairs={{0,16},{8,24},{16,0},{24,8},{1,17},{9,25},{17,1},{25,9},{2,18},{10... | collective-permute-start | bytes 4325384 | tf_op jit(solution)/shard_map/ppermute | solution.py:33
  592.9 32.9 %collective-permute-start.19 = (bf16[704,1024]{1,0:T(8,128)(2,1)}, bf16[704,1024]{1,0:T(8,128)(2,1)S(1)}, u32[]{:S(2)}, u32[]{:S(2)}) collective-permute-start(bf16[704,1024]{1,0:T(8,128)(2,1)} %constant_dynamic-slice_fusion.6), channel_id=1, source_target_pairs={{0,16},{8,24},{16,0},{24,8},{1,17},{9,25},{17,1},{25,9},{2,18},{10... | collective-permute-start | bytes 4325384 | tf_op jit(solution)/shard_map/ppermute | solution.py:33
  628.5 27.4 %collective-permute-start.18 = (bf16[2,512,4,128]{3,1,2,0:T(8,128)(2,1)S(1)}, bf16[2,512,4,128]{3,1,2,0:T(8,128)(2,1)S(1)}, u32[]{:S(2)}, u32[]{:S(2)}) collective-permute-start(bf16[2,512,4,128]{3,1,2,0:T(8,128)(2,1)S(1)} %pad_maximum_fusion.4), channel_id=1, source_target_pairs={{4,0},{5,1},{6,2},{7,3},{12,8},{13,9},{14,10},{15,11},{20,16},{21,... | collective-permute-start | bytes 3145736 | tf_op jit(solution)/shard_map/ppermute | solution.py:813
  663.9 51.4 %collective-permute-start.51 = (bf16[256,1408]{1,0:T(8,128)(2,1)}, bf16[256,1408]{1,0:T(8,128)(2,1)}, u32[]{:S(2)}, u32[]{:S(2)}) collective-permute-start(bf16[256,1408]{1,0:T(8,128)(2,1)} %add_convert_fusion.20.refs_0_), channel_id=1, source_target_pairs={{0,16},{8,24},{16,0},{24,8},{1,17},{9,25},{17,1},{25,9},{2,18},{10... | collective-permute-start | bytes 2162696 | tf_op jit(solution)/shard_map/ppermute | solution.py:33
  677.4 315.7 %reduce-scatter.3.cloned.1.call-start = ((), (), s32[]{:S(2)}) async-start(), calls=%async_computation.4 | async-start | bytes 2621440 | tf_op jit(solution)/shard_map/reduce_scatter | solution.py:816
  678.8 44.2 %collective-permute-start.53 = (bf16[256,1408]{1,0:T(8,128)(2,1)S(1)}, bf16[256,1408]{1,0:T(8,128)(2,1)S(1)}, u32[]{:S(2)}, u32[]{:S(2)}) collective-permute-start(bf16[256,1408]{1,0:T(8,128)(2,1)S(1)} %copy-done.10), channel_id=1, source_target_pairs={{0,16},{8,24},{16,0},{24,8},{1,17},{9,25},{17,1},{25,9},{2,18},{10... | collective-permute-start | bytes 2162696 | tf_op jit(solution)/shard_map/ppermute | solution.py:33
  680.1 45.1 %collective-permute-start.65 = (bf16[352,1024]{1,0:T(8,128)(2,1)}, bf16[352,1024]{1,0:T(8,128)(2,1)S(1)}, u32[]{:S(2)}, u32[]{:S(2)}) collective-permute-start(bf16[352,1024]{1,0:T(8,128)(2,1)} %add_convert_fusion.18.refs_0_), channel_id=1, source_target_pairs={{0,16},{8,24},{16,0},{24,8},{1,17},{9,25},{17,1},{25,9},{2,18},{10... | collective-permute-start | bytes 2162696 | tf_op jit(solution)/shard_map/ppermute | solution.py:33
  681.3 33.9 %collective-permute-start.49 = (f32[148,128]{1,0:T(8,128)S(1)}, f32[148,128]{1,0:T(8,128)S(1)}, u32[]{:S(2)}, u32[]{:S(2)}) collective-permute-start(f32[148,128]{1,0:T(8,128)S(1)} %add.689), channel_id=1, source_target_pairs={{0,16},{8,24},{16,0},{24,8},{1,17},{9,25},{17,1},{25,9},{2,18},{10... | collective-permute-start | bytes 227336 | tf_op jit(solution)/shard_map/ppermute | solution.py:33
  684.1 99.4 %collective-permute-start.29 = (bf16[512,1536]{1,0:T(8,128)(2,1)S(1)}, bf16[512,1536]{1,0:T(8,128)(2,1)S(1)}, u32[]{:S(2)}, u32[]{:S(2)}) collective-permute-start(bf16[512,1536]{1,0:T(8,128)(2,1)S(1)} %constant_dynamic-slice_fusion.3), channel_id=1, source_target_pairs={{0,4},{4,0},{1,5},{5,1},{2,6},{6,2},{3,7},{7,3},{8,12},{12,8},{9,1... | collective-permute-start | bytes 4718600 | tf_op jit(solution)/shard_map/ppermute | solution.py:33
  715.3 23.2 %collective-permute-start.52 = (bf16[256,1408]{1,0:T(8,128)(2,1)}, bf16[256,1408]{1,0:T(8,128)(2,1)S(1)}, u32[]{:S(2)}, u32[]{:S(2)}) collective-permute-start(bf16[256,1408]{1,0:T(8,128)(2,1)} %collective-permute-done.51.refs_1_), channel_id=1, source_target_pairs={{0,4},{4,0},{1,5},{5,1},{2,6},{6,2},{3,7},{7,3},{8,12},{12,8},{9,1... | collective-permute-start | bytes 2162696 | tf_op jit(solution)/shard_map/ppermute | solution.py:33
  723.1 30.9 %collective-permute-start.54 = (bf16[256,1408]{1,0:T(8,128)(2,1)S(1)}, bf16[256,1408]{1,0:T(8,128)(2,1)S(1)}, u32[]{:S(2)}, u32[]{:S(2)}) collective-permute-start(bf16[256,1408]{1,0:T(8,128)(2,1)S(1)} %copy-done.10), channel_id=1, source_target_pairs={{0,4},{4,0},{1,5},{5,1},{2,6},{6,2},{3,7},{7,3},{8,12},{12,8},{9,1... | collective-permute-start | bytes 2162696 | tf_op jit(solution)/shard_map/ppermute | solution.py:33
  723.1 45.3 %collective-permute-start.55 = (bf16[256,1408]{1,0:T(8,128)(2,1)S(1)}, bf16[256,1408]{1,0:T(8,128)(2,1)S(1)}, u32[]{:S(2)}, u32[]{:S(2)}) collective-permute-start(bf16[256,1408]{1,0:T(8,128)(2,1)S(1)} %collective-permute-done.53.refs_1_), channel_id=1, source_target_pairs={{0,4},{4,0},{1,5},{5,1},{2,6},{6,2},{3,7},{7,3},{8,12},{12,8},{9,1... | collective-permute-start | bytes 2162696 | tf_op jit(solution)/shard_map/ppermute | solution.py:33
  725.1 43.5 %collective-permute-start.57 = (bf16[256,1408]{1,0:T(8,128)(2,1)S(1)}, bf16[256,1408]{1,0:T(8,128)(2,1)S(1)}, u32[]{:S(2)}, u32[]{:S(2)}) collective-permute-start(bf16[256,1408]{1,0:T(8,128)(2,1)S(1)} %collective-permute-done.53.refs_1_), channel_id=1, source_target_pairs={{0,8},{8,0},{16,24},{24,16},{1,9},{9,1},{17,25},{25,17},{2,10},{10... | collective-permute-start | bytes 2162696 | tf_op jit(solution)/shard_map/ppermute | solution.py:33
  738.5 32.3 %collective-permute-start.62 = (bf16[256,1408]{1,0:T(8,128)(2,1)}, bf16[256,1408]{1,0:T(8,128)(2,1)S(1)}, u32[]{:S(2)}, u32[]{:S(2)}) collective-permute-start(bf16[256,1408]{1,0:T(8,128)(2,1)} %collective-permute-done.51.refs_1_), channel_id=1, source_target_pairs={{0,8},{8,0},{16,24},{24,16},{1,9},{9,1},{17,25},{25,17},{2,10},{10... | collective-permute-start | bytes 2162696 | tf_op jit(solution)/shard_map/ppermute | solution.py:33
  754.0 60.6 %collective-permute-start.72 = (bf16[704,1024]{1,0:T(8,128)(2,1)S(1)}, bf16[704,1024]{1,0:T(8,128)(2,1)}, u32[]{:S(2)}, u32[]{:S(2)}) collective-permute-start(bf16[704,1024]{1,0:T(8,128)(2,1)S(1)} %copy-done.7), channel_id=1, source_target_pairs={{0,16},{8,24},{16,0},{24,8},{1,17},{9,25},{17,1},{25,9},{2,18},{10... | collective-permute-start | bytes 4325384 | tf_op jit(solution)/shard_map/ppermute | solution.py:33
  768.4 14.9 %collective-permute-start.30 = (bf16[256,1024]{1,0:T(8,128)(2,1)S(1)}, bf16[256,1024]{1,0:T(8,128)(2,1)S(1)}, u32[]{:S(2)}, u32[]{:S(2)}) collective-permute-start(bf16[256,1024]{1,0:T(8,128)(2,1)S(1)} %constant_dynamic-slice_fusion.2), channel_id=1, source_target_pairs={{0,4},{4,0},{1,5},{5,1},{2,6},{6,2},{3,7},{7,3},{8,12},{12,8},{9,1... | collective-permute-start | bytes 1572872 | tf_op jit(solution)/shard_map/ppermute | solution.py:33
  769.5 46.9 %collective-permute-start.75 = (bf16[704,1024]{1,0:T(8,128)(2,1)}, bf16[704,1024]{1,0:T(8,128)(2,1)}, u32[]{:S(2)}, u32[]{:S(2)}) collective-permute-start(bf16[704,1024]{1,0:T(8,128)(2,1)} %add_convert_fusion.11.refs_0_), channel_id=1, source_target_pairs={{0,16},{8,24},{16,0},{24,8},{1,17},{9,25},{17,1},{25,9},{2,18},{10... | collective-permute-start | bytes 4325384 | tf_op jit(solution)/shard_map/ppermute | solution.py:33
  771.7 27.0 %collective-permute-start.66 = (bf16[352,1024]{1,0:T(8,128)(2,1)}, bf16[352,1024]{1,0:T(8,128)(2,1)}, u32[]{:S(2)}, u32[]{:S(2)}) collective-permute-start(bf16[352,1024]{1,0:T(8,128)(2,1)} %add_convert_fusion.18.refs_0_), channel_id=1, source_target_pairs={{0,4},{4,0},{1,5},{5,1},{2,6},{6,2},{3,7},{7,3},{8,12},{12,8},{9,1... | collective-permute-start | bytes 2162696 | tf_op jit(solution)/shard_map/ppermute | solution.py:33
  783.2 29.1 %collective-permute-start.67 = (bf16[352,1024]{1,0:T(8,128)(2,1)S(1)}, bf16[352,1024]{1,0:T(8,128)(2,1)}, u32[]{:S(2)}, u32[]{:S(2)}) collective-permute-start(bf16[352,1024]{1,0:T(8,128)(2,1)S(1)} %collective-permute-done.65.refs_1_), channel_id=1, source_target_pairs={{0,4},{4,0},{1,5},{5,1},{2,6},{6,2},{3,7},{7,3},{8,12},{12,8},{9,1... | collective-permute-start | bytes 2162696 | tf_op jit(solution)/shard_map/ppermute | solution.py:33
  783.5 29.7 %collective-permute-start.69 = (bf16[352,1024]{1,0:T(8,128)(2,1)S(1)}, bf16[352,1024]{1,0:T(8,128)(2,1)S(1)}, u32[]{:S(2)}, u32[]{:S(2)}) collective-permute-start(bf16[352,1024]{1,0:T(8,128)(2,1)S(1)} %collective-permute-done.65.refs_1_), channel_id=1, source_target_pairs={{0,8},{8,0},{16,24},{24,16},{1,9},{9,1},{17,25},{25,17},{2,10},{10... | collective-permute-start | bytes 2162696 | tf_op jit(solution)/shard_map/ppermute | solution.py:33
  798.8 20.0 %collective-permute-start.56 = (bf16[256,1408]{1,0:T(8,128)(2,1)S(1)}, bf16[256,1408]{1,0:T(8,128)(2,1)S(1)}, u32[]{:S(2)}, u32[]{:S(2)}) collective-permute-start(bf16[256,1408]{1,0:T(8,128)(2,1)S(1)} %copy-done.11), channel_id=1, source_target_pairs={{0,8},{8,0},{16,24},{24,16},{1,9},{9,1},{17,25},{25,17},{2,10},{10... | collective-permute-start | bytes 2162696 | tf_op jit(solution)/shard_map/ppermute | solution.py:33
  812.3 8.7 collective-permute-start.59
  816.4 34.5 %collective-permute-start.33 = (bf16[704,1024]{1,0:T(8,128)(2,1)S(1)}, bf16[704,1024]{1,0:T(8,128)(2,1)}, u32[]{:S(2)}, u32[]{:S(2)}) collective-permute-start(bf16[704,1024]{1,0:T(8,128)(2,1)S(1)} %copy-done.8), channel_id=1, source_target_pairs={{0,16},{8,24},{16,0},{24,8},{1,17},{9,25},{17,1},{25,9},{2,18},{10... | collective-permute-start | bytes 4325384 | tf_op jit(solution)/shard_map/ppermute | solution.py:33
  819.6 8.7 collective-permute-start.68
  820.6 9.6 collective-permute-start.70
  821.9 10.1 collective-permute-start.71
  822.8 49.7 %collective-permute-start.31 = (bf16[256,1536]{1,0:T(8,128)(2,1)}, bf16[256,1536]{1,0:T(8,128)(2,1)}, u32[]{:S(2)}, u32[]{:S(2)}) collective-permute-start(bf16[256,1536]{1,0:T(8,128)(2,1)} %constant_dynamic-slice_fusion.1), channel_id=1, source_target_pairs={{0,16},{8,24},{16,0},{24,8},{1,17},{9,25},{17,1},{25,9},{2,18},{10... | collective-permute-start | bytes 2359304 | tf_op jit(solution)/shard_map/ppermute | solution.py:33
  830.1 42.3 %collective-permute-start.32 = (bf16[128,1024]{1,0:T(8,128)(2,1)S(1)}, bf16[128,1024]{1,0:T(8,128)(2,1)S(1)}, u32[]{:S(2)}, u32[]{:S(2)}) collective-permute-start(bf16[128,1024]{1,0:T(8,128)(2,1)S(1)} %constant_dynamic-slice_fusion), channel_id=1, source_target_pairs={{0,16},{8,24},{16,0},{24,8},{1,17},{9,25},{17,1},{25,9},{2,18},{10... | collective-permute-start | bytes 786440 | tf_op jit(solution)/shard_map/ppermute | solution.py:33
  832.0 44.5 %collective-permute-start.74 = (bf16[704,1024]{1,0:T(8,128)(2,1)}, bf16[704,1024]{1,0:T(8,128)(2,1)}, u32[]{:S(2)}, u32[]{:S(2)}) collective-permute-start(bf16[704,1024]{1,0:T(8,128)(2,1)} %collective-permute-done.72.refs_1_), channel_id=1, source_target_pairs={{0,8},{8,0},{16,24},{24,16},{1,9},{9,1},{17,25},{25,17},{2,10},{10... | collective-permute-start | bytes 4325384 | tf_op jit(solution)/shard_map/ppermute | solution.py:33
  836.6 41.3 %collective-permute-start.76 = (bf16[704,1024]{1,0:T(8,128)(2,1)}, bf16[704,1024]{1,0:T(8,128)(2,1)}, u32[]{:S(2)}, u32[]{:S(2)}) collective-permute-start(bf16[704,1024]{1,0:T(8,128)(2,1)} %add_convert_fusion.11.refs_0_), channel_id=1, source_target_pairs={{0,8},{8,0},{16,24},{24,16},{1,9},{9,1},{17,25},{25,17},{2,10},{10... | collective-permute-start | bytes 4325384 | tf_op jit(solution)/shard_map/ppermute | solution.py:33
  851.0 27.5 %collective-permute-start.77 = (bf16[704,1024]{1,0:T(8,128)(2,1)}, bf16[704,1024]{1,0:T(8,128)(2,1)}, u32[]{:S(2)}, u32[]{:S(2)}) collective-permute-start(bf16[704,1024]{1,0:T(8,128)(2,1)} %collective-permute-done.75.refs_1_), channel_id=1, source_target_pairs={{0,8},{8,0},{16,24},{24,16},{1,9},{9,1},{17,25},{25,17},{2,10},{10... | collective-permute-start | bytes 4325384 | tf_op jit(solution)/shard_map/ppermute | solution.py:33
  876.5 35.3 %collective-permute-start.34 = (bf16[256,1536]{1,0:T(8,128)(2,1)}, bf16[256,1536]{1,0:T(8,128)(2,1)}, u32[]{:S(2)}, u32[]{:S(2)}) collective-permute-start(bf16[256,1536]{1,0:T(8,128)(2,1)} %add_convert_fusion.17.refs_0_), channel_id=1, source_target_pairs={{0,16},{8,24},{16,0},{24,8},{1,17},{9,25},{17,1},{25,9},{2,18},{10... | collective-permute-start | bytes 2359304 | tf_op jit(solution)/shard_map/ppermute | solution.py:33
  877.9 26.4 %collective-permute-start.60 = (bf16[256,1408]{1,0:T(8,128)(2,1)}, bf16[256,1408]{1,0:T(8,128)(2,1)}, u32[]{:S(2)}, u32[]{:S(2)}) collective-permute-start(bf16[256,1408]{1,0:T(8,128)(2,1)} %add_convert_fusion.20.refs_0_), channel_id=1, source_target_pairs={{0,4},{4,0},{1,5},{5,1},{2,6},{6,2},{3,7},{7,3},{8,12},{12,8},{9,1... | collective-permute-start | bytes 2162696 | tf_op jit(solution)/shard_map/ppermute | solution.py:33
  878.5 23.3 %collective-permute-start.41 = (bf16[128,1024]{1,0:T(8,128)(2,1)S(1)}, bf16[128,1024]{1,0:T(8,128)(2,1)S(1)}, u32[]{:S(2)}, u32[]{:S(2)}) collective-permute-start(bf16[128,1024]{1,0:T(8,128)(2,1)S(1)} %add_convert_fusion.27.refs_0_), channel_id=1, source_target_pairs={{0,16},{8,24},{16,0},{24,8},{1,17},{9,25},{17,1},{25,9},{2,18},{10... | collective-permute-start | bytes 786440 | tf_op jit(solution)/shard_map/ppermute | solution.py:33
  879.1 23.2 %collective-permute-start.42 = (bf16[128,1024]{1,0:T(8,128)(2,1)S(1)}, bf16[128,1024]{1,0:T(8,128)(2,1)S(1)}, u32[]{:S(2)}, u32[]{:S(2)}) collective-permute-start(bf16[128,1024]{1,0:T(8,128)(2,1)S(1)} %add_convert_fusion.27.refs_0_), channel_id=1, source_target_pairs={{0,4},{4,0},{1,5},{5,1},{2,6},{6,2},{3,7},{7,3},{8,12},{12,8},{9,1... | collective-permute-start | bytes 786440 | tf_op jit(solution)/shard_map/ppermute | solution.py:33
  880.5 21.8 %collective-permute-start.44 = (bf16[128,1024]{1,0:T(8,128)(2,1)S(1)}, bf16[128,1024]{1,0:T(8,128)(2,1)S(1)}, u32[]{:S(2)}, u32[]{:S(2)}) collective-permute-start(bf16[128,1024]{1,0:T(8,128)(2,1)S(1)} %add_convert_fusion.27.refs_0_), channel_id=1, source_target_pairs={{0,8},{8,0},{16,24},{24,16},{1,9},{9,1},{17,25},{25,17},{2,10},{10... | collective-permute-start | bytes 786440 | tf_op jit(solution)/shard_map/ppermute | solution.py:33
  904.3 14.8 %collective-permute-start.63 = (bf16[256,1408]{1,0:T(8,128)(2,1)}, bf16[256,1408]{1,0:T(8,128)(2,1)}, u32[]{:S(2)}, u32[]{:S(2)}) collective-permute-start(bf16[256,1408]{1,0:T(8,128)(2,1)} %collective-permute-done.60.refs_2_), channel_id=1, source_target_pairs={{0,8},{8,0},{16,24},{24,16},{1,9},{9,1},{17,25},{25,17},{2,10},{10... | collective-permute-start | bytes 2162696 | tf_op jit(solution)/shard_map/ppermute | solution.py:33
  909.9 82.5 %collective-permute-start.73 = (bf16[704,1024]{1,0:T(8,128)(2,1)S(1)}, bf16[704,1024]{1,0:T(8,128)(2,1)}, u32[]{:S(2)}, u32[]{:S(2)}) collective-permute-start(bf16[704,1024]{1,0:T(8,128)(2,1)S(1)} %copy-done.7), channel_id=1, source_target_pairs={{0,8},{8,0},{16,24},{24,16},{1,9},{9,1},{17,25},{25,17},{2,10},{10... | collective-permute-start | bytes 4325384 | tf_op jit(solution)/shard_map/ppermute | solution.py:33
  911.2 20.7 %collective-permute-start.35 = (bf16[256,1536]{1,0:T(8,128)(2,1)}, bf16[256,1536]{1,0:T(8,128)(2,1)}, u32[]{:S(2)}, u32[]{:S(2)}) collective-permute-start(bf16[256,1536]{1,0:T(8,128)(2,1)} %add_convert_fusion.17.refs_0_), channel_id=1, source_target_pairs={{0,4},{4,0},{1,5},{5,1},{2,6},{6,2},{3,7},{7,3},{8,12},{12,8},{9,1... | collective-permute-start | bytes 2359304 | tf_op jit(solution)/shard_map/ppermute | solution.py:33
  911.8 36.0 %collective-permute-start.36 = (bf16[256,1536]{1,0:T(8,128)(2,1)}, bf16[256,1536]{1,0:T(8,128)(2,1)}, u32[]{:S(2)}, u32[]{:S(2)}) collective-permute-start(bf16[256,1536]{1,0:T(8,128)(2,1)} %collective-permute-done.34.refs_1_), channel_id=1, source_target_pairs={{0,4},{4,0},{1,5},{5,1},{2,6},{6,2},{3,7},{7,3},{8,12},{12,8},{9,1... | collective-permute-start | bytes 2359304 | tf_op jit(solution)/shard_map/ppermute | solution.py:33
  919.1 28.7 %collective-permute-start.27 = (f32[4,128]{1,0:T(4,128)S(1)}, f32[4,128]{1,0:T(4,128)S(1)}, u32[]{:S(2)}, u32[]{:S(2)}) collective-permute-start(f32[4,128]{1,0:T(4,128)S(1)} %bitcast_add_fusion), channel_id=1, source_target_pairs={{0,16},{8,24},{16,0},{24,8},{1,17},{9,25},{17,1},{25,9},{2,18},{10... | collective-permute-start | bytes 6152 | tf_op jit(solution)/shard_map/ppermute | solution.py:33
  921.1 117.1 %collective-permute-start.37 = (bf16[256,1536]{1,0:T(8,128)(2,1)}, bf16[256,1536]{1,0:T(8,128)(2,1)}, u32[]{:S(2)}, u32[]{:S(2)}) collective-permute-start(bf16[256,1536]{1,0:T(8,128)(2,1)} %add_convert_fusion.17.refs_0_), channel_id=1, source_target_pairs={{0,8},{8,0},{16,24},{24,16},{1,9},{9,1},{17,25},{25,17},{2,10},{10... | collective-permute-start | bytes 2359304 | tf_op jit(solution)/shard_map/ppermute | solution.py:33
  931.9 106.3 %collective-permute-start.38 = (bf16[256,1536]{1,0:T(8,128)(2,1)}, bf16[256,1536]{1,0:T(8,128)(2,1)}, u32[]{:S(2)}, u32[]{:S(2)}) collective-permute-start(bf16[256,1536]{1,0:T(8,128)(2,1)} %collective-permute-done.34.refs_1_), channel_id=1, source_target_pairs={{0,8},{8,0},{16,24},{24,16},{1,9},{9,1},{17,25},{25,17},{2,10},{10... | collective-permute-start | bytes 2359304 | tf_op jit(solution)/shard_map/ppermute | solution.py:33
  947.8 90.4 %collective-permute-start.39 = (bf16[256,1536]{1,0:T(8,128)(2,1)}, bf16[256,1536]{1,0:T(8,128)(2,1)}, u32[]{:S(2)}, u32[]{:S(2)}) collective-permute-start(bf16[256,1536]{1,0:T(8,128)(2,1)} %collective-permute-done.35.refs_2_), channel_id=1, source_target_pairs={{0,8},{8,0},{16,24},{24,16},{1,9},{9,1},{17,25},{25,17},{2,10},{10... | collective-permute-start | bytes 2359304 | tf_op jit(solution)/shard_map/ppermute | solution.py:33
  947.8 90.4 %collective-permute-start.40 = (bf16[256,1536]{1,0:T(8,128)(2,1)}, bf16[256,1536]{1,0:T(8,128)(2,1)}, u32[]{:S(2)}, u32[]{:S(2)}) collective-permute-start(bf16[256,1536]{1,0:T(8,128)(2,1)} %collective-permute-done.36.refs_3_), channel_id=1, source_target_pairs={{0,8},{8,0},{16,24},{24,16},{1,9},{9,1},{17,25},{25,17},{2,10},{10... | collective-permute-start | bytes 2359304 | tf_op jit(solution)/shard_map/ppermute | solution.py:33
  992.4 45.2 %collective-permute-start.28 = (f32[4,128]{1,0:T(4,128)S(1)}, f32[4,128]{1,0:T(4,128)S(1)}, u32[]{:S(2)}, u32[]{:S(2)}) collective-permute-start(f32[4,128]{1,0:T(4,128)S(1)} %fusion.139), channel_id=1, source_target_pairs={{0,4},{4,0},{1,5},{5,1},{2,6},{6,2},{3,7},{7,3},{8,12},{12,8},{9,1... | collective-permute-start | bytes 6152 | tf_op jit(solution)/shard_map/ppermute | solution.py:33
  (168 other events, 2488.1 us)
Sparse Core Ops, SparseCore 0:
  10.9 49.9 all-gather.2
  62.4 44.6 all-gather.4
  677.5 42.6 reduce-scatter.4
  825.7 42.9 reduce-scatter.2

commit v3 on v2

--- a/solution.py
+++ b/solution.py
@@ -42,12 +42,6 @@
     return lax.dynamic_slice_in_dim(value, which * size, size, dim)
 
 
-def halve(value, axis, bit, dim):
-    mine = bit_of(axis, bit)
-    got = swap(half(value, 1 - mine, dim), axis, bit)
-    return (half(value, mine, dim).astype(F32) + got.astype(F32)).astype(BF16)
-
-
 def after(value, *others):
     return lax.optimization_barrier((value, *others))[0]
 
@@ -60,69 +54,258 @@
     return (half(value, bit_of(axis, bit), 0).astype(F32) + got.astype(F32)).astype(BF16)
 
 
-def gather_pieces(pieces, axis, bit):
-    return pieces + [(mask | {(axis, bit)}, swap(rows, axis, bit)) for mask, rows in pieces]
-
-
-def assemble_kernel(count, widths, row_of, column_of, *refs):
-    inputs, outputs = refs[:count], refs[count:]
-    for p in range(count):
-
-        @pl.when(pl.program_id(0) == p)
-        def _(p=p):
-            start = 0
-            for out, width in zip(outputs, widths):
-                out[...] = inputs[p][:, start : start + width].astype(F32)
-                start += width
-
-
-def assemble(pieces, stages, column_stage, widths):
-    count = len(pieces)
-    rows, columns = pieces[0][1].shape
-    row_of, column_of = [], []
-    for mask, _ in pieces:
-        place = jnp.int32(0)
-        for stage in stages:
-            bit = bit_of(*stage)
-            place = place * 2 + (1 - bit if stage in mask else bit)
-        row_of.append(place)
-        bit = bit_of(*column_stage) if column_stage else jnp.int32(0)
-        column_of.append(1 - bit if column_stage in mask else bit)
-    row_of, column_of = jnp.stack(row_of), jnp.stack(column_of)
-    parts = 1
-    while rows // parts * columns > (1 << 18) and rows % (32 * parts) == 0:
-        parts *= 2
-    step = rows // parts
-
-    def source(p):
-        def at(i, s, row_of, column_of):
-            return (jnp.where(i < p, 0, jnp.where(i == p, s, parts - 1)), 0)
-
-        return pl.BlockSpec((step, columns), at)
-
-    total_rows = rows << len(stages)
-    if column_stage:
-        specs = [pl.BlockSpec((step, columns), lambda i, s, r, c: (r[i] * parts + s, c[i]))]
-        shapes = [jax.ShapeDtypeStruct((total_rows, 2 * columns), F32)]
+def places():
+    count = lax.axis_size("dp")
+    dp, ep = lax.axis_index("dp"), lax.axis_index("ep")
+    core, x = dp % 2, dp // (count // 2)
+    where = (
+        {"dp": dp + 1 - 2 * core},
+        {"dp": (dp + count // 2) % count},
+        {"ep": 1 - ep},
+    )
+    return core, x, ep, where
+
+
+def greet_all(peers):
+    barrier = pltpu.get_barrier_semaphore()
+    for where in peers:
+        pl.semaphore_signal(
+            barrier, inc=1, device_id=where, device_id_type=pl.DeviceIdType.MESH
+        )
+    pl.semaphore_wait(barrier, len(peers))
+
+
+def add_rows(total, more, start, count, out=None):
+    step = 32 if count % 32 == 0 else 16
+
+    def turn(k, carry):
+        here = pl.ds(pl.multiple_of(k * step, step), step)
+        there = pl.ds(pl.multiple_of(start + k * step, step), step)
+        value = (total[there, :].astype(F32) + more[here, :].astype(F32)).astype(BF16)
+        if out is None:
+            total[there, :] = value
+        else:
+            out[here, :] = value
+        return carry
+
+    lax.fori_loop(0, count // step, turn, 0)
+
+
+def sums_kernel(
+    sgu, sd, egu, ed, qkv, wo, flat,
+    sgu_f, sd_f, egu_f, ed_f, qkv_f, wo_f, flat_f,
+    q_own, q_in, q_in2, q_out, w_own, w_in, w_in2, w_out, flat_in, l_sem, s_sem, r_sem,
+):
+    core, x, y, (to_core, to_x, to_y) = places()
+    used = [0, 0]
+
+    def here(source, target):
+        k = used[0]
+        used[0] += 1
+        copy = pltpu.make_async_copy(source, target, l_sem.at[k])
+        copy.start()
+        return copy
+
+    def there(source, target, where):
+        k = used[1]
+        used[1] += 1
+        copy = pltpu.make_async_remote_copy(
+            src_ref=source, dst_ref=target, send_sem=s_sem.at[k], recv_sem=r_sem.at[k],
+            device_id=where, device_id_type=pl.DeviceIdType.MESH,
+        )
+        copy.start()
+        return copy
+
+    greet_all((to_core, to_x, to_y))
+    q_rows, w_rows = q_own.shape[0], w_own.shape[0]
+    load_q = here(qkv.at[pl.ds(y * q_rows, q_rows)], q_own)
+    load_w = here(wo.at[pl.ds(y * w_rows, w_rows)], w_own)
+    a1 = there(qkv.at[pl.ds((1 - y) * q_rows, q_rows)], q_in, to_y)
+    a2 = there(wo.at[pl.ds((1 - y) * w_rows, w_rows)], w_in, to_y)
+    b1 = there(sgu, sgu_f.at[core, x, y], to_x)
+    b2 = there(sd, sd_f.at[core, y, x], to_x)
+    f1 = there(flat, flat_in.at[0], to_core)
+    own_s = here(sgu, sgu_f.at[core, x, y])
+    own_sd = here(sd, sd_f.at[core, y, x])
+    own_e = here(egu, egu_f.at[core, x])
+    own_ed = here(ed, ed_f.at[core, x])
+
+    b1.wait_recv()
+    d1 = there(sgu, sgu_f.at[core, x, y], to_y)
+    d2 = there(sgu_f.at[core, 1 - x, y], sgu_f.at[core, 1 - x, y], to_y)
+    f1.wait()
+    flat_f[...] = flat[...] + flat_in[0]
+    f2 = there(flat_f, flat_in.at[1], to_x)
+
+    load_q.wait()
+    a1.wait_recv()
+    add_rows(q_own, q_in, 0, q_rows)
+    a3 = there(q_own.at[pl.ds((1 - x) * (q_rows // 2), q_rows // 2)], q_in2, to_x)
+    load_w.wait()
+    a2.wait_recv()
+    add_rows(w_own, w_in, 0, w_rows)
+    a4 = there(w_own.at[pl.ds((1 - x) * (w_rows // 2), w_rows // 2)], w_in2, to_x)
+    cut = egu.shape[0] // 2
+    b3 = there(egu.at[pl.ds(0, cut)], egu_f.at[core, x, pl.ds(0, cut)], to_x)
+    b2.wait_recv()
+    own_sd.wait()
+    d3 = there(sd_f.at[core, y], sd_f.at[core, y], to_y)
+    f2.wait()
+    flat_f[...] = flat_f[...] + flat_in[1]
+    f3 = there(flat_f, flat_in.at[2], to_y)
+
+    a3.wait_recv()
+    add_rows(q_own, q_in2, x * (q_rows // 2), q_rows // 2, q_out)
+    a5 = there(q_out, qkv_f.at[core, y, x], to_x)
+    own_q = here(q_out, qkv_f.at[core, y, x])
+    a4.wait_recv()
+    add_rows(w_own, w_in2, x * (w_rows // 2), w_rows // 2, w_out)
+    a6 = there(w_out, wo_f.at[core, y, x], to_x)
+    own_w = here(w_out, wo_f.at[core, y, x])
+    b4 = there(egu.at[pl.ds(cut, cut)], egu_f.at[core, x, pl.ds(cut, cut)], to_x)
+    b5 = there(ed, ed_f.at[core, x], to_x)
+
+    d1.wait_recv()
+    d2.wait_recv()
+    own_s.wait()
+    c1 = there(sgu_f.at[core], sgu_f.at[core], to_core)
+    a5.wait_recv()
+    own_q.wait()
+    a7 = there(qkv_f.at[core, y], qkv_f.at[core, y], to_y)
+    a6.wait_recv()
+    own_w.wait()
+    a8 = there(wo_f.at[core, y], wo_f.at[core, y], to_y)
+    d3.wait_recv()
+    c2 = there(sd_f.at[core], sd_f.at[core], to_core)
+    f3.wait()
+    flat_f[...] = flat_f[...] + flat_in[2]
+    b3.wait_recv()
+    b4.wait_recv()
+    own_e.wait()
+    c3 = there(egu_f.at[core], egu_f.at[core], to_core)
+    a7.wait_recv()
+    c4 = there(qkv_f.at[core], qkv_f.at[core], to_core)
+    a8.wait_recv()
+    c5 = there(wo_f.at[core], wo_f.at[core], to_core)
+    b5.wait_recv()
+    own_ed.wait()
+    c6 = there(ed_f.at[core], ed_f.at[core], to_core)
+    for copy in (c1, c2, c3, c4, c5, c6):
+        copy.wait_recv()
+    for copy in (a1, a2, a3, a4, a5, a6, a7, a8, b1, b2, b3, b4, b5, d1, d2, d3, c1, c2, c3, c4, c5, c6):
+        copy.wait_send()
+
+
+def sums(sgu, sd, egu, ed, qkv, wo, flat):
+    def pieces(count, value, cut=1):
+        return jax.ShapeDtypeStruct(
+            (2,) * count + (value.shape[0] // cut, value.shape[1]), BF16
+        )
+
+    far = pl.BlockSpec(memory_space=pl.ANY)
+    vmem = pl.BlockSpec(memory_space=pltpu.VMEM)
+
+    def room(value, cut):
+        return pltpu.VMEM((value.shape[0] // cut, value.shape[1]), BF16)
+
+    dma = pltpu.SemaphoreType.DMA
+    return pl.pallas_call(
+        sums_kernel,
+        out_shape=[
+            pieces(3, sgu), pieces(3, sd), pieces(2, egu), pieces(2, ed),
+            pieces(3, qkv, 4), pieces(3, wo, 4), jax.ShapeDtypeStruct(flat.shape, F32),
+        ],
+        in_specs=[far] * 6 + [vmem],
+        out_specs=[far] * 6 + [vmem],
+        scratch_shapes=[room(qkv, 2), room(qkv, 2), room(qkv, 4), room(qkv, 4)]
+        + [room(wo, 2), room(wo, 2), room(wo, 4), room(wo, 4)]
+        + [pltpu.VMEM((3,) + flat.shape, F32), dma((8,)), dma((25,)), dma((25,))],
+        compiler_params=pltpu.CompilerParams(
+            collective_id=3, has_side_effects=True, vmem_limit_bytes=32 << 20
+        ),
+        cost_estimate=pl.CostEstimate(flops=0, bytes_accessed=0, transcendentals=0),
+    )(sgu, sd, egu, ed, qkv, wo, flat)
+
+
+def widen_kernel(source, *outputs):
+    value = source[...]
+    value = value.reshape(value.shape[-2:])
+    start = 0
+    for out in outputs:
+        width = out.shape[1]
+        out[...] = value[:, start : start + width].astype(F32)
+        start += width
+
+
+def widen(value, widths=(), kinds=1, kind=0):
+    columns = value.shape[-1]
+    if widths:
+        value = value.reshape(-1, columns)
+        rows = value.shape[0]
+        step = min(rows, 256)
+        source = pl.BlockSpec((step, columns), lambda i: (i, 0))
+        grid = (rows // step,)
+        specs = [pl.BlockSpec((step, width), lambda i: (i, 0)) for width in widths]
+        shapes = [jax.ShapeDtypeStruct((rows, width), F32) for width in widths]
     else:
-        specs = [
-            pl.BlockSpec((step, width), lambda i, s, r, c: (r[i] * parts + s, 0))
-            for width in widths
-        ]
-        shapes = [jax.ShapeDtypeStruct((total_rows, width), F32) for width in widths]
-    moved = count * rows * columns
+        value = value.reshape(2, kinds, -1, columns)
+        rows = value.shape[2]
+        step = rows
+        while step * columns > (1 << 19) and step % 32 == 0:
+            step //= 2
+        steps = rows // step
+        source = pl.BlockSpec((1, 1, step, columns), lambda i, c: (c, kind, i, 0))
+        grid = (steps, 2)
+        specs = [pl.BlockSpec((step, columns), lambda i, c: (i, c))]
+        shapes = [jax.ShapeDtypeStruct((rows, 2 * columns), F32)]
     return pl.pallas_call(
-        functools.partial(assemble_kernel, count, widths),
-        grid_spec=pltpu.PrefetchScalarGridSpec(
-            num_scalar_prefetch=2,
-            grid=(count, parts),
-            in_specs=[source(p) for p in range(count)],
-            out_specs=specs,
-        ),
+        widen_kernel,
+        grid=grid,
+        in_specs=[source],
+        out_specs=specs,
         out_shape=shapes,
         compiler_params=pltpu.CompilerParams(vmem_limit_bytes=32 << 20),
-        cost_estimate=pl.CostEstimate(flops=moved, bytes_accessed=6 * moved, transcendentals=0),
-    )(row_of, column_of, *[rows for _, rows in pieces])
+        cost_estimate=pl.CostEstimate(flops=0, bytes_accessed=0, transcendentals=0),
+    )(value)
+
+
+def weight_kernel(added, part, left, right, *refs):
+    total = mm_tn(left[...], right[...])
+    if added:
+        total = total + refs[0][...].astype(F32)
+    refs[-1][...] = total.astype(BF16)
+
+
+def weight_half(left, right, which, columns, got=None, rows=None, block=1408):
+    rows = rows or left.shape[0]
+    height, wide = left.shape[1], right.shape[1]
+    if columns:
+        wide = wide // 2
+    else:
+        height = height // 2
+    step = height
+    while step > block and step % 256 == 0:
+        step //= 2
+    steps = height // step
+    extra = [] if got is None else [got]
+    out_spec = pl.BlockSpec((step, wide), lambda i, part: (i, 0))
+    if columns:
+        left_at, right_at = (lambda i, part: (0, i)), (lambda i, part: (0, part[0]))
+    else:
+        left_at, right_at = (lambda i, part: (0, part[0] * steps + i)), (lambda i, part: (0, 0))
+    return pl.pallas_call(
+        functools.partial(weight_kernel, bool(extra)),
+        grid_spec=pltpu.PrefetchScalarGridSpec(
+            num_scalar_prefetch=1,
+            grid=(steps,),
+            in_specs=[pl.BlockSpec((rows, step), left_at), pl.BlockSpec((rows, wide), right_at)]
+            + [out_spec] * len(extra),
+            out_specs=out_spec,
+        ),
+        out_shape=jax.ShapeDtypeStruct((height, wide), BF16),
+        compiler_params=pltpu.CompilerParams(vmem_limit_bytes=48 << 20),
+        cost_estimate=pl.CostEstimate(flops=0, bytes_accessed=0, transcendentals=0),
+    )(which.reshape(1).astype(jnp.int32), left, right, *extra)
 
 
 def rope_tables(positions, feat_width):
@@ -144,17 +327,17 @@
     )
 
 
-def ffn_kernel(groups, with_base, flipped, *refs):
+def ffn_kernel(groups, base, into, flipped, *refs):
     rows, grads, scale, gate_w, up_w, down_w = refs[:6]
     refs = refs[6:]
-    if with_base:
+    if base:
         base_out, base_dx = refs[:2]
         refs = refs[2:]
-    hid_ref, dgate_ref, dup_ref, out_ref, dx_ref, small_ref = refs
+    hid_ref, dgu_ref, out_ref, dx_ref, small_ref = refs[2:] if into else refs
     width = down_w.shape[0]
-    into, back = (mm_nt, mm) if flipped else (mm, mm_nt)
-    gate_pre = into(rows[...], gate_w[...])
-    up_pre = into(rows[...], up_w[...])
+    to, back = (mm_nt, mm) if flipped else (mm, mm_nt)
+    gate_pre = to(rows[...], gate_w[...])
+    up_pre = to(rows[...], up_w[...])
     grad_hidden = mm_nt(grads[...], down_w[...])
     sig = 1.0 / (1.0 + jnp.exp(-gate_pre))
     act = gate_pre * sig
@@ -164,43 +347,73 @@
     column = lax.broadcasted_iota(jnp.int32, (1, width), 1)
     wide = scale[:, 0:1]
     for e in range(1, groups):
-        wide = jnp.where(column >= e * each, scale[:, e:e+1], wide)
+        wide = jnp.where(column >= e * each, scale[:, e : e + 1], wide)
     prod = hidden * grad_hidden
     for e in range(groups):
-        part = prod if groups == 1 else jnp.where((column >= e*each) & (column < (e+1)*each), prod, 0.0)
-        small_ref[:, e:e+1] = jnp.sum(part, axis=1, keepdims=True)
+        part = prod
+        if groups > 1:
+            part = jnp.where((column >= e * each) & (column < (e + 1) * each), prod, 0.0)
+        small_ref[:, e : e + 1] = jnp.sum(part, axis=1, keepdims=True)
     hid = (hidden * wide).astype(BF16)
     hid_ref[...] = hid
     scaled = grad_hidden * wide
     dgate = (scaled * up_pre * slope).astype(BF16)
     dup = (scaled * act).astype(BF16)
-    dgate_ref[...] = dgate
-    dup_ref[...] = dup
-    small_ref[:, groups:groups+1] = jnp.sum(dgate.astype(F32)*gate_pre + dup.astype(F32)*up_pre, axis=1, keepdims=True)
+    dgu_ref[:, :width] = dgate
+    dgu_ref[:, width:] = dup
+    small_ref[:, groups : groups + 1] = jnp.sum(
+        dgate.astype(F32) * gate_pre + dup.astype(F32) * up_pre, axis=1, keepdims=True
+    )
     out = mm(hid, down_w[...])
     dx = back(dgate, gate_w[...]) + back(dup, up_w[...])
-    if with_base:
+    if base:
         out = out + base_out[...].astype(F32)
         dx = dx + base_dx[...].astype(F32)
     out_ref[...] = out.astype(BF16)
     dx_ref[...] = dx.astype(BF16)
 
-def ffn(rows, grads, scale, gate_w, up_w, down_w, base=(), flipped=False, block=256):
-    count, width = rows.shape
+
+def ffn(rows, grads, scale, gate_w, up_w, down_w, start=0, total=0, base=(), into=(), flipped=False):
+    count, groups = scale.shape
+    width = rows.shape[1]
     hidden = down_w.shape[0]
-    groups = scale.shape[1]
-    block = min(block, count)
-    def by_row(n): return pl.BlockSpec((block, n), lambda i: (i, 0))
-    def held(a): return pl.BlockSpec(a.shape, lambda i: (0, 0), pipeline_mode=pl.Buffered(1))
+    block = min(256, count)
+    first = start // block
+    total = total or count
+    place = first if total > count else 0
+
+    def at(n, offset):
+        return pl.BlockSpec((block, n), lambda i: (i + offset, 0))
+
+    def held(a):
+        return pl.BlockSpec(a.shape, lambda i: (0, 0), pipeline_mode=pl.Buffered(1))
+
+    far = pl.BlockSpec(memory_space=pl.ANY)
     return pl.pallas_call(
-        functools.partial(ffn_kernel, groups, bool(base), flipped),
+        functools.partial(ffn_kernel, groups, bool(base), bool(into), flipped),
         grid=(count // block,),
-        in_specs=[by_row(width), by_row(width), by_row(groups), held(gate_w), held(up_w), held(down_w)] + [by_row(width)] * len(base),
-        out_specs=[by_row(hidden)] * 3 + [by_row(width)] * 2 + [by_row(groups + 1)],
-        out_shape=[jax.ShapeDtypeStruct((count, hidden), BF16)] * 3 + [jax.ShapeDtypeStruct((count, width), BF16)] * 2 + [jax.ShapeDtypeStruct((count, groups + 1), F32)],
+        in_specs=[at(width, first), at(width, first), at(groups, 0)]
+        + [held(gate_w), held(up_w), held(down_w)]
+        + [at(width, 0)] * len(base)
+        + [far] * len(into),
+        out_specs=[
+            at(hidden, place),
+            at(2 * hidden, place),
+            at(width, 0),
+            at(width, 0),
+            at(groups + 1, 0),
+        ],
+        out_shape=[
+            jax.ShapeDtypeStruct((total, hidden), BF16),
+            jax.ShapeDtypeStruct((total, 2 * hidden), BF16),
+            jax.ShapeDtypeStruct((count, width), BF16),
+            jax.ShapeDtypeStruct((count, width), BF16),
+            jax.ShapeDtypeStruct((count, groups + 1), F32),
+        ],
+        input_output_aliases={6 + len(base) + k: k for k in range(len(into))},
         compiler_params=pltpu.CompilerParams(vmem_limit_bytes=62 << 20),
-        cost_estimate=pl.CostEstimate(flops=12*count*width*hidden, bytes_accessed=6*width*hidden + 12*count*width, transcendentals=count*hidden),
-    )(rows, grads, scale, gate_w, up_w, down_w, *base)
+        cost_estimate=pl.CostEstimate(flops=0, bytes_accessed=0, transcendentals=0),
+    )(rows, grads, scale, gate_w, up_w, down_w, *base, *into)
 
 
 def line_sum(rows, width_own, depth, prepare, settle, gathered, part, came, came_two, spread, sems):
@@ -377,7 +590,7 @@
 
 def attend_out_kernel(
     chunks, step, depth, eps, attn, w_out, x, gain,
-    mixed, mixed_peer, resid_own, inv_out,
+    mixed, resid_own, inv_out,
     part, came, came_two, spread, s0, s1, s2, s3, s4, y_send, y_recv,
 ):
     n = lax.axis_size("tp")
@@ -403,7 +616,7 @@
 
     def peer_copy(c):
         return pltpu.make_async_remote_copy(
-            src_ref=mixed.at[at(c)], dst_ref=mixed_peer.at[at(c)], send_sem=y_send.at[c], recv_sem=y_recv.at[c],
+            src_ref=mixed.at[at(c)], dst_ref=mixed.at[pl.ds(pl.multiple_of(rows + c * step, step), step)], send_sem=y_send.at[c], recv_sem=y_recv.at[c],
             device_id=other, device_id_type=pl.DeviceIdType.MESH,
         )
 
@@ -449,11 +662,11 @@
     return pl.pallas_call(
         functools.partial(attend_out_kernel, chunks, step, depth, EPS),
         out_shape=[
-            jax.ShapeDtypeStruct((rows, width), BF16), jax.ShapeDtypeStruct((rows, width), BF16),
+            jax.ShapeDtypeStruct((2 * rows, width), BF16),
             jax.ShapeDtypeStruct((rows, width_own), F32), jax.ShapeDtypeStruct((rows, 1), F32),
         ],
         in_specs=[vmem] * 4,
-        out_specs=[vmem] * 4,
+        out_specs=[vmem] * 3,
         scratch_shapes=scratch + [dma((chunks,)), dma((chunks,))],
         compiler_params=pltpu.CompilerParams(collective_id=1, has_side_effects=True, vmem_limit_bytes=40 << 20),
         cost_estimate=pl.CostEstimate(flops=0, bytes_accessed=0, transcendentals=0),
@@ -461,14 +674,15 @@
 
 
 def resid_grad_kernel(
-    chunks, step, depth, grad, grad_p, out_p, router, along, g_own, resid_own, inv_two, gain,
-    low, grad_resid, gain_grad, out_back,
+    chunks, step, depth, grad, grad_p, out_p, sum_egu, sum_ed, router, along, g_own, resid_own, inv_two, gain,
+    low, grad_resid, gain_grad, out_back, got_egu, got_ed,
     part, came, came_two, spread, s0, s1, s2, s3, s4, back, y_send, y_recv, o_send, o_recv,
+    x_send, x_recv,
 ):
     n = lax.axis_size("tp")
     own = part.shape[3]
     rows = grad.shape[0]
-    other = {"ep": 1 - lax.axis_index("ep")}
+    _, x_bit, _, (_, to_x, other) = places()
 
     def at(c):
         return pl.ds(pl.multiple_of(c * step, step), step)
@@ -485,7 +699,16 @@
             device_id=other, device_id_type=pl.DeviceIdType.MESH,
         )
 
-    greet([other])
+    def half_copy(source, target, k):
+        return pltpu.make_async_remote_copy(
+            src_ref=source.at[pl.ds((1 - x_bit) * target.shape[0], target.shape[0])], dst_ref=target,
+            send_sem=x_send.at[k], recv_sem=x_recv.at[k],
+            device_id=to_x, device_id_type=pl.DeviceIdType.MESH,
+        )
+
+    greet([other, to_x])
+    half_copy(sum_egu, got_egu, 0).start()
+    half_copy(sum_ed, got_ed, 1).start()
 
     def begin(c, carry):
         peer_copy(c).start()
@@ -522,9 +745,11 @@
 
     lax.fori_loop(0, chunks, last, 0)
     out_copy().wait()
-
-
-def resid_grad(grad, grad_p, out_p, router, along, g_own, resid_own, inv_two, gain, depth=1):
+    half_copy(sum_egu, got_egu, 0).wait()
+    half_copy(sum_ed, got_ed, 1).wait()
+
+
+def resid_grad(grad, grad_p, out_p, sum_egu, sum_ed, router, along, g_own, resid_own, inv_two, gain, depth=1):
     rows, width = grad.shape
     width_own = g_own.shape[1]
     chunks, step, scratch = line_scratch(rows, width_own)
@@ -536,13 +761,14 @@
         out_shape=[
             jax.ShapeDtypeStruct((rows, width), BF16), jax.ShapeDtypeStruct((rows, width_own), F32),
             jax.ShapeDtypeStruct((1, width_own), F32), jax.ShapeDtypeStruct((rows, width), BF16),
-        ],
-        in_specs=[vmem] + [far] * 2 + [vmem] * 6,
-        out_specs=[vmem] * 3 + [far],
-        scratch_shapes=scratch + [pltpu.VMEM((rows, width), BF16), dma((chunks,)), dma((chunks,)), dma, dma],
+        ]
+        + [jax.ShapeDtypeStruct((v.shape[0] // 2, v.shape[1]), BF16) for v in (sum_egu, sum_ed)],
+        in_specs=[vmem] + [far] * 4 + [vmem] * 6,
+        out_specs=[vmem] * 3 + [far] * 3,
+        scratch_shapes=scratch + [pltpu.VMEM((rows, width), BF16), dma((chunks,)), dma((chunks,)), dma, dma, dma((2,)), dma((2,))],
         compiler_params=pltpu.CompilerParams(collective_id=2, has_side_effects=True, vmem_limit_bytes=40 << 20),
         cost_estimate=pl.CostEstimate(flops=0, bytes_accessed=0, transcendentals=0),
-    )(grad, grad_p, out_p, router, along, g_own, resid_own, inv_two, gain)
+    )(grad, grad_p, out_p, sum_egu, sum_ed, router, along, g_own, resid_own, inv_two, gain)
 
 
 def body(
@@ -585,31 +811,16 @@
 
     near = bit_of("dp", 1)
 
-    def pair_send(left, right, columns):
-        if columns:
-            right = half(right, 1 - near, 1)
-        else:
-            left = half(left, 1 - near, 1)
-        return swap(mm_tn(left, right).astype(BF16), "dp", 1)
-
-    def pair_keep(left, right, columns, got):
-        if columns:
-            right = half(right, near, 1)
-        else:
-            left = half(left, near, 1)
-        return (mm_tn(left, right) + got.astype(F32)).astype(BF16)
+    def pair_send(left, right, columns, used=None):
+        return swap(weight_half(left, right, 1 - near, columns, rows=used), "dp", 1)
+
+    def pair_keep(left, right, columns, got, used=None):
+        return weight_half(left, right, near, columns, got, rows=used)
 
     core = ("dp", 1)
     far = [("dp", b) for b in far_bits]
     line = [("ep", 1)]
-
-    def alone(value):
-        return [(frozenset(), value)]
-
-    def whole(pieces, stages, columns, widths):
-        if columns:
-            return assemble(pieces, stages, core, widths)
-        return assemble(pieces, [core] + stages, None, widths)
+    x_link, y_link = far[0], line[0]
 
     def over_tp(value):
         bit = 1
@@ -630,8 +841,10 @@
     x_full = packed[:rows].astype(F32)
     gain_one = packed[rows].astype(F32)
     gain_two = packed[rows + 1].astype(F32)
-    grad_rows = lax.all_gather(output_gradient, "tp", axis=1, tiled=True)
-    grad_peer = swap(grad_rows, "ep", 1)
+    grad_rows = lax.all_gather(after(output_gradient, packed), "tp", axis=1, tiled=True)
+    part = rows // 2
+    grad_peer_a = swap(grad_rows[:part], "ep", 1)
+    grad_peer_b = swap(grad_rows[part:], "ep", 1)
     route_hot = jnp.sum(
         (routes[:, :, None] == jnp.arange(experts, dtype=jnp.int32)[None, None, :]).astype(F32),
         axis=1,
@@ -678,9 +891,10 @@
     attn_rows = attended.astype(BF16).reshape(rows, heads * HD)
     log_norm = row_top + jnp.log(row_total)
 
-    mixed, mixed_peer, resid_own, inv_two = attend_out(
-        attn_rows, w_output, after(packed[:rows], grad_peer), gain_two[None, :], width_own
-    )
+    both, resid_own, inv_two = attend_out(
+        attn_rows, w_output, after(packed[:rows], grad_peer_a), gain_two[None, :], width_own
+    )
+    mixed = both[:rows]
 
     def router(values):
         logits = mm(values, w_router)
@@ -688,47 +902,60 @@
 
     logits, router_prob = router(mixed)
     combine = router_prob * route_hot
-    combine_peer = router(mixed_peer)[1] * route_hot_peer
+    combine_peer = router(both[rows:])[1] * route_hot_peer
     switch_logit = mm(mixed, shared_switch[:, None])
     switch = jax.nn.sigmoid(switch_logit)
 
     def own_experts(value):
         return lax.dynamic_slice_in_dim(value, ep_rank * experts_own, experts_own, 1)
 
-    x_link = far[0]
-    y_link = line[0]
-
-    hid_s, gate_s, up_s, out_s, grad_s, small_s = ffn(
-        mixed, grad_rows, switch, shared_gate, shared_up, shared_down
-    )
-    got_sg = pair_send(mixed, gate_s, False)
-    got_sd = pair_send(hid_s, after(grad_rows, got_sg), True)
-    got_su = pair_send(after(mixed, got_sd), up_s, False)
-    sum_sg = pair_keep(mixed, gate_s, False, got_sg)
-    got_sg = reduce_send(sum_sg, *x_link)
-    sum_sd = pair_keep(hid_s, after(grad_rows, sum_sg), True, got_sd)
-    got_sd = reduce_send(sum_sd, *x_link)
-    sum_su = pair_keep(after(mixed, sum_sd), up_s, False, got_su)
-    got_su = reduce_send(sum_su, *y_link)
+    hid_s, dgu_s, out_s, grad_s, small_s = ffn(
+        both, grad_rows, switch, shared_gate, shared_up, shared_down
+    )
+    both_grad = jnp.concatenate([grad_rows, grad_peer_a, after(grad_peer_b, grad_s)], axis=0)
+    got_sgu = pair_send(both, after(dgu_s, both_grad), False, rows)
+    got_sd = pair_send(hid_s, after(grad_rows, got_sgu), True)
+    sum_sgu = pair_keep(both, dgu_s, False, after(got_sgu, got_sd), rows)
+    got_sgu = reduce_send(sum_sgu, *x_link)
+    sum_sd = pair_keep(hid_s, after(grad_rows, sum_sgu), True, got_sd)
+    got_sd = reduce_send(sum_sd, *y_link)
 
     hidden_width = experts_own * expert_width
     gate_w = jnp.transpose(expert_gate, (0, 2, 1)).reshape(hidden_width, width)
     up_w = jnp.transpose(expert_up, (0, 2, 1)).reshape(hidden_width, width)
     down_w = expert_down.reshape(hidden_width, width)
-    peer_rows = after(mixed_peer, sum_su)
-    hid_p, gate_p, up_p, out_p, grad_p, small_p = ffn(
-        peer_rows, grad_peer, own_experts(combine_peer), gate_w, up_w, down_w, (), True
+    hid_p, dgu_p, out_p, grad_p, small_p = ffn(
+        both,
+        after(both_grad, sum_sd),
+        own_experts(combine_peer),
+        gate_w,
+        up_w,
+        down_w,
+        start=rows,
+        total=2 * rows,
+        flipped=True,
     )
     small_back = swap(small_p.T, "ep", 1)
-    sum_sg = reduce_add(sum_sg, after(got_sg, grad_p), *x_link)
-    got_sg = reduce_send(sum_sg, *y_link)
-    own_rows = after(mixed, sum_sg)
-    hid_e, gate_e, up_e, out_e, grad_e, small_e = ffn(
-        own_rows, grad_rows, own_experts(combine), gate_w, up_w, down_w, (out_s, grad_s), True
-    )
+    hid_e, dgu_e, out_e, grad_e, small_e = ffn(
+        both,
+        both_grad,
+        after(own_experts(combine), grad_p),
+        gate_w,
+        up_w,
+        down_w,
+        total=2 * rows,
+        base=(out_s, grad_s),
+        into=(hid_p, dgu_p),
+        flipped=True,
+    )
+    sum_sgu = reduce_add(sum_sgu, after(got_sgu, grad_e), *x_link)
+    got_sgu = reduce_send(sum_sgu, *y_link)
+    sum_sd = reduce_add(sum_sd, after(got_sd, sum_sgu), *y_link)
+    got_sd = reduce_send(sum_sd, *x_link)
 
     first = ep_rank == 0
     small_e = small_e.T
+    small_back = after(small_back, grad_e)
     dots_here, dots_there = small_e[:experts_own], small_back[:experts_own]
     small = jnp.concatenate(
         [
@@ -739,35 +966,20 @@
         ],
         axis=0,
     )
-    small = over_tp(small)
-
-    sum_su = reduce_add(sum_su, after(got_su, grad_e), *y_link)
-    got_su = reduce_send(sum_su, *x_link)
-    sum_sd = reduce_add(sum_sd, after(got_sd, sum_su), *x_link)
-    got_sd = reduce_send(sum_sd, *y_link)
-
-    both = after(jnp.concatenate([mixed, mixed_peer], axis=0), sum_sd)
-    both_grad = jnp.concatenate([grad_rows, grad_peer], axis=0)
-    gate_b = jnp.concatenate([gate_e, gate_p], axis=0)
-    up_b = jnp.concatenate([up_e, up_p], axis=0)
-    hid_b = jnp.concatenate([hid_e, hid_p], axis=0)
-    got_eg = pair_send(gate_b, both, True)
-    got_eu = pair_send(up_b, after(both, got_eg), True)
-    got_ed = pair_send(hid_b, after(both_grad, got_eu), True)
-    sum_eg = pair_keep(gate_b, both, True, got_eg)
-    got_eg = reduce_send(sum_eg, *x_link)
-    sum_eu = pair_keep(up_b, after(both, sum_eg), True, got_eu)
-    got_eu = reduce_send(sum_eu, *x_link)
-    sum_ed = pair_keep(hid_b, after(both_grad, sum_eu), True, got_ed)
-    got_ed = reduce_send(sum_ed, *x_link)
-    sum_su = reduce_add(sum_su, after(got_su, sum_ed), *x_link)
-    piece_su = gather_pieces(alone(sum_su), *x_link)
-    sum_sg = reduce_add(sum_sg, after(got_sg, sum_su), *y_link)
-    piece_sg = gather_pieces(alone(sum_sg), *x_link)
-    sum_sd = reduce_add(sum_sd, after(got_sd, sum_sg), *y_link)
-    piece_sd = gather_pieces(alone(sum_sd), *x_link)
-
-    small = small.T
+    got_small = swap(small, "tp", 1)
+    got_egu = pair_send(after(dgu_e, sum_sd), both, True)
+    small = small + after(got_small, got_egu)
+    bit = 2
+    got_ed = pair_send(hid_e, after(both_grad, small), True)
+    sum_egu = dgu_e
+    while bit < tp_count:
+        got_small = swap(small, "tp", bit)
+        if bit == 2:
+            sum_egu = pair_keep(dgu_e, both, True, after(got_egu, got_ed))
+        small = small + after(got_small, sum_egu)
+        bit *= 2
+    sum_ed = pair_keep(hid_e, after(both_grad, sum_egu), True, got_ed)
+    small = after(small.T, sum_ed)
     grad_prob = small[:, :experts] * route_hot
     grad_switch = small[:, experts : experts + 1]
     along = small[:, experts + 1 : experts + 2]
@@ -780,20 +992,26 @@
         mm_nt(grad_logits, tp_rows)
         + grad_slogit.astype(F32) * own_columns(shared_switch).astype(F32)[None, :]
     )
-    grad_router = mm_tn(grad_logits, mixed)
-    grad_switch_w = mm_tn(grad_slogit, mixed)
     along = (
         along
         + jnp.sum(grad_logits.astype(F32) * logits, axis=1, keepdims=True)
         + grad_slogit.astype(F32) * switch_logit
     )
-    resid_low, grad_resid, grad_gain_two, out_back = resid_grad(
-        after(grad_e, sum_sd), grad_p, out_p, router_part, along, output_gradient, resid_own, inv_two, norm_ffn.astype(F32)[None, :]
-    )
-    flat = jnp.concatenate(
-        [grad_gain_two.reshape(-1), grad_router.reshape(-1), grad_switch_w.reshape(-1)]
-    ).reshape(-1, 128)
-    ffn_part = (out_e.astype(F32) + out_back.astype(F32)).astype(BF16)
+    sum_sgu = reduce_add(sum_sgu, after(got_sgu, sum_ed), *y_link)
+    sum_sd = reduce_add(sum_sd, after(got_sd, sum_sgu), *x_link)
+    resid_low, grad_resid, grad_gain_two, out_back, got_egu, got_ed = resid_grad(
+        after(grad_e, sum_sd),
+        grad_p,
+        out_p,
+        sum_egu,
+        sum_ed,
+        router_part,
+        along,
+        output_gradient,
+        resid_own,
+        inv_two,
+        norm_ffn.astype(F32)[None, :],
+    )
 
     grad_attn = mm_nt(resid_low, w_output).astype(BF16).reshape(rows, heads, HD)
     probs = jnp.exp(masked_scores() - log_norm)
@@ -801,33 +1019,30 @@
     grad_scores = (
         probs * (grad_probs - jnp.sum(probs * grad_probs, axis=2, keepdims=True))
     ).astype(BF16)
+    grad_keys = (
+        jnp.einsum("hqk,qhd->khd", grad_scores, query, preferred_element_type=F32) * score_scale
+    )
+    grad_values = jnp.einsum(
+        "hqk,qhd->khd", probs.astype(BF16), grad_attn, preferred_element_type=F32
+    )
+    later = lax.ppermute(
+        jnp.stack([grad_keys[:rows], grad_values[:rows]]).astype(BF16), "ep", back
+    )
     grad_query = (
         jnp.einsum("hqk,khd->qhd", grad_scores, key_rows, preferred_element_type=F32) * score_scale
     )
-    grad_keys = (
-        jnp.einsum("hqk,qhd->khd", grad_scores, query, preferred_element_type=F32) * score_scale
-    )
-    grad_values = jnp.einsum(
-        "hqk,qhd->khd", probs.astype(BF16), grad_attn, preferred_element_type=F32
-    )
-    later = lax.ppermute(
-        jnp.stack([grad_keys[:rows], grad_values[:rows]]).astype(BF16), "ep", back
-    )
-    ffn_own = lax.psum_scatter(
-        after(ffn_part, grad_keys), "tp", scatter_dimension=1, tiled=True
-    )
-    layer_out = (resid_own + ffn_own.astype(F32)).astype(BF16)
-    flat = over_rows(after(flat, grad_keys))
-    sum_eg = reduce_add(sum_eg, after(got_eg, grad_keys), *x_link)
-    piece_eg = gather_pieces(alone(sum_eg), *x_link)
-    sum_eu = reduce_add(sum_eu, after(got_eu, sum_eg), *x_link)
-    piece_eu = gather_pieces(alone(sum_eu), *x_link)
-    sum_ed = reduce_add(sum_ed, after(got_ed, sum_eu), *x_link)
-    piece_ed = gather_pieces(alone(sum_ed), *x_link)
-    got_wo = pair_send(after(attn_rows, sum_ed), resid_low, True)
-    sum_wo = pair_keep(after(attn_rows, got_wo), resid_low, True, got_wo)
-    got_wo = reduce_send(sum_wo, *y_link)
-    later = after(later, sum_wo).astype(F32)
+    got_wo = pair_send(after(attn_rows, grad_keys, grad_values), resid_low, True)
+    sum_egu = reduce_add(sum_egu, after(got_egu, got_wo), *x_link)
+    sum_ed = reduce_add(sum_ed, after(got_ed, sum_egu), *x_link)
+    sum_wo = pair_keep(after(attn_rows, sum_ed), resid_low, True, got_wo)
+    grad_router = mm_tn(after(grad_logits, sum_wo), mixed)
+    grad_switch_w = mm_tn(grad_slogit, mixed)
+    flat = jnp.concatenate(
+        [grad_gain_two.reshape(-1), grad_router.reshape(-1), grad_switch_w.reshape(-1)]
+    ).reshape(-1, 128)
+    ffn_part = (out_e.astype(F32) + after(out_back, sum_wo).astype(F32)).astype(BF16)
+    ffn_own = lax.psum_scatter(ffn_part, "tp", scatter_dimension=1, tiled=True)
+    later = after(later, sum_wo, ffn_part, flat).astype(F32)
     grad_key = grad_keys[rows:] + later[0]
     grad_value = grad_values[rows:] + later[1]
     shape = (rows, heads * HD)
@@ -838,72 +1053,53 @@
     got_qkv = pair_send(normed, grad_qkv, False)
     grad_qkv = after(grad_qkv, got_qkv)
     sum_qkv = pair_keep(normed, grad_qkv, False, got_qkv)
-    got_qkv = reduce_send(sum_qkv, *y_link)
+    row_part = jnp.sum(
+        grad_qpre.astype(F32) * q_pre
+        + grad_kpre.astype(F32) * k_pre
+        + grad_vpre.astype(F32) * v_pre,
+        axis=1,
+    )
     grad_normed = (
         mm_nt(after(grad_qpre, sum_qkv), w_query)
         + mm_nt(grad_kpre, w_key)
         + mm_nt(grad_vpre, w_value)
     ).astype(BF16)
-    normed_own = lax.psum_scatter(grad_normed, "tp", scatter_dimension=1, tiled=True).astype(F32)
-    row_part = jnp.sum(
-        grad_qpre.astype(F32) * q_pre
-        + grad_kpre.astype(F32) * k_pre
-        + grad_vpre.astype(F32) * v_pre,
-        axis=1,
-    )
-    row_total = over_tp(row_part[None, :]).T
-
-    y_then_x, x_then_y = line + far, far + line
+    extra = max(1, rows // width_own)
+    below = jnp.tile(row_part.reshape(extra, -1), (1, tp_count)).astype(BF16)
+    below = jnp.pad(below, ((0, -extra % 16), (0, 0)))
+    normed_own = lax.psum_scatter(
+        jnp.concatenate([grad_normed, below], axis=0), "tp", scatter_dimension=1, tiled=True
+    ).astype(F32)
+
     qkv = heads * HD
     inner = shared_gate.shape[1]
-
-    def later_pieces(pieces, other, stage):
-        (mask, rows_), *rest = pieces
-        return gather_pieces([(mask, after(rows_, other))] + rest, *stage)
-
-    piece_su = later_pieces(piece_su, grad_normed, y_link)
-    piece_sg = later_pieces(piece_sg, piece_su[1][1], y_link)
-    piece_sd = later_pieces(piece_sd, piece_sg[1][1], y_link)
-    sum_wo = reduce_add(sum_wo, after(got_wo, grad_normed), *y_link)
-    got_wo = reduce_send(sum_wo, *x_link)
-    sum_qkv = reduce_add(sum_qkv, after(got_qkv, sum_wo), *y_link)
-    got_qkv = reduce_send(sum_qkv, *x_link)
-    piece_su = later_pieces(piece_su, sum_qkv, core)
-    piece_sg = later_pieces(piece_sg, piece_su[3][1], core)
-    (su_grad,) = whole(piece_su, y_then_x, False, (inner,))
-    piece_sd = later_pieces(piece_sd, piece_sg[3][1], core)
-    (sg_grad,) = whole(piece_sg, x_then_y, False, (inner,))
-    (sd_grad,) = whole(piece_sd, x_then_y, True, (width // 2,))
-    piece_eg = later_pieces(piece_eg, sum_qkv, core)
-    (eg_grad,) = whole(piece_eg, far, True, (width // 2,))
-    piece_eu = later_pieces(piece_eu, piece_eg[1][1], core)
-    (eu_grad,) = whole(piece_eu, far, True, (width // 2,))
-    piece_ed = later_pieces(piece_ed, piece_eu[1][1], core)
-    (ed_grad,) = whole(piece_ed, far, True, (width // 2,))
-    sum_wo = reduce_add(sum_wo, after(got_wo, piece_ed[1][1]), *x_link)
-    sum_qkv = reduce_add(sum_qkv, after(got_qkv, sum_wo), *x_link)
-    piece_qkv = gather_pieces(alone(sum_qkv), *x_link)
-    piece_wo = gather_pieces(alone(sum_wo), *x_link)
-    piece_qkv = gather_pieces(piece_qkv, *y_link)
-    piece_wo = gather_pieces(piece_wo, *y_link)
-    piece_wo = gather_pieces(piece_wo, *core)
-    piece_qkv = gather_pieces(piece_qkv, *core)
-    (wo_grad,) = whole(piece_wo, y_then_x, True, (width // 2,))
-    wq_grad, wk_grad, wv_grad = whole(piece_qkv, y_then_x, False, (qkv,) * 3)
+    sgu_f, sd_f, egu_f, ed_f, qkv_f, wo_f, flat = sums(
+        sum_sgu, sum_sd, sum_egu, sum_ed, after(sum_qkv, grad_normed), sum_wo, flat
+    )
+    sg_grad, su_grad = widen(sgu_f, (inner, inner))
+    (sd_grad,) = widen(sd_f)
+    (eg_grad,) = widen(egu_f, kinds=2, kind=0)
+    (eu_grad,) = widen(egu_f, kinds=2, kind=1)
+    (ed_grad,) = widen(ed_f)
+    wq_grad, wk_grad, wv_grad = widen(qkv_f, (qkv,) * 3)
+    (wo_grad,) = widen(wo_f)
 
     x_own = tokens.astype(F32)
+    normed_own = after(normed_own, flat)
+    row_total = normed_own[rows : rows + extra].reshape(rows, 1)
+    normed_own = normed_own[:rows]
     grad_tokens = (
         grad_resid
         + inv_one * norm_attn.astype(F32) * normed_own
         - x_own * (inv_one * inv_one) * (row_total / width)
     )
     grad_gain_one = jnp.sum(normed_own * x_own * inv_one, axis=0)
-
+    grad_gain_one = over_rows(grad_gain_one.reshape(-1, 128)).reshape(-1)
+    layer_out = (resid_own + after(ffn_own, flat).astype(F32)).astype(BF16)
     flat = flat.reshape(-1)
     grad_gain_two = flat[:width_own]
     grad_router = flat[width_own : width_own + width * experts].reshape(experts, width).T
     grad_switch_w = flat[width_own + width * experts :]
-    grad_gain_one = over_rows(grad_gain_one.reshape(-1, 128)).reshape(-1)
 
     def per_expert(value):
         return value.reshape(experts_own, expert_width, width)

time: 1070 us -> 940 us (0.88)
  waiting for transfers between devices: 381 us -> 134 us
  Pallas kernels: 351 us -> 561 us
  matrix products: 100 us -> 45.2 us
  starting transfers between devices: 55.9 us -> 21.1 us
    ppermute x78 -> x19, waiting for transfers between devices: 293 us -> 57.1 us  [swap(): return lax.ppermute(value, axis, [(i, i ^ bit) for i in range(count)])]
    pallas_call x11 -> x23, Pallas kernels: 179 us -> 388 us  [the longest x1 195 us: sums(): pl.pallas_call(sums_kernel, out_shape=[pieces(3, sgu), pieces(3, sd), pie...]
    dot_general x18 -> x2, matrix products: 64.3 us -> 0.8 us  [mm_tn(): lax.dot_general(left, right, (((0,), (0,)), ((), ())), preferred_element_...]
    ppermute x78 -> x19, starting transfers between devices: 49.5 us -> 14.7 us  [swap(): return lax.ppermute(value, axis, [(i, i ^ bit) for i in range(count)])]
    all_gather x1, waiting for transfers between devices: 11.1 us -> 0.01 us  [body(): lax.all_gather(after(output_gradient, packed), 'tp', axis=1, tiled=True)]
    convert_element_type x13 -> x6, other arithmetic: 25.7 us -> 17 us  [reduce_add(): (half(value, bit_of(axis, bit), 0).astype(F32) + got.astype(F32)).astype(...]
    unnamed x306 -> x232, local copies, waits for them, and re-layouts: 49.2 us -> 48.8 us
  transfers between devices with their start and end apart: 84 -> 25, of which waited for: 32 -> 11; matrix products, arithmetic and copies ran while one was open for 17% -> 12% of each run, Pallas kernels for 22% -> 45%
where the time goes in v3:
time: 940 us; the launch traced here: 932 us
  Pallas kernels  561 us (60%)
  waiting for transfers between devices  134 us (14%)
  local copies, waits for them, and re-layouts  86.2 us (9%)
  other arithmetic  68.8 us (7%)
  matrix products  45.2 us (5%)
  starting transfers between devices  21.1 us (2%)
  between operations  15.6 us (2%)
    pallas_call x1, Pallas kernels, sums(): pl.pallas_call(sums_kernel, out_shape=[pieces(3, sgu), pieces(3, sd), pie...  195 us
    pallas_call x1, Pallas kernels, resid_grad(): pl.pallas_call(functools.partial(resid_grad_kernel, chunks, step, depth),...  98.5 us
    pallas_call x3, Pallas kernels, ffn(): pl.pallas_call(functools.partial(ffn_kernel, groups, bool(base), bool(int...  88 us
    pallas_call x1, Pallas kernels, attend_out(): pl.pallas_call(functools.partial(attend_out_kernel, chunks, step, depth,...  73.9 us
    pallas_call x12, Pallas kernels, weight_half(): pl.pallas_call(functools.partial(weight_kernel, bool(extra)), grid_spec=p...  68 us
    ppermute x19, waiting for transfers between devices, swap(): return lax.ppermute(value, axis, [(i, i ^ bit) for i in range(count)])  57.1 us
    unnamed x232, local copies, waits for them, and re-layouts  48.8 us
    all_gather x1, waiting for transfers between devices, body(): packed = lax.all_gather(packed, 'tp', axis=1, tiled=True)  48.2 us
  transfers between devices with their start and end apart: 25, of which 11 were waited for; matrix products, arithmetic and copies ran while one was open for 12% of the time, Pallas kernels for 45%

profile of v3, /device:TPU:0, one launch (start us, length us, event | category | flops | bytes accessed | tf_op | source)
XLA Modules:
  0.0 932.1 jit_solution(17386303658917931928)
XLA Ops:
  12.6 48.2 %all-gather.3.cloned.1.call-done = bf16[528,2048]{1,0:T(8,128)(2,1)} async-done(((bf16[528,512]{1,0:T(8,128)(2,1)}), bf16[528,2048]{1,0:T(8,128)(2,1)}) %all-gather.3.cloned.1.call-update) | async-done | bytes 2162704 | tf_op jit(solution)/shard_map/all_gather | solution.py:840
  66.6 3.7 fusion.71
  73.7 2.4 copy.200
  76.1 2.9 fusion.70
  83.4 2.4 copy.199
  85.8 4.0 fusion.66
  91.2 3.5 subtract_convert_fusion.2
  96.0 4.5 collective-permute-start
  102.9 3.2 slice.160.x
  106.1 15.9 %collective-permute-done = bf16[2,512,4,128]{3,1,2,0:T(8,128)(2,1)} collective-permute-done((bf16[2,512,4,128]{3,1,2,0:T(8,128)(2,1)}, bf16[2,512,4,128]{3,1,2,0:T(8,128)(2,1)}, u32[]{:S(2)}, u32[]{:S(2)}) %collective-permute-start) | collective-permute-done | bytes 1048608 | tf_op jit(solution)/shard_map/ppermute | solution.py:866
  125.5 2.5 collective-permute-start.1
  128.0 2.4 fusion.67
  132.3 2.4 fusion.25
  136.4 15.9 %collective-permute-done.1 = bf16[256,2048]{1,0:T(8,128)(2,1)} collective-permute-done((bf16[256,2048]{1,0:T(8,128)(2,1)}, bf16[256,2048]{1,0:T(8,128)(2,1)}, u32[]{:S(2)}, u32[]{:S(2)}) %collective-permute-start.1) | collective-permute-done | bytes 1048608 | tf_op jit(solution)/shard_map/ppermute | solution.py:33
  152.4 73.9 %shard_map.297 = (bf16[1024,2048]{1,0:T(8,128)(2,1)S(1)}, f32[512,512]{1,0:T(8,128)S(1)}, f32[512,1]{1,0:T(8,128)S(1)}) custom-call(bf16[512,512]{1,0:T(8,128)(2,1)S(1)} %copy.197.attn.left, bf16[512,2048]{1,0:T(8,128)(2,1)S(1)} %copy-done.38, bf16[512,2048]{1,0:T(8,128)(2,1)S(1)} %copy-done.21, f32[1,2048]{1,0:T(1,128)S(1)} %get-tuple-element.170.gain), custom_call_target="tpu_custom_call" | custom-call | tf_op jit(solution)/shard_map/pallas_call | solution.py:662
  229.9 29.2 %shard_map.298 = (bf16[512,1408]{1,0:T(8,128)(2,1)}, bf16[512,2816]{1,0:T(8,128)(2,1)}, bf16[512,2048]{1,0:T(8,128)(2,1)}, bf16[512,2048]{1,0:T(8,128)(2,1)}, f32[512,2]{1,0:T(8,128)}) custom-call(bf16[1024,2048]{1,0:T(8,128)(2,1)} %copy-done.2, bf16[512,2048]{1,0:T(8,128)(2,1)} %all-gather.5.cloned.1.call-done.refs_1_.right, f32[512,1]{1,0:T(8,128)} %copy.165.refs_2_, ...), custom_call_target="tpu_custom_call" | custom-call | tf_op jit(solution)/shard_map/pallas_call | solution.py:392
  259.1 2.5 constant_dynamic-update-slice_fusion.1
  263.9 7.1 shard_map.299
  271.0 9.6 %collective-permute-done.3.refs_0_ = bf16[1024,2816]{1,0:T(8,128)(2,1)S(1)} collective-permute-done((bf16[1024,2816]{1,0:T(8,128)(2,1)}, bf16[1024,2816]{1,0:T(8,128)(2,1)S(1)}, u32[]{:S(2)}, u32[]{:S(2)}) %collective-permute-start.3) | collective-permute-done | bytes 5767200 | tf_op jit(solution)/shard_map/ppermute | solution.py:33
  280.7 3.5 shard_map.300
  284.3 5.5 collective-permute-done.4.refs_0_
  291.6 8.7 shard_map.301
  300.3 3.6 constant_dynamic-slice_fusion.2
  305.6 2.5 collective-permute-start.5
  314.6 5.1 shard_map.302
  319.7 2.6 constant_dynamic-slice_fusion.3
  325.7 28.9 %shard_map.303 = (bf16[1024,1408]{1,0:T(8,128)(2,1)}, bf16[1024,2816]{1,0:T(8,128)(2,1)}, bf16[512,2048]{1,0:T(8,128)(2,1)}, bf16[512,2048]{1,0:T(8,128)(2,1)}, f32[512,5]{1,0:T(8,128)}) custom-call(bf16[1024,2048]{1,0:T(8,128)(2,1)} %copy-done.2, bf16[1024,2048]{1,0:T(8,128)(2,1)} %constant_dynamic-update-slice_fusion.refs_1_.right, ...), custom_call_target="tpu_custom_call" | custom-call | tf_op jit(solution)/shard_map/pallas_call | solution.py:392
  354.6 29.9 %shard_map.304 = (bf16[1024,1408]{1,0:T(8,128)(2,1)}, bf16[1024,2816]{1,0:T(8,128)(2,1)}, bf16[512,2048]{1,0:T(8,128)(2,1)}, bf16[512,2048]{1,0:T(8,128)(2,1)}, f32[512,5]{1,0:T(8,128)}) custom-call(bf16[1024,2048]{1,0:T(8,128)(2,1)} %copy-done.2, ...), custom_call_target="tpu_custom_call", output_to_operand_aliasing={{0}: (8, {}), {1}: (9, {})} | custom-call | tf_op jit(solution)/shard_map/pallas_call | solution.py:392
  384.5 5.1 add_convert_fusion.1
  389.6 3.2 add_convert_fusion.6
  392.8 10.2 %shard_map.305 = bf16[2816,1024]{1,0:T(8,128)(2,1)} custom-call(s32[1]{0:T(128)} %bitcast.16.part, bf16[1024,2816]{1,0:T(8,128)(2,1)} %get-tuple-element.112.left, bf16[1024,2048]{1,0:T(8,128)(2,1)S(1)} %copy-done.3), custom_call_target="tpu_custom_call" | custom-call | tf_op jit(solution)/shard_map/pallas_call | solution.py:296
  405.0 7.3 collective-permute-done.11
  415.2 8.1 collective-permute-done.12
  424.0 6.4 shard_map.306
  430.3 2.6 constant_dynamic-slice_fusion
  441.3 10.8 %shard_map.307.sum_egu = bf16[2816,1024]{1,0:T(8,128)(2,1)} custom-call(s32[1]{0:T(128)} %bitcast.15.part, bf16[1024,2816]{1,0:T(8,128)(2,1)} %get-tuple-element.112.left, bf16[1024,2048]{1,0:T(8,128)(2,1)S(1)} %copy-done.4, bf16[2816,1024]{1,0:T(8,128)(2,1)} %collective-permute-done.10.refs_0_), custom_call_target="tpu_custom_call" | custom-call | tf_op jit(solution)/shard_map/pallas_call | solution.py:296
  452.1 5.8 shard_map.308.sum_ed
  458.0 9.2 collective-permute-done.9
  467.2 2.8 add_convert_fusion.5.sgu
  477.0 98.5 %shard_map.309 = (bf16[512,2048]{1,0:T(8,128)(2,1)S(1)}, f32[512,512]{1,0:T(8,128)S(1)}, f32[1,512]{1,0:T(1,128)S(1)}, bf16[512,2048]{1,0:T(8,128)(2,1)S(1)}, bf...) custom-call(bf16[512,2048]{1,0:T(8,128)(2,1)S(1)} %copy-done.34, bf16[512,2048]{1,0:T(8,128)(2,1)S(1)} %copy-done.33, ...), custom_call_target="tpu_custom_call" | custom-call | tf_op jit(solution)/shard_map/pallas_call | solution.py:759
  577.2 7.6 multiply_reduce_fusion
  584.8 2.6 fusion.13
  587.4 5.1 multiply_convert_fusion
  599.2 3.6 fusion.16
  602.9 3.0 add_convert_fusion.egu
  611.6 12.8 %collective-permute-done.16 = bf16[2,512,4,128]{3,1,2,0:T(8,128)(2,1)} collective-permute-done((bf16[2,512,4,128]{3,1,2,0:T(8,128)(2,1)}, bf16[2,512,4,128]{3,1,2,0:T(8,128)(2,1)}, u32[]{:S(2)}, u32[]{:S(2)}) %collective-permute-start.16) | collective-permute-done | bytes 1048608 | tf_op jit(solution)/shard_map/ppermute | solution.py:1028
  630.4 3.5 shard_map.312
  634.0 2.5 copy.188
  636.6 2.5 copy.187
  639.1 2.5 copy.189
  641.6 3.3 add_reduce_fusion
  648.4 5.4 shard_map.313.qkv
  653.9 2.9 add_convert_fusion.2
  667.3 194.7 %shard_map.314 = (bf16[2,2,2,256,2816]{4,3,2,1,0:T(8,128)(2,1)}, bf16[2,2,2,352,1024]{4,3,2,1,0:T(8,128)(2,1)S(1)}, bf16[2,2,1408,1024]{3,2,1,0:T(8,128)(2,1)}, ...) custom-call(bf16[256,2816]{1,0:T(8,128)(2,1)S(1)} %copy-done.25, ...), custom_call_target="tpu_custom_call" | custom-call | tf_op jit(solution)/shard_map/pallas_call | solution.py:212
  862.0 2.5 copy-done.24
  867.1 2.8 fusion.32
  873.4 4.3 copy-done.8
  877.6 5.4 shard_map.319
  883.1 5.2 shard_map.320
  888.3 5.3 shard_map.315
  896.4 4.3 copy-done.15
  900.7 8.6 shard_map.317
  909.3 5.6 shard_map.318
  915.6 5.2 shard_map.321
  (366 shorter events, 118.7 us)
Async XLA Ops:
  7.2 300.9 %copy-start = (bf16[2048,8]{0,1:T(8,128)(2,1)S(1)}, bf16[2048,8]{0,1:T(8,128)(2,1)}, u32[]{:S(2)}) copy-start(bf16[2048,8]{0,1:T(8,128)(2,1)} %param.25) | copy-start | bytes 98308
  7.2 53.6 %all-gather.3.cloned.1.call-start = ((), (), s32[]{:S(2)}) async-start(), calls=%async_computation.2 | async-start | bytes 2703360 | tf_op jit(solution)/shard_map/all_gather | solution.py:840
  10.7 111.3 %all-gather.5.cloned.1.call-start = ((), (), s32[]{:S(2)}) async-start(), calls=%async_computation.3 | async-start | bytes 2621440 | tf_op jit(solution)/shard_map/all_gather | solution.py:844
  12.6 78.5 %copy-start.68 = (f32[512,64]{1,0:T(8,128)}, f32[512,64]{1,0:T(8,128)S(1)}, u32[]{:S(2)}) copy-start(f32[512,64]{1,0:T(8,128)S(1)} %get-tuple-element.202) | copy-start | bytes 393220
  63.5 6.8 copy-start.93
  63.5 802.3 %reduce-scatter.5.cloned.1.call-start = ((), (), s32[]{:S(2)}) async-start(), calls=%async_computation.5 | async-start | bytes 2703360 | tf_op jit(solution)/shard_map/reduce_scatter | solution.py:1070
  66.6 19.2 %copy-start.10 = (bf16[512,2048]{1,0:T(8,128)(2,1)}, bf16[512,2048]{1,0:T(8,128)(2,1)S(1)}, u32[]{:S(2)}) copy-start(bf16[512,2048]{1,0:T(8,128)(2,1)S(1)} %fusion.5.left) | copy-start | bytes 6291460
  91.1 9.3 %copy-start.100 = (s32[1024]{0:T(1024)S(1)}, s32[1024]{0:T(1024)}, u32[]{:S(2)}) copy-start(s32[1024]{0:T(1024)} %param.34) | copy-start | bytes 12292
  91.2 9.4 %copy-start.97 = (bf16[2048]{0:T(1024)(128)(2,1)S(1)}, bf16[2048]{0:T(1024)(128)(2,1)}, u32[]{:S(2)}) copy-start(bf16[2048]{0:T(1024)(128)(2,1)} %param.26) | copy-start | bytes 12292
  94.7 11.5 %copy-start.78 = (bf16[512,4,64]{2,0,1:T(8,128)(2,1)}, bf16[512,4,64]{2,0,1:T(8,128)(2,1)S(1)}, u32[]{:S(2)}) copy-start(bf16[512,4,64]{2,0,1:T(8,128)(2,1)S(1)} %get-tuple-element.192) | copy-start | bytes 786436
  94.7 11.5 %copy-start.81 = (bf16[512,4,64]{2,0,1:T(8,128)(2,1)}, bf16[512,4,64]{2,0,1:T(8,128)(2,1)S(1)}, u32[]{:S(2)}) copy-start(bf16[512,4,64]{2,0,1:T(8,128)(2,1)S(1)} %get-tuple-element.193) | copy-start | bytes 786436
  94.7 7.2 copy-start.75
  96.0 26.1 %collective-permute-start = (bf16[2,512,4,128]{3,1,2,0:T(8,128)(2,1)}, bf16[2,512,4,128]{3,1,2,0:T(8,128)(2,1)}, u32[]{:S(2)}, u32[]{:S(2)}) collective-permute-start(bf16[2,512,4,128]{3,1,2,0:T(8,128)(2,1)} %pad_maximum_fusion), channel_id=1, source_target_pairs={{0,4},{1,5},{2,6},{3,7},{8,12},{9,13},{10,14},{11,15},{16,20},{17,... | collective-permute-start | bytes 3145736 | tf_op jit(solution)/shard_map/ppermute | solution.py:866
  102.9 25.1 %copy-start.71 = (bf16[512,4,64]{2,0,1:T(8,128)(2,1)S(1)}, bf16[512,4,64]{2,0,1:T(8,128)(2,1)}, u32[]{:S(2)}) copy-start(bf16[512,4,64]{2,0,1:T(8,128)(2,1)} %get-tuple-element.166) | copy-start | bytes 786436
  102.9 25.1 %copy-start.73 = (bf16[512,4,64]{2,0,1:T(8,128)(2,1)S(1)}, bf16[512,4,64]{2,0,1:T(8,128)(2,1)}, u32[]{:S(2)}) copy-start(bf16[512,4,64]{2,0,1:T(8,128)(2,1)} %get-tuple-element.167) | copy-start | bytes 786436
  123.9 6.5 copy-start.92
  123.9 8.4 copy-start.85
  125.5 26.9 %collective-permute-start.1 = (bf16[256,2048]{1,0:T(8,128)(2,1)}, bf16[256,2048]{1,0:T(8,128)(2,1)}, u32[]{:S(2)}, u32[]{:S(2)}) collective-permute-start(bf16[256,2048]{1,0:T(8,128)(2,1)} %get-tuple-element.175), channel_id=1, source_target_pairs={{0,4},{4,0},{1,5},{5,1},{2,6},{6,2},{3,7},{7,3},{8,12},{12,8},{9,1... | collective-permute-start | bytes 3145736 | tf_op jit(solution)/shard_map/ppermute | solution.py:33
  128.0 131.1 %collective-permute-start.2 = (bf16[256,2048]{1,0:T(8,128)(2,1)}, bf16[256,2048]{1,0:T(8,128)(2,1)}, u32[]{:S(2)}, u32[]{:S(2)}) collective-permute-start(bf16[256,2048]{1,0:T(8,128)(2,1)} %get-tuple-element.174), channel_id=1, source_target_pairs={{0,4},{4,0},{1,5},{5,1},{2,6},{6,2},{3,7},{7,3},{8,12},{12,8},{9,1... | collective-permute-start | bytes 3145736 | tf_op jit(solution)/shard_map/ppermute | solution.py:33
  135.0 17.4 %copy-start.21 = (bf16[512,2048]{1,0:T(8,128)(2,1)S(1)}, bf16[512,2048]{1,0:T(8,128)(2,1)}, u32[]{:S(2)}) copy-start(bf16[512,2048]{1,0:T(8,128)(2,1)} %slice.160.x) | copy-start | bytes 6291460
  135.0 17.4 %copy-start.38 = (bf16[512,2048]{1,0:T(8,128)(2,1)S(1)}, bf16[512,2048]{1,0:T(8,128)(2,1)}, u32[]{:S(2)}) copy-start(bf16[512,2048]{1,0:T(8,128)(2,1)} %w_out.1) | copy-start | bytes 6291460
  263.9 16.8 %copy-start.7 = (bf16[512,2048]{1,0:T(8,128)(2,1)S(1)}, bf16[512,2048]{1,0:T(8,128)(2,1)}, u32[]{:S(2)}) copy-start(bf16[512,2048]{1,0:T(8,128)(2,1)} %all-gather.5.cloned.1.call-done.refs_1_.right) | copy-start | bytes 6291460
  263.9 16.8 %copy-start.22 = (bf16[512,1408]{1,0:T(8,128)(2,1)S(1)}, bf16[512,1408]{1,0:T(8,128)(2,1)}, u32[]{:S(2)}) copy-start(bf16[512,1408]{1,0:T(8,128)(2,1)} %get-tuple-element.94.left) | copy-start | bytes 4325380
  271.0 9.6 %collective-permute-start.3 = (bf16[1024,2816]{1,0:T(8,128)(2,1)}, bf16[1024,2816]{1,0:T(8,128)(2,1)S(1)}, u32[]{:S(2)}, u32[]{:S(2)}) collective-permute-start(bf16[1024,2816]{1,0:T(8,128)(2,1)} %shard_map.299), channel_id=1, source_target_pairs={{0,8},{8,0},{16,24},{24,16},{1,9},{9,1},{17,25},{25,17},{2,10},{10... | collective-permute-start | bytes 17301512 | tf_op jit(solution)/shard_map/ppermute | solution.py:33
  284.1 5.6 collective-permute-start.4
  303.9 80.6 %collective-permute-start.7 = (bf16[512,2816]{1,0:T(8,128)(2,1)}, bf16[512,2816]{1,0:T(8,128)(2,1)}, u32[]{:S(2)}, u32[]{:S(2)}) collective-permute-start(bf16[512,2816]{1,0:T(8,128)(2,1)} %constant_dynamic-slice_fusion.2), channel_id=1, source_target_pairs={{0,16},{8,24},{16,0},{24,8},{1,17},{9,25},{17,1},{25,9},{2,18},{10... | collective-permute-start | bytes 8650760 | tf_op jit(solution)/shard_map/ppermute | solution.py:33
  305.5 17.3 %copy-start.61 = (f32[512,8]{1,0:T(8,128)}, f32[512,8]{1,0:T(8,128)S(1)}, u32[]{:S(2)}) copy-start(f32[512,8]{1,0:T(8,128)S(1)} %copy.168) | copy-start | bytes 49156
  305.6 18.2 %collective-permute-start.5 = (f32[512,8]{1,0:T(8,128)S(1)}, f32[512,8]{1,0:T(8,128)}, u32[]{:S(2)}, u32[]{:S(2)}) collective-permute-start(f32[512,8]{1,0:T(8,128)S(1)} %copy.168), channel_id=1, source_target_pairs={{0,4},{4,0},{1,5},{5,1},{2,6},{6,2},{3,7},{7,3},{8,12},{12,8},{9,1... | collective-permute-start | bytes 49160 | tf_op jit(solution)/shard_map/ppermute | solution.py:33
  310.4 12.2 %copy-start.54 = (f32[512,8]{1,0:T(8,128)}, f32[512,8]{1,0:T(8,128)S(1)}, u32[]{:S(2)}) copy-start(f32[512,8]{1,0:T(8,128)S(1)} %copy.166) | copy-start | bytes 49156
  322.3 67.3 %collective-permute-start.6 = (bf16[704,1024]{1,0:T(8,128)(2,1)}, bf16[704,1024]{1,0:T(8,128)(2,1)}, u32[]{:S(2)}, u32[]{:S(2)}) collective-permute-start(bf16[704,1024]{1,0:T(8,128)(2,1)} %constant_dynamic-slice_fusion.3), channel_id=1, source_target_pairs={{0,4},{4,0},{1,5},{5,1},{2,6},{6,2},{3,7},{7,3},{8,12},{12,8},{9,1... | collective-permute-start | bytes 4325384 | tf_op jit(solution)/shard_map/ppermute | solution.py:33
  403.0 21.0 %copy-start.9 = (bf16[1024,1408]{1,0:T(8,128)(2,1)S(1)}, bf16[1024,1408]{1,0:T(8,128)(2,1)}, u32[]{:S(2)}) copy-start(bf16[1024,1408]{1,0:T(8,128)(2,1)} %get-tuple-element.110.left) | copy-start | bytes 8650756
  403.0 20.2 %collective-permute-start.10 = (bf16[2816,1024]{1,0:T(8,128)(2,1)}, bf16[2816,1024]{1,0:T(8,128)(2,1)}, u32[]{:S(2)}, u32[]{:S(2)}) collective-permute-start(bf16[2816,1024]{1,0:T(8,128)(2,1)} %shard_map.305), channel_id=1, source_target_pairs={{0,8},{8,0},{16,24},{24,16},{1,9},{9,1},{17,25},{25,17},{2,10},{10... | collective-permute-start | bytes 17301512 | tf_op jit(solution)/shard_map/ppermute | solution.py:33
  403.0 9.3 collective-permute-start.11
  415.1 8.2 collective-permute-start.12
  430.3 8.8 collective-permute-start.13
  432.9 34.3 %collective-permute-start.9 = (bf16[256,2816]{1,0:T(8,128)(2,1)}, bf16[256,2816]{1,0:T(8,128)(2,1)}, u32[]{:S(2)}, u32[]{:S(2)}) collective-permute-start(bf16[256,2816]{1,0:T(8,128)(2,1)} %constant_dynamic-slice_fusion), channel_id=1, source_target_pairs={{0,4},{4,0},{1,5},{5,1},{2,6},{6,2},{3,7},{7,3},{8,12},{12,8},{9,1... | collective-permute-start | bytes 4325384 | tf_op jit(solution)/shard_map/ppermute | solution.py:33
  437.4 32.6 %collective-permute-start.8 = (bf16[352,1024]{1,0:T(8,128)(2,1)S(1)}, bf16[352,1024]{1,0:T(8,128)(2,1)S(1)}, u32[]{:S(2)}, u32[]{:S(2)}) collective-permute-start(bf16[352,1024]{1,0:T(8,128)(2,1)S(1)} %constant_dynamic-slice_fusion.1), channel_id=1, source_target_pairs={{0,16},{8,24},{16,0},{24,8},{1,17},{9,25},{17,1},{25,9},{2,18},{10... | collective-permute-start | bytes 2162696 | tf_op jit(solution)/shard_map/ppermute | solution.py:33
  437.9 33.2 %collective-permute-start.14 = (f32[10,512]{0,1:T(8,128)}, f32[10,512]{0,1:T(8,128)S(1)}, u32[]{:S(2)}, u32[]{:S(2)}) collective-permute-start(f32[10,512]{0,1:T(8,128)} %add.233), channel_id=1, source_target_pairs={{0,2},{1,3},{2,0},{3,1},{4,6},{5,7},{6,4},{7,5},{8,10},{9,11},{10,... | collective-permute-start | bytes 61448 | tf_op jit(solution)/shard_map/ppermute | solution.py:33
  452.1 15.1 %copy-start.46 = (bf16[512,2816]{1,0:T(8,128)(2,1)S(1)}, bf16[512,2816]{1,0:T(8,128)(2,1)}, u32[]{:S(2)}) copy-start(bf16[512,2816]{1,0:T(8,128)(2,1)} %add_convert_fusion.1) | copy-start | bytes 8650756
  457.9 13.2 %copy-start.12 = (bf16[1408,1024]{1,0:T(8,128)(2,1)}, bf16[1408,1024]{1,0:T(8,128)(2,1)S(1)}, u32[]{:S(2)}) copy-start(bf16[1408,1024]{1,0:T(8,128)(2,1)S(1)} %shard_map.308.sum_ed) | copy-start | bytes 8650756
  457.9 12.1 %copy-start.59 = (bf16[704,1024]{1,0:T(8,128)(2,1)S(1)}, bf16[704,1024]{1,0:T(8,128)(2,1)}, u32[]{:S(2)}) copy-start(bf16[704,1024]{1,0:T(8,128)(2,1)} %add_convert_fusion.6) | copy-start | bytes 4325380
  458.0 13.2 %copy-start.88 = (f32[10,512]{0,1:T(8,128)S(1)}, f32[10,512]{0,1:T(8,128)}, u32[]{:S(2)}) copy-start(f32[10,512]{0,1:T(8,128)} %add.233) | copy-start | bytes 61444
  458.0 13.2 %copy-start.55 = (f32[512,8]{1,0:T(8,128)S(1)}, f32[512,8]{1,0:T(8,128)}, u32[]{:S(2)}) copy-start(f32[512,8]{1,0:T(8,128)} %copy-done.54) | copy-start | bytes 49156
  458.0 13.2 %copy-start.62 = (f32[512,8]{1,0:T(8,128)S(1)}, f32[512,8]{1,0:T(8,128)}, u32[]{:S(2)}) copy-start(f32[512,8]{1,0:T(8,128)} %copy-done.61) | copy-start | bytes 49156
  477.0 98.6 %copy-start.39 = (bf16[512,2048]{1,0:T(8,128)(2,1)S(1)}, bf16[512,2048]{1,0:T(8,128)(2,1)}, u32[]{:S(2)}) copy-start(bf16[512,2048]{1,0:T(8,128)(2,1)} %w_out.1) | copy-start | bytes 6291460
  575.6 9.2 copy-start.40
  575.6 9.1 slice-start.6
  577.2 7.6 slice-start.7
  587.3 7.0 copy-start.58
  595.4 7.5 collective-permute-start.15
  596.9 27.5 %collective-permute-start.16 = (bf16[2,512,4,128]{3,1,2,0:T(8,128)(2,1)}, bf16[2,512,4,128]{3,1,2,0:T(8,128)(2,1)}, u32[]{:S(2)}, u32[]{:S(2)}) collective-permute-start(bf16[2,512,4,128]{3,1,2,0:T(8,128)(2,1)} %pad_maximum_fusion.2), channel_id=1, source_target_pairs={{4,0},{5,1},{6,2},{7,3},{12,8},{13,9},{14,10},{15,11},{20,16},{21,... | collective-permute-start | bytes 3145736 | tf_op jit(solution)/shard_map/ppermute | solution.py:1028
  611.6 14.2 %copy-start.57 = (f32[1024,4,128]{2,0,1:T(8,128)S(1)}, f32[1024,4,128]{2,0,1:T(8,128)}, u32[]{:S(2)}) copy-start(f32[1024,4,128]{2,0,1:T(8,128)} %copy-done.56) | copy-start | bytes 6291460
  633.9 14.5 %collective-permute-start.17 = (bf16[1024,1536]{1,0:T(8,128)(2,1)}, bf16[1024,1536]{1,0:T(8,128)(2,1)}, u32[]{:S(2)}, u32[]{:S(2)}) collective-permute-start(bf16[1024,1536]{1,0:T(8,128)(2,1)} %shard_map.312), channel_id=1, source_target_pairs={{0,8},{8,0},{16,24},{24,16},{1,9},{9,1},{17,25},{25,17},{2,10},{10... | collective-permute-start | bytes 9437192 | tf_op jit(solution)/shard_map/ppermute | solution.py:33
  658.4 262.5 %reduce-scatter.3.cloned.1.call-start = ((), (), s32[]{:S(2)}) async-start(), calls=%async_computation.4 | async-start | bytes 2621440 | tf_op jit(solution)/shard_map/reduce_scatter | solution.py:1044
  667.3 199.7 %copy-start.94 = (f32[512]{0:T(512)S(1)}, f32[512]{0:T(512)}, u32[]{:S(2)}) copy-start(f32[512]{0:T(512)} %copy-done.93) | copy-start | bytes 6148
  667.3 199.7 %copy-start.95 = (f32[512]{0:T(512)S(1)}, f32[512]{0:T(512)}, u32[]{:S(2)}) copy-start(f32[512]{0:T(512)} %get-tuple-element.203) | copy-start | bytes 6148
  869.9 1.2 collective-permute-start.18
  871.1 49.7 %collective-permute-start.19 = (f32[4,128]{1,0:T(4,128)S(1)}, f32[4,128]{1,0:T(4,128)S(1)}, u32[]{:S(2)}, u32[]{:S(2)}) collective-permute-start(f32[4,128]{1,0:T(4,128)S(1)} %bitcast_add_fusion), channel_id=1, source_target_pairs={{0,16},{8,24},{16,0},{24,8},{1,17},{9,25},{17,1},{25,9},{2,18},{10... | collective-permute-start | bytes 6152 | tf_op jit(solution)/shard_map/ppermute | solution.py:33
  877.6 10.7 %slice-start = ((s8[6291456]{0:T(1024)(128)(4,1)}), s8[4194304]{0:T(1024)(128)(4,1)S(1)}, s32[]{:S(2)}) async-start(s8[6291456]{0:T(1024)(128)(4,1)} %bitcast.145), calls=%async_computation.6 | async-start | bytes 8388608
  893.6 15.6 %slice-start.4 = ((s8[5767168]{0:T(1024)(128)(4,1)}), s8[1572864]{0:T(1024)(128)(4,1)S(1)}, s32[]{:S(2)}) async-start(s8[5767168]{0:T(1024)(128)(4,1)} %bitcast.151), calls=%async_computation.10 | async-start | bytes 3145728
  900.7 8.6 slice-start.5
  909.3 6.4 slice-start.3
  915.6 9.5 %copy-start.1 = (bf16[2048,8]{0,1:T(8,128)(2,1)S(1)}, bf16[2048,8]{0,1:T(8,128)(2,1)}, u32[]{:S(2)}) copy-start(bf16[2048,8]{0,1:T(8,128)(2,1)} %param.25) | copy-start | bytes 98308
  920.9 3.7 collective-permute-start.20
  (72 other events, 223.6 us)
Sparse Core Ops, SparseCore 0:
  10.9 49.9 all-gather.2
  63.6 44.6 all-gather.4
  658.5 44.4 reduce-scatter.4
  705.2 43.2 reduce-scatter.2

commit v4 on v3

--- a/solution.py
+++ b/solution.py
@@ -91,13 +91,18 @@
     lax.fori_loop(0, count // step, turn, 0)
 
 
-def sums_kernel(
-    sgu, sd, egu, ed, qkv, wo, flat,
-    sgu_f, sd_f, egu_f, ed_f, qkv_f, wo_f, flat_f,
-    q_own, q_in, q_in2, q_out, w_own, w_in, w_in2, w_out, flat_in, l_sem, s_sem, r_sem,
+def tail_kernel(
+    scale,
+    sgu, sd, egu, ed, flat, normed, w_query, w_key, w_value, attn,
+    low, w_out, query, keys, values, lse, query_seg, key_seg, cos, sin,
+    sgu_f, sd_f, egu_f, ed_f, qkv_f, wo_f, flat_f, grad_normed, row_part,
+    normed_v, wq_v, wk_v, wv_v, attn_v, grad_attn, grad_key, grad_value, early, came, grad_qkv,
+    q_sent, q_half, q_in, q_in2, q_out, w_sent, w_half, w_in, w_in2, w_out_v,
+    e_own, e_in, d_own, d_in, flat_in, l_sem, s_sem, r_sem,
 ):
     core, x, y, (to_core, to_x, to_y) = places()
     used = [0, 0]
+    sent = []
 
     def here(source, target):
         k = used[0]
@@ -106,125 +111,244 @@
         copy.start()
         return copy
 
-    def there(source, target, where):
+    def remote(source, target, where):
         k = used[1]
         used[1] += 1
-        copy = pltpu.make_async_remote_copy(
+        return pltpu.make_async_remote_copy(
             src_ref=source, dst_ref=target, send_sem=s_sem.at[k], recv_sem=r_sem.at[k],
             device_id=where, device_id_type=pl.DeviceIdType.MESH,
         )
+
+    def there(source, target, where):
+        copy = remote(source, target, where)
         copy.start()
+        sent.append(copy)
         return copy
 
+    rows = query.shape[0]
+    heads = query.shape[1] // HD
+    mine = heads * HD
+    q_rows, w_rows = q_in.shape[0], w_in.shape[0]
+    e_rows, d_rows = e_own.shape[0], d_own.shape[0]
     greet_all((to_core, to_x, to_y))
-    q_rows, w_rows = q_own.shape[0], w_own.shape[0]
-    load_q = here(qkv.at[pl.ds(y * q_rows, q_rows)], q_own)
-    load_w = here(wo.at[pl.ds(y * w_rows, w_rows)], w_own)
-    a1 = there(qkv.at[pl.ds((1 - y) * q_rows, q_rows)], q_in, to_y)
-    a2 = there(wo.at[pl.ds((1 - y) * w_rows, w_rows)], w_in, to_y)
-    b1 = there(sgu, sgu_f.at[core, x, y], to_x)
-    b2 = there(sd, sd_f.at[core, y, x], to_x)
+
+    b3 = there(egu.at[pl.ds((1 - x) * e_rows, e_rows)], e_in, to_x)
+    b4 = there(ed.at[pl.ds((1 - x) * d_rows, d_rows)], d_in, to_x)
     f1 = there(flat, flat_in.at[0], to_core)
-    own_s = here(sgu, sgu_f.at[core, x, y])
-    own_sd = here(sd, sd_f.at[core, y, x])
-    own_e = here(egu, egu_f.at[core, x])
-    own_ed = here(ed, ed_f.at[core, x])
-
-    b1.wait_recv()
-    d1 = there(sgu, sgu_f.at[core, x, y], to_y)
-    d2 = there(sgu_f.at[core, 1 - x, y], sgu_f.at[core, 1 - x, y], to_y)
-    f1.wait()
+    load_attn = here(attn, attn_v)
+    load_normed = here(normed, normed_v)
+    loads = [here(w_query, wq_v), here(w_key, wk_v), here(w_value, wv_v)]
+    load_e = here(egu.at[pl.ds(x * e_rows, e_rows)], e_own)
+    load_d = here(ed.at[pl.ds(x * d_rows, d_rows)], d_own)
+    own_s = here(sgu, sgu_f.at[core, y])
+    own_sd = [here(sd.at[p], sd_f.at[core, p, y]) for p in range(2)]
+
+    grad_attn[...] = mm_nt(low[...], w_out[...]).astype(BF16)
+    key_at = (y - 1) * rows + lax.broadcasted_iota(jnp.int32, (1, 2 * rows), 1)
+    query_at = y * rows + lax.broadcasted_iota(jnp.int32, (rows, 1), 0)
+    allowed = (query_seg[...] == key_seg[...]) & (key_at <= query_at)
+    sums_of = jnp.zeros((rows, 1), F32)
+    early_copies = []
+    for h in range(heads):
+        own = slice(h * HD, (h + 1) * HD)
+        q, k, v, g = query[:, own], keys[:, own], values[:, own], grad_attn[:, own]
+        scores = jnp.where(allowed, mm_nt(q, k) * scale, NEG)
+        probs = jnp.exp(scores - lse[:, h : h + 1])
+        grad_probs = mm_nt(g, v)
+        weighted = probs * grad_probs
+        grad_scores = (weighted - probs * jnp.sum(weighted, axis=1, keepdims=True)).astype(BF16)
+        grad_q = mm(grad_scores, k) * scale
+        grad_k = mm_tn(grad_scores, q) * scale
+        grad_v = mm_tn(probs.astype(BF16), g)
+        grad_key[:, own] = grad_k[rows:]
+        grad_value[:, own] = grad_v[rows:]
+        early[h, 0] = grad_k[:rows].astype(BF16)
+        early[h, 1] = grad_v[:rows].astype(BF16)
+        copy = remote(early.at[h], came.at[h], to_y)
+        early_copies.append(copy)
+
+        @pl.when(y == 1)
+        def _(copy=copy):
+            copy.start()
+
+        sums_of = sums_of + jnp.sum(grad_q * q.astype(F32), axis=1, keepdims=True)
+        turned = grad_q * cos[...] + pltpu.roll(grad_q, HD // 2, 1) * sin[...]
+        grad_qkv[:, own] = turned.astype(BF16)
+
+    d1 = there(sgu.at[0], sgu_f.at[core, y, 0], to_y)
+    load_attn.wait()
+    half_of = low.shape[1] // 2
+    w_sent[...] = mm_tn(attn_v[...], low[:, pl.ds(pl.multiple_of((1 - core) * half_of, half_of), half_of)]).astype(BF16)
+    a0 = there(w_sent, w_half, to_core)
+    w_own = mm_tn(attn_v[...], low[:, pl.ds(pl.multiple_of(core * half_of, half_of), half_of)])
+    f1.wait_recv()
     flat_f[...] = flat[...] + flat_in[0]
     f2 = there(flat_f, flat_in.at[1], to_x)
-
-    load_q.wait()
-    a1.wait_recv()
-    add_rows(q_own, q_in, 0, q_rows)
-    a3 = there(q_own.at[pl.ds((1 - x) * (q_rows // 2), q_rows // 2)], q_in2, to_x)
-    load_w.wait()
-    a2.wait_recv()
-    add_rows(w_own, w_in, 0, w_rows)
-    a4 = there(w_own.at[pl.ds((1 - x) * (w_rows // 2), w_rows // 2)], w_in2, to_x)
-    cut = egu.shape[0] // 2
-    b3 = there(egu.at[pl.ds(0, cut)], egu_f.at[core, x, pl.ds(0, cut)], to_x)
-    b2.wait_recv()
-    own_sd.wait()
-    d3 = there(sd_f.at[core, y], sd_f.at[core, y], to_y)
-    f2.wait()
+    a0.wait_recv()
+    w_half[...] = (w_own + w_half[...].astype(F32)).astype(BF16)
+    a2 = there(w_half.at[pl.ds((1 - y) * w_rows, w_rows)], w_in, to_y)
+
+    for h in range(heads):
+        own = slice(h * HD, (h + 1) * HD)
+
+        @pl.when(y == 0)
+        def _(h=h, own=own):
+            early_copies[h].wait_recv()
+            grad_key[:, own] = grad_key[:, own] + came[h, 0].astype(F32)
+            grad_value[:, own] = grad_value[:, own] + came[h, 1].astype(F32)
+
+        @pl.when(y == 1)
+        def _(h=h):
+            early_copies[h].wait_send()
+
+        grad_k, grad_v = grad_key[:, own], grad_value[:, own]
+        sums_of = sums_of + jnp.sum(
+            grad_k * keys[rows:, own].astype(F32) + grad_v * values[rows:, own].astype(F32),
+            axis=1, keepdims=True,
+        )
+        turned = grad_k * cos[...] + pltpu.roll(grad_k, HD // 2, 1) * sin[...]
+        grad_qkv[:, mine + h * HD : mine + (h + 1) * HD] = turned.astype(BF16)
+        grad_qkv[:, 2 * mine + h * HD : 2 * mine + (h + 1) * HD] = grad_v.astype(BF16)
+    row_part[...] = sums_of
+
+    load_normed.wait()
+    tall = q_half.shape[0]
+    step = tall // 4
+
+    def product(i, which):
+        start = pl.multiple_of(which * tall + i * step, step)
+        return mm_tn(normed_v[:, pl.ds(start, step)], grad_qkv[...])
+
+    a0q = []
+    for i in range(4):
+        q_sent[i * step : (i + 1) * step, :] = product(i, 1 - core).astype(BF16)
+        a0q.append(there(q_sent.at[pl.ds(i * step, step)], q_half.at[pl.ds(i * step, step)], to_core))
+    for i in range(4):
+        value = product(i, core)
+        a0q[i].wait_recv()
+        here_rows = slice(i * step, (i + 1) * step)
+        q_half[here_rows, :] = (value + q_half[here_rows, :].astype(F32)).astype(BF16)
+    a1 = there(q_half.at[pl.ds((1 - y) * q_rows, q_rows)], q_in, to_y)
+    d2 = there(sgu.at[1], sgu_f.at[core, y, 1], to_y)
+    for copy in loads:
+        copy.wait()
+    grad_normed[...] = (
+        mm_nt(grad_qkv[:, :mine], wq_v[...])
+        + mm_nt(grad_qkv[:, mine : 2 * mine], wk_v[...])
+        + mm_nt(grad_qkv[:, 2 * mine :], wv_v[...])
+    ).astype(BF16)
+
+    load_e.wait()
+    b3.wait_recv()
+    add_rows(e_own, e_in, 0, e_rows)
+    f2.wait_recv()
+    f2.wait_send()
     flat_f[...] = flat_f[...] + flat_in[1]
     f3 = there(flat_f, flat_in.at[2], to_y)
-
+    a2.wait_recv()
+    add_rows(w_half, w_in, y * w_rows, w_rows)
+    a4 = there(w_half.at[pl.ds(y * w_rows + (1 - x) * (w_rows // 2), w_rows // 2)], w_in2, to_x)
+    load_d.wait()
+    b4.wait_recv()
+    add_rows(d_own, d_in, 0, d_rows)
+    a1.wait_recv()
+    add_rows(q_half, q_in, y * q_rows, q_rows)
+    a3 = there(q_half.at[pl.ds(y * q_rows + (1 - x) * (q_rows // 2), q_rows // 2)], q_in2, to_x)
+    cut = e_rows // 2
+    b5 = there(e_own.at[pl.ds(0, cut)], egu_f.at[core, x, pl.ds(0, cut)], to_x)
+    own_e = here(e_own, egu_f.at[core, x])
+    own_ed = here(d_own, ed_f.at[core, x])
+    d3 = [there(sd.at[p], sd_f.at[core, p, y], to_y) for p in range(2)]
+    a4.wait_recv()
+    add_rows(w_half, w_in2, y * w_rows + x * (w_rows // 2), w_rows // 2, w_out_v)
+    a6 = there(w_out_v, wo_f.at[core, y, x], to_x)
+    own_w = here(w_out_v, wo_f.at[core, y, x])
     a3.wait_recv()
-    add_rows(q_own, q_in2, x * (q_rows // 2), q_rows // 2, q_out)
+    add_rows(q_half, q_in2, y * q_rows + x * (q_rows // 2), q_rows // 2, q_out)
     a5 = there(q_out, qkv_f.at[core, y, x], to_x)
     own_q = here(q_out, qkv_f.at[core, y, x])
-    a4.wait_recv()
-    add_rows(w_own, w_in2, x * (w_rows // 2), w_rows // 2, w_out)
-    a6 = there(w_out, wo_f.at[core, y, x], to_x)
-    own_w = here(w_out, wo_f.at[core, y, x])
-    b4 = there(egu.at[pl.ds(cut, cut)], egu_f.at[core, x, pl.ds(cut, cut)], to_x)
-    b5 = there(ed, ed_f.at[core, x], to_x)
-
+    b7 = there(e_own.at[pl.ds(cut, cut)], egu_f.at[core, x, pl.ds(cut, cut)], to_x)
+    b6 = there(d_own, ed_f.at[core, x], to_x)
+    own_s.wait()
     d1.wait_recv()
     d2.wait_recv()
-    own_s.wait()
     c1 = there(sgu_f.at[core], sgu_f.at[core], to_core)
+    a6.wait_recv()
+    own_w.wait()
+    a8 = there(wo_f.at[core, y], wo_f.at[core, y], to_y)
     a5.wait_recv()
     own_q.wait()
     a7 = there(qkv_f.at[core, y], qkv_f.at[core, y], to_y)
-    a6.wait_recv()
-    own_w.wait()
-    a8 = there(wo_f.at[core, y], wo_f.at[core, y], to_y)
-    d3.wait_recv()
+    for copy in own_sd:
+        copy.wait()
+    for copy in d3:
+        copy.wait_recv()
     c2 = there(sd_f.at[core], sd_f.at[core], to_core)
-    f3.wait()
+    f3.wait_recv()
+    f3.wait_send()
     flat_f[...] = flat_f[...] + flat_in[2]
-    b3.wait_recv()
-    b4.wait_recv()
     own_e.wait()
+    b5.wait_recv()
+    b7.wait_recv()
     c3 = there(egu_f.at[core], egu_f.at[core], to_core)
+    a8.wait_recv()
+    c5 = there(wo_f.at[core], wo_f.at[core], to_core)
     a7.wait_recv()
     c4 = there(qkv_f.at[core], qkv_f.at[core], to_core)
-    a8.wait_recv()
-    c5 = there(wo_f.at[core], wo_f.at[core], to_core)
-    b5.wait_recv()
     own_ed.wait()
+    b6.wait_recv()
     c6 = there(ed_f.at[core], ed_f.at[core], to_core)
     for copy in (c1, c2, c3, c4, c5, c6):
         copy.wait_recv()
-    for copy in (a1, a2, a3, a4, a5, a6, a7, a8, b1, b2, b3, b4, b5, d1, d2, d3, c1, c2, c3, c4, c5, c6):
-        copy.wait_send()
-
-
-def sums(sgu, sd, egu, ed, qkv, wo, flat):
-    def pieces(count, value, cut=1):
-        return jax.ShapeDtypeStruct(
-            (2,) * count + (value.shape[0] // cut, value.shape[1]), BF16
-        )
+    for copy in sent:
+        if copy is not f2 and copy is not f3:
+            copy.wait_send()
+
+
+def tail(sgu, sd, egu, ed, flat, normed, w_query, w_key, w_value, attn, low, w_out, query, keys, values, lse, query_seg, key_seg, cos, sin):
+    rows, width = low.shape
+    mine = query.shape[1]
+    heads = mine // HD
+
+    def pieces(count, height, wide):
+        return jax.ShapeDtypeStruct((2,) * count + (height, wide), BF16)
 
     far = pl.BlockSpec(memory_space=pl.ANY)
     vmem = pl.BlockSpec(memory_space=pltpu.VMEM)
 
-    def room(value, cut):
-        return pltpu.VMEM((value.shape[0] // cut, value.shape[1]), BF16)
-
+    def room(*shape, kind=BF16):
+        return pltpu.VMEM(shape, kind)
+
+    half_of = width // 2
     dma = pltpu.SemaphoreType.DMA
     return pl.pallas_call(
-        sums_kernel,
+        functools.partial(tail_kernel, 1.0 / math.sqrt(HD)),
         out_shape=[
-            pieces(3, sgu), pieces(3, sd), pieces(2, egu), pieces(2, ed),
-            pieces(3, qkv, 4), pieces(3, wo, 4), jax.ShapeDtypeStruct(flat.shape, F32),
+            pieces(3, *sgu.shape[1:]), pieces(3, *sd.shape[1:]),
+            pieces(2, egu.shape[0] // 2, egu.shape[1]), pieces(2, ed.shape[0] // 2, ed.shape[1]),
+            pieces(3, half_of // 4, 3 * mine), pieces(3, mine // 4, half_of),
+            jax.ShapeDtypeStruct(flat.shape, F32), jax.ShapeDtypeStruct((rows, width), BF16),
+            jax.ShapeDtypeStruct((rows, 1), F32),
         ],
-        in_specs=[far] * 6 + [vmem],
-        out_specs=[far] * 6 + [vmem],
-        scratch_shapes=[room(qkv, 2), room(qkv, 2), room(qkv, 4), room(qkv, 4)]
-        + [room(wo, 2), room(wo, 2), room(wo, 4), room(wo, 4)]
-        + [pltpu.VMEM((3,) + flat.shape, F32), dma((8,)), dma((25,)), dma((25,))],
+        in_specs=[far] * 4 + [vmem] + [far] * 5 + [vmem] * 10,
+        out_specs=[far] * 6 + [vmem] * 3,
+        scratch_shapes=[
+            room(rows, width), room(width, mine), room(width, mine), room(width, mine), room(rows, mine),
+            room(rows, mine), room(rows, mine, kind=F32), room(rows, mine, kind=F32),
+            room(heads, 2, rows, HD), room(heads, 2, rows, HD), room(rows, 3 * mine),
+            room(half_of, 3 * mine), room(half_of, 3 * mine), room(half_of // 2, 3 * mine),
+            room(half_of // 4, 3 * mine), room(half_of // 4, 3 * mine),
+            room(mine, half_of), room(mine, half_of), room(mine // 2, half_of),
+            room(mine // 4, half_of), room(mine // 4, half_of),
+            room(egu.shape[0] // 2, egu.shape[1]), room(egu.shape[0] // 2, egu.shape[1]),
+            room(ed.shape[0] // 2, ed.shape[1]), room(ed.shape[0] // 2, ed.shape[1]),
+            room(3, *flat.shape, kind=F32), dma((16,)), dma((40,)), dma((40,)),
+        ],
         compiler_params=pltpu.CompilerParams(
-            collective_id=3, has_side_effects=True, vmem_limit_bytes=32 << 20
+            collective_id=3, has_side_effects=True, vmem_limit_bytes=62 << 20
         ),
         cost_estimate=pl.CostEstimate(flops=0, bytes_accessed=0, transcendentals=0),
-    )(sgu, sd, egu, ed, qkv, wo, flat)
+    )(sgu, sd, egu, ed, flat, normed, w_query, w_key, w_value, attn, low, w_out, query, keys, values, lse, query_seg, key_seg, cos, sin)
 
 
 def widen_kernel(source, *outputs):
@@ -327,13 +451,37 @@
     )
 
 
-def ffn_kernel(groups, base, into, flipped, *refs):
+def ffn_kernel(groups, base, into, flipped, carry, *refs):
     rows, grads, scale, gate_w, up_w, down_w = refs[:6]
     refs = refs[6:]
     if base:
         base_out, base_dx = refs[:2]
         refs = refs[2:]
-    hid_ref, dgu_ref, out_ref, dx_ref, small_ref = refs[2:] if into else refs
+    if into:
+        refs = refs[2:]
+    sources, refs = refs[: len(carry)], refs[len(carry) :]
+    hid_ref, dgu_ref, out_ref, dx_ref, small_ref, *refs = refs
+    copies = []
+    if carry:
+        send_sem, recv_sem = refs[-2:]
+        _, x, y, where = places()
+        for m, (link, count, start, stride) in enumerate(carry):
+            first = start + (1 - (x, y)[link - 1]) * stride
+            copies.append(
+                pltpu.make_async_remote_copy(
+                    src_ref=sources[m].at[pl.ds(first, count)], dst_ref=refs[m],
+                    send_sem=send_sem.at[m], recv_sem=recv_sem.at[m],
+                    device_id=where[link], device_id_type=pl.DeviceIdType.MESH,
+                )
+            )
+        links = sorted({link for link, _, _, _ in carry})
+
+        @pl.when(pl.program_id(0) == 0)
+        def _():
+            greet_all([where[link] for link in links])
+            for copy in copies:
+                copy.start()
+
     width = down_w.shape[0]
     to, back = (mm_nt, mm) if flipped else (mm, mm_nt)
     gate_pre = to(rows[...], gate_w[...])
@@ -371,9 +519,15 @@
         dx = dx + base_dx[...].astype(F32)
     out_ref[...] = out.astype(BF16)
     dx_ref[...] = dx.astype(BF16)
-
-
-def ffn(rows, grads, scale, gate_w, up_w, down_w, start=0, total=0, base=(), into=(), flipped=False):
+    if carry:
+
+        @pl.when(pl.program_id(0) == pl.num_programs(0) - 1)
+        def _():
+            for copy in copies:
+                copy.wait()
+
+
+def ffn(rows, grads, scale, gate_w, up_w, down_w, start=0, total=0, base=(), into=(), flipped=False, carry=(), number=None):
     count, groups = scale.shape
     width = rows.shape[1]
     hidden = down_w.shape[0]
@@ -390,33 +544,40 @@
 
     far = pl.BlockSpec(memory_space=pl.ANY)
     return pl.pallas_call(
-        functools.partial(ffn_kernel, groups, bool(base), bool(into), flipped),
+        functools.partial(
+            ffn_kernel, groups, bool(base), bool(into), flipped, tuple(c[1:] for c in carry)
+        ),
         grid=(count // block,),
         in_specs=[at(width, first), at(width, first), at(groups, 0)]
         + [held(gate_w), held(up_w), held(down_w)]
         + [at(width, 0)] * len(base)
-        + [far] * len(into),
+        + [far] * (len(into) + len(carry)),
         out_specs=[
             at(hidden, place),
             at(2 * hidden, place),
             at(width, 0),
             at(width, 0),
             at(groups + 1, 0),
-        ],
+        ]
+        + [far] * len(carry),
         out_shape=[
             jax.ShapeDtypeStruct((total, hidden), BF16),
             jax.ShapeDtypeStruct((total, 2 * hidden), BF16),
             jax.ShapeDtypeStruct((count, width), BF16),
             jax.ShapeDtypeStruct((count, width), BF16),
             jax.ShapeDtypeStruct((count, groups + 1), F32),
-        ],
+        ]
+        + [jax.ShapeDtypeStruct((c[2], c[0].shape[1]), BF16) for c in carry],
+        scratch_shapes=[pltpu.SemaphoreType.DMA((len(carry),))] * 2 if carry else [],
         input_output_aliases={6 + len(base) + k: k for k in range(len(into))},
-        compiler_params=pltpu.CompilerParams(vmem_limit_bytes=62 << 20),
+        compiler_params=pltpu.CompilerParams(
+            vmem_limit_bytes=62 << 20, collective_id=number, has_side_effects=bool(carry)
+        ),
         cost_estimate=pl.CostEstimate(flops=0, bytes_accessed=0, transcendentals=0),
-    )(rows, grads, scale, gate_w, up_w, down_w, *base, *into)
-
-
-def line_sum(rows, width_own, depth, prepare, settle, gathered, part, came, came_two, spread, sems):
+    )(rows, grads, scale, gate_w, up_w, down_w, *base, *into, *[c[0] for c in carry])
+
+
+def line_sum(depth, prepare, settle, gathered, beside, part, came, came_two, spread, sems):
     n = lax.axis_size("tp")
     me = lax.axis_index("tp")
     chunks, _, step, _ = part.shape
@@ -529,6 +690,8 @@
         pass_sums(t)
         pass_own(t)
         pass_out(t)
+        if beside is not None:
+            beside(t)
         return carry
 
     lax.fori_loop(0, chunks + 2 * (n - 1) * depth, turn, 0)
@@ -589,9 +752,9 @@
 
 
 def attend_out_kernel(
-    chunks, step, depth, eps, attn, w_out, x, gain,
-    mixed, resid_own, inv_out,
-    part, came, came_two, spread, s0, s1, s2, s3, s4, y_send, y_recv,
+    chunks, step, depth, eps, attn, w_out, x, gain, grads,
+    mixed, resid_own, inv_out, grads_peer,
+    part, came, came_two, spread, s0, s1, s2, s3, s4, y_send, y_recv, g_send, g_recv,
 ):
     n = lax.axis_size("tp")
     me = lax.axis_index("tp")
@@ -599,6 +762,11 @@
     rows = attn.shape[0]
     other = {"ep": 1 - lax.axis_index("ep")}
     greet([other])
+    grads_copy = pltpu.make_async_remote_copy(
+        src_ref=grads.at[pl.ds(0, grads_peer.shape[0])], dst_ref=grads_peer, send_sem=g_send, recv_sem=g_recv,
+        device_id=other, device_id_type=pl.DeviceIdType.MESH,
+    )
+    grads_copy.start()
     block = max(step, min(rows, 128))
 
     def product(b, carry):
@@ -644,7 +812,7 @@
 
         peer_copy(c).start()
 
-    line_sum(rows, own, depth, prepare, settle, gathered, part, came, came_two, spread, (s0, s1, s2, s3, s4))
+    line_sum(depth, prepare, settle, gathered, None, part, came, came_two, spread, (s0, s1, s2, s3, s4))
 
     def last(c, carry):
         peer_copy(c).wait_recv()
@@ -652,37 +820,41 @@
         return carry
 
     lax.fori_loop(0, chunks, last, 0)
-
-
-def attend_out(attn, w_out, x, gain, width_own, depth=1):
+    grads_copy.wait()
+
+
+def attend_out(attn, w_out, x, gain, grads, width_own, depth=1):
     rows, width = x.shape
     chunks, step, scratch = line_scratch(rows, width_own)
     vmem = pl.BlockSpec(memory_space=pltpu.VMEM)
+    far = pl.BlockSpec(memory_space=pl.ANY)
     dma = pltpu.SemaphoreType.DMA
     return pl.pallas_call(
         functools.partial(attend_out_kernel, chunks, step, depth, EPS),
         out_shape=[
             jax.ShapeDtypeStruct((2 * rows, width), BF16),
             jax.ShapeDtypeStruct((rows, width_own), F32), jax.ShapeDtypeStruct((rows, 1), F32),
+            jax.ShapeDtypeStruct((rows // 2, width), BF16),
         ],
-        in_specs=[vmem] * 4,
-        out_specs=[vmem] * 3,
-        scratch_shapes=scratch + [dma((chunks,)), dma((chunks,))],
+        in_specs=[vmem] * 4 + [far],
+        out_specs=[vmem] * 3 + [far],
+        scratch_shapes=scratch + [dma((chunks,)), dma((chunks,)), dma, dma],
         compiler_params=pltpu.CompilerParams(collective_id=1, has_side_effects=True, vmem_limit_bytes=40 << 20),
         cost_estimate=pl.CostEstimate(flops=0, bytes_accessed=0, transcendentals=0),
-    )(attn, w_out, x, gain)
+    )(attn, w_out, x, gain, grads)
 
 
 def resid_grad_kernel(
-    chunks, step, depth, grad, grad_p, out_p, sum_egu, sum_ed, router, along, g_own, resid_own, inv_two, gain,
-    low, grad_resid, gain_grad, out_back, got_egu, got_ed,
+    chunks, step, depth, tiles, grad, grad_p, out_p, dgu, hid, both, both_grad, sgu, sd, router, along, g_own, resid_own, inv_two, gain,
+    low, grad_resid, gain_grad, out_back, sum_egu, sum_ed, sgu_x, sd_x,
     part, came, came_two, spread, s0, s1, s2, s3, s4, back, y_send, y_recv, o_send, o_recv,
-    x_send, x_recv,
+    dgu_v, hid_v, both_v, both_grad_v, sent_egu, sent_ed, came_egu, came_ed,
+    s_own, s_in, d_own, d_in, l_sem, w_send, w_recv, w_out, r_send, r_recv, r_out,
 ):
     n = lax.axis_size("tp")
     own = part.shape[3]
     rows = grad.shape[0]
-    _, x_bit, _, (_, to_x, other) = places()
+    core, x, y, (to_core, to_x, other) = places()
 
     def at(c):
         return pl.ds(pl.multiple_of(c * step, step), step)
@@ -699,22 +871,102 @@
             device_id=other, device_id_type=pl.DeviceIdType.MESH,
         )
 
-    def half_copy(source, target, k):
+    loads = [
+        pltpu.make_async_copy(source, target, l_sem.at[m])
+        for m, (source, target) in enumerate(
+            (
+                (dgu, dgu_v),
+                (both, both_v),
+                (hid, hid_v),
+                (both_grad, both_grad_v),
+                (sgu.at[pl.ds(x * s_own.shape[0], s_own.shape[0])], s_own),
+                (sd.at[pl.ds(y * d_own.shape[0], d_own.shape[0])], d_own),
+            )
+        )
+    ]
+    kinds = ((dgu_v, both_v, sent_egu, came_egu, sum_egu), (hid_v, both_grad_v, sent_ed, came_ed, sum_ed))
+
+    def sum_copies(m):
+        source, target, where = (
+            (sgu.at[pl.ds((1 - x) * s_own.shape[0], s_own.shape[0])], s_in, to_x),
+            (sd.at[pl.ds((1 - y) * d_own.shape[0], d_own.shape[0])], d_in, other),
+            (s_own, sgu_x.at[x], to_x),
+            (d_own, sd_x.at[x], to_x),
+        )[m]
         return pltpu.make_async_remote_copy(
-            src_ref=source.at[pl.ds((1 - x_bit) * target.shape[0], target.shape[0])], dst_ref=target,
-            send_sem=x_send.at[k], recv_sem=x_recv.at[k],
-            device_id=to_x, device_id_type=pl.DeviceIdType.MESH,
+            src_ref=source, dst_ref=target, send_sem=r_send.at[m], recv_sem=r_recv.at[m],
+            device_id=where, device_id_type=pl.DeviceIdType.MESH,
         )
 
-    greet([other, to_x])
-    half_copy(sum_egu, got_egu, 0).start()
-    half_copy(sum_ed, got_ed, 1).start()
+    def own_out(m):
+        return pltpu.make_async_copy((s_own, d_own)[m], (sgu_x, sd_x)[m].at[x], r_out.at[m])
+
+    def shared(m):
+        sum_copies(m).wait_recv()
+        add_rows((s_own, d_own)[m], (s_in, d_in)[m], 0, (s_own, d_own)[m].shape[0])
+        sum_copies(2 + m).start()
+        own_out(m).start()
+
+    def tile_copy(m, b):
+        return pltpu.make_async_remote_copy(
+            src_ref=kinds[m][2].at[b], dst_ref=kinds[m][3].at[b], send_sem=w_send.at[b, m], recv_sem=w_recv.at[b, m],
+            device_id=to_core, device_id_type=pl.DeviceIdType.MESH,
+        )
+
+    def tile_out(m, b):
+        tall = kinds[m][3].shape[1]
+        return pltpu.make_async_copy(
+            kinds[m][3].at[b], kinds[m][4].at[pl.ds(pl.multiple_of(b * tall, tall), tall)], w_out.at[b, m]
+        )
+
+    def tile(m, b, which):
+        left, right = kinds[m][:2]
+        tall, wide = kinds[m][3].shape[1:]
+        return mm_tn(
+            left[...] if tiles == 1 else left[:, pl.ds(pl.multiple_of(b * tall, tall), tall)],
+            right[:, pl.ds(pl.multiple_of(which * wide, wide), wide)],
+        )
+
+    def weights(t):
+        @pl.when(t == 0)
+        def _():
+            for copy in loads:
+                copy.wait()
+
+        @pl.when(t < tiles)
+        def _():
+            for m in range(2):
+                kinds[m][2][t] = tile(m, t, 1 - core).astype(BF16)
+                tile_copy(m, t).start()
+
+        @pl.when(t == tiles)
+        def _():
+            shared(0)
+
+        @pl.when(t == tiles + tiles // 2 + 1)
+        def _():
+            shared(1)
+
+        @pl.when((t >= tiles) & (t < 2 * tiles))
+        def _():
+            b = t - tiles
+            for m in range(2):
+                value = tile(m, b, core)
+                tile_copy(m, b).wait_recv()
+                kinds[m][3][b] = (value + kinds[m][3][b].astype(F32)).astype(BF16)
+                tile_out(m, b).start()
+
+    for copy in loads:
+        copy.start()
+    greet([other, to_core, to_x])
+    sum_copies(0).start()
 
     def begin(c, carry):
         peer_copy(c).start()
         return carry
 
     lax.fori_loop(0, chunks, begin, 0)
+    sum_copies(1).start()
     out_copy().start()
     gain_grad[...] = jnp.zeros_like(gain_grad)
 
@@ -737,7 +989,7 @@
         for s in range(n):
             low[at(c), s * own:(s + 1) * own] = spread[c, s]
 
-    line_sum(rows, own, depth, prepare, settle, gathered, part, came, came_two, spread, (s0, s1, s2, s3, s4))
+    line_sum(depth, prepare, settle, gathered, weights, part, came, came_two, spread, (s0, s1, s2, s3, s4))
 
     def last(c, carry):
         peer_copy(c).wait_send()
@@ -745,30 +997,47 @@
 
     lax.fori_loop(0, chunks, last, 0)
     out_copy().wait()
-    half_copy(sum_egu, got_egu, 0).wait()
-    half_copy(sum_ed, got_ed, 1).wait()
-
-
-def resid_grad(grad, grad_p, out_p, sum_egu, sum_ed, router, along, g_own, resid_own, inv_two, gain, depth=1):
+
+    def done(b, carry):
+        for m in range(2):
+            tile_copy(m, b).wait_send()
+            tile_out(m, b).wait()
+        return carry
+
+    lax.fori_loop(0, tiles, done, 0)
+    for m in range(2):
+        sum_copies(m).wait_send()
+        sum_copies(2 + m).wait()
+        own_out(m).wait()
+
+
+def resid_grad(grad, grad_p, out_p, dgu, hid, both, both_grad, sgu, sd, router, along, g_own, resid_own, inv_two, gain, depth=1):
     rows, width = grad.shape
     width_own = g_own.shape[1]
     chunks, step, scratch = line_scratch(rows, width_own)
+    hidden = hid.shape[1]
+    tiles = 11 if hidden % (11 * 128) == 0 else 1
     vmem = pl.BlockSpec(memory_space=pltpu.VMEM)
     far = pl.BlockSpec(memory_space=pl.ANY)
     dma = pltpu.SemaphoreType.DMA
     return pl.pallas_call(
-        functools.partial(resid_grad_kernel, chunks, step, depth),
+        functools.partial(resid_grad_kernel, chunks, step, depth, tiles),
         out_shape=[
             jax.ShapeDtypeStruct((rows, width), BF16), jax.ShapeDtypeStruct((rows, width_own), F32),
             jax.ShapeDtypeStruct((1, width_own), F32), jax.ShapeDtypeStruct((rows, width), BF16),
         ]
-        + [jax.ShapeDtypeStruct((v.shape[0] // 2, v.shape[1]), BF16) for v in (sum_egu, sum_ed)],
-        in_specs=[vmem] + [far] * 4 + [vmem] * 6,
-        out_specs=[vmem] * 3 + [far] * 3,
-        scratch_shapes=scratch + [pltpu.VMEM((rows, width), BF16), dma((chunks,)), dma((chunks,)), dma, dma, dma((2,)), dma((2,))],
-        compiler_params=pltpu.CompilerParams(collective_id=2, has_side_effects=True, vmem_limit_bytes=40 << 20),
+        + [jax.ShapeDtypeStruct((k * hidden, width // 2), BF16) for k in (2, 1)]
+        + [jax.ShapeDtypeStruct((2, v.shape[0] // 2, v.shape[1]), BF16) for v in (sgu, sd)],
+        in_specs=[vmem] + [far] * 8 + [vmem] * 6,
+        out_specs=[vmem] * 3 + [far] * 5,
+        scratch_shapes=scratch + [pltpu.VMEM((rows, width), BF16), dma((chunks,)), dma((chunks,)), dma, dma]
+        + [pltpu.VMEM(v.shape, BF16) for v in (dgu, hid, both, both_grad)]
+        + [pltpu.VMEM((tiles, k * hidden // tiles, width // 2), BF16) for k in (2, 1, 2, 1)]
+        + [pltpu.VMEM((v.shape[0] // 2, v.shape[1]), BF16) for v in (sgu, sgu, sd, sd)]
+        + [dma((6,)), dma((tiles, 2)), dma((tiles, 2)), dma((tiles, 2)), dma((4,)), dma((4,)), dma((2,))],
+        compiler_params=pltpu.CompilerParams(collective_id=2, has_side_effects=True, vmem_limit_bytes=63 << 20),
         cost_estimate=pl.CostEstimate(flops=0, bytes_accessed=0, transcendentals=0),
-    )(grad, grad_p, out_p, sum_egu, sum_ed, router, along, g_own, resid_own, inv_two, gain)
+    )(grad, grad_p, out_p, dgu, hid, both, both_grad, sgu, sd, router, along, g_own, resid_own, inv_two, gain)
 
 
 def body(
@@ -812,7 +1081,8 @@
     near = bit_of("dp", 1)
 
     def pair_send(left, right, columns, used=None):
-        return swap(weight_half(left, right, 1 - near, columns, rows=used), "dp", 1)
+        sent = weight_half(left, right, 1 - near, columns, rows=used)
+        return sent, swap(sent, "dp", 1)
 
     def pair_keep(left, right, columns, got, used=None):
         return weight_half(left, right, near, columns, got, rows=used)
@@ -823,6 +1093,12 @@
     x_link, y_link = far[0], line[0]
 
     def over_tp(value):
+        if tp_count <= 4:
+            others = [
+                lax.ppermute(value, "tp", [(i, (i + d) % tp_count) for i in range(tp_count)])
+                for d in range(1, tp_count)
+            ]
+            return sum(others, value)
         bit = 1
         while bit < tp_count:
             value = value + swap(value, "tp", bit)
@@ -842,9 +1118,6 @@
     gain_one = packed[rows].astype(F32)
     gain_two = packed[rows + 1].astype(F32)
     grad_rows = lax.all_gather(after(output_gradient, packed), "tp", axis=1, tiled=True)
-    part = rows // 2
-    grad_peer_a = swap(grad_rows[:part], "ep", 1)
-    grad_peer_b = swap(grad_rows[part:], "ep", 1)
     route_hot = jnp.sum(
         (routes[:, :, None] == jnp.arange(experts, dtype=jnp.int32)[None, None, :]).astype(F32),
         axis=1,
@@ -891,8 +1164,8 @@
     attn_rows = attended.astype(BF16).reshape(rows, heads * HD)
     log_norm = row_top + jnp.log(row_total)
 
-    both, resid_own, inv_two = attend_out(
-        attn_rows, w_output, after(packed[:rows], grad_peer_a), gain_two[None, :], width_own
+    both, resid_own, inv_two, grad_peer_a = attend_out(
+        attn_rows, w_output, packed[:rows], gain_two[None, :], grad_rows, width_own
     )
     mixed = both[:rows]
 
@@ -909,22 +1182,28 @@
     def own_experts(value):
         return lax.dynamic_slice_in_dim(value, ep_rank * experts_own, experts_own, 1)
 
-    hid_s, dgu_s, out_s, grad_s, small_s = ffn(
-        both, grad_rows, switch, shared_gate, shared_up, shared_down
-    )
-    both_grad = jnp.concatenate([grad_rows, grad_peer_a, after(grad_peer_b, grad_s)], axis=0)
-    got_sgu = pair_send(both, after(dgu_s, both_grad), False, rows)
-    got_sd = pair_send(hid_s, after(grad_rows, got_sgu), True)
-    sum_sgu = pair_keep(both, dgu_s, False, after(got_sgu, got_sd), rows)
-    got_sgu = reduce_send(sum_sgu, *x_link)
+    hid_s, dgu_s, out_s, grad_s, small_s, grad_peer_b = ffn(
+        both,
+        grad_rows,
+        switch,
+        shared_gate,
+        shared_up,
+        shared_down,
+        carry=[(grad_rows, 2, rows // 2, rows // 2, 0)],
+        number=4,
+    )
+    both_grad = jnp.concatenate([grad_rows, grad_peer_a, grad_peer_b], axis=0)
+    sent, got_sgu = pair_send(both, dgu_s, False, rows)
+    sent, got_sd = pair_send(hid_s, after(grad_rows, sent), True)
+    sum_sgu = pair_keep(both, after(dgu_s, sent, both_grad), False, got_sgu, rows)
     sum_sd = pair_keep(hid_s, after(grad_rows, sum_sgu), True, got_sd)
-    got_sd = reduce_send(sum_sd, *y_link)
+    quarter = sum_sgu.shape[0] // 4
 
     hidden_width = experts_own * expert_width
     gate_w = jnp.transpose(expert_gate, (0, 2, 1)).reshape(hidden_width, width)
     up_w = jnp.transpose(expert_up, (0, 2, 1)).reshape(hidden_width, width)
     down_w = expert_down.reshape(hidden_width, width)
-    hid_p, dgu_p, out_p, grad_p, small_p = ffn(
+    hid_p, dgu_p, out_p, grad_p, small_p, got_sgu_a, got_sd = ffn(
         both,
         after(both_grad, sum_sd),
         own_experts(combine_peer),
@@ -934,9 +1213,14 @@
         start=rows,
         total=2 * rows,
         flipped=True,
+        carry=[
+            (sum_sgu, 2, quarter, 0, 2 * quarter),
+            (sum_sd, 1, sum_sd.shape[0] // 2, 0, sum_sd.shape[0] // 2),
+        ],
+        number=5,
     )
     small_back = swap(small_p.T, "ep", 1)
-    hid_e, dgu_e, out_e, grad_e, small_e = ffn(
+    hid_e, dgu_e, out_e, grad_e, small_e, got_sgu_b = ffn(
         both,
         both_grad,
         after(own_experts(combine), grad_p),
@@ -947,11 +1231,10 @@
         base=(out_s, grad_s),
         into=(hid_p, dgu_p),
         flipped=True,
-    )
-    sum_sgu = reduce_add(sum_sgu, after(got_sgu, grad_e), *x_link)
-    got_sgu = reduce_send(sum_sgu, *y_link)
-    sum_sd = reduce_add(sum_sd, after(got_sd, sum_sgu), *y_link)
-    got_sd = reduce_send(sum_sd, *x_link)
+        carry=[(sum_sgu, 2, quarter, quarter, 2 * quarter)],
+        number=6,
+    )
+    got_sgu = jnp.concatenate([got_sgu_a, got_sgu_b], axis=0)
 
     first = ep_rank == 0
     small_e = small_e.T
@@ -966,20 +1249,7 @@
         ],
         axis=0,
     )
-    got_small = swap(small, "tp", 1)
-    got_egu = pair_send(after(dgu_e, sum_sd), both, True)
-    small = small + after(got_small, got_egu)
-    bit = 2
-    got_ed = pair_send(hid_e, after(both_grad, small), True)
-    sum_egu = dgu_e
-    while bit < tp_count:
-        got_small = swap(small, "tp", bit)
-        if bit == 2:
-            sum_egu = pair_keep(dgu_e, both, True, after(got_egu, got_ed))
-        small = small + after(got_small, sum_egu)
-        bit *= 2
-    sum_ed = pair_keep(hid_e, after(both_grad, sum_egu), True, got_ed)
-    small = after(small.T, sum_ed)
+    small = over_tp(small).T
     grad_prob = small[:, :experts] * route_hot
     grad_switch = small[:, experts : experts + 1]
     along = small[:, experts + 1 : experts + 2]
@@ -997,14 +1267,21 @@
         + jnp.sum(grad_logits.astype(F32) * logits, axis=1, keepdims=True)
         + grad_slogit.astype(F32) * switch_logit
     )
-    sum_sgu = reduce_add(sum_sgu, after(got_sgu, sum_ed), *y_link)
-    sum_sd = reduce_add(sum_sd, after(got_sd, sum_sgu), *x_link)
-    resid_low, grad_resid, grad_gain_two, out_back, got_egu, got_ed = resid_grad(
-        after(grad_e, sum_sd),
+    grad_router = mm_tn(grad_logits, mixed)
+    grad_switch_w = mm_tn(grad_slogit, mixed)
+    sum_sgu = reduce_add(sum_sgu, got_sgu, *y_link)
+    sum_sd = reduce_add(sum_sd, got_sd, *x_link)
+
+    resid_low, grad_resid, grad_gain_two, out_back, sum_egu, sum_ed, sgu_x, sd_x = resid_grad(
+        grad_e,
         grad_p,
         out_p,
-        sum_egu,
-        sum_ed,
+        dgu_e,
+        hid_e,
+        both,
+        both_grad,
+        sum_sgu,
+        sum_sd,
         router_part,
         along,
         output_gradient,
@@ -1013,57 +1290,39 @@
         norm_ffn.astype(F32)[None, :],
     )
 
-    grad_attn = mm_nt(resid_low, w_output).astype(BF16).reshape(rows, heads, HD)
-    probs = jnp.exp(masked_scores() - log_norm)
-    grad_probs = jnp.einsum("qhd,khd->hqk", grad_attn, value_rows, preferred_element_type=F32)
-    grad_scores = (
-        probs * (grad_probs - jnp.sum(probs * grad_probs, axis=2, keepdims=True))
-    ).astype(BF16)
-    grad_keys = (
-        jnp.einsum("hqk,qhd->khd", grad_scores, query, preferred_element_type=F32) * score_scale
-    )
-    grad_values = jnp.einsum(
-        "hqk,qhd->khd", probs.astype(BF16), grad_attn, preferred_element_type=F32
-    )
-    later = lax.ppermute(
-        jnp.stack([grad_keys[:rows], grad_values[:rows]]).astype(BF16), "ep", back
-    )
-    grad_query = (
-        jnp.einsum("hqk,khd->qhd", grad_scores, key_rows, preferred_element_type=F32) * score_scale
-    )
-    got_wo = pair_send(after(attn_rows, grad_keys, grad_values), resid_low, True)
-    sum_egu = reduce_add(sum_egu, after(got_egu, got_wo), *x_link)
-    sum_ed = reduce_add(sum_ed, after(got_ed, sum_egu), *x_link)
-    sum_wo = pair_keep(after(attn_rows, sum_ed), resid_low, True, got_wo)
-    grad_router = mm_tn(after(grad_logits, sum_wo), mixed)
-    grad_switch_w = mm_tn(grad_slogit, mixed)
     flat = jnp.concatenate(
         [grad_gain_two.reshape(-1), grad_router.reshape(-1), grad_switch_w.reshape(-1)]
     ).reshape(-1, 128)
-    ffn_part = (out_e.astype(F32) + after(out_back, sum_wo).astype(F32)).astype(BF16)
-    ffn_own = lax.psum_scatter(ffn_part, "tp", scatter_dimension=1, tiled=True)
-    later = after(later, sum_wo, ffn_part, flat).astype(F32)
-    grad_key = grad_keys[rows:] + later[0]
-    grad_value = grad_values[rows:] + later[1]
-    shape = (rows, heads * HD)
-    grad_qpre = rotate(grad_query, cos_table, -sin_table).astype(BF16).reshape(shape)
-    grad_kpre = rotate(grad_key, cos_table, -sin_table).astype(BF16).reshape(shape)
-    grad_vpre = grad_value.astype(BF16).reshape(shape)
-    grad_qkv = jnp.concatenate([grad_qpre, grad_kpre, grad_vpre], axis=1)
-    got_qkv = pair_send(normed, grad_qkv, False)
-    grad_qkv = after(grad_qkv, got_qkv)
-    sum_qkv = pair_keep(normed, grad_qkv, False, got_qkv)
-    row_part = jnp.sum(
-        grad_qpre.astype(F32) * q_pre
-        + grad_kpre.astype(F32) * k_pre
-        + grad_vpre.astype(F32) * v_pre,
-        axis=1,
-    )
-    grad_normed = (
-        mm_nt(after(grad_qpre, sum_qkv), w_query)
-        + mm_nt(grad_kpre, w_key)
-        + mm_nt(grad_vpre, w_value)
-    ).astype(BF16)
+    qkv = heads * HD
+    inner = shared_gate.shape[1]
+    ffn_part = (out_e.astype(F32) + out_back.astype(F32)).astype(BF16)
+    ffn_own = lax.psum_scatter(
+        ffn_part, "tp", scatter_dimension=1, tiled=True
+    )
+    flat = after(flat, ffn_part)
+    sgu_f, sd_f, egu_f, ed_f, qkv_f, wo_f, flat, grad_normed, row_part = tail(
+        sgu_x,
+        sd_x,
+        sum_egu,
+        sum_ed,
+        flat,
+        normed,
+        w_query,
+        w_key,
+        w_value,
+        attn_rows,
+        resid_low,
+        w_output,
+        query.reshape(rows, qkv),
+        key_rows.reshape(2 * rows, qkv),
+        value_rows.reshape(2 * rows, qkv),
+        log_norm[:, :, 0].T,
+        query_seg[:, None],
+        key_seg[None, :],
+        jnp.concatenate([cos_table, cos_table], axis=1),
+        jnp.concatenate([sin_table, -sin_table], axis=1),
+    )
+
     extra = max(1, rows // width_own)
     below = jnp.tile(row_part.reshape(extra, -1), (1, tp_count)).astype(BF16)
     below = jnp.pad(below, ((0, -extra % 16), (0, 0)))
@@ -1071,11 +1330,6 @@
         jnp.concatenate([grad_normed, below], axis=0), "tp", scatter_dimension=1, tiled=True
     ).astype(F32)
 
-    qkv = heads * HD
-    inner = shared_gate.shape[1]
-    sgu_f, sd_f, egu_f, ed_f, qkv_f, wo_f, flat = sums(
-        sum_sgu, sum_sd, sum_egu, sum_ed, after(sum_qkv, grad_normed), sum_wo, flat
-    )
     sg_grad, su_grad = widen(sgu_f, (inner, inner))
     (sd_grad,) = widen(sd_f)
     (eg_grad,) = widen(egu_f, kinds=2, kind=0)
@@ -1085,7 +1339,7 @@
     (wo_grad,) = widen(wo_f)
 
     x_own = tokens.astype(F32)
-    normed_own = after(normed_own, flat)
+    normed_own = after(normed_own, sg_grad, sd_grad, eg_grad, eu_grad, ed_grad)
     row_total = normed_own[rows : rows + extra].reshape(rows, 1)
     normed_own = normed_own[:rows]
     grad_tokens = (

time: 940 us -> 898 us (0.955)
  Pallas kernels: 561 us -> 625 us
  local copies, waits for them, and re-layouts: 86.2 us -> 45.4 us
  matrix products: 45.2 us -> 23.2 us
  other arithmetic: 68.8 us -> 52 us
  waiting for transfers between devices: 134 us -> 119 us
  starting transfers between devices: 21.1 us -> 11.7 us
    pallas_call x2, Pallas kernels: 293 us -> 366 us  [the longest x1 249 us: tail(): pl.pallas_call(functools.partial(tail_kernel, 1.0 / math.sqrt(HD)), out_s...]
    ppermute x19 -> x7, waiting for transfers between devices: 57.1 us -> 0.68 us  [swap(): return lax.ppermute(value, axis, [(i, i ^ bit) for i in range(count)])]
    pallas_call x12 -> x4, Pallas kernels: 68 us -> 24.8 us  [weight_half(): pl.pallas_call(functools.partial(weight_kernel, bool(extra)), grid_spec=p...]
    pallas_call x3, Pallas kernels: 88 us -> 119 us  [ffn(): pl.pallas_call(functools.partial(ffn_kernel, groups, bool(base), bool(int...]
    reduce_scatter x1, waiting for transfers between devices: 0.01 us -> 28.4 us  [body(): ffn_own = lax.psum_scatter(ffn_part, 'tp', scatter_dimension=1, tiled=True)]
    unnamed x232 -> x136, local copies, waits for them, and re-layouts: 48.8 us -> 28.3 us
    dot_general x4 -> x0, matrix products: 15.6 us -> none  [the longest x1 7.58 us: body(): jnp.einsum('qhd,khd->hqk', grad_attn, value_rows, preferred_element_type=...]
    ppermute x19 -> x7, starting transfers between devices: 14.7 us -> 4.04 us  [swap(): return lax.ppermute(value, axis, [(i, i ^ bit) for i in range(count)])]
  transfers between devices with their start and end apart: 25 -> 15, of which waited for: 11 -> 8; matrix products, arithmetic and copies ran while one was open for 12% -> 7% of each run, Pallas kernels for 45% -> 10%
where the time goes in v4:
time: 898 us; the launch traced here: 891 us
  Pallas kernels  625 us (70%)
  waiting for transfers between devices  119 us (13%)
  other arithmetic  52 us (6%)
  local copies, waits for them, and re-layouts  45.4 us (5%)
  matrix products  23.2 us (3%)
  between operations  14.8 us (2%)
  starting transfers between devices  11.7 us (1%)
    pallas_call x1, Pallas kernels, tail(): pl.pallas_call(functools.partial(tail_kernel, 1.0 / math.sqrt(HD)), out_s...  249 us
    pallas_call x3, Pallas kernels, ffn(): pl.pallas_call(functools.partial(ffn_kernel, groups, bool(base), bool(int...  119 us
    pallas_call x1, Pallas kernels, resid_grad(): pl.pallas_call(functools.partial(resid_grad_kernel, chunks, step, depth,...  117 us
    pallas_call x1, Pallas kernels, attend_out(): pl.pallas_call(functools.partial(attend_out_kernel, chunks, step, depth,...  76.2 us
    all_gather x1, waiting for transfers between devices, body(): packed = lax.all_gather(packed, 'tp', axis=1, tiled=True)  48.1 us
    pallas_call x7, Pallas kernels, widen(): pl.pallas_call(widen_kernel, grid=grid, in_specs=[source], out_specs=spec...  37.9 us
    reduce_scatter x1, waiting for transfers between devices, body(): ffn_own = lax.psum_scatter(ffn_part, 'tp', scatter_dimension=1, tiled=True)  28.4 us
    unnamed x136, local copies, waits for them, and re-layouts  28.3 us
  transfers between devices with their start and end apart: 15, of which 8 were waited for; matrix products, arithmetic and copies ran while one was open for 7% of the time, Pallas kernels for 10%

profile of v4, /device:TPU:0, one launch (start us, length us, event | category | flops | bytes accessed | tf_op | source)
XLA Modules:
  0.0 891.1 jit_solution(2279281346972932111)
XLA Ops:
  8.7 2.0 maximum_maximum_fusion
  10.8 1.9 fusion.39
  12.7 48.1 %all-gather.3.cloned.1.call-done = bf16[528,2048]{1,0:T(8,128)(2,1)} async-done(((bf16[528,512]{1,0:T(8,128)(2,1)}), bf16[528,2048]{1,0:T(8,128)(2,1)}) %all-gather.3.cloned.1.call-update) | async-done | bytes 2162704 | tf_op jit(solution)/shard_map/all_gather | solution.py:1116
  60.8 2.2 fusion.3
  64.7 1.3 copy-done.22
  67.4 1.3 copy.172
  68.7 1.3 copy.171
  70.0 3.6 fusion.59
  73.7 1.3 copy.173
  76.3 3.5 convolution_convert_fusion
  80.6 3.9 multiply_subtract_fusion.1
  84.5 1.3 pad_maximum_fusion
  85.8 4.9 collective-permute-start
  92.1 1.5 slice.110.x
  94.0 18.0 %collective-permute-done = bf16[2,512,4,128]{3,1,2,0:T(8,128)(2,1)} collective-permute-done((bf16[2,512,4,128]{3,1,2,0:T(8,128)(2,1)}, bf16[2,512,4,128]{3,1,2,0:T(8,128)(2,1)}, u32[]{:S(2)}, u32[]{:S(2)}) %collective-permute-start) | collective-permute-done | bytes 1048608 | tf_op jit(solution)/shard_map/ppermute | solution.py:1139
  112.0 2.4 fusion.51
  114.4 2.2 fusion
  116.6 2.5 fusion.1
  119.1 3.9 fusion.18
  124.2 1.8 copy-done.8
  126.0 1.6 copy-done.9
  127.6 76.2 %shard_map.297 = (bf16[1024,2048]{1,0:T(8,128)(2,1)S(1)}, f32[512,512]{1,0:T(8,128)S(1)}, f32[512,1]{1,0:T(8,128)S(1)}, bf16[256,2048]{1,0:T(8,128)(2,1)S(1)}) custom-call(bf16[512,512]{1,0:T(8,128)(2,1)S(1)} %copy.170.attn, bf16[512,2048]{1,0:T(8,128)(2,1)S(1)} %copy-done.8, bf16[512,2048]{1,0:T(8,128)(2,1)S(1)} %copy-done.9, ...), custom_call_target="tpu_custom_call" | custom-call | tf_op jit(solution)/shard_map/pallas_call | solution.py:832
  203.8 2.0 copy-done.1
  207.3 31.8 %shard_map.298 = (bf16[512,1408]{1,0:T(8,128)(2,1)}, bf16[512,2816]{1,0:T(8,128)(2,1)}, bf16[512,2048]{1,0:T(8,128)(2,1)}, bf16[512,2048]{1,0:T(8,128)(2,1)}, f3...) custom-call(bf16[1024,2048]{1,0:T(8,128)(2,1)} %copy-done.1, ...), custom_call_target="tpu_custom_call" | custom-call | tf_op jit(solution)/shard_map/pallas_call | solution.py:546
  239.2 1.8 copy-done.6
  241.0 7.1 shard_map.299
  251.9 2.3 copy_bitcast_fusion.3.query
  254.2 3.3 shard_map.300
  259.6 2.3 fusion.56
  262.0 1.5 copy.163
  263.5 1.5 copy.165
  267.9 1.5 constant_dynamic-update-slice_fusion.2
  274.3 1.9 dynamic-slice_multiply_fusion.refs_2_
  276.2 1.8 copy-done.7
  278.0 8.8 shard_map.301.refs_6_.refs_10_
  286.9 5.6 shard_map.302.refs_7_
  292.5 44.4 %shard_map.303 = (bf16[1024,1408]{1,0:T(8,128)(2,1)}, bf16[1024,2816]{1,0:T(8,128)(2,1)}, bf16[512,2048]{1,0:T(8,128)(2,1)}, bf16[512,2048]{1,0:T(8,128)(2,1)}, ...) custom-call(bf16[1024,2048]{1,0:T(8,128)(2,1)} %copy-done.1, ...), custom_call_target="tpu_custom_call" | custom-call | tf_op jit(solution)/shard_map/pallas_call | solution.py:546
  337.4 43.1 %shard_map.304 = (bf16[1024,1408]{1,0:T(8,128)(2,1)}, bf16[1024,2816]{1,0:T(8,128)(2,1)}, bf16[512,2048]{1,0:T(8,128)(2,1)}, bf16[512,2048]{1,0:T(8,128)(2,1)}, ...) custom-call(bf16[1024,2048]{1,0:T(8,128)(2,1)} %copy-done.1, ...), custom_call_target="tpu_custom_call", output_to_operand_aliasing={{0}: (8, {}), {1}: (9, {})} | custom-call | tf_op jit(solution)/shard_map/pallas_call | solution.py:546
  380.5 5.1 add_convert_fusion.sgu
  386.2 1.9 collective-permute-start.7
  388.8 1.7 add_convert_fusion.2.sd
  390.5 4.4 collective-permute-done.7
  395.0 13.6 %collective-permute-done.6 = f32[10,512]{0,1:T(8,128)S(1)} collective-permute-done((f32[10,512]{0,1:T(8,128)S(1)}, f32[10,512]{0,1:T(8,128)S(1)}, u32[]{:S(2)}, u32[]{:S(2)}) %collective-permute-start.6) | collective-permute-done | bytes 20512 | tf_op jit(solution)/shard_map/ppermute | solution.py:1098
  409.7 2.0 fusion.10
  411.7 2.0 fusion.19
  415.8 117.4 %shard_map.305 = (bf16[512,2048]{1,0:T(8,128)(2,1)}, f32[512,512]{1,0:T(8,128)}, f32[1,512]{1,0:T(1,128)}, bf16[512,2048]{1,0:T(8,128)(2,1)}, bf16[2816,1024]{1,...) custom-call(bf16[512,2048]{1,0:T(8,128)(2,1)} %get-tuple-element.91.grad, ...), custom_call_target="tpu_custom_call" | custom-call | tf_op jit(solution)/shard_map/pallas_call | solution.py:1023
  533.3 4.5 add_convert_fusion.1
  538.4 249.0 %shard_map.306 = (bf16[2,2,2,256,2816]{4,3,2,1,0:T(8,128)(2,1)}, bf16[2,2,2,352,1024]{4,3,2,1,0:T(8,128)(2,1)}, bf16[2,2,1408,1024]{3,2,1,0:T(8,128)(2,1)}, bf16...) custom-call(bf16[2,256,2816]{2,1,0:T(8,128)(2,1)} %get-tuple-element, ...), custom_call_target="tpu_custom_call" | custom-call | tf_op jit(solution)/shard_map/pallas_call | solution.py:324
  788.6 3.2 fusion.7
  792.4 4.7 copy-done.5
  797.1 5.7 shard_map.309
  802.8 5.5 shard_map.310
  809.1 8.3 shard_map.307
  817.4 5.6 shard_map.308
  823.8 5.2 shard_map.311
  829.1 5.6 reduce-scatter.5.cloned.1.call-done
  835.9 1.4 fusion.25
  838.5 1.5 collective-permute-start.9
  840.6 3.2 copy-done.10
  843.8 5.2 shard_map.312
  849.0 2.1 shard_map.313
  851.8 28.4 %reduce-scatter.3.cloned.1.call-done = bf16[512,512]{1,0:T(8,128)(2,1)} async-done(((bf16[512,2048]{1,0:T(8,128)(2,1)}), bf16[512,512]{1,0:T(8,128)(2,1)}) %reduce-scatter.3.cloned.1.call-update) | async-done | bytes 524304 | tf_op jit(solution)/shard_map/reduce_scatter | solution.py:1299
  880.2 1.5 collective-permute-start.10
  881.7 2.0 add_convert_fusion.3
  (220 shorter events, 38.1 us)
Async XLA Ops:
  7.2 251.6 %copy-start = (bf16[2048,8]{0,1:T(8,128)(2,1)S(1)}, bf16[2048,8]{0,1:T(8,128)(2,1)}, u32[]{:S(2)}) copy-start(bf16[2048,8]{0,1:T(8,128)(2,1)} %param.25) | copy-start | bytes 98308
  7.2 53.6 %all-gather.3.cloned.1.call-start = ((), (), s32[]{:S(2)}) async-start(), calls=%async_computation.2 | async-start | bytes 2703360 | tf_op jit(solution)/shard_map/all_gather | solution.py:1116
  10.7 101.2 %all-gather.5.cloned.1.call-start = ((), (), s32[]{:S(2)}) async-start(), calls=%async_computation.3 | async-start | bytes 2621440 | tf_op jit(solution)/shard_map/all_gather | solution.py:1120
  60.8 3.3 copy-start.20
  63.1 771.6 %reduce-scatter.5.cloned.1.call-start = ((), (), s32[]{:S(2)}) async-start(), calls=%async_computation.5 | async-start | bytes 2703360 | tf_op jit(solution)/shard_map/reduce_scatter | solution.py:1329
  63.1 2.8 copy-start.33
  80.6 10.1 %copy-start.53 = (s32[1024]{0:T(1024)S(1)}, s32[1024]{0:T(1024)}, u32[]{:S(2)}) copy-start(s32[1024]{0:T(1024)} %param.34) | copy-start | bytes 12292
  80.6 10.1 %copy-start.50 = (bf16[2048]{0:T(1024)(128)(2,1)S(1)}, bf16[2048]{0:T(1024)(128)(2,1)}, u32[]{:S(2)}) copy-start(bf16[2048]{0:T(1024)(128)(2,1)} %param.26) | copy-start | bytes 12292
  84.5 9.1 %copy-start.23 = (bf16[512,4,64]{2,0,1:T(8,128)(2,1)}, bf16[512,4,64]{2,0,1:T(8,128)(2,1)S(1)}, u32[]{:S(2)}) copy-start(bf16[512,4,64]{2,0,1:T(8,128)(2,1)S(1)} %get-tuple-element.136) | copy-start | bytes 786436
  84.5 9.1 %copy-start.25 = (bf16[512,4,64]{2,0,1:T(8,128)(2,1)}, bf16[512,4,64]{2,0,1:T(8,128)(2,1)S(1)}, u32[]{:S(2)}) copy-start(bf16[512,4,64]{2,0,1:T(8,128)(2,1)S(1)} %get-tuple-element.137) | copy-start | bytes 786436
  85.8 26.2 %collective-permute-start = (bf16[2,512,4,128]{3,1,2,0:T(8,128)(2,1)}, bf16[2,512,4,128]{3,1,2,0:T(8,128)(2,1)}, u32[]{:S(2)}, u32[]{:S(2)}) collective-permute-start(bf16[2,512,4,128]{3,1,2,0:T(8,128)(2,1)} %pad_maximum_fusion), channel_id=1, source_target_pairs={{0,4},{1,5},{2,6},{3,7},{8,12},{9,13},{10,14},{11,15},{16,20},{17,... | collective-permute-start | bytes 3145736 | tf_op jit(solution)/shard_map/ppermute | solution.py:1139
  90.8 3.1 copy-start.48
  93.6 20.8 %copy-start.35 = (pred[512,1024]{1,0:T(8,128)(4,1)S(1)}, pred[512,1024]{1,0:T(8,128)(4,1)}, u32[]{:S(2)}) copy-start(pred[512,1024]{1,0:T(8,128)(4,1)} %compare_and_fusion) | copy-start | bytes 1572868
  93.6 20.8 %copy-start.38 = (bf16[512,4,64]{2,0,1:T(8,128)(2,1)S(1)}, bf16[512,4,64]{2,0,1:T(8,128)(2,1)}, u32[]{:S(2)}) copy-start(bf16[512,4,64]{2,0,1:T(8,128)(2,1)} %get-tuple-element.154) | copy-start | bytes 786436
  93.6 20.8 %copy-start.39 = (bf16[512,4,64]{2,0,1:T(8,128)(2,1)S(1)}, bf16[512,4,64]{2,0,1:T(8,128)(2,1)}, u32[]{:S(2)}) copy-start(bf16[512,4,64]{2,0,1:T(8,128)(2,1)} %get-tuple-element.155) | copy-start | bytes 786436
  119.1 5.1 copy-start.3
  124.2 79.6 %copy-start.13 = (bf16[512,512]{1,0:T(8,128)(2,1)}, bf16[512,512]{1,0:T(8,128)(2,1)S(1)}, u32[]{:S(2)}) copy-start(bf16[512,512]{1,0:T(8,128)(2,1)S(1)} %copy.170.attn) | copy-start | bytes 1572868
  203.8 2.6 copy-start.14
  203.8 35.4 %copy-start.19 = (f32[512,1]{1,0:T(8,128)}, f32[512,1]{1,0:T(8,128)S(1)}, u32[]{:S(2)}) copy-start(f32[512,1]{1,0:T(8,128)S(1)} %get-tuple-element.102.inv_two) | copy-start | bytes 6148
  241.0 7.1 copy-start.49
  241.0 8.5 copy-start.51
  241.0 9.2 %copy-start.32 = (f32[512,64]{1,0:T(8,128)S(1)}, f32[512,64]{1,0:T(8,128)}, u32[]{:S(2)}) copy-start(f32[512,64]{1,0:T(8,128)} %get-tuple-element.164) | copy-start | bytes 393220
  241.0 10.0 %copy-start.31 = (f32[512,64]{1,0:T(8,128)S(1)}, f32[512,64]{1,0:T(8,128)}, u32[]{:S(2)}) copy-start(f32[512,64]{1,0:T(8,128)} %get-tuple-element.163) | copy-start | bytes 393220
  241.0 10.0 %copy-start.44 = (f32[512,64]{1,0:T(8,128)S(1)}, f32[512,64]{1,0:T(8,128)}, u32[]{:S(2)}) copy-start(f32[512,64]{1,0:T(8,128)} %get-tuple-element.162) | copy-start | bytes 393220
  248.1 6.1 copy-start.4
  248.1 28.1 %collective-permute-start.1 = (bf16[1024,2816]{1,0:T(8,128)(2,1)}, bf16[1024,2816]{1,0:T(8,128)(2,1)}, u32[]{:S(2)}, u32[]{:S(2)}) collective-permute-start(bf16[1024,2816]{1,0:T(8,128)(2,1)} %shard_map.299), channel_id=1, source_target_pairs={{0,8},{8,0},{16,24},{24,16},{1,9},{9,1},{17,25},{25,17},{2,10},{10... | collective-permute-start | bytes 17301512 | tf_op jit(solution)/shard_map/ppermute | solution.py:33
  248.2 26.0 %collective-permute-start.3 = (f32[512,8]{1,0:T(8,128)S(1)}, f32[512,8]{1,0:T(8,128)}, u32[]{:S(2)}, u32[]{:S(2)}) collective-permute-start(f32[512,8]{1,0:T(8,128)S(1)} %copy.152), channel_id=1, source_target_pairs={{0,4},{4,0},{1,5},{5,1},{2,6},{6,2},{3,7},{7,3},{8,12},{12,8},{9,1... | collective-permute-start | bytes 49160 | tf_op jit(solution)/shard_map/ppermute | solution.py:33
  249.5 4.6 copy-start.11
  254.1 3.5 copy-start.24
  254.1 3.5 copy-start.26
  254.1 4.6 copy-start.2
  257.4 29.4 %collective-permute-start.2 = (bf16[1408,1024]{1,0:T(8,128)(2,1)}, bf16[1408,1024]{1,0:T(8,128)(2,1)}, u32[]{:S(2)}, u32[]{:S(2)}) collective-permute-start(bf16[1408,1024]{1,0:T(8,128)(2,1)} %shard_map.300), channel_id=1, source_target_pairs={{0,8},{8,0},{16,24},{24,16},{1,9},{9,1},{17,25},{25,17},{2,10},{10... | collective-permute-start | bytes 8650760 | tf_op jit(solution)/shard_map/ppermute | solution.py:33
  261.8 3.6 copy-start.29
  263.4 3.0 copy-start.37
  278.0 8.8 copy-start.12
  336.9 48.7 %collective-permute-start.4 = (f32[5,512]{0,1:T(8,128)}, f32[5,512]{0,1:T(8,128)S(1)}, u32[]{:S(2)}, u32[]{:S(2)}) collective-permute-start(f32[5,512]{0,1:T(8,128)} %bitcast.163), channel_id=1, source_target_pairs={{0,4},{4,0},{1,5},{5,1},{2,6},{6,2},{3,7},{7,3},{8,12},{12,8},{9,1... | collective-permute-start | bytes 30728 | tf_op jit(solution)/shard_map/ppermute | solution.py:33
  380.5 5.1 copy-start.42
  380.5 5.1 copy-start.46
  380.5 8.3 copy-start.40
  385.6 3.2 copy-start.21
  386.2 8.7 collective-permute-start.7
  388.2 20.4 %collective-permute-start.6 = (f32[10,512]{0,1:T(8,128)S(1)}, f32[10,512]{0,1:T(8,128)S(1)}, u32[]{:S(2)}, u32[]{:S(2)}) collective-permute-start(f32[10,512]{0,1:T(8,128)S(1)} %pad_maximum_fusion.3), channel_id=1, source_target_pairs={{0,2},{1,3},{2,0},{3,1},{4,6},{5,7},{6,4},{7,5},{8,10},{9,11},{10,... | collective-permute-start | bytes 61448 | tf_op jit(solution)/shard_map/ppermute | solution.py:1098
  388.2 20.4 %collective-permute-start.5 = (f32[10,512]{0,1:T(8,128)S(1)}, f32[10,512]{0,1:T(8,128)S(1)}, u32[]{:S(2)}, u32[]{:S(2)}) collective-permute-start(f32[10,512]{0,1:T(8,128)S(1)} %pad_maximum_fusion.3), channel_id=1, source_target_pairs={{0,1},{1,2},{2,3},{3,0},{4,5},{5,6},{6,7},{7,4},{8,9},{9,10},{10,1... | collective-permute-start | bytes 61448 | tf_op jit(solution)/shard_map/ppermute | solution.py:1098
  388.8 20.5 %copy-start.30 = (f32[512,1]{1,0:T(8,128)S(1)}, f32[512,1]{1,0:T(8,128)}, u32[]{:S(2)}) copy-start(f32[512,1]{1,0:T(8,128)} %copy.149.refs_2_) | copy-start | bytes 6148
  388.8 20.5 %copy-start.45 = (f32[512,1]{1,0:T(8,128)S(1)}, f32[512,1]{1,0:T(8,128)}, u32[]{:S(2)}) copy-start(f32[512,1]{1,0:T(8,128)} %copy.158) | copy-start | bytes 6148
  533.2 4.5 copy-start.54
  791.8 88.4 %reduce-scatter.3.cloned.1.call-start = ((), (), s32[]{:S(2)}) async-start(), calls=%async_computation.4 | async-start | bytes 2621440 | tf_op jit(solution)/shard_map/reduce_scatter | solution.py:1299
  792.4 4.7 copy-start.5
  797.1 11.3 %slice-start = ((s8[11534336]{0:T(1024)(128)(4,1)}), s8[4194304]{0:T(1024)(128)(4,1)S(1)}, s32[]{:S(2)}) async-start(s8[11534336]{0:T(1024)(128)(4,1)} %bitcast.112), calls=%async_computation.6 | async-start | bytes 8388608
  797.1 11.3 %slice-start.1 = ((s8[11534336]{0:T(1024)(128)(4,1)}), s8[4194304]{0:T(1024)(128)(4,1)S(1)}, s32[]{:S(2)}) async-start(s8[11534336]{0:T(1024)(128)(4,1)} %bitcast.112), calls=%async_computation.7 | async-start | bytes 8388608
  802.8 6.2 slice-start.2
  808.4 9.0 %slice-start.5 = ((s8[5767168]{0:T(1024)(128)(4,1)}), s8[4194304]{0:T(1024)(128)(4,1)S(1)}, s32[]{:S(2)}) async-start(s8[5767168]{0:T(1024)(128)(4,1)} %bitcast.119), calls=%async_computation.11 | async-start | bytes 8388608
  809.1 8.3 slice-start.6
  817.4 5.7 slice-start.3
  817.4 6.4 slice-start.4
  823.8 12.1 %copy-start.34 = (bf16[512,512]{1,0:T(8,128)(2,1)S(1)}, bf16[512,512]{1,0:T(8,128)(2,1)}, u32[]{:S(2)}) copy-start(bf16[512,512]{1,0:T(8,128)(2,1)} %param.18) | copy-start | bytes 1572868
  823.8 12.1 %copy-start.41 = (f32[512,512]{1,0:T(8,128)S(1)}, f32[512,512]{1,0:T(8,128)}, u32[]{:S(2)}) copy-start(f32[512,512]{1,0:T(8,128)} %get-tuple-element.113) | copy-start | bytes 3145732
  829.1 8.3 copy-start.47
  837.3 1.2 collective-permute-start.8
  838.5 41.7 %collective-permute-start.9 = (f32[4,128]{1,0:T(4,128)S(1)}, f32[4,128]{1,0:T(4,128)S(1)}, u32[]{:S(2)}, u32[]{:S(2)}) collective-permute-start(f32[4,128]{1,0:T(4,128)S(1)} %bitcast_add_fusion), channel_id=1, source_target_pairs={{0,16},{8,24},{16,0},{24,8},{1,17},{9,25},{17,1},{25,9},{2,18},{10... | collective-permute-start | bytes 6152 | tf_op jit(solution)/shard_map/ppermute | solution.py:33
  840.6 3.2 copy-start.10
  843.8 5.2 copy-start.16
  849.0 32.7 %copy-start.15 = (f32[512,512]{1,0:T(8,128)S(1)}, f32[512,512]{1,0:T(8,128)}, u32[]{:S(2)}) copy-start(f32[512,512]{1,0:T(8,128)} %copy-done.14) | copy-start | bytes 3145732
  880.2 3.6 collective-permute-start.10
  (13 other events, 23.2 us)
Sparse Core Ops, SparseCore 0:
  10.9 49.9 all-gather.2
  63.2 44.6 all-gather.4
  791.9 42.7 reduce-scatter.4
  837.0 43.2 reduce-scatter.2

commit v5 on v4

--- a/solution.py
+++ b/solution.py
@@ -93,12 +93,12 @@
 
 def tail_kernel(
     scale,
-    sgu, sd, egu, ed, flat, normed, w_query, w_key, w_value, attn,
-    low, w_out, query, keys, values, lse, query_seg, key_seg, cos, sin,
-    sgu_f, sd_f, egu_f, ed_f, qkv_f, wo_f, flat_f, grad_normed, row_part,
+    sgu, sd, egu, ed, flat, normed, w_query, w_key, w_value, attn, ffn,
+    tokens, inv_one, low, w_out, query, keys, values, lse, query_seg, key_seg, cos, sin,
+    sgu_f, sd_f, egu_f, ed_f, qkv_f, wo_f, flat_f, ffn_own, normed_own, row_total, gain_f,
     normed_v, wq_v, wk_v, wv_v, attn_v, grad_attn, grad_key, grad_value, early, came, grad_qkv,
     q_sent, q_half, q_in, q_in2, q_out, w_sent, w_half, w_in, w_in2, w_out_v,
-    e_own, e_in, d_own, d_in, flat_in, l_sem, s_sem, r_sem,
+    e_own, e_in, flat_in, ffn_in, grad_normed, normed_in, row_in, gain_in, l_sem, s_sem, r_sem,
 ):
     core, x, y, (to_core, to_x, to_y) = places()
     used = [0, 0]
@@ -129,17 +129,26 @@
     heads = query.shape[1] // HD
     mine = heads * HD
     q_rows, w_rows = q_in.shape[0], w_in.shape[0]
-    e_rows, d_rows = e_own.shape[0], d_own.shape[0]
-    greet_all((to_core, to_x, to_y))
+    e_rows = e_own.shape[0]
+    n, me = lax.axis_size("tp"), lax.axis_index("tp")
+    tp = [{"tp": (me + d) % n} for d in range(1, n)]
+    own_width = ffn_own.shape[1]
+
+    def columns(d):
+        return pl.ds(pl.multiple_of(((me + d) % n) * own_width, own_width), own_width)
+
+    greet_all([to_core, to_x, to_y] + tp)
 
     b3 = there(egu.at[pl.ds((1 - x) * e_rows, e_rows)], e_in, to_x)
-    b4 = there(ed.at[pl.ds((1 - x) * d_rows, d_rows)], d_in, to_x)
+    b6 = there(ed, ed_f.at[core, x], to_x)
     f1 = there(flat, flat_in.at[0], to_core)
+    z_ffn = [there(ffn.at[:, columns(d)], ffn_in.at[d], tp[d - 1]) for d in range(1, n)]
+    own_ffn = here(ffn.at[:, columns(0)], ffn_in.at[0])
     load_attn = here(attn, attn_v)
     load_normed = here(normed, normed_v)
     loads = [here(w_query, wq_v), here(w_key, wk_v), here(w_value, wv_v)]
     load_e = here(egu.at[pl.ds(x * e_rows, e_rows)], e_own)
-    load_d = here(ed.at[pl.ds(x * d_rows, d_rows)], d_own)
+    own_ed = here(ed, ed_f.at[core, x])
     own_s = here(sgu, sgu_f.at[core, y])
     own_sd = [here(sd.at[p], sd_f.at[core, p, y]) for p in range(2)]
 
@@ -209,7 +218,8 @@
         turned = grad_k * cos[...] + pltpu.roll(grad_k, HD // 2, 1) * sin[...]
         grad_qkv[:, mine + h * HD : mine + (h + 1) * HD] = turned.astype(BF16)
         grad_qkv[:, 2 * mine + h * HD : 2 * mine + (h + 1) * HD] = grad_v.astype(BF16)
-    row_part[...] = sums_of
+    row_in[0] = jnp.broadcast_to(sums_of, (rows, 128)).T[:8]
+    z_rows = [there(row_in.at[0], row_in.at[d], tp[d - 1]) for d in range(1, n)]
 
     load_normed.wait()
     tall = q_half.shape[0]
@@ -237,6 +247,7 @@
         + mm_nt(grad_qkv[:, mine : 2 * mine], wk_v[...])
         + mm_nt(grad_qkv[:, 2 * mine :], wv_v[...])
     ).astype(BF16)
+    z_normed = [there(grad_normed.at[:, columns(d)], normed_in.at[d], tp[d - 1]) for d in range(1, n)]
 
     load_e.wait()
     b3.wait_recv()
@@ -248,31 +259,53 @@
     a2.wait_recv()
     add_rows(w_half, w_in, y * w_rows, w_rows)
     a4 = there(w_half.at[pl.ds(y * w_rows + (1 - x) * (w_rows // 2), w_rows // 2)], w_in2, to_x)
-    load_d.wait()
-    b4.wait_recv()
-    add_rows(d_own, d_in, 0, d_rows)
     a1.wait_recv()
     add_rows(q_half, q_in, y * q_rows, q_rows)
     a3 = there(q_half.at[pl.ds(y * q_rows + (1 - x) * (q_rows // 2), q_rows // 2)], q_in2, to_x)
     cut = e_rows // 2
     b5 = there(e_own.at[pl.ds(0, cut)], egu_f.at[core, x, pl.ds(0, cut)], to_x)
     own_e = here(e_own, egu_f.at[core, x])
-    own_ed = here(d_own, ed_f.at[core, x])
     d3 = [there(sd.at[p], sd_f.at[core, p, y], to_y) for p in range(2)]
+    for copy in z_normed + z_rows:
+        copy.wait_recv()
+    total = grad_normed[:, columns(0)].astype(F32)
+    row_sum = row_in[0]
+    for d in range(1, n):
+        total = total + normed_in[d].astype(F32)
+        row_sum = row_sum + row_in[d]
+    normed_own[...] = total
+    row_total[...] = row_sum
+    gain = jnp.sum(total * tokens[...].astype(F32) * inv_one[...], axis=0, keepdims=True)
+    gain_f[...] = jnp.broadcast_to(gain, gain_f.shape)
+    g1 = there(gain_f, gain_in.at[0], to_core)
     a4.wait_recv()
     add_rows(w_half, w_in2, y * w_rows + x * (w_rows // 2), w_rows // 2, w_out_v)
     a6 = there(w_out_v, wo_f.at[core, y, x], to_x)
     own_w = here(w_out_v, wo_f.at[core, y, x])
+    g1.wait_recv()
+    g1.wait_send()
+    gain_f[...] = gain_f[...] + gain_in[0]
+    g2 = there(gain_f, gain_in.at[1], to_x)
     a3.wait_recv()
     add_rows(q_half, q_in2, y * q_rows + x * (q_rows // 2), q_rows // 2, q_out)
     a5 = there(q_out, qkv_f.at[core, y, x], to_x)
     own_q = here(q_out, qkv_f.at[core, y, x])
     b7 = there(e_own.at[pl.ds(cut, cut)], egu_f.at[core, x, pl.ds(cut, cut)], to_x)
-    b6 = there(d_own, ed_f.at[core, x], to_x)
+    own_ffn.wait()
+    for copy in z_ffn:
+        copy.wait_recv()
+    total = ffn_in[0].astype(F32)
+    for d in range(1, n):
+        total = total + ffn_in[d].astype(F32)
+    ffn_own[...] = total
     own_s.wait()
     d1.wait_recv()
     d2.wait_recv()
     c1 = there(sgu_f.at[core], sgu_f.at[core], to_core)
+    g2.wait_recv()
+    g2.wait_send()
+    gain_f[...] = gain_f[...] + gain_in[1]
+    g3 = there(gain_f, gain_in.at[2], to_y)
     a6.wait_recv()
     own_w.wait()
     a8 = there(wo_f.at[core, y], wo_f.at[core, y], to_y)
@@ -298,14 +331,17 @@
     own_ed.wait()
     b6.wait_recv()
     c6 = there(ed_f.at[core], ed_f.at[core], to_core)
+    g3.wait_recv()
+    g3.wait_send()
+    gain_f[...] = gain_f[...] + gain_in[2]
     for copy in (c1, c2, c3, c4, c5, c6):
         copy.wait_recv()
     for copy in sent:
-        if copy is not f2 and copy is not f3:
+        if all(copy is not other for other in (f2, f3, g1, g2, g3)):
             copy.wait_send()
 
 
-def tail(sgu, sd, egu, ed, flat, normed, w_query, w_key, w_value, attn, low, w_out, query, keys, values, lse, query_seg, key_seg, cos, sin):
+def tail(sgu, sd, egu, ed, flat, normed, w_query, w_key, w_value, attn, ffn, tokens, inv_one, low, w_out, query, keys, values, lse, query_seg, key_seg, cos, sin):
     rows, width = low.shape
     mine = query.shape[1]
     heads = mine // HD
@@ -320,18 +356,20 @@
         return pltpu.VMEM(shape, kind)
 
     half_of = width // 2
+    n = lax.axis_size("tp")
     dma = pltpu.SemaphoreType.DMA
     return pl.pallas_call(
         functools.partial(tail_kernel, 1.0 / math.sqrt(HD)),
         out_shape=[
             pieces(3, *sgu.shape[1:]), pieces(3, *sd.shape[1:]),
-            pieces(2, egu.shape[0] // 2, egu.shape[1]), pieces(2, ed.shape[0] // 2, ed.shape[1]),
+            pieces(2, egu.shape[0] // 2, egu.shape[1]), pieces(2, *ed.shape),
             pieces(3, half_of // 4, 3 * mine), pieces(3, mine // 4, half_of),
-            jax.ShapeDtypeStruct(flat.shape, F32), jax.ShapeDtypeStruct((rows, width), BF16),
-            jax.ShapeDtypeStruct((rows, 1), F32),
+            jax.ShapeDtypeStruct(flat.shape, F32), jax.ShapeDtypeStruct(tokens.shape, F32),
+            jax.ShapeDtypeStruct(tokens.shape, F32), jax.ShapeDtypeStruct((8, rows), F32),
+            jax.ShapeDtypeStruct((8, tokens.shape[1]), F32),
         ],
-        in_specs=[far] * 4 + [vmem] + [far] * 5 + [vmem] * 10,
-        out_specs=[far] * 6 + [vmem] * 3,
+        in_specs=[far] * 4 + [vmem] + [far] * 6 + [vmem] * 12,
+        out_specs=[far] * 6 + [vmem] * 5,
         scratch_shapes=[
             room(rows, width), room(width, mine), room(width, mine), room(width, mine), room(rows, mine),
             room(rows, mine), room(rows, mine, kind=F32), room(rows, mine, kind=F32),
@@ -341,14 +379,15 @@
             room(mine, half_of), room(mine, half_of), room(mine // 2, half_of),
             room(mine // 4, half_of), room(mine // 4, half_of),
             room(egu.shape[0] // 2, egu.shape[1]), room(egu.shape[0] // 2, egu.shape[1]),
-            room(ed.shape[0] // 2, ed.shape[1]), room(ed.shape[0] // 2, ed.shape[1]),
-            room(3, *flat.shape, kind=F32), dma((16,)), dma((40,)), dma((40,)),
+            room(3, *flat.shape, kind=F32), room(n, *tokens.shape), room(rows, width), room(n, *tokens.shape),
+            room(n, 8, rows, kind=F32), room(3, 8, tokens.shape[1], kind=F32),
+            dma((16,)), dma((36 + heads + 3 * n,)), dma((36 + heads + 3 * n,)),
         ],
         compiler_params=pltpu.CompilerParams(
             collective_id=3, has_side_effects=True, vmem_limit_bytes=62 << 20
         ),
         cost_estimate=pl.CostEstimate(flops=0, bytes_accessed=0, transcendentals=0),
-    )(sgu, sd, egu, ed, flat, normed, w_query, w_key, w_value, attn, low, w_out, query, keys, values, lse, query_seg, key_seg, cos, sin)
+    )(sgu, sd, egu, ed, flat, normed, w_query, w_key, w_value, attn, ffn, tokens, inv_one, low, w_out, query, keys, values, lse, query_seg, key_seg, cos, sin)
 
 
 def widen_kernel(source, *outputs):
@@ -361,7 +400,7 @@
         start += width
 
 
-def widen(value, widths=(), kinds=1, kind=0):
+def widen(value, widths=(), kinds=1, kind=0, across=2):
     columns = value.shape[-1]
     if widths:
         value = value.reshape(-1, columns)
@@ -372,16 +411,16 @@
         specs = [pl.BlockSpec((step, width), lambda i: (i, 0)) for width in widths]
         shapes = [jax.ShapeDtypeStruct((rows, width), F32) for width in widths]
     else:
-        value = value.reshape(2, kinds, -1, columns)
+        value = value.reshape(across, kinds, -1, columns)
         rows = value.shape[2]
         step = rows
         while step * columns > (1 << 19) and step % 32 == 0:
             step //= 2
         steps = rows // step
         source = pl.BlockSpec((1, 1, step, columns), lambda i, c: (c, kind, i, 0))
-        grid = (steps, 2)
+        grid = (steps, across)
         specs = [pl.BlockSpec((step, columns), lambda i, c: (i, c))]
-        shapes = [jax.ShapeDtypeStruct((rows, 2 * columns), F32)]
+        shapes = [jax.ShapeDtypeStruct((rows, across * columns), F32)]
     return pl.pallas_call(
         widen_kernel,
         grid=grid,
@@ -452,7 +491,7 @@
 
 
 def ffn_kernel(groups, base, into, flipped, carry, *refs):
-    rows, grads, scale, gate_w, up_w, down_w = refs[:6]
+    rows, grads, scale, *stored = refs[:6]
     refs = refs[6:]
     if base:
         base_out, base_dx = refs[:2]
@@ -461,6 +500,17 @@
         refs = refs[2:]
     sources, refs = refs[: len(carry)], refs[len(carry) :]
     hid_ref, dgu_ref, out_ref, dx_ref, small_ref, *refs = refs
+    *refs, gate_w, up_w, down_w, w_sem = refs
+    weights = [
+        pltpu.make_async_copy(source, target, w_sem.at[m])
+        for m, (source, target) in enumerate(zip(stored, (gate_w, up_w, down_w)))
+    ]
+
+    @pl.when(pl.program_id(0) == 0)
+    def _():
+        for copy in weights:
+            copy.start()
+
     copies = []
     if carry:
         send_sem, recv_sem = refs[-2:]
@@ -481,6 +531,11 @@
             greet_all([where[link] for link in links])
             for copy in copies:
                 copy.start()
+
+    @pl.when(pl.program_id(0) == 0)
+    def _():
+        for copy in weights:
+            copy.wait()
 
     width = down_w.shape[0]
     to, back = (mm_nt, mm) if flipped else (mm, mm_nt)
@@ -539,9 +594,6 @@
     def at(n, offset):
         return pl.BlockSpec((block, n), lambda i: (i + offset, 0))
 
-    def held(a):
-        return pl.BlockSpec(a.shape, lambda i: (0, 0), pipeline_mode=pl.Buffered(1))
-
     far = pl.BlockSpec(memory_space=pl.ANY)
     return pl.pallas_call(
         functools.partial(
@@ -549,7 +601,7 @@
         ),
         grid=(count // block,),
         in_specs=[at(width, first), at(width, first), at(groups, 0)]
-        + [held(gate_w), held(up_w), held(down_w)]
+        + [far] * 3
         + [at(width, 0)] * len(base)
         + [far] * (len(into) + len(carry)),
         out_specs=[
@@ -568,7 +620,9 @@
             jax.ShapeDtypeStruct((count, groups + 1), F32),
         ]
         + [jax.ShapeDtypeStruct((c[2], c[0].shape[1]), BF16) for c in carry],
-        scratch_shapes=[pltpu.SemaphoreType.DMA((len(carry),))] * 2 if carry else [],
+        scratch_shapes=([pltpu.SemaphoreType.DMA((len(carry),))] * 2 if carry else [])
+        + [pltpu.VMEM(w.shape, BF16) for w in (gate_w, up_w, down_w)]
+        + [pltpu.SemaphoreType.DMA((3,))],
         input_output_aliases={6 + len(base) + k: k for k in range(len(into))},
         compiler_params=pltpu.CompilerParams(
             vmem_limit_bytes=62 << 20, collective_id=number, has_side_effects=bool(carry)
@@ -845,11 +899,13 @@
 
 
 def resid_grad_kernel(
-    chunks, step, depth, tiles, grad, grad_p, out_p, dgu, hid, both, both_grad, sgu, sd, router, along, g_own, resid_own, inv_two, gain,
-    low, grad_resid, gain_grad, out_back, sum_egu, sum_ed, sgu_x, sd_x,
+    chunks, step, depth, tiles, grad, grad_p, out_p, dgu, hid, both, both_grad, sgu, sd,
+    small_e, small_p, small_s, prob, hot, logits, switch, w_small, g_own, resid_own, inv_two, gain,
+    low, grad_resid, gain_grad, out_back, sum_egu, sum_ed, sgu_x, sd_x, grad_small,
     part, came, came_two, spread, s0, s1, s2, s3, s4, back, y_send, y_recv, o_send, o_recv,
     dgu_v, hid_v, both_v, both_grad_v, sent_egu, sent_ed, came_egu, came_ed,
     s_own, s_in, d_own, d_in, l_sem, w_send, w_recv, w_out, r_send, r_recv, r_out,
+    router, along, small_y, small_z, ed_in, ed_out, t_send, t_recv, e_send, e_recv, e_out,
 ):
     n = lax.axis_size("tp")
     own = part.shape[3]
@@ -913,6 +969,20 @@
             device_id=to_core, device_id_type=pl.DeviceIdType.MESH,
         )
 
+    def x_copy(b):
+        wide = ed_in.shape[2]
+        return pltpu.make_async_remote_copy(
+            src_ref=came_ed.at[b, :, pl.ds(pl.multiple_of((1 - x) * wide, wide), wide)], dst_ref=ed_in.at[b],
+            send_sem=e_send.at[b], recv_sem=e_recv.at[b],
+            device_id=to_x, device_id_type=pl.DeviceIdType.MESH,
+        )
+
+    def x_out(b):
+        tall = ed_in.shape[1]
+        return pltpu.make_async_copy(
+            ed_out.at[b], sum_ed.at[pl.ds(pl.multiple_of(b * tall, tall), tall)], e_out.at[b]
+        )
+
     def tile_out(m, b):
         tall = kinds[m][3].shape[1]
         return pltpu.make_async_copy(
@@ -933,17 +1003,21 @@
             for copy in loads:
                 copy.wait()
 
+        @pl.when(t == 1)
+        def _():
+            gates()
+
         @pl.when(t < tiles)
         def _():
             for m in range(2):
                 kinds[m][2][t] = tile(m, t, 1 - core).astype(BF16)
                 tile_copy(m, t).start()
 
-        @pl.when(t == tiles)
+        @pl.when(t == tiles * 8 // 11)
         def _():
             shared(0)
 
-        @pl.when(t == tiles + tiles // 2 + 1)
+        @pl.when(t == tiles * 14 // 11)
         def _():
             shared(1)
 
@@ -954,11 +1028,24 @@
                 value = tile(m, b, core)
                 tile_copy(m, b).wait_recv()
                 kinds[m][3][b] = (value + kinds[m][3][b].astype(F32)).astype(BF16)
-                tile_out(m, b).start()
+                if m == 0:
+                    tile_out(m, b).start()
+                else:
+                    x_copy(b).start()
 
     for copy in loads:
         copy.start()
-    greet([other, to_core, to_x])
+    me = lax.axis_index("tp")
+
+    def small_copy(d):
+        return pltpu.make_async_remote_copy(
+            src_ref=small_z.at[0] if d else small_p, dst_ref=small_z.at[d] if d else small_y,
+            send_sem=t_send.at[d], recv_sem=t_recv.at[d],
+            device_id={"tp": (me + d) % n} if d else other, device_id_type=pl.DeviceIdType.MESH,
+        )
+
+    greet_all([other, to_core, to_x] + [{"tp": (me + d) % n} for d in range(1, n)])
+    small_copy(0).start()
     sum_copies(0).start()
 
     def begin(c, carry):
@@ -969,6 +1056,36 @@
     sum_copies(1).start()
     out_copy().start()
     gain_grad[...] = jnp.zeros_like(gain_grad)
+    experts_own = small_e.shape[0] - 1
+    experts = 2 * experts_own
+    small_copy(0).wait_recv()
+    here, there = small_e[:experts_own, :], small_y[:experts_own, :]
+    small_z[0] = jnp.zeros_like(small_z[0])
+    small_z[0, :experts_own] = jnp.where(y == 0, here, there)
+    small_z[0, experts_own:experts] = jnp.where(y == 0, there, here)
+    small_z[0, experts : experts + 1] = small_s[:1, :]
+    small_z[0, experts + 1 : experts + 2] = small_s[1:, :] + small_e[experts_own:, :] + small_y[experts_own:, :]
+    for d in range(1, n):
+        small_copy(d).start()
+
+    def gates():
+        total = small_z[0]
+        for d in range(1, n):
+            small_copy(d).wait_recv()
+            total = total + small_z[d]
+        slots = prob.shape[1]
+        total = jnp.concatenate([total, jnp.zeros((128 - total.shape[0], rows), F32)], axis=0).T
+        grad_prob = total[:, :slots] * hot[...]
+        inner = jnp.sum(prob[...] * grad_prob, axis=1, keepdims=True)
+        sw = switch[...]
+        grad_switch = total[:, experts : experts + 1] * sw * (1.0 - sw)
+        place = lax.broadcasted_iota(jnp.int32, (1, slots), 1)
+        grads = jnp.where(place == experts, grad_switch, prob[...] * (grad_prob - inner)).astype(BF16)
+        router[...] = mm_nt(grads, w_small[...])
+        along[...] = total[:, experts + 1 : experts + 2] + jnp.sum(
+            grads.astype(F32) * logits[...], axis=1, keepdims=True
+        )
+        grad_small[...] = mm_tn(grads, both_v[:rows, :])
 
     def prepare(c):
         peer_copy(c).wait_recv()
@@ -999,19 +1116,33 @@
     out_copy().wait()
 
     def done(b, carry):
-        for m in range(2):
-            tile_copy(m, b).wait_send()
-            tile_out(m, b).wait()
+        x_copy(b).wait_recv()
+        wide = ed_in.shape[2]
+        own = came_ed[b, :, pl.ds(pl.multiple_of(x * wide, wide), wide)]
+        ed_out[b] = (own.astype(F32) + ed_in[b].astype(F32)).astype(BF16)
+        x_out(b).start()
+        tile_copy(0, b).wait_send()
+        tile_copy(1, b).wait_send()
+        tile_out(0, b).wait()
+        x_copy(b).wait_send()
         return carry
 
     lax.fori_loop(0, tiles, done, 0)
+
+    def written(b, carry):
+        x_out(b).wait()
+        return carry
+
+    lax.fori_loop(0, tiles, written, 0)
     for m in range(2):
         sum_copies(m).wait_send()
         sum_copies(2 + m).wait()
         own_out(m).wait()
-
-
-def resid_grad(grad, grad_p, out_p, dgu, hid, both, both_grad, sgu, sd, router, along, g_own, resid_own, inv_two, gain, depth=1):
+    for d in range(n):
+        small_copy(d).wait_send()
+
+
+def resid_grad(grad, grad_p, out_p, dgu, hid, both, both_grad, sgu, sd, small_e, small_p, small_s, prob, hot, logits, switch, w_small, g_own, resid_own, inv_two, gain, depth=1):
     rows, width = grad.shape
     width_own = g_own.shape[1]
     chunks, step, scratch = line_scratch(rows, width_own)
@@ -1026,18 +1157,23 @@
             jax.ShapeDtypeStruct((rows, width), BF16), jax.ShapeDtypeStruct((rows, width_own), F32),
             jax.ShapeDtypeStruct((1, width_own), F32), jax.ShapeDtypeStruct((rows, width), BF16),
         ]
-        + [jax.ShapeDtypeStruct((k * hidden, width // 2), BF16) for k in (2, 1)]
-        + [jax.ShapeDtypeStruct((2, v.shape[0] // 2, v.shape[1]), BF16) for v in (sgu, sd)],
-        in_specs=[vmem] + [far] * 8 + [vmem] * 6,
-        out_specs=[vmem] * 3 + [far] * 5,
+        + [jax.ShapeDtypeStruct((2 * hidden, width // 2), BF16), jax.ShapeDtypeStruct((hidden, width // 4), BF16)]
+        + [jax.ShapeDtypeStruct((2, v.shape[0] // 2, v.shape[1]), BF16) for v in (sgu, sd)]
+        + [jax.ShapeDtypeStruct((prob.shape[1], width), F32)],
+        in_specs=[vmem] + [far] * 8 + [vmem] * 12,
+        out_specs=[vmem] * 3 + [far] * 5 + [vmem],
         scratch_shapes=scratch + [pltpu.VMEM((rows, width), BF16), dma((chunks,)), dma((chunks,)), dma, dma]
         + [pltpu.VMEM(v.shape, BF16) for v in (dgu, hid, both, both_grad)]
         + [pltpu.VMEM((tiles, k * hidden // tiles, width // 2), BF16) for k in (2, 1, 2, 1)]
         + [pltpu.VMEM((v.shape[0] // 2, v.shape[1]), BF16) for v in (sgu, sgu, sd, sd)]
-        + [dma((6,)), dma((tiles, 2)), dma((tiles, 2)), dma((tiles, 2)), dma((4,)), dma((4,)), dma((2,))],
+        + [dma((6,)), dma((tiles, 2)), dma((tiles, 2)), dma((tiles, 2)), dma((4,)), dma((4,)), dma((2,))]
+        + [pltpu.VMEM((rows, width_own), F32), pltpu.VMEM((rows, 1), F32)]
+        + [pltpu.VMEM(small_e.shape, F32), pltpu.VMEM((lax.axis_size("tp"), 16, rows), F32)]
+        + [pltpu.VMEM((tiles, hidden // tiles, width // 4), BF16)] * 2
+        + [dma((lax.axis_size("tp"),))] * 2 + [dma((tiles,))] * 3,
         compiler_params=pltpu.CompilerParams(collective_id=2, has_side_effects=True, vmem_limit_bytes=63 << 20),
         cost_estimate=pl.CostEstimate(flops=0, bytes_accessed=0, transcendentals=0),
-    )(grad, grad_p, out_p, dgu, hid, both, both_grad, sgu, sd, router, along, g_own, resid_own, inv_two, gain)
+    )(grad, grad_p, out_p, dgu, hid, both, both_grad, sgu, sd, small_e, small_p, small_s, prob, hot, logits, switch, w_small, g_own, resid_own, inv_two, gain)
 
 
 def body(
@@ -1219,7 +1355,6 @@
         ],
         number=5,
     )
-    small_back = swap(small_p.T, "ep", 1)
     hid_e, dgu_e, out_e, grad_e, small_e, got_sgu_b = ffn(
         both,
         both_grad,
@@ -1236,43 +1371,17 @@
     )
     got_sgu = jnp.concatenate([got_sgu_a, got_sgu_b], axis=0)
 
-    first = ep_rank == 0
-    small_e = small_e.T
-    small_back = after(small_back, grad_e)
-    dots_here, dots_there = small_e[:experts_own], small_back[:experts_own]
-    small = jnp.concatenate(
-        [
-            jnp.where(first, dots_here, dots_there),
-            jnp.where(first, dots_there, dots_here),
-            small_s.T[:1],
-            small_s.T[1:] + small_e[experts_own:] + small_back[experts_own:],
-        ],
-        axis=0,
-    )
-    small = over_tp(small).T
-    grad_prob = small[:, :experts] * route_hot
-    grad_switch = small[:, experts : experts + 1]
-    along = small[:, experts + 1 : experts + 2]
-    grad_logits = (
-        router_prob * (grad_prob - jnp.sum(router_prob * grad_prob, axis=1, keepdims=True))
-    ).astype(BF16)
-    grad_slogit = (grad_switch * switch * (1.0 - switch)).astype(BF16)
-    tp_rows = lax.dynamic_slice_in_dim(w_router, tp_rank * width_own, width_own, 0)
-    router_part = (
-        mm_nt(grad_logits, tp_rows)
-        + grad_slogit.astype(F32) * own_columns(shared_switch).astype(F32)[None, :]
-    )
-    along = (
-        along
-        + jnp.sum(grad_logits.astype(F32) * logits, axis=1, keepdims=True)
-        + grad_slogit.astype(F32) * switch_logit
-    )
-    grad_router = mm_tn(grad_logits, mixed)
-    grad_switch_w = mm_tn(grad_slogit, mixed)
     sum_sgu = reduce_add(sum_sgu, got_sgu, *y_link)
     sum_sd = reduce_add(sum_sd, got_sd, *x_link)
 
-    resid_low, grad_resid, grad_gain_two, out_back, sum_egu, sum_ed, sgu_x, sd_x = resid_grad(
+    tp_rows = lax.dynamic_slice_in_dim(w_router, tp_rank * width_own, width_own, 0)
+    spare = 16 - experts - 1
+
+    def slots(value, more=None):
+        more = jnp.zeros((value.shape[0], 1), value.dtype) if more is None else more
+        return jnp.pad(jnp.concatenate([value, more], axis=1), ((0, 0), (0, spare)))
+
+    resid_low, grad_resid, grad_gain_two, out_back, sum_egu, sum_ed, sgu_x, sd_x, grad_small = resid_grad(
         grad_e,
         grad_p,
         out_p,
@@ -1282,8 +1391,14 @@
         both_grad,
         sum_sgu,
         sum_sd,
-        router_part,
-        along,
+        small_e.T,
+        small_p.T,
+        small_s.T,
+        slots(router_prob),
+        slots(route_hot),
+        slots(logits, switch_logit),
+        switch,
+        slots(tp_rows, own_columns(shared_switch)[:, None]),
         output_gradient,
         resid_own,
         inv_two,
@@ -1291,16 +1406,12 @@
     )
 
     flat = jnp.concatenate(
-        [grad_gain_two.reshape(-1), grad_router.reshape(-1), grad_switch_w.reshape(-1)]
+        [grad_gain_two.reshape(-1), grad_small[: experts + 1].reshape(-1)]
     ).reshape(-1, 128)
     qkv = heads * HD
     inner = shared_gate.shape[1]
     ffn_part = (out_e.astype(F32) + out_back.astype(F32)).astype(BF16)
-    ffn_own = lax.psum_scatter(
-        ffn_part, "tp", scatter_dimension=1, tiled=True
-    )
-    flat = after(flat, ffn_part)
-    sgu_f, sd_f, egu_f, ed_f, qkv_f, wo_f, flat, grad_normed, row_part = tail(
+    sgu_f, sd_f, egu_f, ed_f, qkv_f, wo_f, flat, ffn_own, normed_own, row_total, grad_gain_one = tail(
         sgu_x,
         sd_x,
         sum_egu,
@@ -1311,6 +1422,9 @@
         w_key,
         w_value,
         attn_rows,
+        ffn_part,
+        tokens,
+        inv_one,
         resid_low,
         w_output,
         query.reshape(rows, qkv),
@@ -1323,33 +1437,22 @@
         jnp.concatenate([sin_table, -sin_table], axis=1),
     )
 
-    extra = max(1, rows // width_own)
-    below = jnp.tile(row_part.reshape(extra, -1), (1, tp_count)).astype(BF16)
-    below = jnp.pad(below, ((0, -extra % 16), (0, 0)))
-    normed_own = lax.psum_scatter(
-        jnp.concatenate([grad_normed, below], axis=0), "tp", scatter_dimension=1, tiled=True
-    ).astype(F32)
-
     sg_grad, su_grad = widen(sgu_f, (inner, inner))
     (sd_grad,) = widen(sd_f)
     (eg_grad,) = widen(egu_f, kinds=2, kind=0)
     (eu_grad,) = widen(egu_f, kinds=2, kind=1)
-    (ed_grad,) = widen(ed_f)
+    (ed_grad,) = widen(ed_f, across=4)
     wq_grad, wk_grad, wv_grad = widen(qkv_f, (qkv,) * 3)
     (wo_grad,) = widen(wo_f)
 
     x_own = tokens.astype(F32)
-    normed_own = after(normed_own, sg_grad, sd_grad, eg_grad, eu_grad, ed_grad)
-    row_total = normed_own[rows : rows + extra].reshape(rows, 1)
-    normed_own = normed_own[:rows]
     grad_tokens = (
         grad_resid
         + inv_one * norm_attn.astype(F32) * normed_own
-        - x_own * (inv_one * inv_one) * (row_total / width)
-    )
-    grad_gain_one = jnp.sum(normed_own * x_own * inv_one, axis=0)
-    grad_gain_one = over_rows(grad_gain_one.reshape(-1, 128)).reshape(-1)
-    layer_out = (resid_own + after(ffn_own, flat).astype(F32)).astype(BF16)
+        - x_own * (inv_one * inv_one) * (row_total[0][:, None] / width)
+    )
+    grad_gain_one = grad_gain_one[0]
+    layer_out = (resid_own + ffn_own).astype(BF16)
     flat = flat.reshape(-1)
     grad_gain_two = flat[:width_own]
     grad_router = flat[width_own : width_own + width * experts].reshape(experts, width).T

time: 898 us -> 814 us (0.906)
  waiting for transfers between devices: 119 us -> 66.3 us
  Pallas kernels: 625 us -> 599 us
  local copies, waits for them, and re-layouts: 45.4 us -> 56.9 us
    reduce_scatter x2 -> x0, waiting for transfers between devices: 34.1 us -> none  [the longest x1 28.4 us: body(): ffn_own = lax.psum_scatter(ffn_part, 'tp', scatter_dimension=1, tiled=True)]
    ppermute x3 -> x0, waiting for transfers between devices: 18 us -> none  [over_tp(): lax.ppermute(value, 'tp', [(i, (i + d) % tp_count) for i in range(tp_coun...]
    pallas_call x1, Pallas kernels: 249 us -> 232 us  [tail(): pl.pallas_call(functools.partial(tail_kernel, 1.0 / math.sqrt(HD)), out_s...]
    pallas_call x3, Pallas kernels: 119 us -> 107 us  [ffn(): pl.pallas_call(functools.partial(ffn_kernel, groups, bool(base), bool(int...]
    unnamed x136 -> x127, local copies, waits for them, and re-layouts: 28.3 us -> 27.1 us
  transfers between devices with their start and end apart: 15 -> 6, of which waited for: 8 -> 2; matrix products, arithmetic and copies ran while one was open for 7% -> 7% of each run, Pallas kernels for 10% -> 1%
where the time goes in v5:
time: 814 us; the launch traced here: 808 us
  Pallas kernels  599 us (74%)
  waiting for transfers between devices  66.3 us (8%)
  local copies, waits for them, and re-layouts  56.9 us (7%)
  other arithmetic  46.3 us (6%)
  matrix products  18.1 us (2%)
  between operations  14.9 us (2%)
    pallas_call x1, Pallas kernels, tail(): pl.pallas_call(functools.partial(tail_kernel, 1.0 / math.sqrt(HD)), out_s...  232 us
    pallas_call x1, Pallas kernels, resid_grad(): pl.pallas_call(functools.partial(resid_grad_kernel, chunks, step, depth,...  121 us
    pallas_call x3, Pallas kernels, ffn(): pl.pallas_call(functools.partial(ffn_kernel, groups, bool(base), bool(int...  107 us
    pallas_call x1, Pallas kernels, attend_out(): pl.pallas_call(functools.partial(attend_out_kernel, chunks, step, depth,...  76.8 us
    all_gather x1, waiting for transfers between devices, body(): packed = lax.all_gather(packed, 'tp', axis=1, tiled=True)  48.1 us
    pallas_call x7, Pallas kernels, widen(): pl.pallas_call(widen_kernel, grid=grid, in_specs=[source], out_specs=spec...  37.7 us
    unnamed x127, local copies, waits for them, and re-layouts  27.1 us
    pallas_call x4, Pallas kernels, weight_half(): pl.pallas_call(functools.partial(weight_kernel, bool(extra)), grid_spec=p...  24.6 us
  transfers between devices with their start and end apart: 6, of which 2 were waited for; matrix products, arithmetic and copies ran while one was open for 7% of the time, Pallas kernels for 1%

profile of v5, /device:TPU:0, one launch (start us, length us, event | category | flops | bytes accessed | tf_op | source)
XLA Modules:
  0.0 807.7 jit_solution(13486647132435345936)
XLA Ops:
  8.7 2.0 maximum_maximum_fusion
  10.8 1.9 fusion.22
  12.7 48.1 %all-gather.3.cloned.1.call-done = bf16[528,2048]{1,0:T(8,128)(2,1)} async-done(((bf16[528,512]{1,0:T(8,128)(2,1)}), bf16[528,2048]{1,0:T(8,128)(2,1)}) %all-gather.3.cloned.1.call-update) | async-done | bytes 2162704 | tf_op jit(solution)/shard_map/all_gather | solution.py:1252
  60.8 2.2 fusion.2
  64.7 1.3 fusion.36
  66.1 1.3 copy.176
  67.4 1.3 copy.175
  68.7 3.8 fusion.37
  72.6 1.3 copy.177
  73.9 1.3 copy.178
  75.2 3.5 convolution_convert_fusion
  79.5 3.9 multiply_subtract_fusion.2
  83.4 1.3 pad_maximum_fusion
  84.7 4.6 collective-permute-start
  89.5 1.3 compare_and_fusion
  90.7 1.5 slice.78.x
  92.6 18.1 %collective-permute-done = bf16[2,512,4,128]{3,1,2,0:T(8,128)(2,1)} collective-permute-done((bf16[2,512,4,128]{3,1,2,0:T(8,128)(2,1)}, bf16[2,512,4,128]{3,1,2,0:T(8,128)(2,1)}, u32[]{:S(2)}, u32[]{:S(2)}) %collective-permute-start) | collective-permute-done | bytes 1048608 | tf_op jit(solution)/shard_map/ppermute | solution.py:1275
  110.8 2.4 fusion.30
  113.2 2.2 fusion
  115.4 2.5 fusion.1
  117.9 3.9 fusion.12
  121.7 1.3 copy.174.attn
  123.0 1.8 copy-done.10
  124.8 1.6 copy-done.11
  126.4 76.8 %shard_map.297 = (bf16[1024,2048]{1,0:T(8,128)(2,1)S(1)}, f32[512,512]{1,0:T(8,128)S(1)}, f32[512,1]{1,0:T(8,128)S(1)}, bf16[256,2048]{1,0:T(8,128)(2,1)S(1)}) custom-call(bf16[512,512]{1,0:T(8,128)(2,1)S(1)} %copy.174.attn, bf16[512,2048]{1,0:T(8,128)(2,1)S(1)} %copy-done.10, bf16[512,2048]{1,0:T(8,128)(2,1)S(1)} %copy-done.11, ...), custom_call_target="tpu_custom_call" | custom-call | tf_op jit(solution)/shard_map/pallas_call | solution.py:886
  203.3 2.0 copy-done.2
  206.8 30.8 %shard_map.298 = (bf16[512,1408]{1,0:T(8,128)(2,1)}, bf16[512,2816]{1,0:T(8,128)(2,1)}, bf16[512,2048]{1,0:T(8,128)(2,1)}, bf16[512,2048]{1,0:T(8,128)(2,1)}, f3...) custom-call(bf16[1024,2048]{1,0:T(8,128)(2,1)} %copy-done.2, ...), custom_call_target="tpu_custom_call" | custom-call | tf_op jit(solution)/shard_map/pallas_call | solution.py:598
  237.7 1.8 copy-done.8
  239.5 7.0 shard_map.299
  246.7 1.4 collective-permute-start.3
  249.7 1.6 pad.19.w_small
  252.7 1.9 pad_maximum_fusion.3.cos
  254.6 1.9 pad_maximum_fusion.4.sin
  257.3 2.4 copy_bitcast_fusion.3.query
  260.8 3.3 shard_map.300
  265.1 2.3 fusion.34
  268.2 1.5 copy.166
  269.8 1.5 copy.168
  275.1 1.5 constant_dynamic-update-slice_fusion.2
  281.8 1.9 dynamic-slice_multiply_fusion.refs_2_
  283.8 1.8 copy-done.9
  285.6 8.8 %shard_map.301.refs_6_.refs_10_ = bf16[1024,2816]{1,0:T(8,128)(2,1)} custom-call(s32[1]{0:T(128)} %bitcast.13.part, bf16[1024,2048]{1,0:T(8,128)(2,1)} %copy-done.2, bf16[512,2816]{1,0:T(8,128)(2,1)S(1)} %copy-done.9, bf16[1024,2816]{1,0:T(8,128)(2,1)} %collective-permute-done.1.refs_0_), custom_call_target="tpu_custom_call" | custom-call | tf_op jit(solution)/shard_map/pallas_call | solution.py:459
  294.4 5.5 shard_map.302.refs_7_
  300.0 38.0 %shard_map.303 = (bf16[1024,1408]{1,0:T(8,128)(2,1)}, bf16[1024,2816]{1,0:T(8,128)(2,1)}, bf16[512,2048]{1,0:T(8,128)(2,1)}, bf16[512,2048]{1,0:T(8,128)(2,1)}, ...) custom-call(bf16[1024,2048]{1,0:T(8,128)(2,1)} %copy-done.2, ...), custom_call_target="tpu_custom_call" | custom-call | tf_op jit(solution)/shard_map/pallas_call | solution.py:598
  337.9 37.9 %shard_map.304 = (bf16[1024,1408]{1,0:T(8,128)(2,1)}, bf16[1024,2816]{1,0:T(8,128)(2,1)}, bf16[512,2048]{1,0:T(8,128)(2,1)}, bf16[512,2048]{1,0:T(8,128)(2,1)}, ...) custom-call(bf16[1024,2048]{1,0:T(8,128)(2,1)} %copy-done.2, ...), custom_call_target="tpu_custom_call", output_to_operand_aliasing={{0}: (8, {}), {1}: (9, {})} | custom-call | tf_op jit(solution)/shard_map/pallas_call | solution.py:598
  375.9 1.8 copy.158
  378.4 3.2 add_convert_fusion.2.sd
  381.6 4.1 add_convert_fusion.sgu
  385.7 120.9 %shard_map.305 = (bf16[512,2048]{1,0:T(8,128)(2,1)}, f32[512,512]{1,0:T(8,128)}, f32[1,512]{1,0:T(1,128)}, bf16[512,2048]{1,0:T(8,128)(2,1)}, bf16[2816,1024]{1,...) custom-call(bf16[512,2048]{1,0:T(8,128)(2,1)} %get-tuple-element.89., ...), custom_call_target="tpu_custom_call" | custom-call | tf_op jit(solution)/shard_map/pallas_call | solution.py:1154
  507.6 1.3 maximum_bitcast_fusion.flat
  508.9 4.4 add_convert_fusion.1.ffn
  513.3 231.9 %shard_map.306 = (bf16[2,2,2,256,2816]{4,3,2,1,0:T(8,128)(2,1)}, bf16[2,2,2,352,1024]{4,3,2,1,0:T(8,128)(2,1)}, bf16[2,2,1408,1024]{3,2,1,0:T(8,128)(2,1)}, bf16...) custom-call(bf16[2,256,2816]{2,1,0:T(8,128)(2,1)} %get-tuple-element, ...), custom_call_target="tpu_custom_call" | custom-call | tf_op jit(solution)/shard_map/pallas_call | solution.py:361
  747.3 1.3 slice_bitcast_fusion
  748.7 4.3 copy-done.6
  752.9 5.4 shard_map.311
  758.4 5.4 shard_map.312
  765.5 1.3 slice.72
  766.8 5.3 shard_map.307
  772.1 2.1 shard_map.308
  774.8 4.3 copy-done.7
  779.1 8.6 %shard_map.309 = (f32[2048,1408]{1,0:T(8,128)}, f32[2048,1408]{1,0:T(8,128)}) custom-call(bf16[2048,2816]{1,0:T(8,128)(2,1)S(1)} %bitcast.94), custom_call_target="tpu_custom_call" | custom-call | tf_op jit(solution)/shard_map/pallas_call | solution.py:424
  787.7 5.6 shard_map.310
  794.1 5.3 shard_map.313
  799.4 1.3 multiply_subtract_fusion
  (186 shorter events, 29.1 us)
Async XLA Ops:
  7.2 241.7 %copy-start = (bf16[2048,8]{0,1:T(8,128)(2,1)S(1)}, bf16[2048,8]{0,1:T(8,128)(2,1)}, u32[]{:S(2)}) copy-start(bf16[2048,8]{0,1:T(8,128)(2,1)} %param.25) | copy-start | bytes 98308
  7.2 53.6 %all-gather.3.cloned.1.call-start = ((), (), s32[]{:S(2)}) async-start(), calls=%async_computation | async-start | bytes 2703360 | tf_op jit(solution)/shard_map/all_gather | solution.py:1252
  10.7 100.0 %all-gather.5.cloned.1.call-start = ((), (), s32[]{:S(2)}) async-start(), calls=%async_computation.1 | async-start | bytes 2621440 | tf_op jit(solution)/shard_map/all_gather | solution.py:1256
  60.8 3.2 copy-start.21
  63.1 1.6 copy-start.31
  64.7 1.3 copy-start.22
  79.5 9.9 %copy-start.52 = (s32[1024]{0:T(1024)S(1)}, s32[1024]{0:T(1024)}, u32[]{:S(2)}) copy-start(s32[1024]{0:T(1024)} %param.34) | copy-start | bytes 12292
  79.5 9.9 %copy-start.49 = (bf16[2048]{0:T(1024)(128)(2,1)S(1)}, bf16[2048]{0:T(1024)(128)(2,1)}, u32[]{:S(2)}) copy-start(bf16[2048]{0:T(1024)(128)(2,1)} %param.26) | copy-start | bytes 12292
  83.4 8.8 %copy-start.23 = (bf16[512,4,64]{2,0,1:T(8,128)(2,1)}, bf16[512,4,64]{2,0,1:T(8,128)(2,1)S(1)}, u32[]{:S(2)}) copy-start(bf16[512,4,64]{2,0,1:T(8,128)(2,1)S(1)} %get-tuple-element.128) | copy-start | bytes 786436
  83.4 8.8 %copy-start.25 = (bf16[512,4,64]{2,0,1:T(8,128)(2,1)}, bf16[512,4,64]{2,0,1:T(8,128)(2,1)S(1)}, u32[]{:S(2)}) copy-start(bf16[512,4,64]{2,0,1:T(8,128)(2,1)S(1)} %get-tuple-element.129) | copy-start | bytes 786436
  84.7 26.1 %collective-permute-start = (bf16[2,512,4,128]{3,1,2,0:T(8,128)(2,1)}, bf16[2,512,4,128]{3,1,2,0:T(8,128)(2,1)}, u32[]{:S(2)}, u32[]{:S(2)}) collective-permute-start(bf16[2,512,4,128]{3,1,2,0:T(8,128)(2,1)} %pad_maximum_fusion), channel_id=1, source_target_pairs={{0,4},{1,5},{2,6},{3,7},{8,12},{9,13},{10,14},{11,15},{16,20},{17,... | collective-permute-start | bytes 3145736 | tf_op jit(solution)/shard_map/ppermute | solution.py:1275
  89.4 3.1 copy-start.47
  90.7 1.8 copy-start.29
  92.2 21.0 %copy-start.32 = (pred[512,1024]{1,0:T(8,128)(4,1)S(1)}, pred[512,1024]{1,0:T(8,128)(4,1)}, u32[]{:S(2)}) copy-start(pred[512,1024]{1,0:T(8,128)(4,1)} %compare_and_fusion) | copy-start | bytes 1572868
  92.2 21.0 %copy-start.35 = (bf16[512,4,64]{2,0,1:T(8,128)(2,1)S(1)}, bf16[512,4,64]{2,0,1:T(8,128)(2,1)}, u32[]{:S(2)}) copy-start(bf16[512,4,64]{2,0,1:T(8,128)(2,1)} %get-tuple-element.142) | copy-start | bytes 786436
  92.2 21.0 %copy-start.36 = (bf16[512,4,64]{2,0,1:T(8,128)(2,1)S(1)}, bf16[512,4,64]{2,0,1:T(8,128)(2,1)}, u32[]{:S(2)}) copy-start(bf16[512,4,64]{2,0,1:T(8,128)(2,1)} %get-tuple-element.143) | copy-start | bytes 786436
  115.4 2.5 copy-start.33
  117.9 5.1 copy-start.4
  123.0 80.2 %copy-start.14 = (bf16[512,512]{1,0:T(8,128)(2,1)}, bf16[512,512]{1,0:T(8,128)(2,1)S(1)}, u32[]{:S(2)}) copy-start(bf16[512,512]{1,0:T(8,128)(2,1)S(1)} %copy.174.attn) | copy-start | bytes 1572868
  123.0 1.8 copy-start.10
  124.8 1.6 copy-start.11
  203.3 2.0 copy-start.2
  203.3 2.6 copy-start.15
  203.3 2.6 copy-start.18
  203.3 34.4 %copy-start.20 = (f32[512,1]{1,0:T(8,128)}, f32[512,1]{1,0:T(8,128)S(1)}, u32[]{:S(2)}) copy-start(f32[512,1]{1,0:T(8,128)S(1)} %get-tuple-element.99.inv_two) | copy-start | bytes 6148
  237.7 1.8 copy-start.8
  239.5 7.0 copy-start.48
  239.5 8.6 %copy-start.50 = (bf16[512]{0:T(512)(128)(2,1)S(1)}, bf16[512]{0:T(512)(128)(2,1)}, u32[]{:S(2)}) copy-start(bf16[512]{0:T(512)(128)(2,1)} %param.19) | copy-start | bytes 3076
  239.5 12.7 %copy-start.51 = (bf16[512]{0:T(512)(128)(2,1)S(1)}, bf16[512]{0:T(512)(128)(2,1)}, u32[]{:S(2)}) copy-start(bf16[512]{0:T(512)(128)(2,1)} %param.24) | copy-start | bytes 3076
  246.5 13.2 %copy-start.24 = (bf16[512,4,64]{2,0,1:T(8,128)(2,1)S(1)}, bf16[512,4,64]{2,0,1:T(8,128)(2,1)}, u32[]{:S(2)}) copy-start(bf16[512,4,64]{2,0,1:T(8,128)(2,1)} %copy-done.23) | copy-start | bytes 786436
  246.5 13.2 %copy-start.26 = (bf16[512,4,64]{2,0,1:T(8,128)(2,1)S(1)}, bf16[512,4,64]{2,0,1:T(8,128)(2,1)}, u32[]{:S(2)}) copy-start(bf16[512,4,64]{2,0,1:T(8,128)(2,1)} %copy-done.25) | copy-start | bytes 786436
  246.5 37.2 %collective-permute-start.1 = (bf16[1024,2816]{1,0:T(8,128)(2,1)}, bf16[1024,2816]{1,0:T(8,128)(2,1)}, u32[]{:S(2)}, u32[]{:S(2)}) collective-permute-start(bf16[1024,2816]{1,0:T(8,128)(2,1)} %shard_map.299), channel_id=1, source_target_pairs={{0,8},{8,0},{16,24},{24,16},{1,9},{9,1},{17,25},{25,17},{2,10},{10... | collective-permute-start | bytes 17301512 | tf_op jit(solution)/shard_map/ppermute | solution.py:33
  246.7 35.2 %collective-permute-start.3 = (f32[512,8]{1,0:T(8,128)S(1)}, f32[512,8]{1,0:T(8,128)}, u32[]{:S(2)}, u32[]{:S(2)}) collective-permute-start(f32[512,8]{1,0:T(8,128)S(1)} %copy.154), channel_id=1, source_target_pairs={{0,4},{4,0},{1,5},{5,1},{2,6},{6,2},{3,7},{7,3},{8,12},{12,8},{9,1... | collective-permute-start | bytes 49160 | tf_op jit(solution)/shard_map/ppermute | solution.py:33
  248.1 12.7 %copy-start.5 = (bf16[512,2048]{1,0:T(8,128)(2,1)S(1)}, bf16[512,2048]{1,0:T(8,128)(2,1)}, u32[]{:S(2)}) copy-start(bf16[512,2048]{1,0:T(8,128)(2,1)} %all-gather.5.cloned.1.call-done.grads.refs_1_.refs_6_.right) | copy-start | bytes 6291460
  257.3 3.5 copy-start.12
  260.8 3.5 copy-start.3
  264.1 30.3 %collective-permute-start.2 = (bf16[1408,1024]{1,0:T(8,128)(2,1)}, bf16[1408,1024]{1,0:T(8,128)(2,1)}, u32[]{:S(2)}, u32[]{:S(2)}) collective-permute-start(bf16[1408,1024]{1,0:T(8,128)(2,1)} %shard_map.300), channel_id=1, source_target_pairs={{0,8},{8,0},{16,24},{24,16},{1,9},{9,1},{17,25},{25,17},{2,10},{10... | collective-permute-start | bytes 8650760 | tf_op jit(solution)/shard_map/ppermute | solution.py:33
  268.2 4.6 copy-start.30
  269.8 4.0 copy-start.34
  271.4 3.5 copy-start.44
  274.9 1.7 copy-start.19
  275.1 2.5 copy-start.42
  276.6 2.8 copy-start.45
  283.8 1.8 copy-start.9
  285.6 8.8 %copy-start.13 = (bf16[512,1408]{1,0:T(8,128)(2,1)S(1)}, bf16[512,1408]{1,0:T(8,128)(2,1)}, u32[]{:S(2)}) copy-start(bf16[512,1408]{1,0:T(8,128)(2,1)} %get-tuple-element.77.left) | copy-start | bytes 4325380
  337.9 39.8 %copy-start.46 = (f32[512,5]{1,0:T(8,128)S(1)}, f32[512,5]{1,0:T(8,128)}, u32[]{:S(2)}) copy-start(f32[512,5]{1,0:T(8,128)} %get-tuple-element.97) | copy-start | bytes 30724
  337.9 40.5 %copy-start.37 = (bf16[704,1024]{1,0:T(8,128)(2,1)S(1)}, bf16[704,1024]{1,0:T(8,128)(2,1)}, u32[]{:S(2)}) copy-start(bf16[704,1024]{1,0:T(8,128)(2,1)} %get-tuple-element.95) | copy-start | bytes 4325380
  375.9 5.7 copy-start.38
  378.4 3.2 copy-start.39
  748.7 4.3 copy-start.6
  752.9 13.8 %slice-start = ((s8[6291456]{0:T(1024)(128)(4,1)}), s8[4194304]{0:T(1024)(128)(4,1)S(1)}, s32[]{:S(2)}) async-start(s8[6291456]{0:T(1024)(128)(4,1)} %bitcast.95), calls=%async_computation.2 | async-start | bytes 8388608
  758.4 5.4 copy-start.16
  758.4 5.4 copy-start.43
  758.4 8.4 %slice-start.1 = ((s8[6291456]{0:T(1024)(128)(4,1)}), s8[2097152]{0:T(1024)(128)(4,1)S(1)}, s32[]{:S(2)}) async-start(s8[6291456]{0:T(1024)(128)(4,1)} %bitcast.95), calls=%async_computation.3 | async-start | bytes 4194304
  766.8 5.3 copy-start.17
  772.0 15.6 %slice-start.4 = ((s8[5767168]{0:T(1024)(128)(4,1)}), s8[1572864]{0:T(1024)(128)(4,1)S(1)}, s32[]{:S(2)}) async-start(s8[5767168]{0:T(1024)(128)(4,1)} %bitcast.101), calls=%async_computation.6 | async-start | bytes 3145728
  774.8 4.3 copy-start.7
  779.1 8.6 %slice-start.5 = ((s8[5767168]{0:T(1024)(128)(4,1)}), s8[4194304]{0:T(1024)(128)(4,1)S(1)}, s32[]{:S(2)}) async-start(s8[5767168]{0:T(1024)(128)(4,1)} %bitcast.101), calls=%async_computation.7 | async-start | bytes 8388608
  787.7 5.7 slice-start.2
  787.7 6.4 slice-start.3
  794.1 5.3 copy-start.27
  794.1 5.3 copy-start.40
  794.1 5.3 copy-start.41
  794.1 6.6 copy-start.1
  (1 other events, 0.8 us)
Sparse Core Ops, SparseCore 0:
  10.9 49.9 all-gather.2
  63.2 44.6 all-gather.4

commit v6 on v5

--- a/solution.py
+++ b/solution.py
@@ -3,6 +3,7 @@
 
 import jax
 import jax.numpy as jnp
+import numpy as np
 from jax import lax
 from jax.experimental import pallas as pl
 from jax.experimental.pallas import tpu as pltpu
@@ -89,6 +90,273 @@
         return carry
 
     lax.fori_loop(0, count // step, turn, 0)
+
+
+def front_kernel(
+    scale, chunks, tokens, gains, cotangent, w_query, w_key, w_value, segments, freq,
+    x, normed, inv_one, gain_two, grads, query, keys, values, attn, lse, query_seg, key_seg, cos, sin,
+    wq_v, wk_v, wv_v, gains_in, l_sem, x_send, x_recv, s_sem, r_sem, kv_send, kv_recv,
+):
+    n, me = lax.axis_size("tp"), lax.axis_index("tp")
+    y = lax.axis_index("ep")
+    rows, own = tokens.shape
+    heads = query.shape[1] // HD
+    step = rows // chunks
+    to_y = {"ep": 1 - y}
+    tp = [{"tp": (me + d) % n} for d in range(1, n)]
+
+    def remote(source, target, send_sem, recv_sem, where):
+        return pltpu.make_async_remote_copy(
+            src_ref=source, dst_ref=target, send_sem=send_sem, recv_sem=recv_sem,
+            device_id=where, device_id_type=pl.DeviceIdType.MESH,
+        )
+
+    def piece(c, s):
+        return (pl.ds(c * step, step), pl.ds(pl.multiple_of(s * own, own), own))
+
+    def x_copy(c, s, to_right):
+        return remote(
+            x.at[piece(c, s)], x.at[piece(c, s)], x_send.at[c, s, 1 if to_right else 0], x_recv.at[c, s],
+            {"tp": me + 1 if to_right else me - 1},
+        )
+
+    loads = [
+        pltpu.make_async_copy(a, b, l_sem.at[m])
+        for m, (a, b) in enumerate(((w_key, wk_v), (w_value, wv_v), (w_query, wq_v)))
+    ]
+    for copy in loads:
+        copy.start()
+    x[:, pl.ds(pl.multiple_of(me * own, own), own)] = tokens[...]
+    gains_in[0] = gains[...]
+    greet_all([to_y] + tp)
+    for c in range(chunks):
+
+        @pl.when(me > 0)
+        def _(c=c):
+            x_copy(c, me, False).start()
+
+        @pl.when(me < n - 1)
+        def _(c=c):
+            x_copy(c, me, True).start()
+
+    g_copies = [remote(gains_in.at[0], gains_in.at[d], s_sem.at[d - 1], r_sem.at[d - 1], tp[d - 1]) for d in range(1, n)]
+    for copy in g_copies:
+        copy.start()
+
+    at = (y * rows + lax.broadcasted_iota(jnp.int32, (rows, 1), 0)).astype(F32)
+    angle = at * freq[...]
+    cos[...] = jnp.cos(angle)
+    lane = lax.broadcasted_iota(jnp.int32, (1, HD), 1)
+    sin[...] = jnp.where(lane < HD // 2, 1.0, -1.0) * jnp.sin(angle)
+    whole = segments[...].astype(F32)
+    mine = jnp.where(y == 0, whole[:, :rows], whole[:, rows : 2 * rows])
+    query_seg[...] = jnp.broadcast_to(mine, (128, rows)).T[:, :1]
+    key_seg[:, :rows] = jnp.where(y == 0, -1.0, whole[:, :rows])
+    key_seg[:, rows:] = mine
+
+    for d in range(1, n):
+        for c in range(chunks):
+
+            @pl.when(me >= d)
+            def _(c=c, d=d):
+                x_copy(c, me - d, True).wait_recv()
+
+                @pl.when(me < n - 1)
+                def _():
+                    x_copy(c, me - d, True).start()
+
+            @pl.when(me + d < n)
+            def _(c=c, d=d):
+                x_copy(c, me + d, False).wait_recv()
+
+                @pl.when(me > 0)
+                def _():
+                    x_copy(c, me + d, False).start()
+
+    mine_at = pl.ds(pl.multiple_of(me * own, own), own)
+    c_copies = [
+        remote(cotangent, grads.at[:, mine_at], s_sem.at[n - 2 + d], r_sem.at[n - 2 + d], tp[d - 1]) for d in range(1, n)
+    ]
+    handed = n == 4
+    for d, copy in enumerate(c_copies, 1):
+
+        @pl.when(((me + d) % n - me != n - 1) & (me - (me + d) % n != n - 1) if handed else me >= 0)
+        def _(copy=copy):
+            copy.start()
+
+    inner = (me > 0) & (me < n - 1)
+
+    def hand_on():
+        upward = me == n - 2
+        origin = pl.ds(pl.multiple_of(jnp.where(upward, 0, n - 1) * own, own), own)
+        arrival = jnp.where(upward, n - 2 + n - 1, n - 2 + 1)
+        return remote(
+            grads.at[:, origin], grads.at[:, origin], s_sem.at[2 * n - 2], r_sem.at[arrival],
+            {"tp": jnp.where(upward, n - 1, 0)},
+        )
+    own_grads = pltpu.make_async_copy(cotangent, grads.at[:, mine_at], l_sem.at[3])
+    own_grads.start()
+    for copy in g_copies:
+        copy.wait_recv()
+    gain_one = []
+    for s in range(n):
+        row = gains_in[0, :2, :].astype(F32) * jnp.where(me == s, 1.0, 0.0)
+        for d in range(1, n):
+            row = row + gains_in[d, :2, :].astype(F32) * jnp.where((me - d + n) % n == s, 1.0, 0.0)
+        gain_one.append(row[:1])
+        gain_two[:, s * own : (s + 1) * own] = row[1:]
+
+    block = min(rows, 128)
+    for b in range(rows // block):
+        here = slice(b * block, (b + 1) * block)
+        square = jnp.zeros((block, 1), F32)
+        for s in range(n):
+            part = x[here, s * own : (s + 1) * own].astype(F32)
+            square = square + jnp.sum(part * part, axis=1, keepdims=True)
+        inv = lax.rsqrt(square / (n * own) + EPS)
+        inv_one[here, :] = inv
+        for s in range(n):
+            columns = slice(s * own, (s + 1) * own)
+            normed[here, columns] = (x[here, columns].astype(F32) * inv * gain_one[s]).astype(BF16)
+
+    def rope(value):
+        return value * cos[...] - pltpu.roll(value, HD // 2, 1) * sin[...]
+
+    loads[0].wait()
+    loads[1].wait()
+    key_pre = mm(normed[...], wk_v[...])
+    value_pre = mm(normed[...], wv_v[...])
+
+    @pl.when(y == 0)
+    def _():
+        keys[:rows, :] = jnp.zeros((rows, heads * HD), BF16)
+        values[:rows, :] = jnp.zeros((rows, heads * HD), BF16)
+
+    def kv_copy(h, m):
+        array = (keys, values)[m]
+        part = pl.ds(h * HD, HD)
+        return remote(
+            array.at[pl.ds(rows, rows), part], array.at[pl.ds(0, rows), part], kv_send.at[h, m], kv_recv.at[h, m], to_y
+        )
+
+    for h in range(heads):
+        part = slice(h * HD, (h + 1) * HD)
+        keys[rows:, part] = rope(key_pre[:, part]).astype(BF16)
+        values[rows:, part] = value_pre[:, part].astype(BF16)
+
+        @pl.when(y == 0)
+        def _(h=h):
+            kv_copy(h, 0).start()
+            kv_copy(h, 1).start()
+
+    loads[2].wait()
+    query_pre = mm(normed[...], wq_v[...])
+    for h in range(heads):
+        part = slice(h * HD, (h + 1) * HD)
+        query[:, part] = rope(query_pre[:, part]).astype(BF16)
+
+    if handed:
+
+        @pl.when(inner)
+        def _():
+            c_copies[1].wait_recv()
+            hand_on().start()
+
+    key_at = (y - 1) * rows + lax.broadcasted_iota(jnp.int32, (1, 2 * rows), 1)
+    query_at = y * rows + lax.broadcasted_iota(jnp.int32, (rows, 1), 0)
+    allowed = (query_seg[...] == key_seg[...]) & (key_at <= query_at)
+    for h in range(heads):
+        part = slice(h * HD, (h + 1) * HD)
+
+        @pl.when(y == 1)
+        def _(h=h):
+            kv_copy(h, 0).wait_recv()
+            kv_copy(h, 1).wait_recv()
+
+        scores = jnp.where(allowed, mm_nt(query[:, part], keys[:, part]) * scale, NEG)
+        top = jnp.max(scores, axis=1, keepdims=True)
+        shifted = jnp.exp(scores - top)
+        total = jnp.sum(shifted, axis=1, keepdims=True)
+        weights = (shifted * (1.0 / total)).astype(BF16)
+        attn[:, part] = mm(weights, values[:, part]).astype(BF16)
+        lse[:, h : h + 1] = top + jnp.log(total)
+
+    for h in range(heads):
+
+        @pl.when(y == 0)
+        def _(h=h):
+            kv_copy(h, 0).wait_send()
+            kv_copy(h, 1).wait_send()
+
+    for c in range(chunks):
+        for s in range(n):
+
+            @pl.when((s <= me) & (me < n - 1))
+            def _(c=c, s=s):
+                x_copy(c, s, True).wait_send()
+
+            @pl.when((s >= me) & (me > 0))
+            def _(c=c, s=s):
+                x_copy(c, s, False).wait_send()
+
+    own_grads.wait()
+    for d, copy in enumerate(c_copies, 1):
+
+        if handed and d == 2:
+
+            @pl.when(jnp.logical_not(inner))
+            def _(copy=copy):
+                copy.wait_recv()
+
+        else:
+            copy.wait_recv()
+
+        @pl.when(((me + d) % n - me != n - 1) & (me - (me + d) % n != n - 1) if handed else me >= 0)
+        def _(copy=copy):
+            copy.wait_send()
+
+    if handed:
+
+        @pl.when(inner)
+        def _():
+            hand_on().wait_send()
+
+    for copy in g_copies:
+        copy.wait_send()
+
+
+def front(tokens, gains, cotangent, w_query, w_key, w_value, segments, freq):
+    rows, own = tokens.shape
+    n = lax.axis_size("tp")
+    width = n * own
+    mine = w_query.shape[1]
+    heads = mine // HD
+    chunks = 8 if n <= 4 else 2
+    far = pl.BlockSpec(memory_space=pl.ANY)
+    vmem = pl.BlockSpec(memory_space=pltpu.VMEM)
+    dma = pltpu.SemaphoreType.DMA
+
+    def shape(*dims, kind=BF16):
+        return jax.ShapeDtypeStruct(dims, kind)
+
+    return pl.pallas_call(
+        functools.partial(front_kernel, 1.0 / math.sqrt(HD), chunks),
+        out_shape=[
+            shape(rows, width), shape(rows, width), shape(rows, 1, kind=F32), shape(1, width, kind=F32),
+            shape(rows, width), shape(rows, mine), shape(2 * rows, mine), shape(2 * rows, mine), shape(rows, mine),
+            shape(rows, heads, kind=F32), shape(rows, 1, kind=F32), shape(1, 2 * rows, kind=F32),
+            shape(rows, HD, kind=F32), shape(rows, HD, kind=F32),
+        ],
+        in_specs=[vmem] * 2 + [far] * 4 + [vmem] * 2,
+        out_specs=[vmem] * 4 + [far] + [vmem] * 9,
+        scratch_shapes=[pltpu.VMEM((width, mine), BF16)] * 3
+        + [pltpu.VMEM((n, 16, own), BF16), dma((4,)), dma((chunks, n, 2)), dma((chunks, n))]
+        + [dma((2 * n,)), dma((2 * n,)), dma((heads, 2)), dma((heads, 2))],
+        compiler_params=pltpu.CompilerParams(
+            collective_id=7, has_side_effects=True, vmem_limit_bytes=62 << 20
+        ),
+        cost_estimate=pl.CostEstimate(flops=0, bytes_accessed=0, transcendentals=0),
+    )(tokens, gains, cotangent, w_query, w_key, w_value, segments, freq)
 
 
 def tail_kernel(
@@ -141,6 +409,7 @@
 
     b3 = there(egu.at[pl.ds((1 - x) * e_rows, e_rows)], e_in, to_x)
     b6 = there(ed, ed_f.at[core, x], to_x)
+    d3 = [there(sd.at[0], sd_f.at[core, 0, y], to_y)]
     f1 = there(flat, flat_in.at[0], to_core)
     z_ffn = [there(ffn.at[:, columns(d)], ffn_in.at[d], tp[d - 1]) for d in range(1, n)]
     own_ffn = here(ffn.at[:, columns(0)], ffn_in.at[0])
@@ -252,6 +521,8 @@
     load_e.wait()
     b3.wait_recv()
     add_rows(e_own, e_in, 0, e_rows)
+    cut, cut_b = e_rows // 64 * 16, e_rows * 5 // 128 * 16
+    b5a = there(e_own.at[pl.ds(0, cut)], egu_f.at[core, x, pl.ds(0, cut)], to_x)
     f2.wait_recv()
     f2.wait_send()
     flat_f[...] = flat_f[...] + flat_in[1]
@@ -262,10 +533,8 @@
     a1.wait_recv()
     add_rows(q_half, q_in, y * q_rows, q_rows)
     a3 = there(q_half.at[pl.ds(y * q_rows + (1 - x) * (q_rows // 2), q_rows // 2)], q_in2, to_x)
-    cut = e_rows // 2
-    b5 = there(e_own.at[pl.ds(0, cut)], egu_f.at[core, x, pl.ds(0, cut)], to_x)
     own_e = here(e_own, egu_f.at[core, x])
-    d3 = [there(sd.at[p], sd_f.at[core, p, y], to_y) for p in range(2)]
+    d3.append(there(sd.at[1], sd_f.at[core, 1, y], to_y))
     for copy in z_normed + z_rows:
         copy.wait_recv()
     total = grad_normed[:, columns(0)].astype(F32)
@@ -290,7 +559,8 @@
     add_rows(q_half, q_in2, y * q_rows + x * (q_rows // 2), q_rows // 2, q_out)
     a5 = there(q_out, qkv_f.at[core, y, x], to_x)
     own_q = here(q_out, qkv_f.at[core, y, x])
-    b7 = there(e_own.at[pl.ds(cut, cut)], egu_f.at[core, x, pl.ds(cut, cut)], to_x)
+    b5 = there(e_own.at[pl.ds(cut, cut_b - cut)], egu_f.at[core, x, pl.ds(cut, cut_b - cut)], to_x)
+    b7 = there(e_own.at[pl.ds(cut_b, e_rows - cut_b)], egu_f.at[core, x, pl.ds(cut_b, e_rows - cut_b)], to_x)
     own_ffn.wait()
     for copy in z_ffn:
         copy.wait_recv()
@@ -298,6 +568,9 @@
     for d in range(1, n):
         total = total + ffn_in[d].astype(F32)
     ffn_own[...] = total
+    own_ed.wait()
+    b6.wait_recv()
+    c6 = there(ed_f.at[core], ed_f.at[core], to_core)
     own_s.wait()
     d1.wait_recv()
     d2.wait_recv()
@@ -321,20 +594,20 @@
     f3.wait_send()
     flat_f[...] = flat_f[...] + flat_in[2]
     own_e.wait()
+    b5a.wait_recv()
     b5.wait_recv()
+    c3 = there(egu_f.at[core, :, pl.ds(0, cut_b)], egu_f.at[core, :, pl.ds(0, cut_b)], to_core)
     b7.wait_recv()
-    c3 = there(egu_f.at[core], egu_f.at[core], to_core)
+    rest = pl.ds(cut_b, e_rows - cut_b)
+    c7 = there(egu_f.at[core, :, rest], egu_f.at[core, :, rest], to_core)
     a8.wait_recv()
     c5 = there(wo_f.at[core], wo_f.at[core], to_core)
     a7.wait_recv()
     c4 = there(qkv_f.at[core], qkv_f.at[core], to_core)
-    own_ed.wait()
-    b6.wait_recv()
-    c6 = there(ed_f.at[core], ed_f.at[core], to_core)
     g3.wait_recv()
     g3.wait_send()
     gain_f[...] = gain_f[...] + gain_in[2]
-    for copy in (c1, c2, c3, c4, c5, c6):
+    for copy in (c1, c2, c3, c4, c5, c6, c7):
         copy.wait_recv()
     for copy in sent:
         if all(copy is not other for other in (f2, f3, g1, g2, g3)):
@@ -381,7 +654,7 @@
             room(egu.shape[0] // 2, egu.shape[1]), room(egu.shape[0] // 2, egu.shape[1]),
             room(3, *flat.shape, kind=F32), room(n, *tokens.shape), room(rows, width), room(n, *tokens.shape),
             room(n, 8, rows, kind=F32), room(3, 8, tokens.shape[1], kind=F32),
-            dma((16,)), dma((36 + heads + 3 * n,)), dma((36 + heads + 3 * n,)),
+            dma((16,)), dma((38 + heads + 3 * n,)), dma((38 + heads + 3 * n,)),
         ],
         compiler_params=pltpu.CompilerParams(
             collective_id=3, has_side_effects=True, vmem_limit_bytes=62 << 20
@@ -469,25 +742,6 @@
         compiler_params=pltpu.CompilerParams(vmem_limit_bytes=48 << 20),
         cost_estimate=pl.CostEstimate(flops=0, bytes_accessed=0, transcendentals=0),
     )(which.reshape(1).astype(jnp.int32), left, right, *extra)
-
-
-def rope_tables(positions, feat_width):
-    half_width = feat_width // 2
-    inv_freq = ROPE_BASE ** (-(jnp.arange(half_width, dtype=F32) * 2.0) / feat_width)
-    angles = positions.astype(F32)[:, None] * inv_freq[None, :]
-    return (jnp.cos(angles), jnp.sin(angles))
-
-
-def rotate(tensor, cos_table, sin_table):
-    half_width = tensor.shape[-1] // 2
-    first_half = tensor[..., :half_width]
-    second_half = tensor[..., half_width:]
-    cos_b = cos_table[:, None, :]
-    sin_b = sin_table[:, None, :]
-    return jnp.concatenate(
-        [first_half * cos_b - second_half * sin_b, second_half * cos_b + first_half * sin_b],
-        axis=-1,
-    )
 
 
 def ffn_kernel(groups, base, into, flipped, carry, *refs):
@@ -1246,62 +1500,24 @@
             value = value + swap(value, axis, bit)
         return value
 
-    packed = jnp.concatenate(
-        [tokens, norm_attn[None, :], norm_ffn[None, :], jnp.zeros((14, width_own), BF16)], axis=0
+    qkv = heads * HD
+    freq = ROPE_BASE ** (-(np.arange(HD // 2, dtype=np.float64) * 2.0) / HD)
+    freq = jnp.asarray(np.concatenate([freq, freq])[None, :], F32)
+    gains = jnp.pad(jnp.stack([norm_attn, norm_ffn]), ((0, 14), (0, 0)))
+    (
+        x_full, normed, inv_one, gain_two, grad_rows, query, key_rows, value_rows, attn_rows, log_norm,
+        query_seg, key_seg, cos_table, sin_table,
+    ) = front(
+        tokens, gains, output_gradient, w_query, w_key, w_value, segments.reshape(1, -1), freq
     )
-    packed = lax.all_gather(packed, "tp", axis=1, tiled=True)
-    x_full = packed[:rows].astype(F32)
-    gain_one = packed[rows].astype(F32)
-    gain_two = packed[rows + 1].astype(F32)
-    grad_rows = lax.all_gather(after(output_gradient, packed), "tp", axis=1, tiled=True)
     route_hot = jnp.sum(
         (routes[:, :, None] == jnp.arange(experts, dtype=jnp.int32)[None, None, :]).astype(F32),
         axis=1,
     )
     route_hot_peer = swap(route_hot, "ep", 1)
 
-    inv_one = lax.rsqrt(jnp.mean(x_full * x_full, axis=1, keepdims=True) + EPS)
-    normed = (x_full * inv_one * gain_one).astype(BF16)
-    q_pre = mm(normed, w_query)
-    k_pre = mm(normed, w_key)
-    v_pre = mm(normed, w_value)
-    positions = ep_rank * rows + jnp.arange(rows, dtype=jnp.int32)
-    cos_table, sin_table = rope_tables(positions, HD)
-    query = rotate(q_pre.reshape(rows, heads, HD), cos_table, sin_table).astype(BF16)
-    key_own = rotate(k_pre.reshape(rows, heads, HD), cos_table, sin_table).astype(BF16)
-    value_own = v_pre.astype(BF16).reshape(rows, heads, HD)
-    forth = [(i, i + 1) for i in range(ep_count - 1)]
-    back = [(i + 1, i) for i in range(ep_count - 1)]
-    earlier = lax.ppermute(jnp.stack([key_own, value_own]), "ep", forth)
-    earlier = after(earlier, grad_rows)
-    key_rows = jnp.concatenate([earlier[0], key_own], axis=0)
-    value_rows = jnp.concatenate([earlier[1], value_own], axis=0)
-    key_pos = (ep_rank - 1) * rows + jnp.arange(2 * rows, dtype=jnp.int32)
-    seg_rows = segments.reshape(ep_count, rows)
-    query_seg = lax.dynamic_index_in_dim(seg_rows, ep_rank, 0, keepdims=False)
-    before_seg = lax.dynamic_index_in_dim(
-        seg_rows, jnp.maximum(ep_rank - 1, 0), 0, keepdims=False
-    )
-    key_seg = jnp.concatenate([jnp.where(ep_rank > 0, before_seg, -1), query_seg])
-    allowed = (query_seg[:, None] == key_seg[None, :]) & (key_pos[None, :] <= positions[:, None])
-
-    def masked_scores():
-        scores = (
-            jnp.einsum("qhd,khd->hqk", query, key_rows, preferred_element_type=F32) * score_scale
-        )
-        return jnp.where(allowed[None], scores, NEG)
-
-    scores = masked_scores()
-    row_top = jnp.max(scores, axis=2, keepdims=True)
-    shifted = jnp.exp(scores - row_top)
-    row_total = jnp.sum(shifted, axis=2, keepdims=True)
-    weights = (shifted / row_total).astype(BF16)
-    attended = jnp.einsum("hqk,khd->qhd", weights, value_rows, preferred_element_type=F32)
-    attn_rows = attended.astype(BF16).reshape(rows, heads * HD)
-    log_norm = row_top + jnp.log(row_total)
-
     both, resid_own, inv_two, grad_peer_a = attend_out(
-        attn_rows, w_output, packed[:rows], gain_two[None, :], grad_rows, width_own
+        attn_rows, w_output, x_full, gain_two, grad_rows, width_own
     )
     mixed = both[:rows]
 
@@ -1408,7 +1624,6 @@
     flat = jnp.concatenate(
         [grad_gain_two.reshape(-1), grad_small[: experts + 1].reshape(-1)]
     ).reshape(-1, 128)
-    qkv = heads * HD
     inner = shared_gate.shape[1]
     ffn_part = (out_e.astype(F32) + out_back.astype(F32)).astype(BF16)
     sgu_f, sd_f, egu_f, ed_f, qkv_f, wo_f, flat, ffn_own, normed_own, row_total, grad_gain_one = tail(
@@ -1427,14 +1642,14 @@
         inv_one,
         resid_low,
         w_output,
-        query.reshape(rows, qkv),
-        key_rows.reshape(2 * rows, qkv),
-        value_rows.reshape(2 * rows, qkv),
-        log_norm[:, :, 0].T,
-        query_seg[:, None],
-        key_seg[None, :],
-        jnp.concatenate([cos_table, cos_table], axis=1),
-        jnp.concatenate([sin_table, -sin_table], axis=1),
+        query,
+        key_rows,
+        value_rows,
+        log_norm,
+        query_seg,
+        key_seg,
+        cos_table,
+        sin_table,
     )
 
     sg_grad, su_grad = widen(sgu_f, (inner, inner))

time: 814 us -> 760 us (0.934)
  Pallas kernels: 599 us -> 677 us
  waiting for transfers between devices: 66.3 us -> 0.01 us
  other arithmetic: 46.3 us -> 23.8 us
  between operations: 14.9 us -> 1.21 us
  matrix products: 18.1 us -> 5.15 us
  local copies, waits for them, and re-layouts: 56.9 us -> 45.8 us
    pallas_call x0 -> x1, Pallas kernels: none -> 82.7 us  [front(): pl.pallas_call(functools.partial(front_kernel, 1.0 / math.sqrt(HD), chunk...]
    all_gather x2 -> x0, waiting for transfers between devices: 48.1 us -> none  [the longest x1 48.1 us: body(): packed = lax.all_gather(packed, 'tp', axis=1, tiled=True)]
    ppermute x1 -> x0, waiting for transfers between devices: 18.1 us -> none  [body(): earlier = lax.ppermute(jnp.stack([key_own, value_own]), 'ep', forth)]
    pallas_call x1, Pallas kernels: 232 us -> 221 us  [tail(): pl.pallas_call(functools.partial(tail_kernel, 1.0 / math.sqrt(HD)), out_s...]
    unnamed x127 -> x83, local copies, waits for them, and re-layouts: 27.1 us -> 25.4 us
  transfers between devices with their start and end apart: 6 -> 3, of which waited for: 2 -> 0; matrix products, arithmetic and copies ran while one was open for 7% -> 3% of each run, Pallas kernels for 1% -> 2%
where the time goes in v6:
time: 760 us; the launch traced here: 755 us
  Pallas kernels  677 us (89%)
  local copies, waits for them, and re-layouts  45.8 us (6%)
  other arithmetic  23.8 us (3%)
    pallas_call x1, Pallas kernels, tail(): pl.pallas_call(functools.partial(tail_kernel, 1.0 / math.sqrt(HD)), out_s...  221 us
    pallas_call x1, Pallas kernels, resid_grad(): pl.pallas_call(functools.partial(resid_grad_kernel, chunks, step, depth,...  122 us
    pallas_call x3, Pallas kernels, ffn(): pl.pallas_call(functools.partial(ffn_kernel, groups, bool(base), bool(int...  106 us
    pallas_call x1, Pallas kernels, attend_out(): pl.pallas_call(functools.partial(attend_out_kernel, chunks, step, depth,...  83 us
    pallas_call x1, Pallas kernels, front(): pl.pallas_call(functools.partial(front_kernel, 1.0 / math.sqrt(HD), chunk...  82.7 us
    pallas_call x7, Pallas kernels, widen(): pl.pallas_call(widen_kernel, grid=grid, in_specs=[source], out_specs=spec...  37.9 us
    unnamed x83, local copies, waits for them, and re-layouts  25.4 us
    pallas_call x4, Pallas kernels, weight_half(): pl.pallas_call(functools.partial(weight_kernel, bool(extra)), grid_spec=p...  24.4 us
  transfers between devices with their start and end apart: 3, of which 0 were waited for; matrix products, arithmetic and copies ran while one was open for 3% of the time, Pallas kernels for 2%

profile of v6, /device:TPU:0, one launch (start us, length us, event | category | flops | bytes accessed | tf_op | source)
XLA Modules:
  0.0 754.5 jit_solution(4156813667853760924)
XLA Ops:
  0.7 0.7 stack.10
  2.0 0.7 reshape.133
  3.3 82.7 %shard_map.306 = (bf16[512,2048]{1,0:T(8,128)(2,1)}, bf16[512,2048]{1,0:T(8,128)(2,1)}, f32[512,1]{1,0:T(8,128)}, f32[1,2048]{1,0:T(1,128)}, bf16[512,2048]{1,0:...) custom-call(bf16[512,512]{1,0:T(8,128)(2,1)} %tokens.3, ...), custom_call_target="tpu_custom_call" | custom-call | tf_op jit(solution)/shard_map/pallas_call | solution.py:342
  86.1 1.6 copy-done.3
  87.7 1.6 copy-done.9
  89.3 1.0 copy-done.14
  90.3 1.6 copy-done.16
  91.9 0.7 copy-done.18
  92.6 83.0 %shard_map.307 = (bf16[1024,2048]{1,0:T(8,128)(2,1)S(1)}, f32[512,512]{1,0:T(8,128)S(1)}, f32[512,1]{1,0:T(8,128)S(1)}, bf16[256,2048]{1,0:T(8,128)(2,1)S(1)}) custom-call(bf16[512,512]{1,0:T(8,128)(2,1)S(1)} %copy-done.14, bf16[512,2048]{1,0:T(8,128)(2,1)S(1)} %copy-done.9, bf16[512,2048]{1,0:T(8,128)(2,1)S(1)} %copy-done.16, f32[1,2048]{1,0:T(1,128)S(1)} %copy-done.18, ...), custom_call_target="tpu_custom_call" | custom-call | tf_op jit(solution)/shard_map/pallas_call | solution.py:1140
  175.7 2.0 copy-done.2
  178.3 0.9 copy.79.refs_2_.switch
  179.2 31.0 %shard_map.308 = (bf16[512,1408]{1,0:T(8,128)(2,1)}, bf16[512,2816]{1,0:T(8,128)(2,1)}, bf16[512,2048]{1,0:T(8,128)(2,1)}, bf16[512,2048]{1,0:T(8,128)(2,1)}, f3...) custom-call(bf16[1024,2048]{1,0:T(8,128)(2,1)} %copy-done.2, bf16[512,2048]{1,0:T(8,128)(2,1)} %get-tuple-element.95.grads.refs_1_.refs_6_.right, ...), custom_call_target="tpu_custom_call" | custom-call | tf_op jit(solution)/shard_map/pallas_call | solution.py:852
  210.3 1.8 copy-done.7
  212.1 7.1 shard_map.309
  219.2 3.3 shard_map.310
  223.0 0.8 copy.82
  223.9 0.9 collective-permute-start.2
  224.8 2.3 fusion.13
  227.1 2.3 fusion.14
  229.4 0.8 copy.83
  230.2 0.8 dynamic_slice.23
  231.5 0.7 copy-done.20
  232.2 1.9 dynamic-slice_multiply_fusion.1.refs_2_
  234.1 1.2 fusion.11
  235.2 1.8 fusion.12
  237.0 1.5 constant_dynamic-update-slice_fusion.2
  238.5 1.0 constant_dynamic-update-slice_fusion.1
  239.5 1.0 constant_dynamic-update-slice_fusion.refs_1_.both_grad
  241.1 0.7 pad.37.prob
  241.9 1.7 pad.38.hot
  243.5 1.7 copy.88
  245.3 0.7 pad.23.logits
  246.2 0.7 pad.24.w_small
  246.9 1.9 dynamic-slice_multiply_fusion.refs_2_
  248.9 1.8 copy-done.8
  250.7 8.8 %shard_map.311.refs_6_.refs_10_ = bf16[1024,2816]{1,0:T(8,128)(2,1)} custom-call(s32[1]{0:T(128)} %bitcast.3.part, bf16[1024,2048]{1,0:T(8,128)(2,1)} %copy-done.2, bf16[512,2816]{1,0:T(8,128)(2,1)S(1)} %copy-done.8, bf16[1024,2816]{1,0:T(8,128)(2,1)} %collective-permute-done.refs_0_), custom_call_target="tpu_custom_call" | custom-call | tf_op jit(solution)/shard_map/pallas_call | solution.py:732
  259.5 5.1 shard_map.312.refs_7_
  264.7 38.0 %shard_map.313 = (bf16[1024,1408]{1,0:T(8,128)(2,1)}, bf16[1024,2816]{1,0:T(8,128)(2,1)}, bf16[512,2048]{1,0:T(8,128)(2,1)}, bf16[512,2048]{1,0:T(8,128)(2,1)}, ...) custom-call(bf16[1024,2048]{1,0:T(8,128)(2,1)} %copy-done.2, ...), custom_call_target="tpu_custom_call" | custom-call | tf_op jit(solution)/shard_map/pallas_call | solution.py:852
  302.7 37.4 %shard_map.314 = (bf16[1024,1408]{1,0:T(8,128)(2,1)}, bf16[1024,2816]{1,0:T(8,128)(2,1)}, bf16[512,2048]{1,0:T(8,128)(2,1)}, bf16[512,2048]{1,0:T(8,128)(2,1)}, ...) custom-call(bf16[1024,2048]{1,0:T(8,128)(2,1)} %copy-done.2, ...), custom_call_target="tpu_custom_call", output_to_operand_aliasing={{0}: (8, {}), {1}: (9, {})} | custom-call | tf_op jit(solution)/shard_map/pallas_call | solution.py:852
  340.1 1.8 copy.86
  341.9 0.7 copy.87
  342.6 3.2 add_convert_fusion.2.sd
  345.8 4.1 add_convert_fusion.sgu
  349.9 121.6 %shard_map.315 = (bf16[512,2048]{1,0:T(8,128)(2,1)}, f32[512,512]{1,0:T(8,128)}, f32[1,512]{1,0:T(1,128)}, bf16[512,2048]{1,0:T(8,128)(2,1)}, bf16[2816,1024]{1,...) custom-call(bf16[512,2048]{1,0:T(8,128)(2,1)} %get-tuple-element.103, ...), custom_call_target="tpu_custom_call" | custom-call | tf_op jit(solution)/shard_map/pallas_call | solution.py:1408
  471.6 0.9 reshape.122
  472.5 1.3 maximum_bitcast_fusion.flat
  473.8 4.4 add_convert_fusion.1.ffn
  478.2 221.1 %shard_map.316 = (bf16[2,2,2,256,2816]{4,3,2,1,0:T(8,128)(2,1)}, bf16[2,2,2,352,1024]{4,3,2,1,0:T(8,128)(2,1)}, bf16[2,2,1408,1024]{3,2,1,0:T(8,128)(2,1)}, bf16...) custom-call(bf16[2,256,2816]{2,1,0:T(8,128)(2,1)} %get-tuple-element, ...), custom_call_target="tpu_custom_call" | custom-call | tf_op jit(solution)/shard_map/pallas_call | solution.py:634
  699.4 1.3 slice_bitcast_fusion.1
  700.6 0.9 slice.38
  701.5 1.3 slice_bitcast_fusion
  702.8 4.3 copy-done.5
  707.1 5.4 shard_map.321
  712.5 5.2 shard_map.322
  717.8 0.7 slice_multiply_fusion
  718.5 1.3 slice.35
  719.8 5.3 shard_map.317
  725.1 2.1 shard_map.318
  727.9 4.3 copy-done.6
  732.2 8.6 %shard_map.319 = (f32[2048,1408]{1,0:T(8,128)}, f32[2048,1408]{1,0:T(8,128)}) custom-call(bf16[2048,2816]{1,0:T(8,128)(2,1)S(1)} %bitcast.42), custom_call_target="tpu_custom_call" | custom-call | tf_op jit(solution)/shard_map/pallas_call | solution.py:697
  740.8 5.6 shard_map.320
  746.4 0.7 slice-done.3
  747.1 5.6 shard_map.323
  752.8 1.5 multiply_subtract_fusion
  (93 shorter events, 4.7 us)
Async XLA Ops:
  0.6 224.1 %copy-start = (bf16[2048,8]{0,1:T(8,128)(2,1)S(1)}, bf16[2048,8]{0,1:T(8,128)(2,1)}, u32[]{:S(2)}) copy-start(bf16[2048,8]{0,1:T(8,128)(2,1)} %param.26) | copy-start | bytes 98308
  86.1 1.6 copy-start.3
  87.7 1.6 copy-start.9
  89.3 1.0 copy-start.14
  90.3 1.6 copy-start.16
  91.9 0.7 copy-start.18
  175.7 2.0 copy-start.2
  175.7 2.6 copy-start.12
  175.7 2.6 copy-start.17
  210.3 1.8 copy-start.7
  212.1 7.2 copy-start.4
  212.1 7.2 copy-start.10
  219.2 29.6 %collective-permute-start = (bf16[1024,2816]{1,0:T(8,128)(2,1)}, bf16[1024,2816]{1,0:T(8,128)(2,1)}, u32[]{:S(2)}, u32[]{:S(2)}) collective-permute-start(bf16[1024,2816]{1,0:T(8,128)(2,1)} %shard_map.309), channel_id=1, source_target_pairs={{0,8},{8,0},{16,24},{24,16},{1,9},{9,1},{17,25},{25,17},{2,10},{10... | collective-permute-start | bytes 17301512 | tf_op jit(solution)/shard_map/ppermute | solution.py:34
  219.2 3.8 copy-start.31
  222.5 37.0 %collective-permute-start.1 = (bf16[1408,1024]{1,0:T(8,128)(2,1)}, bf16[1408,1024]{1,0:T(8,128)(2,1)}, u32[]{:S(2)}, u32[]{:S(2)}) collective-permute-start(bf16[1408,1024]{1,0:T(8,128)(2,1)} %shard_map.310), channel_id=1, source_target_pairs={{0,8},{8,0},{16,24},{24,16},{1,9},{9,1},{17,25},{25,17},{2,10},{10... | collective-permute-start | bytes 8650760 | tf_op jit(solution)/shard_map/ppermute | solution.py:34
  223.9 23.1 %collective-permute-start.2 = (f32[512,8]{1,0:T(8,128)}, f32[512,8]{1,0:T(8,128)}, u32[]{:S(2)}, u32[]{:S(2)}) collective-permute-start(f32[512,8]{1,0:T(8,128)} %copy.82), channel_id=1, source_target_pairs={{0,4},{4,0},{1,5},{5,1},{2,6},{6,2},{3,7},{7,3},{8,12},{12,8},{9,1... | collective-permute-start | bytes 49160 | tf_op jit(solution)/shard_map/ppermute | solution.py:34
  231.5 0.7 copy-start.20
  237.0 2.5 copy-start.25
  238.5 2.1 copy-start.32
  238.5 2.7 copy-start.21
  238.5 5.1 copy-start.33
  239.5 7.4 copy-start.26
  248.9 1.8 copy-start.8
  250.7 8.8 %copy-start.11 = (bf16[512,1408]{1,0:T(8,128)(2,1)S(1)}, bf16[512,1408]{1,0:T(8,128)(2,1)}, u32[]{:S(2)}) copy-start(bf16[512,1408]{1,0:T(8,128)(2,1)} %get-tuple-element.91.left) | copy-start | bytes 4325380
  302.7 39.2 %copy-start.30 = (f32[512,5]{1,0:T(8,128)S(1)}, f32[512,5]{1,0:T(8,128)}, u32[]{:S(2)}) copy-start(f32[512,5]{1,0:T(8,128)} %get-tuple-element.111) | copy-start | bytes 30724
  302.7 39.9 %copy-start.22 = (bf16[704,1024]{1,0:T(8,128)(2,1)S(1)}, bf16[704,1024]{1,0:T(8,128)(2,1)}, u32[]{:S(2)}) copy-start(bf16[704,1024]{1,0:T(8,128)(2,1)} %get-tuple-element.109) | copy-start | bytes 4325380
  340.1 5.7 copy-start.23
  342.6 3.2 copy-start.24
  702.8 4.3 copy-start.5
  707.1 12.7 %slice-start = ((s8[6291456]{0:T(1024)(128)(4,1)}), s8[4194304]{0:T(1024)(128)(4,1)S(1)}, s32[]{:S(2)}) async-start(s8[6291456]{0:T(1024)(128)(4,1)} %bitcast.43), calls=%async_computation | async-start | bytes 8388608
  712.5 7.3 slice-start.1
  719.8 5.3 copy-start.15
  725.1 15.6 %slice-start.4 = ((s8[5767168]{0:T(1024)(128)(4,1)}), s8[1572864]{0:T(1024)(128)(4,1)S(1)}, s32[]{:S(2)}) async-start(s8[5767168]{0:T(1024)(128)(4,1)} %bitcast.49), calls=%async_computation.4 | async-start | bytes 3145728
  727.9 4.3 copy-start.6
  732.2 8.6 %slice-start.5 = ((s8[5767168]{0:T(1024)(128)(4,1)}), s8[4194304]{0:T(1024)(128)(4,1)S(1)}, s32[]{:S(2)}) async-start(s8[5767168]{0:T(1024)(128)(4,1)} %bitcast.49), calls=%async_computation.5 | async-start | bytes 8388608
  740.7 5.7 slice-start.2
  740.8 6.4 slice-start.3
  747.1 5.6 copy-start.13
  747.1 5.6 copy-start.19
  747.1 5.6 copy-start.27
  747.1 5.6 copy-start.28
  747.1 5.6 copy-start.29
  752.7 1.6 copy-start.1

commit v7 on v6

--- a/solution.py
+++ b/solution.py
@@ -93,9 +93,9 @@
 
 
 def front_kernel(
-    scale, chunks, tokens, gains, cotangent, w_query, w_key, w_value, segments, freq,
-    x, normed, inv_one, gain_two, grads, query, keys, values, attn, lse, query_seg, key_seg, cos, sin,
-    wq_v, wk_v, wv_v, gains_in, l_sem, x_send, x_recv, s_sem, r_sem, kv_send, kv_recv,
+    scale, chunks, tokens, gains, cotangent, w_query, w_key, w_value, segments, freq, routes,
+    x, normed, inv_one, gain_two, grads, query, keys, values, attn, lse, query_seg, key_seg, cos, sin, hot, hot_peer,
+    hot_low, wq_v, wk_v, wv_v, gains_in, l_sem, x_send, x_recv, s_sem, r_sem, kv_send, kv_recv,
 ):
     n, me = lax.axis_size("tp"), lax.axis_index("tp")
     y = lax.axis_index("ep")
@@ -142,6 +142,17 @@
     g_copies = [remote(gains_in.at[0], gains_in.at[d], s_sem.at[d - 1], r_sem.at[d - 1], tp[d - 1]) for d in range(1, n)]
     for copy in g_copies:
         copy.start()
+
+    top = routes.shape[0]
+    chosen = jnp.concatenate([routes[...].astype(F32), jnp.zeros((128 - top, rows), F32)], axis=0).T
+    slot = lax.broadcasted_iota(jnp.int32, (1, hot.shape[1]), 1).astype(F32)
+    used = jnp.zeros(hot.shape, F32)
+    for k in range(top):
+        used = used + jnp.where(chosen[:, k : k + 1] == slot, 1.0, 0.0)
+    hot[...] = used
+    hot_low[...] = used.astype(BF16)
+    hot_copy = remote(hot_low, hot_peer, s_sem.at[2 * n - 1], r_sem.at[2 * n - 1], to_y)
+    hot_copy.start()
 
     at = (y * rows + lax.broadcasted_iota(jnp.int32, (rows, 1), 0)).astype(F32)
     angle = at * freq[...]
@@ -323,9 +334,10 @@
 
     for copy in g_copies:
         copy.wait_send()
-
-
-def front(tokens, gains, cotangent, w_query, w_key, w_value, segments, freq):
+    hot_copy.wait()
+
+
+def front(tokens, gains, cotangent, w_query, w_key, w_value, segments, freq, routes, slots):
     rows, own = tokens.shape
     n = lax.axis_size("tp")
     width = n * own
@@ -345,28 +357,29 @@
             shape(rows, width), shape(rows, width), shape(rows, 1, kind=F32), shape(1, width, kind=F32),
             shape(rows, width), shape(rows, mine), shape(2 * rows, mine), shape(2 * rows, mine), shape(rows, mine),
             shape(rows, heads, kind=F32), shape(rows, 1, kind=F32), shape(1, 2 * rows, kind=F32),
-            shape(rows, HD, kind=F32), shape(rows, HD, kind=F32),
+            shape(rows, HD, kind=F32), shape(rows, HD, kind=F32), shape(rows, slots, kind=F32), shape(rows, slots),
         ],
-        in_specs=[vmem] * 2 + [far] * 4 + [vmem] * 2,
-        out_specs=[vmem] * 4 + [far] + [vmem] * 9,
-        scratch_shapes=[pltpu.VMEM((width, mine), BF16)] * 3
+        in_specs=[vmem] * 2 + [far] * 4 + [vmem] * 3,
+        out_specs=[vmem] * 4 + [far] + [vmem] * 11,
+        scratch_shapes=[pltpu.VMEM((rows, slots), BF16)]
+        + [pltpu.VMEM((width, mine), BF16)] * 3
         + [pltpu.VMEM((n, 16, own), BF16), dma((4,)), dma((chunks, n, 2)), dma((chunks, n))]
         + [dma((2 * n,)), dma((2 * n,)), dma((heads, 2)), dma((heads, 2))],
         compiler_params=pltpu.CompilerParams(
-            collective_id=7, has_side_effects=True, vmem_limit_bytes=62 << 20
+            collective_id=7, has_side_effects=True, vmem_limit_bytes=44 << 20
         ),
         cost_estimate=pl.CostEstimate(flops=0, bytes_accessed=0, transcendentals=0),
-    )(tokens, gains, cotangent, w_query, w_key, w_value, segments, freq)
+    )(tokens, gains, cotangent, w_query, w_key, w_value, segments, freq, routes)
 
 
 def tail_kernel(
     scale,
-    sgu, sd, egu, ed, flat, normed, w_query, w_key, w_value, attn, ffn,
+    _sgu, _sd, egu, _ed, flat, normed, w_query, w_key, w_value, attn, ffn,
     tokens, inv_one, low, w_out, query, keys, values, lse, query_seg, key_seg, cos, sin,
     sgu_f, sd_f, egu_f, ed_f, qkv_f, wo_f, flat_f, ffn_own, normed_own, row_total, gain_f,
     normed_v, wq_v, wk_v, wv_v, attn_v, grad_attn, grad_key, grad_value, early, came, grad_qkv,
     q_sent, q_half, q_in, q_in2, q_out, w_sent, w_half, w_in, w_in2, w_out_v,
-    e_own, e_in, flat_in, ffn_in, grad_normed, normed_in, row_in, gain_in, l_sem, s_sem, r_sem,
+    e_own, e_in, flat_in, ffn_in, ffn_sent, ffn_came, grad_normed, normed_in, row_in, gain_in, l_sem, s_sem, r_sem,
 ):
     core, x, y, (to_core, to_x, to_y) = places()
     used = [0, 0]
@@ -408,18 +421,17 @@
     greet_all([to_core, to_x, to_y] + tp)
 
     b3 = there(egu.at[pl.ds((1 - x) * e_rows, e_rows)], e_in, to_x)
-    b6 = there(ed, ed_f.at[core, x], to_x)
-    d3 = [there(sd.at[0], sd_f.at[core, 0, y], to_y)]
+    b6 = there(ed_f.at[core, x], ed_f.at[core, x], to_x)
+    d3 = [there(sd_f.at[core, 0, y], sd_f.at[core, 0, y], to_y)]
     f1 = there(flat, flat_in.at[0], to_core)
-    z_ffn = [there(ffn.at[:, columns(d)], ffn_in.at[d], tp[d - 1]) for d in range(1, n)]
-    own_ffn = here(ffn.at[:, columns(0)], ffn_in.at[0])
+    z_ffn = [
+        there(ffn.at[pl.ds(rows, rows), columns(d)], ffn_in.at[n + d], tp[d - 1]) for d in range(1, n)
+    ]
+    own_ffn = [here(ffn.at[pl.ds(m * rows, rows), columns(0)], ffn_in.at[m * n]) for m in (1, 0)]
     load_attn = here(attn, attn_v)
     load_normed = here(normed, normed_v)
     loads = [here(w_query, wq_v), here(w_key, wk_v), here(w_value, wv_v)]
     load_e = here(egu.at[pl.ds(x * e_rows, e_rows)], e_own)
-    own_ed = here(ed, ed_f.at[core, x])
-    own_s = here(sgu, sgu_f.at[core, y])
-    own_sd = [here(sd.at[p], sd_f.at[core, p, y]) for p in range(2)]
 
     grad_attn[...] = mm_nt(low[...], w_out[...]).astype(BF16)
     key_at = (y - 1) * rows + lax.broadcasted_iota(jnp.int32, (1, 2 * rows), 1)
@@ -453,7 +465,7 @@
         turned = grad_q * cos[...] + pltpu.roll(grad_q, HD // 2, 1) * sin[...]
         grad_qkv[:, own] = turned.astype(BF16)
 
-    d1 = there(sgu.at[0], sgu_f.at[core, y, 0], to_y)
+    d1 = there(sgu_f.at[core, y, 1 - x], sgu_f.at[core, y, 1 - x], to_y)
     load_attn.wait()
     half_of = low.shape[1] // 2
     w_sent[...] = mm_tn(attn_v[...], low[:, pl.ds(pl.multiple_of((1 - core) * half_of, half_of), half_of)]).astype(BF16)
@@ -508,7 +520,6 @@
         here_rows = slice(i * step, (i + 1) * step)
         q_half[here_rows, :] = (value + q_half[here_rows, :].astype(F32)).astype(BF16)
     a1 = there(q_half.at[pl.ds((1 - y) * q_rows, q_rows)], q_in, to_y)
-    d2 = there(sgu.at[1], sgu_f.at[core, y, 1], to_y)
     for copy in loads:
         copy.wait()
     grad_normed[...] = (
@@ -517,6 +528,7 @@
         + mm_nt(grad_qkv[:, 2 * mine :], wv_v[...])
     ).astype(BF16)
     z_normed = [there(grad_normed.at[:, columns(d)], normed_in.at[d], tp[d - 1]) for d in range(1, n)]
+    z_own = [there(ffn.at[pl.ds(0, rows), columns(d)], ffn_in.at[d], tp[d - 1]) for d in range(1, n)]
 
     load_e.wait()
     b3.wait_recv()
@@ -534,7 +546,16 @@
     add_rows(q_half, q_in, y * q_rows, q_rows)
     a3 = there(q_half.at[pl.ds(y * q_rows + (1 - x) * (q_rows // 2), q_rows // 2)], q_in2, to_x)
     own_e = here(e_own, egu_f.at[core, x])
-    d3.append(there(sd.at[1], sd_f.at[core, 1, y], to_y))
+    d3.append(there(sd_f.at[core, 1, y], sd_f.at[core, 1, y], to_y))
+    for copy in own_ffn:
+        copy.wait()
+    for copy in z_ffn:
+        copy.wait_recv()
+    total = ffn_in[n].astype(F32)
+    for m in range(n + 1, 2 * n):
+        total = total + ffn_in[m].astype(F32)
+    ffn_sent[...] = total.astype(BF16)
+    o1 = there(ffn_sent, ffn_came, to_y)
     for copy in z_normed + z_rows:
         copy.wait_recv()
     total = grad_normed[:, columns(0)].astype(F32)
@@ -561,19 +582,9 @@
     own_q = here(q_out, qkv_f.at[core, y, x])
     b5 = there(e_own.at[pl.ds(cut, cut_b - cut)], egu_f.at[core, x, pl.ds(cut, cut_b - cut)], to_x)
     b7 = there(e_own.at[pl.ds(cut_b, e_rows - cut_b)], egu_f.at[core, x, pl.ds(cut_b, e_rows - cut_b)], to_x)
-    own_ffn.wait()
-    for copy in z_ffn:
-        copy.wait_recv()
-    total = ffn_in[0].astype(F32)
-    for d in range(1, n):
-        total = total + ffn_in[d].astype(F32)
-    ffn_own[...] = total
-    own_ed.wait()
     b6.wait_recv()
     c6 = there(ed_f.at[core], ed_f.at[core], to_core)
-    own_s.wait()
     d1.wait_recv()
-    d2.wait_recv()
     c1 = there(sgu_f.at[core], sgu_f.at[core], to_core)
     g2.wait_recv()
     g2.wait_send()
@@ -585,8 +596,6 @@
     a5.wait_recv()
     own_q.wait()
     a7 = there(qkv_f.at[core, y], qkv_f.at[core, y], to_y)
-    for copy in own_sd:
-        copy.wait()
     for copy in d3:
         copy.wait_recv()
     c2 = there(sd_f.at[core], sd_f.at[core], to_core)
@@ -607,6 +616,13 @@
     g3.wait_recv()
     g3.wait_send()
     gain_f[...] = gain_f[...] + gain_in[2]
+    for copy in z_own:
+        copy.wait_recv()
+    o1.wait_recv()
+    total = ffn_came[...].astype(F32)
+    for m in range(n):
+        total = total + ffn_in[m].astype(F32)
+    ffn_own[...] = total
     for copy in (c1, c2, c3, c4, c5, c6, c7):
         copy.wait_recv()
     for copy in sent:
@@ -634,8 +650,8 @@
     return pl.pallas_call(
         functools.partial(tail_kernel, 1.0 / math.sqrt(HD)),
         out_shape=[
-            pieces(3, *sgu.shape[1:]), pieces(3, *sd.shape[1:]),
-            pieces(2, egu.shape[0] // 2, egu.shape[1]), pieces(2, *ed.shape),
+            jax.ShapeDtypeStruct(sgu.shape, BF16), jax.ShapeDtypeStruct(sd.shape, BF16),
+            pieces(2, egu.shape[0] // 2, egu.shape[1]), jax.ShapeDtypeStruct(ed.shape, BF16),
             pieces(3, half_of // 4, 3 * mine), pieces(3, mine // 4, half_of),
             jax.ShapeDtypeStruct(flat.shape, F32), jax.ShapeDtypeStruct(tokens.shape, F32),
             jax.ShapeDtypeStruct(tokens.shape, F32), jax.ShapeDtypeStruct((8, rows), F32),
@@ -652,10 +668,11 @@
             room(mine, half_of), room(mine, half_of), room(mine // 2, half_of),
             room(mine // 4, half_of), room(mine // 4, half_of),
             room(egu.shape[0] // 2, egu.shape[1]), room(egu.shape[0] // 2, egu.shape[1]),
-            room(3, *flat.shape, kind=F32), room(n, *tokens.shape), room(rows, width), room(n, *tokens.shape),
+            room(3, *flat.shape, kind=F32), room(2 * n, *tokens.shape), room(*tokens.shape), room(*tokens.shape), room(rows, width), room(n, *tokens.shape),
             room(n, 8, rows, kind=F32), room(3, 8, tokens.shape[1], kind=F32),
-            dma((16,)), dma((38 + heads + 3 * n,)), dma((38 + heads + 3 * n,)),
+            dma((18,)), dma((38 + heads + 4 * n,)), dma((38 + heads + 4 * n,)),
         ],
+        input_output_aliases={0: 0, 1: 1, 3: 3},
         compiler_params=pltpu.CompilerParams(
             collective_id=3, has_side_effects=True, vmem_limit_bytes=62 << 20
         ),
@@ -687,7 +704,7 @@
         value = value.reshape(across, kinds, -1, columns)
         rows = value.shape[2]
         step = rows
-        while step * columns > (1 << 19) and step % 32 == 0:
+        while step * columns > (1 << 20) and step % 32 == 0:
             step //= 2
         steps = rows // step
         source = pl.BlockSpec((1, 1, step, columns), lambda i, c: (c, kind, i, 0))
@@ -700,7 +717,7 @@
         in_specs=[source],
         out_specs=specs,
         out_shape=shapes,
-        compiler_params=pltpu.CompilerParams(vmem_limit_bytes=32 << 20),
+        compiler_params=pltpu.CompilerParams(vmem_limit_bytes=24 << 20),
         cost_estimate=pl.CostEstimate(flops=0, bytes_accessed=0, transcendentals=0),
     )(value)
 
@@ -744,13 +761,11 @@
     )(which.reshape(1).astype(jnp.int32), left, right, *extra)
 
 
-def ffn_kernel(groups, base, into, flipped, carry, *refs):
+def ffn_kernel(groups, base, flipped, carry, *refs):
     rows, grads, scale, *stored = refs[:6]
     refs = refs[6:]
     if base:
         base_out, base_dx = refs[:2]
-        refs = refs[2:]
-    if into:
         refs = refs[2:]
     sources, refs = refs[: len(carry)], refs[len(carry) :]
     hid_ref, dgu_ref, out_ref, dx_ref, small_ref, *refs = refs
@@ -824,8 +839,9 @@
     out = mm(hid, down_w[...])
     dx = back(dgate, gate_w[...]) + back(dup, up_w[...])
     if base:
-        out = out + base_out[...].astype(F32)
-        dx = dx + base_dx[...].astype(F32)
+        own = jnp.where(2 * pl.program_id(0) >= pl.num_programs(0), 1.0, 0.0)
+        out = out + own * base_out[...].astype(F32)
+        dx = dx + own * base_dx[...].astype(F32)
     out_ref[...] = out.astype(BF16)
     dx_ref[...] = dx.astype(BF16)
     if carry:
@@ -836,39 +852,42 @@
                 copy.wait()
 
 
-def ffn(rows, grads, scale, gate_w, up_w, down_w, start=0, total=0, base=(), into=(), flipped=False, carry=(), number=None):
-    count, groups = scale.shape
+def ffn(rows, grads, scale, gate_w, up_w, down_w, count, base=(), flipped=False, carry=(), number=None):
+    groups = scale.shape[1]
     width = rows.shape[1]
     hidden = down_w.shape[0]
     block = min(256, count)
-    first = start // block
-    total = total or count
-    place = first if total > count else 0
-
-    def at(n, offset):
-        return pl.BlockSpec((block, n), lambda i: (i + offset, 0))
+    steps = count // block
+
+    def at(n):
+        if base:
+            return pl.BlockSpec((block, n), lambda i: ((i + steps // 2) % steps, 0))
+        return pl.BlockSpec((block, n), lambda i: (i, 0))
+
+    def late(n):
+        return pl.BlockSpec((block, n), lambda i: (jnp.maximum(i - steps // 2, 0), 0))
 
     far = pl.BlockSpec(memory_space=pl.ANY)
     return pl.pallas_call(
         functools.partial(
-            ffn_kernel, groups, bool(base), bool(into), flipped, tuple(c[1:] for c in carry)
+            ffn_kernel, groups, bool(base), flipped, tuple(c[1:] for c in carry)
         ),
-        grid=(count // block,),
-        in_specs=[at(width, first), at(width, first), at(groups, 0)]
+        grid=(steps,),
+        in_specs=[at(width), at(width), at(groups)]
         + [far] * 3
-        + [at(width, 0)] * len(base)
-        + [far] * (len(into) + len(carry)),
+        + [late(width)] * len(base)
+        + [far] * len(carry),
         out_specs=[
-            at(hidden, place),
-            at(2 * hidden, place),
-            at(width, 0),
-            at(width, 0),
-            at(groups + 1, 0),
+            at(hidden),
+            at(2 * hidden),
+            at(width),
+            at(width),
+            at(groups + 1),
         ]
         + [far] * len(carry),
         out_shape=[
-            jax.ShapeDtypeStruct((total, hidden), BF16),
-            jax.ShapeDtypeStruct((total, 2 * hidden), BF16),
+            jax.ShapeDtypeStruct((count, hidden), BF16),
+            jax.ShapeDtypeStruct((count, 2 * hidden), BF16),
             jax.ShapeDtypeStruct((count, width), BF16),
             jax.ShapeDtypeStruct((count, width), BF16),
             jax.ShapeDtypeStruct((count, groups + 1), F32),
@@ -877,12 +896,11 @@
         scratch_shapes=([pltpu.SemaphoreType.DMA((len(carry),))] * 2 if carry else [])
         + [pltpu.VMEM(w.shape, BF16) for w in (gate_w, up_w, down_w)]
         + [pltpu.SemaphoreType.DMA((3,))],
-        input_output_aliases={6 + len(base) + k: k for k in range(len(into))},
         compiler_params=pltpu.CompilerParams(
             vmem_limit_bytes=62 << 20, collective_id=number, has_side_effects=bool(carry)
         ),
         cost_estimate=pl.CostEstimate(flops=0, bytes_accessed=0, transcendentals=0),
-    )(rows, grads, scale, gate_w, up_w, down_w, *base, *into, *[c[0] for c in carry])
+    )(rows, grads, scale, gate_w, up_w, down_w, *base, *[c[0] for c in carry])
 
 
 def line_sum(depth, prepare, settle, gathered, beside, part, came, came_two, spread, sems):
@@ -1060,8 +1078,8 @@
 
 
 def attend_out_kernel(
-    chunks, step, depth, eps, attn, w_out, x, gain, grads,
-    mixed, resid_own, inv_out, grads_peer,
+    chunks, step, depth, experts, attn, w_out, x, gain, grads, w_small, hot, hot_peer,
+    mixed, resid_own, inv_out, grads_peer, logits, prob, switch, gates,
     part, came, came_two, spread, s0, s1, s2, s3, s4, y_send, y_recv, g_send, g_recv,
 ):
     n = lax.axis_size("tp")
@@ -1102,6 +1120,17 @@
     def settle(c, total):
         return total.astype(BF16)
 
+    place = lax.broadcasted_iota(jnp.int32, (1, w_small.shape[0]), 1)
+    here = lax.axis_index("ep") == 0
+
+    def chances(scores):
+        scores = jnp.where(place < experts, scores, NEG)
+        raised = jnp.exp(scores - jnp.max(scores, axis=1, keepdims=True))
+        return jnp.where(place < experts, raised / jnp.sum(raised, axis=1, keepdims=True), 0.0)
+
+    def own_gates(value):
+        return jnp.where(here, value[:, : experts // 2], value[:, experts // 2 : experts])
+
     def gathered(c):
         resid = []
         square = jnp.zeros((step, 1), F32)
@@ -1109,7 +1138,7 @@
             piece = x[at(c), s * own:(s + 1) * own].astype(F32) + spread[c, s].astype(F32)
             resid.append(piece)
             square = square + jnp.sum(piece * piece, axis=1, keepdims=True)
-        inv = lax.rsqrt(square / (n * own) + eps)
+        inv = lax.rsqrt(square / (n * own) + EPS)
         inv_out[at(c), :] = inv
         for s in range(n):
             mixed[at(c), s * own:(s + 1) * own] = (resid[s] * inv * gain[:, s * own:(s + 1) * own]).astype(BF16)
@@ -1121,6 +1150,13 @@
         peer_copy(c).start()
 
     line_sum(depth, prepare, settle, gathered, None, part, came, came_two, spread, (s0, s1, s2, s3, s4))
+
+    scores = mm_nt(mixed[:rows, :], w_small[...])
+    chance = chances(scores)
+    logits[...] = scores
+    prob[...] = chance
+    switch[...] = 1.0 / (1.0 + jnp.exp(-scores[:, experts : experts + 1]))
+    gates[:rows, :] = own_gates(chance * hot[...])
 
     def last(c, carry):
         peer_copy(c).wait_recv()
@@ -1128,35 +1164,39 @@
         return carry
 
     lax.fori_loop(0, chunks, last, 0)
+    chance = chances(mm_nt(mixed[rows:, :], w_small[...]))
+    gates[rows:, :] = own_gates(chance * hot_peer[...].astype(F32))
     grads_copy.wait()
 
 
-def attend_out(attn, w_out, x, gain, grads, width_own, depth=1):
+def attend_out(attn, w_out, x, gain, grads, w_small, hot, hot_peer, experts, width_own, depth=1):
     rows, width = x.shape
     chunks, step, scratch = line_scratch(rows, width_own)
     vmem = pl.BlockSpec(memory_space=pltpu.VMEM)
     far = pl.BlockSpec(memory_space=pl.ANY)
     dma = pltpu.SemaphoreType.DMA
     return pl.pallas_call(
-        functools.partial(attend_out_kernel, chunks, step, depth, EPS),
+        functools.partial(attend_out_kernel, chunks, step, depth, experts),
         out_shape=[
             jax.ShapeDtypeStruct((2 * rows, width), BF16),
             jax.ShapeDtypeStruct((rows, width_own), F32), jax.ShapeDtypeStruct((rows, 1), F32),
             jax.ShapeDtypeStruct((rows // 2, width), BF16),
+            jax.ShapeDtypeStruct(hot.shape, F32), jax.ShapeDtypeStruct(hot.shape, F32),
+            jax.ShapeDtypeStruct((rows, 1), F32), jax.ShapeDtypeStruct((2 * rows, experts // 2), F32),
         ],
-        in_specs=[vmem] * 4 + [far],
-        out_specs=[vmem] * 3 + [far],
+        in_specs=[vmem] * 4 + [far] + [vmem] * 3,
+        out_specs=[vmem] * 3 + [far] + [vmem] * 4,
         scratch_shapes=scratch + [dma((chunks,)), dma((chunks,)), dma, dma],
         compiler_params=pltpu.CompilerParams(collective_id=1, has_side_effects=True, vmem_limit_bytes=40 << 20),
         cost_estimate=pl.CostEstimate(flops=0, bytes_accessed=0, transcendentals=0),
-    )(attn, w_out, x, gain, grads)
+    )(attn, w_out, x, gain, grads, w_small, hot, hot_peer)
 
 
 def resid_grad_kernel(
-    chunks, step, depth, tiles, grad, grad_p, out_p, dgu, hid, both, both_grad, sgu, sd,
+    chunks, step, depth, tiles, grads_all, dgu, hid, both, both_grad, sgu, sd,
     small_e, small_p, small_s, prob, hot, logits, switch, w_small, g_own, resid_own, inv_two, gain,
-    low, grad_resid, gain_grad, out_back, sum_egu, sum_ed, sgu_x, sd_x, grad_small,
-    part, came, came_two, spread, s0, s1, s2, s3, s4, back, y_send, y_recv, o_send, o_recv,
+    low, grad_resid, gain_grad, sum_egu, ed_f, sgu_f, sd_f, grad_small,
+    part, came, came_two, spread, s0, s1, s2, s3, s4, back, y_send, y_recv, grad,
     dgu_v, hid_v, both_v, both_grad_v, sent_egu, sent_ed, came_egu, came_ed,
     s_own, s_in, d_own, d_in, l_sem, w_send, w_recv, w_out, r_send, r_recv, r_out,
     router, along, small_y, small_z, ed_in, ed_out, t_send, t_recv, e_send, e_recv, e_out,
@@ -1164,6 +1204,7 @@
     n = lax.axis_size("tp")
     own = part.shape[3]
     rows = grad.shape[0]
+    load_grad = pltpu.make_async_copy(grads_all.at[pl.ds(0, rows)], grad, l_sem.at[6])
     core, x, y, (to_core, to_x, other) = places()
 
     def at(c):
@@ -1171,13 +1212,7 @@
 
     def peer_copy(c):
         return pltpu.make_async_remote_copy(
-            src_ref=grad_p.at[at(c)], dst_ref=back.at[at(c)], send_sem=y_send.at[c], recv_sem=y_recv.at[c],
-            device_id=other, device_id_type=pl.DeviceIdType.MESH,
-        )
-
-    def out_copy():
-        return pltpu.make_async_remote_copy(
-            src_ref=out_p, dst_ref=out_back, send_sem=o_send, recv_sem=o_recv,
+            src_ref=grads_all.at[pl.ds(pl.multiple_of(rows + c * step, step), step)], dst_ref=back.at[at(c)], send_sem=y_send.at[c], recv_sem=y_recv.at[c],
             device_id=other, device_id_type=pl.DeviceIdType.MESH,
         )
 
@@ -1194,14 +1229,15 @@
             )
         )
     ]
-    kinds = ((dgu_v, both_v, sent_egu, came_egu, sum_egu), (hid_v, both_grad_v, sent_ed, came_ed, sum_ed))
+    kinds = ((dgu_v, both_v, sent_egu, came_egu, sum_egu), (hid_v, both_grad_v, sent_ed, came_ed, None))
 
     def sum_copies(m):
         source, target, where = (
             (sgu.at[pl.ds((1 - x) * s_own.shape[0], s_own.shape[0])], s_in, to_x),
             (sd.at[pl.ds((1 - y) * d_own.shape[0], d_own.shape[0])], d_in, other),
-            (s_own, sgu_x.at[x], to_x),
-            (d_own, sd_x.at[x], to_x),
+            (s_own, sgu_f.at[core, y, x], to_x),
+            (d_own, sd_f.at[core, x, y], to_x),
+            (s_own, sgu_f.at[core, y, x], other),
         )[m]
         return pltpu.make_async_remote_copy(
             src_ref=source, dst_ref=target, send_sem=r_send.at[m], recv_sem=r_recv.at[m],
@@ -1209,12 +1245,15 @@
         )
 
     def own_out(m):
-        return pltpu.make_async_copy((s_own, d_own)[m], (sgu_x, sd_x)[m].at[x], r_out.at[m])
+        target = (sgu_f.at[core, y, x], sd_f.at[core, x, y])[m]
+        return pltpu.make_async_copy((s_own, d_own)[m], target, r_out.at[m])
 
     def shared(m):
         sum_copies(m).wait_recv()
         add_rows((s_own, d_own)[m], (s_in, d_in)[m], 0, (s_own, d_own)[m].shape[0])
         sum_copies(2 + m).start()
+        if m == 0:
+            sum_copies(4).start()
         own_out(m).start()
 
     def tile_copy(m, b):
@@ -1234,7 +1273,7 @@
     def x_out(b):
         tall = ed_in.shape[1]
         return pltpu.make_async_copy(
-            ed_out.at[b], sum_ed.at[pl.ds(pl.multiple_of(b * tall, tall), tall)], e_out.at[b]
+            ed_out.at[b], ed_f.at[core, x, pl.ds(pl.multiple_of(b * tall, tall), tall)], e_out.at[b]
         )
 
     def tile_out(m, b):
@@ -1287,6 +1326,7 @@
                 else:
                     x_copy(b).start()
 
+    load_grad.start()
     for copy in loads:
         copy.start()
     me = lax.axis_index("tp")
@@ -1308,7 +1348,6 @@
 
     lax.fori_loop(0, chunks, begin, 0)
     sum_copies(1).start()
-    out_copy().start()
     gain_grad[...] = jnp.zeros_like(gain_grad)
     experts_own = small_e.shape[0] - 1
     experts = 2 * experts_own
@@ -1335,13 +1374,18 @@
         grad_switch = total[:, experts : experts + 1] * sw * (1.0 - sw)
         place = lax.broadcasted_iota(jnp.int32, (1, slots), 1)
         grads = jnp.where(place == experts, grad_switch, prob[...] * (grad_prob - inner)).astype(BF16)
-        router[...] = mm_nt(grads, w_small[...])
+        width = w_small.shape[1] // n
+        router[...] = mm(grads, w_small[:, pl.ds(pl.multiple_of(me * width, width), width)])
         along[...] = total[:, experts + 1 : experts + 2] + jnp.sum(
             grads.astype(F32) * logits[...], axis=1, keepdims=True
         )
         grad_small[...] = mm_tn(grads, both_v[:rows, :])
 
     def prepare(c):
+        @pl.when(c == 0)
+        def _():
+            load_grad.wait()
+
         peer_copy(c).wait_recv()
         for s in range(n):
             columns = slice(s * own, (s + 1) * own)
@@ -1367,7 +1411,6 @@
         return carry
 
     lax.fori_loop(0, chunks, last, 0)
-    out_copy().wait()
 
     def done(b, carry):
         x_copy(b).wait_recv()
@@ -1392,12 +1435,13 @@
         sum_copies(m).wait_send()
         sum_copies(2 + m).wait()
         own_out(m).wait()
+    sum_copies(4).wait()
     for d in range(n):
         small_copy(d).wait_send()
 
 
-def resid_grad(grad, grad_p, out_p, dgu, hid, both, both_grad, sgu, sd, small_e, small_p, small_s, prob, hot, logits, switch, w_small, g_own, resid_own, inv_two, gain, depth=1):
-    rows, width = grad.shape
+def resid_grad(grads_all, dgu, hid, both, both_grad, sgu, sd, small_e, small_p, small_s, prob, hot, logits, switch, w_small, g_own, resid_own, inv_two, gain, depth=1):
+    rows, width = grads_all.shape[0] // 2, grads_all.shape[1]
     width_own = g_own.shape[1]
     chunks, step, scratch = line_scratch(rows, width_own)
     hidden = hid.shape[1]
@@ -1409,25 +1453,28 @@
         functools.partial(resid_grad_kernel, chunks, step, depth, tiles),
         out_shape=[
             jax.ShapeDtypeStruct((rows, width), BF16), jax.ShapeDtypeStruct((rows, width_own), F32),
-            jax.ShapeDtypeStruct((1, width_own), F32), jax.ShapeDtypeStruct((rows, width), BF16),
+            jax.ShapeDtypeStruct((1, width_own), F32),
         ]
-        + [jax.ShapeDtypeStruct((2 * hidden, width // 2), BF16), jax.ShapeDtypeStruct((hidden, width // 4), BF16)]
-        + [jax.ShapeDtypeStruct((2, v.shape[0] // 2, v.shape[1]), BF16) for v in (sgu, sd)]
+        + [jax.ShapeDtypeStruct((2 * hidden, width // 2), BF16), jax.ShapeDtypeStruct((2, 2, hidden, width // 4), BF16)]
+        + [
+            jax.ShapeDtypeStruct((2, 2, 2, sgu.shape[0] // 2, sgu.shape[1]), BF16),
+            jax.ShapeDtypeStruct((2, 2, 2, sd.shape[0] // 2, sd.shape[1]), BF16),
+        ]
         + [jax.ShapeDtypeStruct((prob.shape[1], width), F32)],
-        in_specs=[vmem] + [far] * 8 + [vmem] * 12,
-        out_specs=[vmem] * 3 + [far] * 5 + [vmem],
-        scratch_shapes=scratch + [pltpu.VMEM((rows, width), BF16), dma((chunks,)), dma((chunks,)), dma, dma]
+        in_specs=[far] * 7 + [vmem] * 12,
+        out_specs=[vmem] * 3 + [far] * 4 + [vmem],
+        scratch_shapes=scratch + [pltpu.VMEM((rows, width), BF16), dma((chunks,)), dma((chunks,)), pltpu.VMEM((rows, width), BF16)]
         + [pltpu.VMEM(v.shape, BF16) for v in (dgu, hid, both, both_grad)]
         + [pltpu.VMEM((tiles, k * hidden // tiles, width // 2), BF16) for k in (2, 1, 2, 1)]
         + [pltpu.VMEM((v.shape[0] // 2, v.shape[1]), BF16) for v in (sgu, sgu, sd, sd)]
-        + [dma((6,)), dma((tiles, 2)), dma((tiles, 2)), dma((tiles, 2)), dma((4,)), dma((4,)), dma((2,))]
+        + [dma((7,)), dma((tiles, 2)), dma((tiles, 2)), dma((tiles, 2)), dma((5,)), dma((5,)), dma((2,))]
         + [pltpu.VMEM((rows, width_own), F32), pltpu.VMEM((rows, 1), F32)]
         + [pltpu.VMEM(small_e.shape, F32), pltpu.VMEM((lax.axis_size("tp"), 16, rows), F32)]
         + [pltpu.VMEM((tiles, hidden // tiles, width // 4), BF16)] * 2
         + [dma((lax.axis_size("tp"),))] * 2 + [dma((tiles,))] * 3,
         compiler_params=pltpu.CompilerParams(collective_id=2, has_side_effects=True, vmem_limit_bytes=63 << 20),
         cost_estimate=pl.CostEstimate(flops=0, bytes_accessed=0, transcendentals=0),
-    )(grad, grad_p, out_p, dgu, hid, both, both_grad, sgu, sd, small_e, small_p, small_s, prob, hot, logits, switch, w_small, g_own, resid_own, inv_two, gain)
+    )(grads_all, dgu, hid, both, both_grad, sgu, sd, small_e, small_p, small_s, prob, hot, logits, switch, w_small, g_own, resid_own, inv_two, gain)
 
 
 def body(
@@ -1504,35 +1551,19 @@
     freq = ROPE_BASE ** (-(np.arange(HD // 2, dtype=np.float64) * 2.0) / HD)
     freq = jnp.asarray(np.concatenate([freq, freq])[None, :], F32)
     gains = jnp.pad(jnp.stack([norm_attn, norm_ffn]), ((0, 14), (0, 0)))
+    slots = 16
+    w_small = jnp.concatenate(
+        [w_router.T, shared_switch[None, :], jnp.zeros((slots - experts - 1, width), BF16)], axis=0
+    )
     (
         x_full, normed, inv_one, gain_two, grad_rows, query, key_rows, value_rows, attn_rows, log_norm,
-        query_seg, key_seg, cos_table, sin_table,
+        query_seg, key_seg, cos_table, sin_table, hot, hot_peer,
     ) = front(
-        tokens, gains, output_gradient, w_query, w_key, w_value, segments.reshape(1, -1), freq
+        tokens, gains, output_gradient, w_query, w_key, w_value, segments.reshape(1, -1), freq, routes.T, slots
     )
-    route_hot = jnp.sum(
-        (routes[:, :, None] == jnp.arange(experts, dtype=jnp.int32)[None, None, :]).astype(F32),
-        axis=1,
+    both, resid_own, inv_two, grad_peer_a, logits, router_prob, switch, gates = attend_out(
+        attn_rows, w_output, x_full, gain_two, grad_rows, w_small, hot, hot_peer, experts, width_own
     )
-    route_hot_peer = swap(route_hot, "ep", 1)
-
-    both, resid_own, inv_two, grad_peer_a = attend_out(
-        attn_rows, w_output, x_full, gain_two, grad_rows, width_own
-    )
-    mixed = both[:rows]
-
-    def router(values):
-        logits = mm(values, w_router)
-        return logits, jax.nn.softmax(logits, axis=1)
-
-    logits, router_prob = router(mixed)
-    combine = router_prob * route_hot
-    combine_peer = router(both[rows:])[1] * route_hot_peer
-    switch_logit = mm(mixed, shared_switch[:, None])
-    switch = jax.nn.sigmoid(switch_logit)
-
-    def own_experts(value):
-        return lax.dynamic_slice_in_dim(value, ep_rank * experts_own, experts_own, 1)
 
     hid_s, dgu_s, out_s, grad_s, small_s, grad_peer_b = ffn(
         both,
@@ -1541,6 +1572,7 @@
         shared_gate,
         shared_up,
         shared_down,
+        rows,
         carry=[(grad_rows, 2, rows // 2, rows // 2, 0)],
         number=4,
     )
@@ -1549,72 +1581,48 @@
     sent, got_sd = pair_send(hid_s, after(grad_rows, sent), True)
     sum_sgu = pair_keep(both, after(dgu_s, sent, both_grad), False, got_sgu, rows)
     sum_sd = pair_keep(hid_s, after(grad_rows, sum_sgu), True, got_sd)
-    quarter = sum_sgu.shape[0] // 4
 
     hidden_width = experts_own * expert_width
     gate_w = jnp.transpose(expert_gate, (0, 2, 1)).reshape(hidden_width, width)
     up_w = jnp.transpose(expert_up, (0, 2, 1)).reshape(hidden_width, width)
     down_w = expert_down.reshape(hidden_width, width)
-    hid_p, dgu_p, out_p, grad_p, small_p, got_sgu_a, got_sd = ffn(
+    hid_e, dgu_e, out_e, grad_e, small_e, got_sgu, got_sd = ffn(
         both,
         after(both_grad, sum_sd),
-        own_experts(combine_peer),
+        gates,
         gate_w,
         up_w,
         down_w,
-        start=rows,
-        total=2 * rows,
+        2 * rows,
+        base=(out_s, grad_s),
         flipped=True,
         carry=[
-            (sum_sgu, 2, quarter, 0, 2 * quarter),
+            (sum_sgu, 2, sum_sgu.shape[0] // 2, 0, sum_sgu.shape[0] // 2),
             (sum_sd, 1, sum_sd.shape[0] // 2, 0, sum_sd.shape[0] // 2),
         ],
         number=5,
     )
-    hid_e, dgu_e, out_e, grad_e, small_e, got_sgu_b = ffn(
-        both,
-        both_grad,
-        after(own_experts(combine), grad_p),
-        gate_w,
-        up_w,
-        down_w,
-        total=2 * rows,
-        base=(out_s, grad_s),
-        into=(hid_p, dgu_p),
-        flipped=True,
-        carry=[(sum_sgu, 2, quarter, quarter, 2 * quarter)],
-        number=6,
-    )
-    got_sgu = jnp.concatenate([got_sgu_a, got_sgu_b], axis=0)
 
     sum_sgu = reduce_add(sum_sgu, got_sgu, *y_link)
     sum_sd = reduce_add(sum_sd, got_sd, *x_link)
 
-    tp_rows = lax.dynamic_slice_in_dim(w_router, tp_rank * width_own, width_own, 0)
-    spare = 16 - experts - 1
-
-    def slots(value, more=None):
-        more = jnp.zeros((value.shape[0], 1), value.dtype) if more is None else more
-        return jnp.pad(jnp.concatenate([value, more], axis=1), ((0, 0), (0, spare)))
-
-    resid_low, grad_resid, grad_gain_two, out_back, sum_egu, sum_ed, sgu_x, sd_x, grad_small = resid_grad(
+    small_t = small_e.T
+    resid_low, grad_resid, grad_gain_two, sum_egu, ed_f, sgu_f, sd_f, grad_small = resid_grad(
         grad_e,
-        grad_p,
-        out_p,
         dgu_e,
         hid_e,
         both,
         both_grad,
         sum_sgu,
         sum_sd,
-        small_e.T,
-        small_p.T,
+        small_t[:, :rows],
+        small_t[:, rows:],
         small_s.T,
-        slots(router_prob),
-        slots(route_hot),
-        slots(logits, switch_logit),
+        router_prob,
+        hot,
+        logits,
         switch,
-        slots(tp_rows, own_columns(shared_switch)[:, None]),
+        w_small,
         output_gradient,
         resid_own,
         inv_two,
@@ -1625,19 +1633,18 @@
         [grad_gain_two.reshape(-1), grad_small[: experts + 1].reshape(-1)]
     ).reshape(-1, 128)
     inner = shared_gate.shape[1]
-    ffn_part = (out_e.astype(F32) + out_back.astype(F32)).astype(BF16)
     sgu_f, sd_f, egu_f, ed_f, qkv_f, wo_f, flat, ffn_own, normed_own, row_total, grad_gain_one = tail(
-        sgu_x,
-        sd_x,
+        sgu_f,
+        sd_f,
         sum_egu,
-        sum_ed,
+        ed_f,
         flat,
         normed,
         w_query,
         w_key,
         w_value,
         attn_rows,
-        ffn_part,
+        out_e,
         tokens,
         inv_one,
         resid_low,

time: 760 us -> 729 us (0.959)
  Pallas kernels: 677 us -> 666 us
  other arithmetic: 23.8 us -> 13.1 us
    pallas_call x3 -> x2, Pallas kernels: 106 us -> 101 us  [ffn(): pl.pallas_call(functools.partial(ffn_kernel, groups, bool(base), flipped,...]
    unnamed x83 -> x104, local copies, waits for them, and re-layouts: 25.4 us -> 29.1 us
  transfers between devices with their start and end apart: 3 -> 2, of which waited for: 0 -> 0; matrix products, arithmetic and copies ran while one was open for 3% -> 1% of each run, Pallas kernels for 2% -> 2%
where the time goes in v7:
time: 729 us; the launch traced here: 723 us
  Pallas kernels  666 us (91%)
  local copies, waits for them, and re-layouts  42.2 us (6%)
  other arithmetic  13.1 us (2%)
    pallas_call x1, Pallas kernels, tail(): pl.pallas_call(functools.partial(tail_kernel, 1.0 / math.sqrt(HD)), out_s...  220 us
    pallas_call x1, Pallas kernels, resid_grad(): pl.pallas_call(functools.partial(resid_grad_kernel, chunks, step, depth,...  120 us
    pallas_call x2, Pallas kernels, ffn(): pl.pallas_call(functools.partial(ffn_kernel, groups, bool(base), flipped,...  101 us
    pallas_call x1, Pallas kernels, attend_out(): pl.pallas_call(functools.partial(attend_out_kernel, chunks, step, depth,...  85.3 us
    pallas_call x1, Pallas kernels, front(): pl.pallas_call(functools.partial(front_kernel, 1.0 / math.sqrt(HD), chunk...  78.8 us
    pallas_call x7, Pallas kernels, widen(): pl.pallas_call(widen_kernel, grid=grid, in_specs=[source], out_specs=spec...  36.6 us
    unnamed x104, local copies, waits for them, and re-layouts  29.1 us
    pallas_call x4, Pallas kernels, weight_half(): pl.pallas_call(functools.partial(weight_kernel, bool(extra)), grid_spec=p...  24.3 us
  transfers between devices with their start and end apart: 2, of which 0 were waited for; matrix products, arithmetic and copies ran while one was open for 1% of the time, Pallas kernels for 2%

profile of v7, /device:TPU:0, one launch (start us, length us, event | category | flops | bytes accessed | tf_op | source)
XLA Modules:
  0.0 723.3 jit_solution(422810405812525175)
XLA Ops:
  0.7 0.8 stack.10
  1.5 0.7 stack.9
  2.2 0.7 broadcast_in_dim.10
  2.9 0.1 pad.9.clone
  3.0 0.8 maximum_maximum_fusion.w_small
  3.8 0.0 copy-start.8
  3.8 1.1 copy-done.8
  4.9 1.0 copy-done.12
  5.9 0.7 copy-done.33
  6.6 0.7 copy-done.34
  7.3 0.7 copy-done.36
  8.0 78.8 %shard_map.306 = (bf16[512,2048]{1,0:T(8,128)(2,1)S(1)}, bf16[512,2048]{1,0:T(8,128)(2,1)S(1)}, f32[512,1]{1,0:T(8,128)S(1)}, f32[1,2048]{1,0:T(1,128)S(1)}, bf1...) custom-call(bf16[512,512]{1,0:T(8,128)(2,1)S(1)} %copy-done.8, ...), custom_call_target="tpu_custom_call" | custom-call | tf_op jit(solution)/shard_map/pallas_call | solution.py:354
  86.7 0.0 copy-start.14
  86.8 1.3 copy-done.14
  88.1 0.0 copy-start.20
  88.2 3.1 copy-done
  91.3 85.3 %shard_map.307 = (bf16[1024,2048]{1,0:T(8,128)(2,1)}, f32[512,512]{1,0:T(8,128)S(1)}, f32[512,1]{1,0:T(8,128)S(1)}, bf16[256,2048]{1,0:T(8,128)(2,1)S(1)}, f32[5...) custom-call(bf16[512,512]{1,0:T(8,128)(2,1)S(1)} %get-tuple-element.81.attn, ...), custom_call_target="tpu_custom_call" | custom-call | tf_op jit(solution)/shard_map/pallas_call | solution.py:1178
  176.7 1.0 copy-done.10
  177.7 0.7 copy-done.16
  178.4 1.0 copy-done.21
  179.4 0.8 copy-done.25
  180.2 0.7 copy-done.30
  180.9 0.7 copy-done.31
  181.6 0.7 copy-done.32
  182.4 30.9 %shard_map.308 = (bf16[512,1408]{1,0:T(8,128)(2,1)}, bf16[512,2816]{1,0:T(8,128)(2,1)}, bf16[512,2048]{1,0:T(8,128)(2,1)}, bf16[512,2048]{1,0:T(8,128)(2,1)}, f3...) custom-call(bf16[1024,2048]{1,0:T(8,128)(2,1)} %get-tuple-element.88.refs_0_.left.both, ...), custom_call_target="tpu_custom_call" | custom-call | tf_op jit(solution)/shard_map/pallas_call | solution.py:871
  213.3 1.8 copy-done.4
  215.1 7.1 shard_map.309
  222.2 3.3 shard_map.310
  225.5 0.5 collective-permute-start.1
  226.0 1.5 constant_dynamic-update-slice_fusion.2
  227.5 0.1 copy-done.22
  227.6 1.0 constant_dynamic-update-slice_fusion.1
  228.6 1.0 constant_dynamic-update-slice_fusion.refs_1_.both_grad
  229.7 1.7 copy.41
  231.3 0.6 reshape_convert_fusion.gain
  231.9 1.2 fusion.3
  233.1 1.8 copy-done.5
  234.9 8.7 %shard_map.311.refs_8_ = bf16[1024,2816]{1,0:T(8,128)(2,1)} custom-call(s32[1]{0:T(128)} %bitcast.3.part, bf16[1024,2048]{1,0:T(8,128)(2,1)} %get-tuple-element.88.refs_0_.left.both, bf16[512,2816]{1,0:T(8,128)(2,1)S(1)} %copy-done.5, bf16[1024,2816]{1,0:T(8,128)(2,1)} %collective-permute-done.refs_0_), custom_call_target="tpu_custom_call" | custom-call | tf_op jit(solution)/shard_map/pallas_call | solution.py:749
  243.6 5.1 shard_map.312.refs_9_
  248.8 70.2 %shard_map.313 = (bf16[1024,1408]{1,0:T(8,128)(2,1)}, bf16[1024,2816]{1,0:T(8,128)(2,1)}, bf16[1024,2048]{1,0:T(8,128)(2,1)}, bf16[1024,2048]{1,0:T(8,128)(2,1)}...) custom-call(bf16[1024,2048]{1,0:T(8,128)(2,1)} %get-tuple-element.88.refs_0_.left.both, ...), custom_call_target="tpu_custom_call" | custom-call | tf_op jit(solution)/shard_map/pallas_call | solution.py:871
  319.0 1.2 copy.40
  320.2 0.6 fusion.4
  320.8 5.1 add_convert_fusion.sgu
  325.9 1.7 add_convert_fusion.1.sd
  327.6 120.1 %shard_map.314 = (bf16[512,2048]{1,0:T(8,128)(2,1)}, f32[512,512]{1,0:T(8,128)}, f32[1,512]{1,0:T(1,128)}, bf16[2816,1024]{1,0:T(8,128)(2,1)}, bf16[2,2,1408,512...) custom-call(bf16[1024,2048]{1,0:T(8,128)(2,1)} %get-tuple-element.10, ...), custom_call_target="tpu_custom_call" | custom-call | tf_op jit(solution)/shard_map/pallas_call | solution.py:1452
  447.7 0.9 reshape.110
  448.7 1.3 maximum_bitcast_fusion.flat
  450.0 220.0 %shard_map.315 = (bf16[2,2,2,256,2816]{4,3,2,1,0:T(8,128)(2,1)}, bf16[2,2,2,352,1024]{4,3,2,1,0:T(8,128)(2,1)}, bf16[2,2,1408,1024]{3,2,1,0:T(8,128)(2,1)}, bf16...) custom-call(bf16[2,2,2,256,2816]{4,3,2,1,0:T(8,128)(2,1)} %get-tuple, ...), custom_call_target="tpu_custom_call", output_to_operand_aliasing={{0}: (0, {}), {1}: (1, {}), {3}: (3, {})} | custom-call | tf_op jit(solution)/shard_map/pallas_call | solution.py:650
  670.0 1.2 slice_bitcast_fusion.1
  671.2 0.9 slice.38
  672.1 1.3 slice_bitcast_fusion
  673.4 4.3 copy-done.2
  677.7 5.1 shard_map.320
  682.8 4.5 shard_map.321
  687.3 0.9 slice_multiply_fusion
  688.2 1.3 slice.35
  689.5 5.3 shard_map.316
  694.8 2.1 shard_map.317
  696.9 0.6 reshape.114
  697.6 4.3 copy-done.3
  701.9 9.1 %shard_map.318 = (f32[2048,1408]{1,0:T(8,128)}, f32[2048,1408]{1,0:T(8,128)}) custom-call(bf16[2048,2816]{1,0:T(8,128)(2,1)S(1)} %bitcast.37), custom_call_target="tpu_custom_call" | custom-call | tf_op jit(solution)/shard_map/pallas_call | solution.py:714
  711.0 5.1 shard_map.319
  716.2 5.3 shard_map.322
  721.5 1.5 multiply_subtract_fusion
  (89 shorter events, 0.2 us)
Async XLA Ops:
  0.6 87.5 %copy-start.6 = (bf16[512,2048]{1,0:T(8,128)(2,1)S(1)}, bf16[512,2048]{1,0:T(8,128)(2,1)}, u32[]{:S(2)}) copy-start(bf16[512,2048]{1,0:T(8,128)(2,1)} %w_out.3) | copy-start | bytes 6291460
  3.8 172.9 %copy-start.23 = (bf16[16,2048]{1,0:T(8,128)(2,1)}, bf16[16,2048]{1,0:T(8,128)(2,1)S(1)}, u32[]{:S(2)}) copy-start(bf16[16,2048]{1,0:T(8,128)(2,1)S(1)} %maximum_maximum_fusion.w_small) | copy-start | bytes 196612
  3.8 1.1 copy-start.8
  4.9 1.0 copy-start.12
  5.9 0.7 copy-start.33
  6.6 0.7 copy-start.34
  7.3 0.7 copy-start.36
  86.7 1.3 copy-start.14
  88.1 88.6 %copy-start.13 = (bf16[512,512]{1,0:T(8,128)(2,1)}, bf16[512,512]{1,0:T(8,128)(2,1)S(1)}, u32[]{:S(2)}) copy-start(bf16[512,512]{1,0:T(8,128)(2,1)S(1)} %get-tuple-element.81.attn) | copy-start | bytes 1572868
  88.1 94.2 %copy-start.17 = (f32[512,16]{1,0:T(8,128)}, f32[512,16]{1,0:T(8,128)S(1)}, u32[]{:S(2)}) copy-start(f32[512,16]{1,0:T(8,128)S(1)} %get-tuple-element.85.hot) | copy-start | bytes 98308
  88.1 94.2 %copy-start.18 = (f32[512,1]{1,0:T(8,128)}, f32[512,1]{1,0:T(8,128)S(1)}, u32[]{:S(2)}) copy-start(f32[512,1]{1,0:T(8,128)S(1)} %get-tuple-element.119.inv_one) | copy-start | bytes 6148
  88.1 94.2 %copy-start.19 = (bf16[1024,512]{1,0:T(8,128)(2,1)}, bf16[1024,512]{1,0:T(8,128)(2,1)S(1)}, u32[]{:S(2)}) copy-start(bf16[1024,512]{1,0:T(8,128)(2,1)S(1)} %get-tuple-element.122.keys) | copy-start | bytes 3145732
  88.1 94.2 %copy-start.20 = (bf16[1024,512]{1,0:T(8,128)(2,1)}, bf16[1024,512]{1,0:T(8,128)(2,1)S(1)}, u32[]{:S(2)}) copy-start(bf16[1024,512]{1,0:T(8,128)(2,1)S(1)} %get-tuple-element.123.values) | copy-start | bytes 3145732
  88.1 94.2 %copy-start.24 = (bf16[512,512]{1,0:T(8,128)(2,1)}, bf16[512,512]{1,0:T(8,128)(2,1)S(1)}, u32[]{:S(2)}) copy-start(bf16[512,512]{1,0:T(8,128)(2,1)S(1)} %get-tuple-element.121.query) | copy-start | bytes 1572868
  88.1 94.2 %copy-start.26 = (f32[512,4]{1,0:T(8,128)}, f32[512,4]{1,0:T(8,128)S(1)}, u32[]{:S(2)}) copy-start(f32[512,4]{1,0:T(8,128)S(1)} %get-tuple-element.124.lse) | copy-start | bytes 24580
  88.1 94.2 %copy-start.27 = (f32[512,1]{1,0:T(8,128)}, f32[512,1]{1,0:T(8,128)S(1)}, u32[]{:S(2)}) copy-start(f32[512,1]{1,0:T(8,128)S(1)} %get-tuple-element.125.query_seg) | copy-start | bytes 6148
  88.1 94.2 %copy-start.28 = (f32[512,128]{1,0:T(8,128)}, f32[512,128]{1,0:T(8,128)S(1)}, u32[]{:S(2)}) copy-start(f32[512,128]{1,0:T(8,128)S(1)} %get-tuple-element.127.cos) | copy-start | bytes 786436
  88.1 94.2 %copy-start.29 = (f32[512,128]{1,0:T(8,128)}, f32[512,128]{1,0:T(8,128)S(1)}, u32[]{:S(2)}) copy-start(f32[512,128]{1,0:T(8,128)S(1)} %get-tuple-element.128.sin) | copy-start | bytes 786436
  88.1 94.2 %copy-start.35 = (f32[1,1024]{1,0:T(1,128)}, f32[1,1024]{1,0:T(1,128)S(1)}, u32[]{:S(2)}) copy-start(f32[1,1024]{1,0:T(1,128)S(1)} %get-tuple-element.126.key_seg) | copy-start | bytes 12292
  88.2 3.2 copy-start
  176.7 1.0 copy-start.10
  177.7 0.7 copy-start.16
  178.4 1.0 copy-start.21
  179.4 0.8 copy-start.25
  180.2 0.7 copy-start.30
  180.9 0.7 copy-start.31
  181.6 0.7 copy-start.32
  213.2 1.8 copy-start.4
  215.1 7.2 copy-start.1
  215.1 7.2 copy-start.7
  222.2 3.8 copy-start.43
  222.2 10.8 %collective-permute-start = (bf16[1024,2816]{1,0:T(8,128)(2,1)}, bf16[1024,2816]{1,0:T(8,128)(2,1)}, u32[]{:S(2)}, u32[]{:S(2)}) collective-permute-start(bf16[1024,2816]{1,0:T(8,128)(2,1)} %shard_map.309), channel_id=1, source_target_pairs={{0,8},{8,0},{16,24},{24,16},{1,9},{9,1},{17,25},{25,17},{2,10},{10... | collective-permute-start | bytes 17301512 | tf_op jit(solution)/shard_map/ppermute | solution.py:34
  225.5 18.1 %collective-permute-start.1 = (bf16[1408,1024]{1,0:T(8,128)(2,1)}, bf16[1408,1024]{1,0:T(8,128)(2,1)}, u32[]{:S(2)}, u32[]{:S(2)}) collective-permute-start(bf16[1408,1024]{1,0:T(8,128)(2,1)} %shard_map.310), channel_id=1, source_target_pairs={{0,8},{8,0},{16,24},{24,16},{1,9},{9,1},{17,25},{25,17},{2,10},{10... | collective-permute-start | bytes 8650760 | tf_op jit(solution)/shard_map/ppermute | solution.py:34
  226.0 1.6 copy-start.22
  226.0 2.6 copy-start.39
  226.0 5.3 copy-start.44
  233.1 1.8 copy-start.5
  320.8 5.1 copy-start.37
  320.8 5.1 copy-start.38
  673.4 4.3 copy-start.2
  677.7 11.8 %slice-start.4 = ((s8[6291456]{0:T(1024)(128)(4,1)}), s8[4194304]{0:T(1024)(128)(4,1)S(1)}, s32[]{:S(2)}) async-start(s8[6291456]{0:T(1024)(128)(4,1)} %bitcast.44), calls=%async_computation.4 | async-start | bytes 8388608
  682.8 6.7 slice-start.5
  687.3 7.4 %copy-start.15 = (bf16[2,2,2,128,1024]{4,3,2,1,0:T(8,128)(2,1)S(1)}, bf16[2,2,2,128,1024]{4,3,2,1,0:T(8,128)(2,1)}, u32[]{:S(2)}) copy-start(bf16[2,2,2,128,1024]{4,3,2,1,0:T(8,128)(2,1)} %get-tuple-element.138) | copy-start | bytes 6291460
  694.8 16.2 %slice-start.2 = ((s8[5767168]{0:T(1024)(128)(4,1)}), s8[1572864]{0:T(1024)(128)(4,1)S(1)}, s32[]{:S(2)}) async-start(s8[5767168]{0:T(1024)(128)(4,1)} %bitcast.41), calls=%async_computation.2 | async-start | bytes 3145728
  697.6 4.3 copy-start.3
  701.9 9.1 %slice-start.3 = ((s8[5767168]{0:T(1024)(128)(4,1)}), s8[4194304]{0:T(1024)(128)(4,1)S(1)}, s32[]{:S(2)}) async-start(s8[5767168]{0:T(1024)(128)(4,1)} %bitcast.41), calls=%async_computation.3 | async-start | bytes 8388608
  701.9 14.3 %slice-start = ((s8[5767168]{0:T(1024)(128)(4,1)}), s8[1572864]{0:T(1024)(128)(4,1)S(1)}, s32[]{:S(2)}) async-start(s8[5767168]{0:T(1024)(128)(4,1)} %bitcast.38), calls=%async_computation | async-start | bytes 3145728
  711.0 5.1 slice-start.1
  716.1 5.3 copy-start.9
  716.1 5.3 copy-start.11
  716.1 5.3 copy-start.40
  716.2 5.3 copy-start.41
  716.2 5.3 copy-start.42

commit v8 on v7

--- a/solution.py
+++ b/solution.py
@@ -465,7 +465,6 @@
         turned = grad_q * cos[...] + pltpu.roll(grad_q, HD // 2, 1) * sin[...]
         grad_qkv[:, own] = turned.astype(BF16)
 
-    d1 = there(sgu_f.at[core, y, 1 - x], sgu_f.at[core, y, 1 - x], to_y)
     load_attn.wait()
     half_of = low.shape[1] // 2
     w_sent[...] = mm_tn(attn_v[...], low[:, pl.ds(pl.multiple_of((1 - core) * half_of, half_of), half_of)]).astype(BF16)
@@ -520,6 +519,7 @@
         here_rows = slice(i * step, (i + 1) * step)
         q_half[here_rows, :] = (value + q_half[here_rows, :].astype(F32)).astype(BF16)
     a1 = there(q_half.at[pl.ds((1 - y) * q_rows, q_rows)], q_in, to_y)
+    d1 = there(sgu_f.at[core, y, 1 - x], sgu_f.at[core, y, 1 - x], to_y)
     for copy in loads:
         copy.wait()
     grad_normed[...] = (
@@ -801,15 +801,18 @@
             for copy in copies:
                 copy.start()
 
-    @pl.when(pl.program_id(0) == 0)
-    def _():
-        for copy in weights:
-            copy.wait()
-
+    def stored_is_here(m):
+        @pl.when(pl.program_id(0) == 0)
+        def _():
+            weights[m].wait()
+
+    stored_is_here(0)
     width = down_w.shape[0]
     to, back = (mm_nt, mm) if flipped else (mm, mm_nt)
     gate_pre = to(rows[...], gate_w[...])
+    stored_is_here(1)
     up_pre = to(rows[...], up_w[...])
+    stored_is_here(2)
     grad_hidden = mm_nt(grads[...], down_w[...])
     sig = 1.0 / (1.0 + jnp.exp(-gate_pre))
     act = gate_pre * sig

time: 729 us -> 726 us (level)
  no operation moved by 1% of the time
where the time goes in v8:
time: 726 us; the launch traced here: 721 us
  Pallas kernels  664 us (91%)
  local copies, waits for them, and re-layouts  42.2 us (6%)
  other arithmetic  13.1 us (2%)
    pallas_call x1, Pallas kernels, tail(): pl.pallas_call(functools.partial(tail_kernel, 1.0 / math.sqrt(HD)), out_s...  220 us
    pallas_call x1, Pallas kernels, resid_grad(): pl.pallas_call(functools.partial(resid_grad_kernel, chunks, step, depth,...  120 us
    pallas_call x2, Pallas kernels, ffn(): pl.pallas_call(functools.partial(ffn_kernel, groups, bool(base), flipped,...  99 us
    pallas_call x1, Pallas kernels, attend_out(): pl.pallas_call(functools.partial(attend_out_kernel, chunks, step, depth,...  85.2 us
    pallas_call x1, Pallas kernels, front(): pl.pallas_call(functools.partial(front_kernel, 1.0 / math.sqrt(HD), chunk...  78.8 us
    pallas_call x7, Pallas kernels, widen(): pl.pallas_call(widen_kernel, grid=grid, in_specs=[source], out_specs=spec...  36.6 us
    unnamed x104, local copies, waits for them, and re-layouts  29.1 us
    pallas_call x4, Pallas kernels, weight_half(): pl.pallas_call(functools.partial(weight_kernel, bool(extra)), grid_spec=p...  24.3 us
  transfers between devices with their start and end apart: 2, of which 0 were waited for; matrix products, arithmetic and copies ran while one was open for 1% of the time, Pallas kernels for 2%

profile of v8, /device:TPU:0, one launch (start us, length us, event | category | flops | bytes accessed | tf_op | source)
XLA Modules:
  0.0 721.1 jit_solution(5709598723543058779)
XLA Ops:
  0.7 0.8 stack.10
  1.5 0.7 stack.9
  2.2 0.7 broadcast_in_dim.10
  2.9 0.1 pad.9.clone
  3.0 0.8 maximum_maximum_fusion.w_small
  3.8 0.0 copy-start.8
  3.8 1.1 copy-done.8
  4.9 1.0 copy-done.12
  5.9 0.7 copy-done.33
  6.6 0.7 copy-done.34
  7.3 0.7 copy-done.36
  8.0 78.8 %shard_map.306 = (bf16[512,2048]{1,0:T(8,128)(2,1)S(1)}, bf16[512,2048]{1,0:T(8,128)(2,1)S(1)}, f32[512,1]{1,0:T(8,128)S(1)}, f32[1,2048]{1,0:T(1,128)S(1)}, bf1...) custom-call(bf16[512,512]{1,0:T(8,128)(2,1)S(1)} %copy-done.8, ...), custom_call_target="tpu_custom_call" | custom-call | tf_op jit(solution)/shard_map/pallas_call | solution.py:354
  86.7 0.0 copy-start.14
  86.8 1.3 copy-done.14
  88.1 0.0 copy-start.24
  88.2 3.1 copy-done
  91.3 85.2 %shard_map.307 = (bf16[1024,2048]{1,0:T(8,128)(2,1)}, f32[512,512]{1,0:T(8,128)S(1)}, f32[512,1]{1,0:T(8,128)S(1)}, bf16[256,2048]{1,0:T(8,128)(2,1)S(1)}, f32[5...) custom-call(bf16[512,512]{1,0:T(8,128)(2,1)S(1)} %get-tuple-element.81.attn, ...), custom_call_target="tpu_custom_call" | custom-call | tf_op jit(solution)/shard_map/pallas_call | solution.py:1181
  176.6 1.0 copy-done.10
  177.5 0.7 copy-done.16
  178.2 1.0 copy-done.21
  179.2 0.8 copy-done.25
  180.0 0.7 copy-done.30
  180.7 0.7 copy-done.31
  181.4 0.7 copy-done.32
  182.2 28.8 %shard_map.308 = (bf16[512,1408]{1,0:T(8,128)(2,1)}, bf16[512,2816]{1,0:T(8,128)(2,1)}, bf16[512,2048]{1,0:T(8,128)(2,1)}, bf16[512,2048]{1,0:T(8,128)(2,1)}, f3...) custom-call(bf16[1024,2048]{1,0:T(8,128)(2,1)} %get-tuple-element.88.refs_0_.left.both, ...), custom_call_target="tpu_custom_call" | custom-call | tf_op jit(solution)/shard_map/pallas_call | solution.py:874
  211.0 1.8 copy-done.4
  212.8 7.1 shard_map.309
  220.0 3.3 shard_map.310
  223.3 0.5 collective-permute-start.1
  223.8 1.5 constant_dynamic-update-slice_fusion.2
  225.3 0.1 copy-done.22
  225.4 1.0 constant_dynamic-update-slice_fusion.1
  226.4 1.0 constant_dynamic-update-slice_fusion.refs_1_.both_grad
  227.4 1.7 copy.41
  229.1 0.6 reshape_convert_fusion.gain
  229.7 1.2 fusion.3
  230.9 1.8 copy-done.5
  232.7 8.7 %shard_map.311.refs_8_ = bf16[1024,2816]{1,0:T(8,128)(2,1)} custom-call(s32[1]{0:T(128)} %bitcast.3.part, bf16[1024,2048]{1,0:T(8,128)(2,1)} %get-tuple-element.88.refs_0_.left.both, bf16[512,2816]{1,0:T(8,128)(2,1)S(1)} %copy-done.5, bf16[1024,2816]{1,0:T(8,128)(2,1)} %collective-permute-done.refs_0_), custom_call_target="tpu_custom_call" | custom-call | tf_op jit(solution)/shard_map/pallas_call | solution.py:749
  241.4 5.1 shard_map.312.refs_9_
  246.6 70.2 %shard_map.313 = (bf16[1024,1408]{1,0:T(8,128)(2,1)}, bf16[1024,2816]{1,0:T(8,128)(2,1)}, bf16[1024,2048]{1,0:T(8,128)(2,1)}, bf16[1024,2048]{1,0:T(8,128)(2,1)}...) custom-call(bf16[1024,2048]{1,0:T(8,128)(2,1)} %get-tuple-element.88.refs_0_.left.both, ...), custom_call_target="tpu_custom_call" | custom-call | tf_op jit(solution)/shard_map/pallas_call | solution.py:874
  316.7 1.2 copy.40
  318.0 0.6 fusion.4
  318.6 5.1 add_convert_fusion.sgu
  323.7 1.7 add_convert_fusion.1.sd
  325.4 120.1 %shard_map.314 = (bf16[512,2048]{1,0:T(8,128)(2,1)}, f32[512,512]{1,0:T(8,128)}, f32[1,512]{1,0:T(1,128)}, bf16[2816,1024]{1,0:T(8,128)(2,1)}, bf16[2,2,1408,512...) custom-call(bf16[1024,2048]{1,0:T(8,128)(2,1)} %get-tuple-element.10, ...), custom_call_target="tpu_custom_call" | custom-call | tf_op jit(solution)/shard_map/pallas_call | solution.py:1455
  445.5 0.9 reshape.110
  446.4 1.3 maximum_bitcast_fusion.flat
  447.8 220.0 %shard_map.315 = (bf16[2,2,2,256,2816]{4,3,2,1,0:T(8,128)(2,1)}, bf16[2,2,2,352,1024]{4,3,2,1,0:T(8,128)(2,1)}, bf16[2,2,1408,1024]{3,2,1,0:T(8,128)(2,1)}, bf16...) custom-call(bf16[2,2,2,256,2816]{4,3,2,1,0:T(8,128)(2,1)} %get-tuple, ...), custom_call_target="tpu_custom_call", output_to_operand_aliasing={{0}: (0, {}), {1}: (1, {}), {3}: (3, {})} | custom-call | tf_op jit(solution)/shard_map/pallas_call | solution.py:650
  667.8 1.2 slice_bitcast_fusion.1
  669.0 0.9 slice.38
  669.9 1.3 slice_bitcast_fusion
  671.2 4.3 copy-done.2
  675.5 5.1 shard_map.320
  680.6 4.5 shard_map.321
  685.2 0.9 slice_multiply_fusion
  686.0 1.3 slice.35
  687.3 5.3 shard_map.316
  692.6 2.1 shard_map.317
  694.8 0.6 reshape.114
  695.4 4.3 copy-done.3
  699.7 9.1 %shard_map.318 = (f32[2048,1408]{1,0:T(8,128)}, f32[2048,1408]{1,0:T(8,128)}) custom-call(bf16[2048,2816]{1,0:T(8,128)(2,1)S(1)} %bitcast.37), custom_call_target="tpu_custom_call" | custom-call | tf_op jit(solution)/shard_map/pallas_call | solution.py:714
  708.8 5.1 shard_map.319
  714.0 5.3 shard_map.322
  719.3 1.5 multiply_subtract_fusion
  (89 shorter events, 0.2 us)
Async XLA Ops:
  0.6 87.5 %copy-start.6 = (bf16[512,2048]{1,0:T(8,128)(2,1)S(1)}, bf16[512,2048]{1,0:T(8,128)(2,1)}, u32[]{:S(2)}) copy-start(bf16[512,2048]{1,0:T(8,128)(2,1)} %w_out.3) | copy-start | bytes 6291460
  3.8 172.7 %copy-start.23 = (bf16[16,2048]{1,0:T(8,128)(2,1)}, bf16[16,2048]{1,0:T(8,128)(2,1)S(1)}, u32[]{:S(2)}) copy-start(bf16[16,2048]{1,0:T(8,128)(2,1)S(1)} %maximum_maximum_fusion.w_small) | copy-start | bytes 196612
  3.8 1.1 copy-start.8
  4.9 1.0 copy-start.12
  5.9 0.7 copy-start.33
  6.6 0.7 copy-start.34
  7.3 0.7 copy-start.36
  86.7 1.3 copy-start.14
  88.1 88.5 %copy-start.13 = (bf16[512,512]{1,0:T(8,128)(2,1)}, bf16[512,512]{1,0:T(8,128)(2,1)S(1)}, u32[]{:S(2)}) copy-start(bf16[512,512]{1,0:T(8,128)(2,1)S(1)} %get-tuple-element.81.attn) | copy-start | bytes 1572868
  88.1 94.1 %copy-start.17 = (f32[512,16]{1,0:T(8,128)}, f32[512,16]{1,0:T(8,128)S(1)}, u32[]{:S(2)}) copy-start(f32[512,16]{1,0:T(8,128)S(1)} %get-tuple-element.85.hot) | copy-start | bytes 98308
  88.1 94.1 %copy-start.18 = (f32[512,1]{1,0:T(8,128)}, f32[512,1]{1,0:T(8,128)S(1)}, u32[]{:S(2)}) copy-start(f32[512,1]{1,0:T(8,128)S(1)} %get-tuple-element.119.inv_one) | copy-start | bytes 6148
  88.1 94.1 %copy-start.19 = (bf16[1024,512]{1,0:T(8,128)(2,1)}, bf16[1024,512]{1,0:T(8,128)(2,1)S(1)}, u32[]{:S(2)}) copy-start(bf16[1024,512]{1,0:T(8,128)(2,1)S(1)} %get-tuple-element.122.keys) | copy-start | bytes 3145732
  88.1 94.1 %copy-start.20 = (bf16[1024,512]{1,0:T(8,128)(2,1)}, bf16[1024,512]{1,0:T(8,128)(2,1)S(1)}, u32[]{:S(2)}) copy-start(bf16[1024,512]{1,0:T(8,128)(2,1)S(1)} %get-tuple-element.123.values) | copy-start | bytes 3145732
  88.1 94.1 %copy-start.24 = (bf16[512,512]{1,0:T(8,128)(2,1)}, bf16[512,512]{1,0:T(8,128)(2,1)S(1)}, u32[]{:S(2)}) copy-start(bf16[512,512]{1,0:T(8,128)(2,1)S(1)} %get-tuple-element.121.query) | copy-start | bytes 1572868
  88.1 94.1 %copy-start.26 = (f32[512,4]{1,0:T(8,128)}, f32[512,4]{1,0:T(8,128)S(1)}, u32[]{:S(2)}) copy-start(f32[512,4]{1,0:T(8,128)S(1)} %get-tuple-element.124.lse) | copy-start | bytes 24580
  88.1 94.1 %copy-start.27 = (f32[512,1]{1,0:T(8,128)}, f32[512,1]{1,0:T(8,128)S(1)}, u32[]{:S(2)}) copy-start(f32[512,1]{1,0:T(8,128)S(1)} %get-tuple-element.125.query_seg) | copy-start | bytes 6148
  88.1 94.1 %copy-start.28 = (f32[512,128]{1,0:T(8,128)}, f32[512,128]{1,0:T(8,128)S(1)}, u32[]{:S(2)}) copy-start(f32[512,128]{1,0:T(8,128)S(1)} %get-tuple-element.127.cos) | copy-start | bytes 786436
  88.1 94.1 %copy-start.29 = (f32[512,128]{1,0:T(8,128)}, f32[512,128]{1,0:T(8,128)S(1)}, u32[]{:S(2)}) copy-start(f32[512,128]{1,0:T(8,128)S(1)} %get-tuple-element.128.sin) | copy-start | bytes 786436
  88.1 94.1 %copy-start.35 = (f32[1,1024]{1,0:T(1,128)}, f32[1,1024]{1,0:T(1,128)S(1)}, u32[]{:S(2)}) copy-start(f32[1,1024]{1,0:T(1,128)S(1)} %get-tuple-element.126.key_seg) | copy-start | bytes 12292
  88.2 3.2 copy-start
  176.6 1.0 copy-start.10
  177.5 0.7 copy-start.16
  178.2 1.0 copy-start.21
  179.2 0.8 copy-start.25
  180.0 0.7 copy-start.30
  180.7 0.7 copy-start.31
  181.4 0.7 copy-start.32
  211.0 1.8 copy-start.4
  212.8 7.2 copy-start.1
  212.8 7.2 copy-start.7
  220.0 3.8 copy-start.43
  220.0 10.8 %collective-permute-start = (bf16[1024,2816]{1,0:T(8,128)(2,1)}, bf16[1024,2816]{1,0:T(8,128)(2,1)}, u32[]{:S(2)}, u32[]{:S(2)}) collective-permute-start(bf16[1024,2816]{1,0:T(8,128)(2,1)} %shard_map.309), channel_id=1, source_target_pairs={{0,8},{8,0},{16,24},{24,16},{1,9},{9,1},{17,25},{25,17},{2,10},{10... | collective-permute-start | bytes 17301512 | tf_op jit(solution)/shard_map/ppermute | solution.py:34
  223.3 18.1 %collective-permute-start.1 = (bf16[1408,1024]{1,0:T(8,128)(2,1)}, bf16[1408,1024]{1,0:T(8,128)(2,1)}, u32[]{:S(2)}, u32[]{:S(2)}) collective-permute-start(bf16[1408,1024]{1,0:T(8,128)(2,1)} %shard_map.310), channel_id=1, source_target_pairs={{0,8},{8,0},{16,24},{24,16},{1,9},{9,1},{17,25},{25,17},{2,10},{10... | collective-permute-start | bytes 8650760 | tf_op jit(solution)/shard_map/ppermute | solution.py:34
  223.8 1.6 copy-start.22
  223.8 2.6 copy-start.39
  223.8 5.3 copy-start.44
  230.9 1.8 copy-start.5
  318.6 5.1 copy-start.37
  318.6 5.1 copy-start.38
  671.2 4.3 copy-start.2
  675.5 11.8 %slice-start.4 = ((s8[6291456]{0:T(1024)(128)(4,1)}), s8[4194304]{0:T(1024)(128)(4,1)S(1)}, s32[]{:S(2)}) async-start(s8[6291456]{0:T(1024)(128)(4,1)} %bitcast.44), calls=%async_computation.4 | async-start | bytes 8388608
  680.6 6.7 slice-start.5
  685.2 7.4 %copy-start.15 = (bf16[2,2,2,128,1024]{4,3,2,1,0:T(8,128)(2,1)S(1)}, bf16[2,2,2,128,1024]{4,3,2,1,0:T(8,128)(2,1)}, u32[]{:S(2)}) copy-start(bf16[2,2,2,128,1024]{4,3,2,1,0:T(8,128)(2,1)} %get-tuple-element.138) | copy-start | bytes 6291460
  692.6 16.2 %slice-start.2 = ((s8[5767168]{0:T(1024)(128)(4,1)}), s8[1572864]{0:T(1024)(128)(4,1)S(1)}, s32[]{:S(2)}) async-start(s8[5767168]{0:T(1024)(128)(4,1)} %bitcast.41), calls=%async_computation.2 | async-start | bytes 3145728
  695.4 4.3 copy-start.3
  699.7 9.1 %slice-start.3 = ((s8[5767168]{0:T(1024)(128)(4,1)}), s8[4194304]{0:T(1024)(128)(4,1)S(1)}, s32[]{:S(2)}) async-start(s8[5767168]{0:T(1024)(128)(4,1)} %bitcast.41), calls=%async_computation.3 | async-start | bytes 8388608
  699.7 14.3 %slice-start = ((s8[5767168]{0:T(1024)(128)(4,1)}), s8[1572864]{0:T(1024)(128)(4,1)S(1)}, s32[]{:S(2)}) async-start(s8[5767168]{0:T(1024)(128)(4,1)} %bitcast.38), calls=%async_computation | async-start | bytes 3145728
  708.8 5.1 slice-start.1
  714.0 5.3 copy-start.9
  714.0 5.3 copy-start.11
  714.0 5.3 copy-start.40
  714.0 5.3 copy-start.41
  714.0 5.3 copy-start.42
